TPU v7x, 32 devices: a whole 2x2x4 slice. The times are simulated.
32 devices in a mesh: group: 8 (over z, x), rep: 4 (over y, core).
Axes of the slice: x: 2, y: 2, z: 4, core: 2. Of those that a mesh axis runs over, the one named last changes fastest.
Arguments:
- inputs: bfloat16 [16384, 1024], P(('group', 'rep')), may hold values from -6 to 6
- lengths: int32 [32, 4], P(('group', 'rep')), may hold values from 1 to 250, 512 in all within a row
- ln1_gain: bfloat16 [1024], P(('group', 'rep')), may hold values from 0.5 to 1.5
- ln1_bias: bfloat16 [1024], P(('group', 'rep')), may hold values from -1.796875 to 1.796875
- w_qkv: bfloat16 [1024, 3072], P(('group', 'rep')), may hold values from -0.1875 to 0.1875
- w_out: bfloat16 [1024, 1024], P(('group', 'rep')), may hold values from -0.5 to 0.5
- scale_attn: bfloat16 [1024], P(('group', 'rep')), may hold values from 0.5 to 1.5
- ln2_gain: bfloat16 [1024], P(('group', 'rep')), may hold values from 0.5 to 1.5
- ln2_bias: bfloat16 [1024], P(('group', 'rep')), may hold values from -1.796875 to 1.796875
- w_gate: bfloat16 [1024, 4096], P(('group', 'rep')), may hold values from -0.1875 to 0.1875
- w_up: bfloat16 [1024, 4096], P(('group', 'rep')), may hold values from -0.1875 to 0.1875
- w_down: bfloat16 [4096, 1024], P(('group', 'rep')), may hold values from -0.125 to 0.125
- scale_mlp: bfloat16 [1024], P(('group', 'rep')), may hold values from 0.5 to 1.5
- grad_out: bfloat16 [16384, 1024], P(('group', 'rep')), may hold values from -6 to 6
Outputs:
- block_out: bfloat16 [16384, 1024], P(('group', 'rep'))
- input_grad: float32 [16384, 1024], P(('group', 'rep'))
- ln1_gain_grad: float32 [1024], P('group')
- ln1_bias_grad: float32 [1024], P('group')
- w_qkv_grad: float32 [1024, 3072], P('group')
- w_out_grad: float32 [1024, 1024], P('group')
- scale_attn_grad: float32 [1024], P('group')
- ln2_gain_grad: float32 [1024], P('group')
- ln2_bias_grad: float32 [1024], P('group')
- w_gate_grad: float32 [1024, 4096], P('group')
- w_up_grad: float32 [1024, 4096], P('group')
- w_down_grad: float32 [4096, 1024], P('group')
- scale_mlp_grad: float32 [1024], P('group')
Inputs may be any that keep to these rules, and one draw needn't show every extreme that they name: Each row of lengths holds one device's clips: 4 lengths that sum to 512, the longest exactly 250.
All inputs are finite; a program needn't handle non-finite values.
Results may differ from a plain program's by a relative error of at most 0.017.
Values may be sent and summed in bfloat16 or wider, within the bound.
No kernel may reach another device: no remote copies, remote signals or barrier semaphores. Data moves between devices by JAX's collectives and lax.ppermute only.
A program may use at most 192 MiB of HBM per device.

v0:
```python
import math

import jax
import jax.numpy as jnp
from jax import lax
from jax.sharding import PartitionSpec as P

HEADS = 16
WINDOW = 128


EPS = 1e-05


def clip_layout(length_row, count):
    clip_ends = jnp.cumsum(length_row)
    clip_starts = clip_ends - length_row
    row_index = jnp.arange(count, dtype=jnp.int32)
    segment = jnp.sum((row_index[:, None] >= clip_ends[None, :]).astype(jnp.int32), axis=1)
    member = (segment[:, None] == jnp.arange(length_row.shape[0], dtype=jnp.int32)[None, :]).astype(
        jnp.int32
    )
    position = row_index - jnp.sum(member * clip_starts[None, :], axis=1)
    return (segment, position)


def rotary_tables(position, width):
    half = width // 2
    freqs = jnp.power(10000.0, -jnp.arange(half, dtype=jnp.float32) * (2.0 / width))
    angles = position.astype(jnp.float32)[:, None] * freqs[None, :]
    cosine = jnp.concatenate([jnp.cos(angles), jnp.cos(angles)], axis=1)
    sine = jnp.concatenate([jnp.sin(angles), jnp.sin(angles)], axis=1)
    return (cosine[:, None, :], sine[:, None, :])


def rotate(values, cosine, sine):
    half = values.shape[-1] // 2
    turned = jnp.concatenate([-values[..., half:], values[..., :half]], axis=-1)
    return values * cosine + turned * sine


def rotate_back(values, cosine, sine):
    half = values.shape[-1] // 2
    turned = jnp.concatenate([values[..., half:], -values[..., :half]], axis=-1)
    return values * cosine + turned * sine


def norm_parts(values):
    mean_value = jnp.mean(values, axis=-1, keepdims=True)
    centered = values - mean_value
    variance = jnp.mean(centered * centered, axis=-1, keepdims=True)
    inverse = lax.rsqrt(variance + EPS)
    return (centered * inverse, inverse)


def norm_back(grad_normed, unit, inverse, gain):
    scaled = grad_normed * gain
    return inverse * (
        scaled
        - jnp.mean(scaled, axis=-1, keepdims=True)
        - unit * jnp.mean(scaled * unit, axis=-1, keepdims=True)
    )


def block_allowed(segment, segment_pad, start, block, window):
    query_index = start + jnp.arange(block, dtype=jnp.int32)
    key_index = start - window + jnp.arange(block + window, dtype=jnp.int32)
    offset = query_index[:, None] - key_index[None, :]
    same_clip = segment[:, None] == segment_pad[None, :]
    return same_clip & (offset >= 0) & (offset < window)


def pad_front(values, window, fill):
    front = jnp.full((window,) + values.shape[1:], fill, values.dtype)
    return jnp.concatenate([front, values], axis=0)


def attention_forward(queries, keys_rot, values, segment, block, window):
    factor = 1.0 / math.sqrt(queries.shape[-1])
    keys_pad = pad_front(keys_rot, window, 0)
    values_pad = pad_front(values, window, 0)
    segment_pad = pad_front(segment, window, -1)
    allowed = block_allowed(segment, segment_pad, 0, block, window)
    scores = (
        jnp.einsum("qhd,khd->hqk", queries, keys_pad, preferred_element_type=jnp.float32) * factor
    )
    masked = jnp.where(allowed[None], scores, -jnp.inf)
    peak = jnp.max(masked, axis=-1, keepdims=True)
    expd = jnp.exp(masked - peak)
    totals = jnp.sum(expd, axis=-1, keepdims=True)
    probs = (expd / totals).astype(jnp.bfloat16)
    outputs = jnp.einsum("hqk,khd->qhd", probs, values_pad, preferred_element_type=jnp.float32)
    log_totals = [peak + jnp.log(totals)]
    return (outputs, log_totals)


def attention_backward(
    queries, keys_rot, values, grad_attended, log_totals, segment, block, window
):
    factor = 1.0 / math.sqrt(queries.shape[-1])
    keys_pad = pad_front(keys_rot, window, 0)
    values_pad = pad_front(values, window, 0)
    segment_pad = pad_front(segment, window, -1)
    grad_keys = jnp.zeros(keys_pad.shape, jnp.float32)
    grad_values = jnp.zeros(values_pad.shape, jnp.float32)
    allowed = block_allowed(segment, segment_pad, 0, block, window)
    scores = (
        jnp.einsum("qhd,khd->hqk", queries, keys_pad, preferred_element_type=jnp.float32) * factor
    )
    probs = jnp.where(
        allowed[None], jnp.exp(jnp.where(allowed[None], scores, -jnp.inf) - log_totals[0]), 0.0
    )
    probs_low = probs.astype(jnp.bfloat16)
    grad_probs = jnp.einsum(
        "qhd,khd->hqk", grad_attended, values_pad, preferred_element_type=jnp.float32
    )
    delta = jnp.sum(probs * grad_probs, axis=-1, keepdims=True)
    grad_scores = (probs * (grad_probs - delta)).astype(jnp.bfloat16)
    grad_queries = (
        jnp.einsum("hqk,khd->qhd", grad_scores, keys_pad, preferred_element_type=jnp.float32)
        * factor
    )
    key_part = (
        jnp.einsum("hqk,qhd->khd", grad_scores, queries, preferred_element_type=jnp.float32)
        * factor
    )
    value_part = jnp.einsum(
        "hqk,qhd->khd", probs_low, grad_attended, preferred_element_type=jnp.float32
    )
    grad_keys = grad_keys.at[0 : block + window].add(key_part)
    grad_values = grad_values.at[0 : block + window].add(value_part)
    return (grad_queries, grad_keys[window:], grad_values[window:])


def shards(
    inputs,
    lengths,
    ln1_gain,
    ln1_bias,
    w_qkv,
    w_out,
    scale_attn,
    ln2_gain,
    ln2_bias,
    w_gate,
    w_up,
    w_down,
    scale_mlp,
    grad_out,
):
    count, width = inputs.shape
    head_width = width // HEADS
    block = min(512, count)
    attn_shards = (ln1_gain, ln1_bias, w_qkv, w_out, scale_attn)
    mlp_shards = (ln2_gain, ln2_bias, w_gate, w_up, w_down, scale_mlp)
    attn_full = (
        lax.all_gather(attn_shards[0], ("group", "rep"), axis=0, tiled=True),
        lax.all_gather(attn_shards[1], ("group", "rep"), axis=0, tiled=True),
        lax.all_gather(attn_shards[2], ("group", "rep"), axis=0, tiled=True),
        lax.all_gather(attn_shards[3], ("group", "rep"), axis=0, tiled=True),
        lax.all_gather(attn_shards[4], ("group", "rep"), axis=0, tiled=True),
    )
    gain_one, bias_one, qkv_full, out_full, attn_scale = attn_full
    segment, position = clip_layout(lengths[0], count)
    cosine, sine = rotary_tables(position, head_width)
    frames = inputs.astype(jnp.float32)
    unit_one, inverse_one = norm_parts(frames)
    gain_one = gain_one.astype(jnp.float32)
    normed = (unit_one * gain_one + bias_one.astype(jnp.float32)).astype(jnp.bfloat16)
    projected = jnp.dot(normed, qkv_full, preferred_element_type=jnp.float32)
    queries = rotate(projected[:, :width].reshape(count, HEADS, head_width), cosine, sine).astype(
        jnp.bfloat16
    )
    keys_rot = rotate(
        projected[:, width : 2 * width].reshape(count, HEADS, head_width), cosine, sine
    ).astype(jnp.bfloat16)
    values = projected[:, 2 * width :].reshape(count, HEADS, head_width).astype(jnp.bfloat16)
    attended, log_totals = attention_forward(queries, keys_rot, values, segment, block, WINDOW)
    attended = attended.reshape(count, width).astype(jnp.bfloat16)
    branch = jnp.dot(attended, out_full, preferred_element_type=jnp.float32)
    attn_scale = attn_scale.astype(jnp.float32)
    middle = frames + attn_scale * branch
    mlp_full = (
        lax.all_gather(mlp_shards[0], ("group", "rep"), axis=0, tiled=True),
        lax.all_gather(mlp_shards[1], ("group", "rep"), axis=0, tiled=True),
        lax.all_gather(mlp_shards[2], ("group", "rep"), axis=0, tiled=True),
        lax.all_gather(mlp_shards[3], ("group", "rep"), axis=0, tiled=True),
        lax.all_gather(mlp_shards[4], ("group", "rep"), axis=0, tiled=True),
        lax.all_gather(mlp_shards[5], ("group", "rep"), axis=0, tiled=True),
    )
    gain_two, bias_two, gate_full, up_full, down_full, mlp_scale = mlp_full
    unit_two, inverse_two = norm_parts(middle)
    gain_two = gain_two.astype(jnp.float32)
    normed_two = (unit_two * gain_two + bias_two.astype(jnp.float32)).astype(jnp.bfloat16)
    gate = jnp.dot(normed_two, gate_full, preferred_element_type=jnp.float32)
    up_value = jnp.dot(normed_two, up_full, preferred_element_type=jnp.float32)
    sigmoid_gate = jax.nn.sigmoid(gate)
    silu_gate = gate * sigmoid_gate
    hidden = (silu_gate * up_value).astype(jnp.bfloat16)
    mlp = jnp.dot(hidden, down_full, preferred_element_type=jnp.float32)
    mlp_scale = mlp_scale.astype(jnp.float32)
    block_out = (middle + mlp_scale * mlp).astype(jnp.bfloat16)
    gain_two_b, bias_two_b, gate_back, up_back, down_back, scale_two_b = (
        lax.all_gather(mlp_shards[0], ("group", "rep"), axis=0, tiled=True),
        lax.all_gather(mlp_shards[1], ("group", "rep"), axis=0, tiled=True),
        lax.all_gather(mlp_shards[2], ("group", "rep"), axis=0, tiled=True),
        lax.all_gather(mlp_shards[3], ("group", "rep"), axis=0, tiled=True),
        lax.all_gather(mlp_shards[4], ("group", "rep"), axis=0, tiled=True),
        lax.all_gather(mlp_shards[5], ("group", "rep"), axis=0, tiled=True),
    )
    cotangent = grad_out.astype(jnp.float32)
    scale_mlp_grad = jnp.sum(cotangent * mlp, axis=0)
    grad_mlp = (mlp_scale * cotangent).astype(jnp.bfloat16)
    w_down_grad = jnp.einsum("tf,td->fd", hidden, grad_mlp, preferred_element_type=jnp.float32)
    grad_hidden = jnp.einsum("td,fd->tf", grad_mlp, down_back, preferred_element_type=jnp.float32)
    grad_gate = (
        grad_hidden * up_value * sigmoid_gate * (1.0 + gate * (1.0 - sigmoid_gate))
    ).astype(jnp.bfloat16)
    grad_up = (grad_hidden * silu_gate).astype(jnp.bfloat16)
    w_gate_grad = jnp.einsum("td,tf->df", normed_two, grad_gate, preferred_element_type=jnp.float32)
    w_up_grad = jnp.einsum("td,tf->df", normed_two, grad_up, preferred_element_type=jnp.float32)
    grad_normed_two = jnp.einsum(
        "tf,df->td", grad_gate, gate_back, preferred_element_type=jnp.float32
    ) + jnp.einsum("tf,df->td", grad_up, up_back, preferred_element_type=jnp.float32)
    ln2_gain_grad = jnp.sum(grad_normed_two * unit_two, axis=0)
    ln2_bias_grad = jnp.sum(grad_normed_two, axis=0)
    grad_middle = cotangent + norm_back(grad_normed_two, unit_two, inverse_two, gain_two)
    mlp_grads = (ln2_gain_grad, ln2_bias_grad, w_gate_grad, w_up_grad, w_down_grad, scale_mlp_grad)
    mlp_part = (
        lax.psum_scatter(mlp_grads[0], "group", scatter_dimension=0, tiled=True),
        lax.psum_scatter(mlp_grads[1], "group", scatter_dimension=0, tiled=True),
        lax.psum_scatter(mlp_grads[2], "group", scatter_dimension=0, tiled=True),
        lax.psum_scatter(mlp_grads[3], "group", scatter_dimension=0, tiled=True),
        lax.psum_scatter(mlp_grads[4], "group", scatter_dimension=0, tiled=True),
        lax.psum_scatter(mlp_grads[5], "group", scatter_dimension=0, tiled=True),
    )
    mlp_summed = (
        lax.psum(mlp_part[0].astype(jnp.bfloat16), "rep").astype(jnp.float32),
        lax.psum(mlp_part[1].astype(jnp.bfloat16), "rep").astype(jnp.float32),
        lax.psum(mlp_part[2].astype(jnp.bfloat16), "rep").astype(jnp.float32),
        lax.psum(mlp_part[3].astype(jnp.bfloat16), "rep").astype(jnp.float32),
        lax.psum(mlp_part[4].astype(jnp.bfloat16), "rep").astype(jnp.float32),
        lax.psum(mlp_part[5].astype(jnp.bfloat16), "rep").astype(jnp.float32),
    )
    gain_one_b, bias_one_b, qkv_back, out_back, scale_one_b = (
        lax.all_gather(attn_shards[0], ("group", "rep"), axis=0, tiled=True),
        lax.all_gather(attn_shards[1], ("group", "rep"), axis=0, tiled=True),
        lax.all_gather(attn_shards[2], ("group", "rep"), axis=0, tiled=True),
        lax.all_gather(attn_shards[3], ("group", "rep"), axis=0, tiled=True),
        lax.all_gather(attn_shards[4], ("group", "rep"), axis=0, tiled=True),
    )
    scale_attn_grad = jnp.sum(grad_middle * branch, axis=0)
    grad_branch = (attn_scale * grad_middle).astype(jnp.bfloat16)
    w_out_grad = jnp.einsum("td,te->de", attended, grad_branch, preferred_element_type=jnp.float32)
    grad_attended = jnp.einsum(
        "te,de->td", grad_branch, out_back, preferred_element_type=jnp.float32
    ).astype(jnp.bfloat16)
    grad_queries, grad_keys, grad_values = attention_backward(
        queries,
        keys_rot,
        values,
        grad_attended.reshape(count, HEADS, head_width),
        log_totals,
        segment,
        block,
        WINDOW,
    )
    grad_projected = jnp.concatenate(
        [
            rotate_back(grad_queries, cosine, sine).reshape(count, width),
            rotate_back(grad_keys, cosine, sine).reshape(count, width),
            grad_values.reshape(count, width),
        ],
        axis=1,
    ).astype(jnp.bfloat16)
    w_qkv_grad = jnp.einsum("td,te->de", normed, grad_projected, preferred_element_type=jnp.float32)
    grad_normed = jnp.einsum(
        "te,de->td", grad_projected, qkv_back, preferred_element_type=jnp.float32
    )
    ln1_gain_grad = jnp.sum(grad_normed * unit_one, axis=0)
    ln1_bias_grad = jnp.sum(grad_normed, axis=0)
    input_grad = grad_middle + norm_back(grad_normed, unit_one, inverse_one, gain_one)
    attn_grads = (ln1_gain_grad, ln1_bias_grad, w_qkv_grad, w_out_grad, scale_attn_grad)
    attn_part = (
        lax.psum_scatter(attn_grads[0], "group", scatter_dimension=0, tiled=True),
        lax.psum_scatter(attn_grads[1], "group", scatter_dimension=0, tiled=True),
        lax.psum_scatter(attn_grads[2], "group", scatter_dimension=0, tiled=True),
        lax.psum_scatter(attn_grads[3], "group", scatter_dimension=0, tiled=True),
        lax.psum_scatter(attn_grads[4], "group", scatter_dimension=0, tiled=True),
    )
    attn_summed = (
        lax.psum(attn_part[0].astype(jnp.bfloat16), "rep").astype(jnp.float32),
        lax.psum(attn_part[1].astype(jnp.bfloat16), "rep").astype(jnp.float32),
        lax.psum(attn_part[2].astype(jnp.bfloat16), "rep").astype(jnp.float32),
        lax.psum(attn_part[3].astype(jnp.bfloat16), "rep").astype(jnp.float32),
        lax.psum(attn_part[4].astype(jnp.bfloat16), "rep").astype(jnp.float32),
    )
    return (block_out, input_grad) + tuple(attn_summed) + tuple(mlp_summed)


def solution(mesh):
    in_specs = (
        P(("group", "rep"), None),
        P(("group", "rep"), None),
        P(("group", "rep")),
        P(("group", "rep")),
        P(("group", "rep"), None),
        P(("group", "rep"), None),
        P(("group", "rep")),
        P(("group", "rep")),
        P(("group", "rep")),
        P(("group", "rep"), None),
        P(("group", "rep"), None),
        P(("group", "rep"), None),
        P(("group", "rep")),
        P(("group", "rep"), None),
    )
    out_specs = (
        P(("group", "rep"), None),
        P(("group", "rep"), None),
        P("group"),
        P("group"),
        P("group", None),
        P("group", None),
        P("group"),
        P("group"),
        P("group"),
        P("group", None),
        P("group", None),
        P("group", None),
        P("group"),
    )
    return jax.shard_map(shards, mesh=mesh, in_specs=in_specs, out_specs=out_specs, check_vma=False)
```

profile of v0, /device:TPU:10, one launch (start us, length us, event | category | flops | bytes accessed | tf_op | source)
XLA Modules:
  0.0 1694.8 jit_solution(3430899315957201151)
XLA Ops:
  15.7 41.9 %all-reduce.16 = (bf16[1024]{0:T(1024)(128)(2,1)S(1)}, bf16[1024]{0:T(1024)(128)(2,1)S(1)}, bf16[1024]{0:T(1024)(128)(2,1)S(1)}, bf16[1024]{0:T(1024)(128)(2,1)S...) all-reduce(bf16[1024]{0:T(1024)(128)(2,1)S(1)} %dynamic-update-slic, ...), channel_id=1, replica_groups=mesh['group'=8,'rep'=4] {'group','rep'}, use_global_device_ids=true, to_apply=%add.5 | all-reduce | flops 6144 | bytes 24576
  62.0 19.8 %all-gather.6.cloned.1.call-done = bf16[1024,3072]{1,0:T(8,128)(2,1)} async-done(((bf16[32,3072]{1,0:T(8,128)(2,1)}), bf16[1024,3072]{1,0:T(8,128)(2,1)}) %all-gather.6.cloned.1.call-update) | async-done | bytes 6291472 | tf_op jit(solution)/shard_map/all_gather | solution.py:159
  81.8 5.8 fusion.68
  88.8 2.3 fusion.71
  91.1 1.9 copy.46
  93.0 2.3 copy.44
  95.3 2.9 copy.45
  98.2 2.3 slice_negate_fusion.2
  100.5 2.5 fusion.27
  103.0 5.8 fusion.1
  108.8 5.0 fusion
  113.9 2.3 copy-done
  116.1 8.0 fusion.33
  124.2 14.5 all-gather.8.cloned.1.call-done
  138.7 4.5 fusion.70
  146.0 73.0 %all-gather.12.cloned.1.call-done = bf16[1024,4096]{1,0:T(8,128)(2,1)} async-done(((bf16[32,4096]{1,0:T(8,128)(2,1)}), bf16[1024,4096]{1,0:T(8,128)(2,1)}) %all-gather.12.cloned.1.call-update) | async-done | bytes 8388624 | tf_op jit(solution)/shard_map/all_gather | solution.py:187
  219.0 11.4 fusion.75
  230.4 67.5 %all-gather.10.cloned.1.call-done = bf16[1024,4096]{1,0:T(8,128)(2,1)} async-done(((bf16[32,4096]{1,0:T(8,128)(2,1)}), bf16[1024,4096]{1,0:T(8,128)(2,1)}) %all-gather.10.cloned.1.call-update) | async-done | bytes 8388624 | tf_op jit(solution)/shard_map/all_gather | solution.py:186
  297.9 11.5 fusion.74
  309.4 67.4 %all-gather.14.cloned.1.call-done = bf16[4096,1024]{1,0:T(8,128)(2,1)} async-done(((bf16[128,1024]{1,0:T(8,128)(2,1)}), bf16[4096,1024]{1,0:T(8,128)(2,1)}) %all-gather.14.cloned.1.call-update) | async-done | bytes 8388624 | tf_op jit(solution)/shard_map/all_gather | solution.py:188
  376.8 16.7 multiply_convert_fusion.1
  393.5 10.6 fusion.76
  404.2 10.9 multiply_reduce_fusion.1
  415.1 9.8 fusion.21
  426.2 3.2 fusion.54
  429.5 3.9 convolution_convert_fusion
  434.9 10.9 fusion.34
  447.4 17.4 %multiply_reduce_fusion = (f32[16,512]{1,0:T(8,128)S(1)}, f32[16,512,640]{2,1,0:T(8,128)}) fusion(f32[16,512]{1,0:T(8,128)S(1)} %log_add_fusion, f32[16,512,640]{2,1,0:T(8,128)} %copy-done, pred[512,640]{1,0:T(8,128)(4,1)S(1)} %fusion.40, bf16[512,16,64]{0,2,1:T(8,128)(2,1)S(1)} %bitcast.67, bf16[512,16,64]{0,2,1:T(8,128)(2,1)S(1)} %bitcast.65), kind=kOutput, calls=%fused_computation.1 | convolution fusion | flops 702537728 | bytes 44433408 | tf_op jit(solution)/shard_map/qhd,khd->hqk/dot_general | solution.py:114
  464.8 15.1 multiply_convert_fusion
  480.0 3.3 bitcast_multiply_fusion
  489.9 9.9 fusion.48
  501.0 10.7 fusion.50
  512.9 10.4 fusion.78
  523.4 11.0 fusion.77
  538.1 192.9 %reduce-scatter.6.cloned.1.call-done = f32[128,3072]{1,0:T(8,128)} async-done(((f32[1024,3072]{1,0:T(8,128)}), f32[128,3072]{1,0:T(8,128)}) %reduce-scatter.6.cloned.1.call-update) | async-done | bytes 1572880 | tf_op jit(solution)/shard_map/reduce_scatter | solution.py:287
  730.9 2.4 convert_element_type.189
  733.4 283.8 %reduce-scatter.14.cloned.1.call-done = f32[512,1024]{1,0:T(8,128)} async-done(((f32[4096,1024]{1,0:T(8,128)}), f32[512,1024]{1,0:T(8,128)}) %reduce-scatter.14.cloned.1.call-update) | async-done | bytes 2097168 | tf_op jit(solution)/shard_map/reduce_scatter | solution.py:234
  1017.2 2.8 convert_element_type.203
  1020.0 282.8 %reduce-scatter.12.cloned.1.call-done = f32[128,4096]{1,0:T(8,128)} async-done(((f32[1024,4096]{1,0:T(8,128)}), f32[128,4096]{1,0:T(8,128)}) %reduce-scatter.12.cloned.1.call-update) | async-done | bytes 2097168 | tf_op jit(solution)/shard_map/reduce_scatter | solution.py:233
  1302.8 2.7 convert_element_type.201
  1305.5 283.2 %reduce-scatter.10.cloned.1.call-done = f32[128,4096]{1,0:T(8,128)} async-done(((f32[1024,4096]{1,0:T(8,128)}), f32[128,4096]{1,0:T(8,128)}) %reduce-scatter.10.cloned.1.call-update) | async-done | bytes 2097168 | tf_op jit(solution)/shard_map/reduce_scatter | solution.py:232
  1588.7 2.7 convert_element_type.199
  1591.5 9.2 fusion.18
  1600.7 30.5 %all-reduce.15 = (bf16[1024]{0:T(1024)(128)(2,1)S(1)}, bf16[1024]{0:T(1024)(128)(2,1)S(1)}, bf16[1024]{0:T(1024)(128)(2,1)S(1)}, bf16[1024]{0:T(1024)(128)(2,1)S...) all-reduce(f32[1024]{0:T(1024)S(1)} %get-tuple-element.55, ...), channel_id=2, replica_groups=mesh['group'=8,'rep'=4] {'group'}, use_global_device_ids=true, to_apply=%region_15.16.clone | all-reduce | flops 6144 | bytes 36864
  1631.6 5.6 all-reduce.17
  1640.3 3.7 fusion.17
  1644.0 34.8 %all-reduce.21.cloned.1.call-done = (bf16[128,3072]{1,0:T(8,128)(2,1)}, bf16[128,1024]{1,0:T(8,128)(2,1)}, bf16[128,4096]{1,0:T(8,128)(2,1)}, bf16[128,4096]{1,0:T(8,128)(2,1)}, bf16[512,1024]{1,0:T(8,128)(2,1)}) async-done(((bf16[128,3072]{1,0:T(8,128)(2,1)}, bf16[128,1024]{1,0:T(8,128)(2,1)}, bf16[128,4096]{1,0:T(8,128)(2,1)}, bf16[128,4096]{1,0:T(8,128)(2,1)}, bf16[512,1024]{1,0:T(8,128)(2,1)}), ...) | async-done | bytes 4194320 | tf_op jit(solution)/shard_map/psum | solution.py:294
  1680.7 2.4 convert_element_type.190
  (184 shorter events, 43.3 us)
Async XLA Ops:
  7.2 53.8 %copy-start.2 = (bf16[512,1024]{1,0:T(8,128)(2,1)S(1)}, bf16[512,1024]{1,0:T(8,128)(2,1)}, u32[]{:S(2)}) copy-start(bf16[512,1024]{1,0:T(8,128)(2,1)} %param.22) | copy-start | bytes 3145732
  7.2 74.7 %all-gather.6.cloned.1.call-start = ((), (), s32[]{:S(2)}) async-start(), calls=%async_computation.5 | async-start | bytes 6488064 | tf_op jit(solution)/shard_map/all_gather | solution.py:159
  7.9 130.8 %all-gather.8.cloned.1.call-start = ((), (), s32[]{:S(2)}) async-start(), calls=%async_computation.6 | async-start | bytes 2162688 | tf_op jit(solution)/shard_map/all_gather | solution.py:160
  8.7 210.3 %all-gather.12.cloned.1.call-start = ((), (), s32[]{:S(2)}) async-start(), calls=%async_computation.8 | async-start | bytes 8650752 | tf_op jit(solution)/shard_map/all_gather | solution.py:187
  9.4 288.5 %all-gather.10.cloned.1.call-start = ((), (), s32[]{:S(2)}) async-start(), calls=%async_computation.7 | async-start | bytes 8650752 | tf_op jit(solution)/shard_map/all_gather | solution.py:186
  10.0 366.8 %all-gather.14.cloned.1.call-start = ((), (), s32[]{:S(2)}) async-start(), calls=%async_computation.9 | async-start | bytes 8650752 | tf_op jit(solution)/shard_map/all_gather | solution.py:188
  10.6 525.7 %reduce-scatter.8.cloned.1.call-start = ((), (), s32[]{:S(2)}) async-start(), calls=%async_computation.11 | async-start | bytes 4718592 | tf_op jit(solution)/shard_map/reduce_scatter | solution.py:288
  57.5 30.1 %copy-start.36 = (f32[1024]{0:T(1024)}, f32[1024]{0:T(1024)S(1)}, u32[]{:S(2)}) copy-start(f32[1024]{0:T(1024)S(1)} %convert_element_type.160) | copy-start | bytes 12292
  57.5 30.1 %copy-start.29 = (f32[1024]{0:T(1024)}, f32[1024]{0:T(1024)S(1)}, u32[]{:S(2)}) copy-start(f32[1024]{0:T(1024)S(1)} %convert_element_type.159) | copy-start | bytes 12292
  61.2 26.5 %copy-start.27 = (f32[512]{0:T(512)}, f32[512]{0:T(512)S(1)}, u32[]{:S(2)}) copy-start(f32[512]{0:T(512)S(1)} %broadcast_multiply_fusion.6) | copy-start | bytes 6148
  61.6 26.0 %copy-start.33 = (f32[512]{0:T(512)}, f32[512]{0:T(512)S(1)}, u32[]{:S(2)}) copy-start(f32[512]{0:T(512)S(1)} %add_rsqrt_fusion.1) | copy-start | bytes 6148
  98.2 2.3 copy-start.1
  98.2 2.3 copy-start.12
  98.2 2.3 copy-start.14
  108.8 7.3 copy-start
  108.8 7.3 copy-start.20
  113.8 10.3 copy-start.25
  230.4 146.4 %copy-start.35 = (f32[1024]{0:T(1024)S(1)}, f32[1024]{0:T(1024)}, u32[]{:S(2)}) copy-start(f32[1024]{0:T(1024)} %convert_element_type.171) | copy-start | bytes 12292
  393.5 10.7 copy-start.9
  393.5 10.7 copy-start.32
  393.5 21.6 %slice-start = ((s8[8388608]{0:T(1024)(128)(4,1)}), s8[4194304]{0:T(1024)(128)(4,1)S(1)}, s32[]{:S(2)}) async-start(s8[8388608]{0:T(1024)(128)(4,1)} %bitcast.73), calls=%async_computation.16 | async-start | bytes 8388608
  404.1 10.9 copy-start.11
  404.1 10.9 slice-start.1
  404.2 10.9 copy-start.42
  415.1 11.1 copy-start.8
  424.9 1.3 copy-start.6
  426.2 3.2 copy-start.10
  434.8 296.1 %reduce-scatter.6.cloned.1.call-start = ((), (), s32[]{:S(2)}) async-start(), calls=%async_computation.10 | async-start | bytes 14155776 | tf_op jit(solution)/shard_map/reduce_scatter | solution.py:287
  445.8 1.6 copy-start.21
  464.8 15.1 copy-start.4
  487.5 2.4 copy-start.19
  487.5 2.4 copy-start.28
  487.5 2.4 copy-start.30
  487.5 2.4 copy-start.34
  487.5 2.4 copy-start.37
  488.5 1.3 copy-start.23
  499.8 517.4 %reduce-scatter.14.cloned.1.call-start = ((), (), s32[]{:S(2)}) async-start(), calls=%async_computation.14 | async-start | bytes 18874368 | tf_op jit(solution)/shard_map/reduce_scatter | solution.py:234
  511.7 791.1 %reduce-scatter.12.cloned.1.call-start = ((), (), s32[]{:S(2)}) async-start(), calls=%async_computation.13 | async-start | bytes 18874368 | tf_op jit(solution)/shard_map/reduce_scatter | solution.py:233
  523.3 1065.4 %reduce-scatter.10.cloned.1.call-start = ((), (), s32[]{:S(2)}) async-start(), calls=%async_computation.12 | async-start | bytes 18874368 | tf_op jit(solution)/shard_map/reduce_scatter | solution.py:232
  534.4 1144.4 %all-reduce.21.cloned.1.call-start = ((), (), s32[]{:S(2)}) async-start(), calls=%async_computation.15 | async-start | bytes 8388608 | tf_op jit(solution)/shard_map/psum | solution.py:294
  1591.4 9.2 copy-start.38
  1591.4 9.2 copy-start.39
  1591.4 9.2 copy-start.40
  1591.4 9.2 copy-start.41
  1591.5 48.9 %copy-start.7 = (f32[512,1024]{1,0:T(8,128)S(1)}, f32[512,1024]{1,0:T(8,128)}, u32[]{:S(2)}) copy-start(f32[512,1024]{1,0:T(8,128)} %copy-done.6) | copy-start | bytes 6291460
  1678.8 4.3 copy-start.18
  1683.1 1.5 copy-start.17
  1684.7 1.5 copy-start.16
  (10 other events, 9.6 us)
Sparse Core Ops, SparseCore 0:
  10.9 70.8 all-gather.5
  84.7 53.9 all-gather.7
  141.6 77.3 all-gather.11
  221.7 76.1 all-gather.9
  300.6 76.1 all-gather.13
  435.0 86.7 reduce-scatter.7
  525.7 205.1 reduce-scatter.5
  735.2 281.9 reduce-scatter.13
  1021.0 281.7 reduce-scatter.11
  1306.9 281.7 reduce-scatter.9
  1592.0 86.8 all-reduce.20
where the time goes:
time: 1710 us; the launch traced here: 1690 us
  waiting for transfers between devices  1320 us (77%)
  matrix products  187 us (11%)
  blocking collectives  78 us (5%)
  other arithmetic  60.9 us (4%)
  local copies, waits for them, and re-layouts  29.9 us (2%)
    reduce_scatter x1, waiting for transfers between devices, shards(): lax.psum_scatter(mlp_grads[4], 'group', scatter_dimension=0, tiled=True)  284 us
    reduce_scatter x1, waiting for transfers between devices, shards(): lax.psum_scatter(mlp_grads[2], 'group', scatter_dimension=0, tiled=True)  283 us
    reduce_scatter x1, waiting for transfers between devices, shards(): lax.psum_scatter(mlp_grads[3], 'group', scatter_dimension=0, tiled=True)  283 us
    reduce_scatter x1, waiting for transfers between devices, shards(): lax.psum_scatter(attn_grads[2], 'group', scatter_dimension=0, tiled=True)  193 us
    all_gather x1, waiting for transfers between devices, shards(): lax.all_gather(mlp_shards[3], ('group', 'rep'), axis=0, tiled=True)  73 us
    unnamed x2, blocking collectives  72.4 us
    all_gather x1, waiting for transfers between devices, shards(): lax.all_gather(mlp_shards[2], ('group', 'rep'), axis=0, tiled=True)  67.5 us
    all_gather x1, waiting for transfers between devices, shards(): lax.all_gather(mlp_shards[4], ('group', 'rep'), axis=0, tiled=True)  67.4 us
  transfers between devices with their start and end apart: 11, of which 10 were waited for; matrix products, arithmetic and copies ran while one was open for 12% of the time, Pallas kernels for 0%

commit v1 on v0

v1 whole, which is shorter than its diff:
```python
import math

import jax
import jax.numpy as jnp
from jax import lax
from jax.sharding import PartitionSpec as P

HEADS = 16
WINDOW = 128
EPS = 1e-05
AXES = ("group", "rep")
BF = jnp.bfloat16
F32 = jnp.float32


def clip_layout(length_row, count):
    clip_ends = jnp.cumsum(length_row)
    clip_starts = clip_ends - length_row
    row_index = jnp.arange(count, dtype=jnp.int32)
    segment = jnp.sum((row_index[:, None] >= clip_ends[None, :]).astype(jnp.int32), axis=1)
    member = (segment[:, None] == jnp.arange(length_row.shape[0], dtype=jnp.int32)[None, :]).astype(
        jnp.int32
    )
    position = row_index - jnp.sum(member * clip_starts[None, :], axis=1)
    return (segment, position)


def rotary_tables(position, width):
    half = width // 2
    freqs = jnp.power(10000.0, -jnp.arange(half, dtype=F32) * (2.0 / width))
    angles = position.astype(F32)[:, None] * freqs[None, :]
    cosine = jnp.concatenate([jnp.cos(angles), jnp.cos(angles)], axis=1)
    sine = jnp.concatenate([jnp.sin(angles), jnp.sin(angles)], axis=1)
    return (cosine[:, None, :], sine[:, None, :])


def rotate(values, cosine, sine):
    half = values.shape[-1] // 2
    turned = jnp.concatenate([-values[..., half:], values[..., :half]], axis=-1)
    return values * cosine + turned * sine


def rotate_back(values, cosine, sine):
    half = values.shape[-1] // 2
    turned = jnp.concatenate([values[..., half:], -values[..., :half]], axis=-1)
    return values * cosine + turned * sine


def norm_parts(values):
    mean_value = jnp.mean(values, axis=-1, keepdims=True)
    centered = values - mean_value
    variance = jnp.mean(centered * centered, axis=-1, keepdims=True)
    inverse = lax.rsqrt(variance + EPS)
    return (centered * inverse, inverse)


def norm_back(grad_normed, unit, inverse, gain):
    scaled = grad_normed * gain
    return inverse * (
        scaled
        - jnp.mean(scaled, axis=-1, keepdims=True)
        - unit * jnp.mean(scaled * unit, axis=-1, keepdims=True)
    )


def block_allowed(segment, segment_pad, start, block, window):
    query_index = start + jnp.arange(block, dtype=jnp.int32)
    key_index = start - window + jnp.arange(block + window, dtype=jnp.int32)
    offset = query_index[:, None] - key_index[None, :]
    same_clip = segment[:, None] == segment_pad[None, :]
    return same_clip & (offset >= 0) & (offset < window)


def pad_front(values, window, fill):
    front = jnp.full((window,) + values.shape[1:], fill, values.dtype)
    return jnp.concatenate([front, values], axis=0)


def attention_forward(queries, keys_rot, values, segment, block, window):
    factor = 1.0 / math.sqrt(queries.shape[-1])
    keys_pad = pad_front(keys_rot, window, 0)
    values_pad = pad_front(values, window, 0)
    segment_pad = pad_front(segment, window, -1)
    allowed = block_allowed(segment, segment_pad, 0, block, window)
    scores = (
        jnp.einsum("qhd,khd->hqk", queries, keys_pad, preferred_element_type=F32) * factor
    )
    masked = jnp.where(allowed[None], scores, -jnp.inf)
    peak = jnp.max(masked, axis=-1, keepdims=True)
    expd = jnp.exp(masked - peak)
    totals = jnp.sum(expd, axis=-1, keepdims=True)
    probs = (expd / totals).astype(BF)
    outputs = jnp.einsum("hqk,khd->qhd", probs, values_pad, preferred_element_type=F32)
    log_totals = peak + jnp.log(totals)
    return (outputs, log_totals)


def attention_backward(
    queries, keys_rot, values, grad_attended, log_totals, segment, block, window
):
    factor = 1.0 / math.sqrt(queries.shape[-1])
    keys_pad = pad_front(keys_rot, window, 0)
    values_pad = pad_front(values, window, 0)
    segment_pad = pad_front(segment, window, -1)
    allowed = block_allowed(segment, segment_pad, 0, block, window)
    scores = (
        jnp.einsum("qhd,khd->hqk", queries, keys_pad, preferred_element_type=F32) * factor
    )
    probs = jnp.where(
        allowed[None], jnp.exp(jnp.where(allowed[None], scores, -jnp.inf) - log_totals), 0.0
    )
    probs_low = probs.astype(BF)
    grad_probs = jnp.einsum("qhd,khd->hqk", grad_attended, values_pad, preferred_element_type=F32)
    delta = jnp.sum(probs * grad_probs, axis=-1, keepdims=True)
    grad_scores = (probs * (grad_probs - delta)).astype(BF)
    grad_queries = (
        jnp.einsum("hqk,khd->qhd", grad_scores, keys_pad, preferred_element_type=F32) * factor
    )
    key_part = (
        jnp.einsum("hqk,qhd->khd", grad_scores, queries, preferred_element_type=F32) * factor
    )
    value_part = jnp.einsum("hqk,qhd->khd", probs_low, grad_attended, preferred_element_type=F32)
    return (grad_queries, key_part[window:], value_part[window:])


def make_links(n_group, n_rep):
    def swap(value, group_bits, rep_bits):
        pairs = [
            (g * n_rep + r, (g ^ group_bits) * n_rep + (r ^ rep_bits))
            for g in range(n_group)
            for r in range(n_rep)
        ]
        return lax.ppermute(value, AXES, pairs)

    return swap


def pick(stacked, index):
    return lax.dynamic_index_in_dim(stacked, index, 0, keepdims=False)


def solution(mesh):
    n_group, n_rep = mesh.shape["group"], mesh.shape["rep"]
    swap = make_links(n_group, n_rep)
    tuned = n_group == 8 and n_rep == 4

    def gather_group(piece, group):
        if not tuned:
            return lax.all_gather(piece, "group", axis=0)
        own = [piece] + [swap(piece, 2 * k, 0) for k in (1, 2, 3)]
        other = [swap(p, 1, 0) for p in own]
        full = jnp.zeros((8,) + piece.shape, piece.dtype)
        for k in range(4):
            for d, p in ((0, own[k]), (1, other[k])):
                at = group ^ (2 * k + d)
                full = lax.dynamic_update_index_in_dim(full, p, at, 0)
        return full

    def gather_all(piece, group, rep):
        if not tuned:
            full = lax.all_gather(piece, AXES, axis=0)
            return full.reshape((n_group, n_rep) + piece.shape)
        base = [piece] + [swap(piece, 2 * k, 0) for k in (1, 2, 3)]
        along_x = [swap(p, 1, 0) for p in base]
        along_y = [swap(p, 0, 2) for p in base]
        both = [swap(along_x[k], 0, 2) if k < 2 else swap(along_y[k], 1, 0) for k in range(4)]
        y = rep // 2
        half = jnp.zeros((8, 2) + piece.shape, piece.dtype)
        zeros = (0,) * piece.ndim
        for k in range(4):
            for dx, dy, p in ((0, 0, base[k]), (1, 0, along_x[k]), (0, 1, along_y[k]), (1, 1, both[k])):
                at = (group ^ (2 * k + dx), y ^ dy) + zeros
                half = lax.dynamic_update_slice(half, p[None, None], at)
        other = swap(half, 0, 1)
        even = rep % 2 == 0
        full = jnp.stack([jnp.where(even, half, other), jnp.where(even, other, half)], axis=2)
        return full.reshape((8, 4) + piece.shape)

    def gather_rep(piece):
        low = jnp.concatenate([piece, swap(piece, 0, 2)], axis=0)
        return jnp.concatenate([low, swap(low, 0, 1)], axis=0)

    def scatter_rep(blocks):
        half = blocks.shape[0] // 2
        low = blocks[:half].astype(F32) + swap(blocks[half:], 0, 1).astype(F32)
        quarter = half // 2
        return low[:quarter] + swap(low[quarter:].astype(BF), 0, 2).astype(F32)

    def scatter_group(grads, group):
        if not tuned:
            return lax.psum_scatter(grads, "group", scatter_dimension=0, tiled=False).astype(F32)
        z, x = group // 2, group % 2
        blocks = grads.reshape((4, 2) + grads.shape[1:])
        there = lax.dynamic_index_in_dim(blocks, x ^ 1, 1, keepdims=False)
        here = lax.dynamic_index_in_dim(blocks, x, 1, keepdims=False)
        came = swap(there, 1, 0)

        def part(k):
            return pick(here, z ^ k).astype(F32) + pick(came, z ^ k).astype(F32)

        arrived = [swap(part(k).astype(BF), 2 * k, 0) for k in (1, 2, 3)]
        return part(0) + (
            arrived[0].astype(F32) + arrived[1].astype(F32) + arrived[2].astype(F32)
        )

    def whole_rep(piece, rep):
        piece = piece.astype(BF)
        if not tuned:
            return lax.all_gather(piece, "rep", axis=0).astype(F32)
        low = jnp.stack([piece, swap(piece, 0, 2)])
        high = swap(low, 0, 1)
        rel = jnp.stack([low[0], high[0], low[1], high[1]])
        return jnp.stack([pick(rel, rep ^ j) for j in range(4)]).astype(F32)

    def scatter_attn(grads, group, rep):
        rows, cols = grads.shape
        if not tuned:
            part = lax.psum_scatter(grads, "group", scatter_dimension=0, tiled=True)
            return lax.psum(part, "rep").astype(F32)
        x, y, core = group % 2, rep // 2, rep % 2
        z = group // 2
        half = cols // 2
        there = lax.dynamic_slice_in_dim(grads, (core ^ 1) * half, half, 1)
        here = lax.dynamic_slice_in_dim(grads, core * half, half, 1)
        chip = (here.astype(F32) + swap(there, 0, 1).astype(F32)).astype(BF)
        chip = chip.reshape(4, 2, rows // 8, 2, half // 2)
        quarter = half // 4

        def add(a, b):
            return (a.astype(F32) + b.astype(F32)).astype(BF)

        def over_x(v):
            return add(
                lax.dynamic_index_in_dim(v, x, 1, keepdims=False),
                swap(lax.dynamic_index_in_dim(v, x ^ 1, 1, keepdims=False), 1, 0),
            )

        def over_y(v):
            return add(
                lax.dynamic_slice_in_dim(v, y * quarter, quarter, v.ndim - 1),
                swap(lax.dynamic_slice_in_dim(v, (y ^ 1) * quarter, quarter, v.ndim - 1), 0, 2),
            )

        first = over_y(over_x(chip[:, :, :, 0]))
        second = over_x(over_y(chip[:, :, :, 1]))
        column = jnp.stack([first, second], axis=2)
        arrived = [swap(pick(column, z ^ k), 2 * k, 0).astype(F32) for k in (1, 2, 3)]
        mine = pick(column, z).astype(F32) + (arrived[0] + arrived[1] + arrived[2])
        full = whole_rep(mine, rep)
        full = full.reshape(2, 2, rows // 8, 2, quarter)
        return full.transpose(2, 1, 3, 0, 4).reshape(rows // 8, cols)

    def sum_all(value):
        if not tuned:
            return lax.psum(value, AXES)
        for bits in ((0, 1), (0, 2), (1, 0), (2, 0), (4, 0)):
            value = value + swap(value, *bits)
        return value

    def shards(
        inputs,
        lengths,
        ln1_gain,
        ln1_bias,
        w_qkv,
        w_out,
        scale_attn,
        ln2_gain,
        ln2_bias,
        w_gate,
        w_up,
        w_down,
        scale_mlp,
        grad_out,
    ):
        count, width = inputs.shape
        head_width = width // HEADS
        group, rep = lax.axis_index("group"), lax.axis_index("rep")
        rows = w_qkv.shape[0]
        ff = w_gate.shape[1]
        part_ff = ff // n_rep
        vectors = jnp.stack([ln1_gain, ln1_bias, scale_attn, ln2_gain, ln2_bias, scale_mlp], axis=1)
        vectors = jnp.pad(vectors, ((0, 0), (0, 128 - vectors.shape[1])))
        bundle = jnp.concatenate([w_qkv, w_out, vectors], axis=1)
        attn_full = gather_all(bundle, group, rep).reshape(width, -1)
        qkv_full = attn_full[:, : 3 * width]
        out_full = attn_full[:, 3 * width : 4 * width]
        vecs = attn_full[:, 4 * width : 4 * width + 6].T.astype(F32)
        gain_one, bias_one, attn_scale, gain_two, bias_two, mlp_scale = [vecs[i] for i in range(6)]

        def columns(w):
            blocks = w.reshape(rows, n_group, n_rep, ff // (n_group * n_rep))
            return blocks.transpose(2, 0, 1, 3).reshape(n_rep, rows, part_ff)

        pair = jnp.stack([columns(w_gate), columns(w_up)], axis=1)
        came = [pick(pair, rep)] + [swap(pick(pair, rep ^ d), 0, d) for d in (1, 2, 3)]
        came = jnp.stack(came)
        gate_up = jnp.stack([pick(came, rep ^ j) for j in range(n_rep)], axis=1)
        gate_up = gate_up.reshape(2, n_rep * rows, part_ff)
        down_rows = w_down.shape[0]
        gate_all = gather_group(gate_up[0], group).reshape(width, part_ff)
        up_all = gather_group(gate_up[1], group).reshape(width, part_ff)
        down_all = gather_group(w_down, group).reshape(part_ff, width)

        cot_all = gather_rep(grad_out)

        segment, position = clip_layout(lengths[0], count)
        cosine, sine = rotary_tables(position, head_width)
        frames = inputs.astype(F32)
        unit_one, inverse_one = norm_parts(frames)
        normed = (unit_one * gain_one + bias_one).astype(BF)
        projected = jnp.dot(normed, qkv_full, preferred_element_type=F32)
        queries = rotate(
            projected[:, :width].reshape(count, HEADS, head_width), cosine, sine
        ).astype(BF)
        keys_rot = rotate(
            projected[:, width : 2 * width].reshape(count, HEADS, head_width), cosine, sine
        ).astype(BF)
        values = projected[:, 2 * width :].reshape(count, HEADS, head_width).astype(BF)
        attended, log_totals = attention_forward(queries, keys_rot, values, segment, count, WINDOW)
        attended = attended.reshape(count, width).astype(BF)
        branch = jnp.dot(attended, out_full, preferred_element_type=F32)
        middle = frames + attn_scale * branch
        unit_two, inverse_two = norm_parts(middle)
        normed_two = (unit_two * gain_two + bias_two).astype(BF)

        normed_all = gather_rep(normed_two)
        gate = jnp.dot(normed_all, gate_all, preferred_element_type=F32)
        up_value = jnp.dot(normed_all, up_all, preferred_element_type=F32)
        sigmoid_gate = jax.nn.sigmoid(gate)
        silu_gate = gate * sigmoid_gate
        hidden = (silu_gate * up_value).astype(BF)
        mlp_part = jnp.dot(hidden, down_all, preferred_element_type=F32).astype(BF)
        mlp = scatter_rep(mlp_part)
        block_out = (middle + mlp_scale * mlp).astype(BF)
        cotangent = grad_out.astype(F32)
        scale_mlp_grad = jnp.sum(cotangent * mlp, axis=0)
        grad_mlp = (mlp_scale * cot_all.astype(F32)).astype(BF)

        def grad_blocks(a, b):
            out = jnp.einsum("td,te->de", a, b, preferred_element_type=F32).astype(BF)
            return out.reshape(n_group, out.shape[0] // n_group, out.shape[1])

        w_down_part = scatter_group(grad_blocks(hidden, grad_mlp), group)
        grad_hidden = jnp.einsum("td,fd->tf", grad_mlp, down_all, preferred_element_type=F32)
        grad_gate = (
            grad_hidden * up_value * sigmoid_gate * (1.0 + gate * (1.0 - sigmoid_gate))
        ).astype(BF)
        grad_up = (grad_hidden * silu_gate).astype(BF)
        grad_normed_part = jnp.einsum(
            "tf,df->td", grad_gate, gate_all, preferred_element_type=F32
        ) + jnp.einsum("tf,df->td", grad_up, up_all, preferred_element_type=F32)
        grad_normed_two = scatter_rep(grad_normed_part.astype(BF))
        w_gate_part = scatter_group(grad_blocks(normed_all, grad_gate), group)
        w_up_part = scatter_group(grad_blocks(normed_all, grad_up), group)

        def hidden_columns(part):
            full = whole_rep(part, rep)
            full = full.reshape(n_rep, full.shape[1], n_group, ff // (n_group * n_rep))
            return full.transpose(1, 2, 0, 3).reshape(full.shape[1], ff)

        w_gate_grad = hidden_columns(w_gate_part)
        w_up_grad = hidden_columns(w_up_part)
        w_down_grad = whole_rep(w_down_part, rep).reshape(n_rep * down_rows, width)

        ln2_gain_grad = jnp.sum(grad_normed_two * unit_two, axis=0)
        ln2_bias_grad = jnp.sum(grad_normed_two, axis=0)
        grad_middle = cotangent + norm_back(grad_normed_two, unit_two, inverse_two, gain_two)
        scale_attn_grad = jnp.sum(grad_middle * branch, axis=0)
        grad_branch = (attn_scale * grad_middle).astype(BF)
        w_out_part = jnp.einsum("td,te->de", attended, grad_branch, preferred_element_type=F32)
        w_out_grad = scatter_attn(w_out_part.astype(BF), group, rep)
        grad_attended = jnp.einsum(
            "te,de->td", grad_branch, out_full, preferred_element_type=F32
        ).astype(BF)
        grad_queries, grad_keys, grad_values = attention_backward(
            queries,
            keys_rot,
            values,
            grad_attended.reshape(count, HEADS, head_width),
            log_totals,
            segment,
            count,
            WINDOW,
        )
        grad_projected = jnp.concatenate(
            [
                rotate_back(grad_queries, cosine, sine).reshape(count, width),
                rotate_back(grad_keys, cosine, sine).reshape(count, width),
                grad_values.reshape(count, width),
            ],
            axis=1,
        ).astype(BF)
        w_qkv_part = jnp.einsum("td,te->de", normed, grad_projected, preferred_element_type=F32)
        w_qkv_grad = scatter_attn(w_qkv_part.astype(BF), group, rep)
        grad_normed = jnp.einsum(
            "te,de->td", grad_projected, qkv_full, preferred_element_type=F32
        )
        ln1_gain_grad = jnp.sum(grad_normed * unit_one, axis=0)
        ln1_bias_grad = jnp.sum(grad_normed, axis=0)
        input_grad = grad_middle + norm_back(grad_normed, unit_one, inverse_one, gain_one)
        small = sum_all(
            jnp.stack(
                [
                    ln1_gain_grad,
                    ln1_bias_grad,
                    scale_attn_grad,
                    ln2_gain_grad,
                    ln2_bias_grad,
                    scale_mlp_grad,
                ]
            )
        )
        own = width // n_group
        small = lax.dynamic_slice_in_dim(small, group * own, own, 1)
        return (
            block_out,
            input_grad,
            small[0],
            small[1],
            w_qkv_grad,
            w_out_grad,
            small[2],
            small[3],
            small[4],
            w_gate_grad,
            w_up_grad,
            w_down_grad,
            small[5],
        )

    rowed, flat = P(AXES, None), P(AXES)
    in_specs = (
        rowed, rowed, flat, flat, rowed, rowed, flat, flat, flat, rowed, rowed, rowed, flat, rowed,
    )
    own_rows, own_flat = P("group", None), P("group")
    out_specs = (
        rowed, rowed, own_flat, own_flat, own_rows, own_rows, own_flat, own_flat, own_flat,
        own_rows, own_rows, own_rows, own_flat,
    )
    return jax.shard_map(shards, mesh=mesh, in_specs=in_specs, out_specs=out_specs, check_vma=False)
```

time: 1710 us -> 688 us (0.40)
  waiting for transfers between devices: 1320 us -> 233 us
  starting transfers between devices: 0.73 us -> 89.1 us
  local copies, waits for them, and re-layouts: 29.9 us -> 113 us
  blocking collectives: 78 us -> 0 us
  matrix products: 187 us -> 158 us
  other arithmetic: 60.9 us -> 83.2 us
    reduce_scatter x5 -> x0, waiting for transfers between devices: 1040 us -> none  [the longest x1 284 us: shards(): lax.psum_scatter(mlp_grads[4], 'group', scatter_dimension=0, tiled=True)]
    all_gather x5 -> x0, waiting for transfers between devices: 242 us -> none  [the longest x1 73 us: shards(): lax.all_gather(mlp_shards[3], ('group', 'rep'), axis=0, tiled=True)]
    ppermute x0 -> x91, waiting for transfers between devices: none -> 233 us  [swap(): return lax.ppermute(value, AXES, pairs)]
    ppermute x0 -> x91, starting transfers between devices: none -> 89.1 us  [swap(): return lax.ppermute(value, AXES, pairs)]
    unnamed x2 -> x0, blocking collectives: 72.4 us -> none
    psum x1 -> x0, waiting for transfers between devices: 34.8 us -> none  [shards(): lax.psum(attn_part[2].astype(jnp.bfloat16), 'rep').astype(jnp.float32)]
    dot_general x18, matrix products: 155 us -> 124 us  [the longest x3 17.3 us: grad_blocks(): out = jnp.einsum('td,te->de', a, b, preferred_element_type=F32).astype(BF)]
    dynamic_update_slice x0 -> x38, local copies, waits for them, and re-layouts: none -> 20 us  [the longest x15 10.9 us: gather_all(): half = lax.dynamic_update_slice(half, p[None, None], at)]
  transfers between devices with their start and end apart: 11 -> 91, of which waited for: 10 -> 43; matrix products, arithmetic and copies ran while one was open for 12% -> 35% of each run, Pallas kernels for 0% -> 0%
where the time goes in v1:
time: 688 us; the launch traced here: 679 us
  waiting for transfers between devices  233 us (34%)
  matrix products  158 us (23%)
  local copies, waits for them, and re-layouts  113 us (16%)
  starting transfers between devices  89.1 us (13%)
  other arithmetic  83.2 us (12%)
    ppermute x91, waiting for transfers between devices, swap(): return lax.ppermute(value, AXES, pairs)  233 us
    ppermute x91, starting transfers between devices, swap(): return lax.ppermute(value, AXES, pairs)  89.1 us
    unnamed x196, local copies, waits for them, and re-layouts  27.9 us
    dot_general x1, matrix products, attention_backward(): jnp.einsum('qhd,khd->hqk', grad_attended, values_pad, preferred_element_t...  17.3 us
    dot_general x3, matrix products, grad_blocks(): out = jnp.einsum('td,te->de', a, b, preferred_element_type=F32).astype(BF)  17.3 us
    dot_general x1, matrix products, shards(): gate = jnp.dot(normed_all, gate_all, preferred_element_type=F32)  16 us
    convert_element_type x1, other arithmetic, attention_backward(): grad_scores = (probs * (grad_probs - delta)).astype(BF)  14.7 us
  transfers between devices with their start and end apart: 91, of which 43 were waited for; matrix products, arithmetic and copies ran while one was open for 35% of the time, Pallas kernels for 0%

profile of v1, /device:TPU:10, one launch (start us, length us, event | category | flops | bytes accessed | tf_op | source)
XLA Modules:
  0.0 679.2 jit_solution(8158345633833987719)
XLA Ops:
  20.4 6.3 collective-permute-done.2
  41.6 9.3 %collective-permute-done.6 = bf16[32,4224]{1,0:T(8,128)(2,1)S(1)} collective-permute-done((bf16[32,4224]{1,0:T(8,128)(2,1)S(1)}, bf16[32,4224]{1,0:T(8,128)(2,1)S(1)}, u32[]{:S(2)}, u32[]{:S(2)}) %collective-permute-start.6) | collective-permute-done | bytes 270368 | tf_op jit(solution)/shard_map/ppermute | solution.py:133
  53.8 5.6 collective-permute-done.8
  61.5 5.4 collective-permute-done.10
  75.5 4.7 collective-permute-done.14
  96.4 4.6 collective-permute-done.28
  102.3 4.8 collective-permute-done.29
  109.9 5.1 collective-permute-done.22
  117.9 6.2 collective-permute-done.39
  130.4 5.8 select_bitcast_fusion.1
  136.2 6.5 pad_maximum_fusion
  145.9 5.8 fusion.8
  165.1 5.8 fusion.1
  171.0 5.2 fusion
  178.3 7.1 %fusion.45 = bf16[16,64,512]{2,1,0:T(8,128)(2,1)S(1)} fusion(f32[16,512,640]{2,1,0:T(8,128)S(1)} %get-tuple-element.166, f32[16,512]{1,0:T(8,128)S(1)} %fusion, f32[16,512]{1,0:T(8,128)S(1)} %get-tuple-element.165, pred[512,640]{1,0:T(8,128)(4,1)S(1)} %fusion.52, bf16[512,16,64]{0,2,1:T(8,128)(2,1)S(1)} %bitcast.422), kind=kOutput, calls=%fused_computation.103 | convolution fusion | flops 697827328 | bytes 23461888 | tf_op jit(solution)/shard_map/hqk,khd->qhd/dot_general | solution.py:93
  185.4 4.6 fusion.124
  203.1 11.2 %collective-permute-done.16 = bf16[512,1024]{1,0:T(8,128)(2,1)S(1)} collective-permute-done((bf16[512,1024]{1,0:T(8,128)(2,1)S(1)}, bf16[512,1024]{1,0:T(8,128)(2,1)S(1)}, u32[]{:S(2)}, u32[]{:S(2)}) %collective-permute-start.16) | collective-permute-done | bytes 1048608 | tf_op jit(solution)/shard_map/ppermute | solution.py:133
  218.3 5.2 collective-permute-done.25
  223.6 14.1 %collective-permute-done.27 = bf16[128,1024]{1,0:T(8,128)(2,1)S(1)} collective-permute-done((bf16[128,1024]{1,0:T(8,128)(2,1)S(1)}, bf16[128,1024]{1,0:T(8,128)(2,1)S(1)}, u32[]{:S(2)}, u32[]{:S(2)}) %collective-permute-start.27) | collective-permute-done | bytes 262176 | tf_op jit(solution)/shard_map/ppermute | solution.py:133
  238.0 11.0 %fusion.60 = f32[2048,1024]{1,0:T(8,128)} fusion(bf16[1024,1024]{1,0:T(8,128)(2,1)S(1)} %bitcast.407, bf16[1024,1024]{1,0:T(8,128)(2,1)S(1)} %collective-permute-done.45, bf16[512,1024]{1,0:T(8,128)(2,1)} %collective-permute-done.44, bf16[512,1024]{1,0:T(8,128)(2,1)} %param.27, f32[1024]{0:T(1024)S(1)} %copy-done.68), kind=kOutput, calls=%fused_computation.117 | convolution fusion | flops 4311744512 | bytes 14684160 | tf_op jit(solution)/shard_map/td,fd->tf/dot_general | solution.py:345
  249.0 10.4 %fusion.122 = f32[2048,1024]{1,0:T(8,128)} fusion(bf16[1024,1024]{1,0:T(8,128)(2,1)S(1)} %bitcast.409, bf16[1024,1024]{1,0:T(8,128)(2,1)S(1)} %collective-permute-done.17, bf16[512,1024]{1,0:T(8,128)(2,1)S(1)} %collective-permute-done.16, bf16[512,1024]{1,0:T(8,128)(2,1)S(1)} %add_convert_fusion.4), kind=kOutput, calls=%fused_computation.377 | convolution fusion | flops 4307550208 | bytes 14680064 | tf_op jit(solution)/shard_map/dot_general | solution.py:329
  259.4 16.0 %multiply_convert_fusion.2 = (bf16[2048,1024]{1,0:T(8,128)(2,1)}, bf16[2048,1024]{1,0:T(8,128)(2,1)}, bf16[2048,1024]{1,0:T(8,128)(2,1)}) fusion(f32[2048,1024]{1,0:T(8,128)} %fusion.60, f32[2048,1024]{1,0:T(8,128)} %fusion.122, bf16[1024,1024]{1,0:T(8,128)(2,1)S(1)} %bitcast.405, bf16[1024,1024]{1,0:T(8,128)(2,1)} %copy-done.77, ...), kind=kOutput, calls=%fused_computation.14 | convolution fusion | flops 4339007488 | bytes 35651584 | tf_op jit(solution)/shard_map/dot_general | solution.py:328
  275.5 7.6 %convolution_convert_fusion.2 = bf16[1024,1024]{1,0:T(8,128)(2,1)S(1)} fusion(bf16[2048,1024]{1,0:T(8,128)(2,1)} %get-tuple-element.59, bf16[1024,1024]{1,0:T(8,128)(2,1)S(1)} %copy-done.76, bf16[512,1024]{1,0:T(8,128)(2,1)} %collective-permute-done.44, bf16[512,1024]{1,0:T(8,128)(2,1)} %param.27, f32[1024]{0:T(1024)S(1)} %copy-done.68), kind=kOutput, calls=%fused_computation.86 | convolution fusion | flops 4312793088 | bytes 10489856 | tf_op jit(solution)/shard_map/td,te->de/dot_general | solution.py:341
  285.1 4.9 convolution_convert_fusion.4
  292.8 10.9 %fusion.136 = f32[2048,1024]{1,0:T(8,128)} fusion(bf16[2048,1024]{1,0:T(8,128)(2,1)} %get-tuple-element.58, bf16[1024,1024]{1,0:T(8,128)(2,1)} %bitcast.410), kind=kOutput, calls=%fused_computation.391 | convolution fusion | flops 4294967296 | bytes 14680064 | tf_op jit(solution)/shard_map/tf,df->td/dot_general | solution.py:352
  303.7 4.8 convolution_convert_fusion.3
  313.3 10.2 %add_convert_fusion = bf16[2048,1024]{1,0:T(8,128)(2,1)S(1)} fusion(f32[2048,1024]{1,0:T(8,128)} %fusion.136, bf16[2048,1024]{1,0:T(8,128)(2,1)} %get-tuple-element.57, bf16[1024,1024]{1,0:T(8,128)(2,1)} %bitcast.406), kind=kOutput, calls=%fused_computation.12 | convolution fusion | flops 4299161600 | bytes 18874368 | tf_op jit(solution)/shard_map/tf,df->td/dot_general | solution.py:350
  323.5 5.1 convolution_convert_fusion.1
  351.8 5.3 collective-permute-done.73
  360.3 8.2 %collective-permute-done.88 = bf16[128,1024]{1,0:T(8,128)(2,1)S(1)} collective-permute-done((bf16[128,1024]{1,0:T(8,128)(2,1)S(1)}, bf16[128,1024]{1,0:T(8,128)(2,1)S(1)}, u32[]{:S(2)}, u32[]{:S(2)}) %collective-permute-start.88) | collective-permute-done | bytes 262176 | tf_op jit(solution)/shard_map/ppermute | solution.py:133
  372.8 22.4 %collective-permute-done.82 = bf16[128,1024]{0,1:T(8,128)(2,1)S(1)} collective-permute-done((bf16[128,1024]{0,1:T(8,128)(2,1)S(1)}, bf16[128,1024]{0,1:T(8,128)(2,1)S(1)}, u32[]{:S(2)}, u32[]{:S(2)}) %collective-permute-start.82) | collective-permute-done | bytes 262176 | tf_op jit(solution)/shard_map/ppermute | solution.py:133
  396.2 5.9 collective-permute-done.81
  417.4 5.5 collective-permute-done.83
  423.0 5.1 collective-permute-done.77
  439.4 17.5 %collective-permute-done.47 = bf16[512,1024]{1,0:T(8,128)(2,1)S(1)} collective-permute-done((bf16[512,1024]{1,0:T(8,128)(2,1)S(1)}, bf16[512,1024]{1,0:T(8,128)(2,1)S(1)}, u32[]{:S(2)}, u32[]{:S(2)}) %collective-permute-start.47) | collective-permute-done | bytes 1048608 | tf_op jit(solution)/shard_map/ppermute | solution.py:133
  457.9 21.0 %collective-permute-done.43 = bf16[512,1024]{1,0:T(8,128)(2,1)S(1)} collective-permute-done((bf16[512,1024]{1,0:T(8,128)(2,1)S(1)}, bf16[512,1024]{1,0:T(8,128)(2,1)S(1)}, u32[]{:S(2)}, u32[]{:S(2)}) %collective-permute-start.43) | collective-permute-done | bytes 1048608 | tf_op jit(solution)/shard_map/ppermute | solution.py:133
  488.9 11.5 %fusion.46 = bf16[640,16,64]{0,2,1:T(8,128)(2,1)} fusion(bf16[512,16,64]{0,2,1:T(8,128)(2,1)S(1)} %bitcast.428, f32[16,512]{1,0:T(8,128)S(1)} %copy-done.63, f32[16,512,640]{2,1,0:T(8,128)} %copy-done, pred[512,640]{1,0:T(8,128)(4,1)S(1)} %fusion.52), kind=kOutput, calls=%fused_computation.104 | convolution fusion | flops 697958400 | bytes 23691264 | tf_op jit(solution)/shard_map/hqk,qhd->khd/dot_general | solution.py:122
  500.4 17.3 %multiply_reduce_fusion = (f32[16,512]{1,0:T(8,128)S(1)}, f32[16,512,640]{2,1,0:T(8,128)}) fusion(f32[16,512]{1,0:T(8,128)S(1)} %copy-done.63, f32[16,512,640]{2,1,0:T(8,128)} %copy-done, pred[512,640]{1,0:T(8,128)(4,1)S(1)} %fusion.52, bf16[512,16,64]{0,2,1:T(8,128)(2,1)S(1)} %bitcast.429, bf16[512,16,64]{0,2,1:T(8,128)(2,1)S(1)} %bitcast.423), kind=kOutput, calls=%fused_computation.1 | convolution fusion | flops 702537728 | bytes 44433408 | tf_op jit(solution)/shard_map/qhd,khd->hqk/dot_general | solution.py:113
  517.8 14.7 %multiply_convert_fusion = bf16[16,512,640]{2,1,0:T(8,128)(2,1)S(1)} fusion(f32[16,512,640]{2,1,0:T(8,128)} %get-tuple-element.169, f32[16,512]{1,0:T(8,128)S(1)} %get-tuple-element.168, f32[16,512]{1,0:T(8,128)S(1)} %copy-done.63, f32[16,512,640]{2,1,0:T(8,128)} %copy-done, pred[512,640]{1,0:T(8,128)(4,1)S(1)} %fusion.52), kind=kLoop, calls=%fused_computation | loop fusion | flops 36700160 | bytes 52822016 | tf_op jit(solution)/shard_map/convert_element_type | solution.py:115
  534.4 4.6 bitcast_multiply_fusion
  544.7 7.2 %convolution_convert_fusion = bf16[1024,3072]{1,0:T(8,128)(2,1)S(1)} fusion(bf16[512,1024]{0,1:T(8,128)(2,1)S(1)} %bitcast.426, bf16[512,1024]{0,1:T(8,128)(2,1)S(1)} %bitcast.440, bf16[512,1024]{0,1:T(8,128)(2,1)S(1)} %bitcast.438, bf16[512,1024]{1,0:T(8,128)(2,1)S(1)} %copy-done.7, f32[1024]{0:T(1024)S(1)} %copy-done.72, f32[1024]{0:T(1024)S(1)} %copy-done.67, ...), kind=kOutput, calls=%fused_computation.20 | convolution fusion | flops 3236954112 | bytes 10498048 | tf_op jit(solution)/shard_map/td,te->de/dot_general | solution.py:394
  556.1 5.3 fusion.22
  603.3 4.8 add_convert_fusion.1
  608.1 6.3 reshape.371
  614.4 4.6 fusion.126
  632.4 4.8 collective-permute-done.56
  638.7 6.6 collective-permute-done.54
  668.7 4.3 collective-permute-done.61
  (545 shorter events, 288.6 us)
Async XLA Ops:
  2.6 27.1 %collective-permute-start.7 = (bf16[32,4224]{1,0:T(8,128)(2,1)S(1)}, bf16[32,4224]{1,0:T(8,128)(2,1)S(1)}, u32[]{:S(2)}, u32[]{:S(2)}) collective-permute-start(bf16[32,4224]{1,0:T(8,128)(2,1)S(1)} %fusion.83), channel_id=1, source_target_pairs={{0,16},{1,17},{2,18},{3,19},{4,20},{5,21},{6,22},{7,23},{8,24},{9,... | collective-permute-start | bytes 811016 | tf_op jit(solution)/shard_map/ppermute | solution.py:133
  7.8 45.6 %collective-permute-start.11 = (bf16[32,4224]{1,0:T(8,128)(2,1)S(1)}, bf16[32,4224]{1,0:T(8,128)(2,1)S(1)}, u32[]{:S(2)}, u32[]{:S(2)}) collective-permute-start(bf16[32,4224]{1,0:T(8,128)(2,1)S(1)} %fusion.83), channel_id=1, source_target_pairs={{0,24},{1,25},{2,26},{3,27},{4,28},{5,29},{6,30},{7,31},{8,16},{9,... | collective-permute-start | bytes 811016 | tf_op jit(solution)/shard_map/ppermute | solution.py:133
  16.6 67.3 %collective-permute-start.20 = (bf16[2,32,1024]{2,1,0:T(8,128)(2,1)}, bf16[2,32,1024]{2,1,0:T(8,128)(2,1)}, u32[]{:S(2)}, u32[]{:S(2)}) collective-permute-start(bf16[2,32,1024]{2,1,0:T(8,128)(2,1)} %get-tuple-element.137), channel_id=1, source_target_pairs={{0,3},{1,2},{2,1},{3,0},{4,7},{5,6},{6,5},{7,4},{8,11},{9,10},{10,... | collective-permute-start | bytes 393224 | tf_op jit(solution)/shard_map/ppermute | solution.py:133
  18.9 65.2 %collective-permute-start.19 = (bf16[2,32,1024]{2,1,0:T(8,128)(2,1)}, bf16[2,32,1024]{2,1,0:T(8,128)(2,1)S(1)}, u32[]{:S(2)}, u32[]{:S(2)}) collective-permute-start(bf16[2,32,1024]{2,1,0:T(8,128)(2,1)} %get-tuple-element.138), channel_id=1, source_target_pairs={{0,2},{1,3},{2,0},{3,1},{4,6},{5,7},{6,4},{7,5},{8,10},{9,11},{10,... | collective-permute-start | bytes 393224 | tf_op jit(solution)/shard_map/ppermute | solution.py:133
  35.6 17.8 %collective-permute-start.9 = (bf16[32,4224]{1,0:T(8,128)(2,1)S(1)}, bf16[32,4224]{1,0:T(8,128)(2,1)S(1)}, u32[]{:S(2)}, u32[]{:S(2)}) collective-permute-start(bf16[32,4224]{1,0:T(8,128)(2,1)S(1)} %collective-permute-done.7), channel_id=1, source_target_pairs={{0,2},{1,3},{2,0},{3,1},{4,6},{5,7},{6,4},{7,5},{8,10},{9,11},{10,... | collective-permute-start | bytes 811016 | tf_op jit(solution)/shard_map/ppermute | solution.py:133
  53.4 32.4 %collective-permute-start.18 = (bf16[2,32,1024]{2,1,0:T(8,128)(2,1)S(1)}, bf16[2,32,1024]{2,1,0:T(8,128)(2,1)S(1)}, u32[]{:S(2)}, u32[]{:S(2)}) collective-permute-start(bf16[2,32,1024]{2,1,0:T(8,128)(2,1)S(1)} %get-tuple-element.139), channel_id=1, source_target_pairs={{0,1},{1,0},{2,3},{3,2},{4,5},{5,4},{6,7},{7,6},{8,9},{9,8},{10,11... | collective-permute-start | bytes 393224 | tf_op jit(solution)/shard_map/ppermute | solution.py:133
  53.4 15.4 %collective-permute-start.13 = (bf16[32,4224]{1,0:T(8,128)(2,1)S(1)}, bf16[32,4224]{1,0:T(8,128)(2,1)S(1)}, u32[]{:S(2)}, u32[]{:S(2)}) collective-permute-start(bf16[32,4224]{1,0:T(8,128)(2,1)S(1)} %collective-permute-done.11), channel_id=1, source_target_pairs={{0,2},{1,3},{2,0},{3,1},{4,6},{5,7},{6,4},{7,5},{8,10},{9,11},{10,... | collective-permute-start | bytes 811016 | tf_op jit(solution)/shard_map/ppermute | solution.py:133
  68.8 25.1 %collective-permute-start.36 = (bf16[128,1024]{1,0:T(8,128)(2,1)}, bf16[128,1024]{1,0:T(8,128)(2,1)}, u32[]{:S(2)}, u32[]{:S(2)}) collective-permute-start(bf16[128,1024]{1,0:T(8,128)(2,1)} %param.25), channel_id=1, source_target_pairs={{0,8},{1,9},{2,10},{3,11},{4,12},{5,13},{6,14},{7,15},{8,0},{9,1},... | collective-permute-start | bytes 786440 | tf_op jit(solution)/shard_map/ppermute | solution.py:133
  80.9 46.5 %collective-permute-start.15 = (bf16[8,2,32,4224]{3,2,1,0:T(8,128)(2,1)}, bf16[8,2,32,4224]{3,2,1,0:T(8,128)(2,1)}, u32[]{:S(2)}, u32[]{:S(2)}) collective-permute-start(bf16[8,2,32,4224]{3,2,1,0:T(8,128)(2,1)} %bitcast_dynamic-update-slice_fusion), channel_id=1, source_target_pairs={{0,1},{1,0},{2,3},{3,2},{4,5},{5,4},{6,7},{7,6},{8,9},{9,8},{10,11... | collective-permute-start | bytes 12976136 | tf_op jit(solution)/shard_map/ppermute | solution.py:133
  84.1 43.1 %collective-permute-start.40 = (bf16[128,1024]{1,0:T(8,128)(2,1)}, bf16[128,1024]{1,0:T(8,128)(2,1)S(1)}, u32[]{:S(2)}, u32[]{:S(2)}) collective-permute-start(bf16[128,1024]{1,0:T(8,128)(2,1)} %param.25), channel_id=1, source_target_pairs={{0,24},{1,25},{2,26},{3,27},{4,28},{5,29},{6,30},{7,31},{8,16},{9,... | collective-permute-start | bytes 786440 | tf_op jit(solution)/shard_map/ppermute | solution.py:133
  85.8 29.3 %collective-permute-start.38 = (bf16[128,1024]{1,0:T(8,128)(2,1)}, bf16[128,1024]{1,0:T(8,128)(2,1)S(1)}, u32[]{:S(2)}, u32[]{:S(2)}) collective-permute-start(bf16[128,1024]{1,0:T(8,128)(2,1)} %param.25), channel_id=1, source_target_pairs={{0,16},{1,17},{2,18},{3,19},{4,20},{5,21},{6,22},{7,23},{8,24},{9,... | collective-permute-start | bytes 786440 | tf_op jit(solution)/shard_map/ppermute | solution.py:133
  115.0 78.6 %collective-permute-start.44 = (bf16[512,1024]{1,0:T(8,128)(2,1)}, bf16[512,1024]{1,0:T(8,128)(2,1)}, u32[]{:S(2)}, u32[]{:S(2)}) collective-permute-start(bf16[512,1024]{1,0:T(8,128)(2,1)} %param.27), channel_id=1, source_target_pairs={{0,2},{1,3},{2,0},{3,1},{4,6},{5,7},{6,4},{7,5},{8,10},{9,11},{10,... | collective-permute-start | bytes 3145736 | tf_op jit(solution)/shard_map/ppermute | solution.py:133
  115.1 100.0 %collective-permute-start.33 = (bf16[128,1024]{1,0:T(8,128)(2,1)}, bf16[128,1024]{1,0:T(8,128)(2,1)}, u32[]{:S(2)}, u32[]{:S(2)}) collective-permute-start(bf16[128,1024]{1,0:T(8,128)(2,1)} %bitcast.59), channel_id=1, source_target_pairs={{0,24},{1,25},{2,26},{3,27},{4,28},{5,29},{6,30},{7,31},{8,16},{9,... | collective-permute-start | bytes 786440 | tf_op jit(solution)/shard_map/ppermute | solution.py:133
  124.1 71.9 %collective-permute-start.31 = (bf16[128,1024]{1,0:T(8,128)(2,1)}, bf16[128,1024]{1,0:T(8,128)(2,1)}, u32[]{:S(2)}, u32[]{:S(2)}) collective-permute-start(bf16[128,1024]{1,0:T(8,128)(2,1)} %bitcast.59), channel_id=1, source_target_pairs={{0,16},{1,17},{2,18},{3,19},{4,20},{5,21},{6,22},{7,23},{8,24},{9,... | collective-permute-start | bytes 786440 | tf_op jit(solution)/shard_map/ppermute | solution.py:133
  127.3 74.5 %collective-permute-start.24 = (bf16[128,1024]{1,0:T(8,128)(2,1)}, bf16[128,1024]{1,0:T(8,128)(2,1)}, u32[]{:S(2)}, u32[]{:S(2)}) collective-permute-start(bf16[128,1024]{1,0:T(8,128)(2,1)} %bitcast.49), channel_id=1, source_target_pairs={{0,16},{1,17},{2,18},{3,19},{4,20},{5,21},{6,22},{7,23},{8,24},{9,... | collective-permute-start | bytes 786440 | tf_op jit(solution)/shard_map/ppermute | solution.py:133
  128.7 62.1 %collective-permute-start.30 = (bf16[128,1024]{1,0:T(8,128)(2,1)}, bf16[128,1024]{1,0:T(8,128)(2,1)}, u32[]{:S(2)}, u32[]{:S(2)}) collective-permute-start(bf16[128,1024]{1,0:T(8,128)(2,1)} %collective-permute-done.29), channel_id=1, source_target_pairs={{0,4},{1,5},{2,6},{3,7},{4,0},{5,1},{6,2},{7,3},{8,12},{9,13},{10,... | collective-permute-start | bytes 786440 | tf_op jit(solution)/shard_map/ppermute | solution.py:133
  190.8 23.5 %collective-permute-start.16 = (bf16[512,1024]{1,0:T(8,128)(2,1)S(1)}, bf16[512,1024]{1,0:T(8,128)(2,1)S(1)}, u32[]{:S(2)}, u32[]{:S(2)}) collective-permute-start(bf16[512,1024]{1,0:T(8,128)(2,1)S(1)} %add_convert_fusion.4), channel_id=1, source_target_pairs={{0,2},{1,3},{2,0},{3,1},{4,6},{5,7},{6,4},{7,5},{8,10},{9,11},{10,... | collective-permute-start | bytes 3145736 | tf_op jit(solution)/shard_map/ppermute | solution.py:133
  196.0 42.0 %collective-permute-start.45 = (bf16[1024,1024]{1,0:T(8,128)(2,1)S(1)}, bf16[1024,1024]{1,0:T(8,128)(2,1)S(1)}, u32[]{:S(2)}, u32[]{:S(2)}) collective-permute-start(bf16[1024,1024]{1,0:T(8,128)(2,1)S(1)} %pad_maximum_fusion.4), channel_id=1, source_target_pairs={{0,1},{1,0},{2,3},{3,2},{4,5},{5,4},{6,7},{7,6},{8,9},{9,8},{10,11... | collective-permute-start | bytes 6291464 | tf_op jit(solution)/shard_map/ppermute | solution.py:133
  200.1 17.8 %collective-permute-start.26 = (bf16[128,1024]{1,0:T(8,128)(2,1)}, bf16[128,1024]{1,0:T(8,128)(2,1)S(1)}, u32[]{:S(2)}, u32[]{:S(2)}) collective-permute-start(bf16[128,1024]{1,0:T(8,128)(2,1)} %bitcast.49), channel_id=1, source_target_pairs={{0,24},{1,25},{2,26},{3,27},{4,28},{5,29},{6,30},{7,31},{8,16},{9,... | collective-permute-start | bytes 786440 | tf_op jit(solution)/shard_map/ppermute | solution.py:133
  215.0 34.0 %collective-permute-start.17 = (bf16[1024,1024]{1,0:T(8,128)(2,1)S(1)}, bf16[1024,1024]{1,0:T(8,128)(2,1)S(1)}, u32[]{:S(2)}, u32[]{:S(2)}) collective-permute-start(bf16[1024,1024]{1,0:T(8,128)(2,1)S(1)} %pad_maximum_fusion.3), channel_id=1, source_target_pairs={{0,1},{1,0},{2,3},{3,2},{4,5},{5,4},{6,7},{7,6},{8,9},{9,8},{10,11... | collective-permute-start | bytes 6291464 | tf_op jit(solution)/shard_map/ppermute | solution.py:133
  215.1 22.7 %collective-permute-start.41 = (bf16[128,1024]{1,0:T(8,128)(2,1)S(1)}, bf16[128,1024]{1,0:T(8,128)(2,1)S(1)}, u32[]{:S(2)}, u32[]{:S(2)}) collective-permute-start(bf16[128,1024]{1,0:T(8,128)(2,1)S(1)} %copy-done.58), channel_id=1, source_target_pairs={{0,4},{1,5},{2,6},{3,7},{4,0},{5,1},{6,2},{7,3},{8,12},{9,13},{10,... | collective-permute-start | bytes 786440 | tf_op jit(solution)/shard_map/ppermute | solution.py:133
  217.9 20.0 %collective-permute-start.34 = (bf16[128,1024]{1,0:T(8,128)(2,1)}, bf16[128,1024]{1,0:T(8,128)(2,1)S(1)}, u32[]{:S(2)}, u32[]{:S(2)}) collective-permute-start(bf16[128,1024]{1,0:T(8,128)(2,1)} %collective-permute-done.33), channel_id=1, source_target_pairs={{0,4},{1,5},{2,6},{3,7},{4,0},{5,1},{6,2},{7,3},{8,12},{9,13},{10,... | collective-permute-start | bytes 786440 | tf_op jit(solution)/shard_map/ppermute | solution.py:133
  223.6 14.2 %collective-permute-start.27 = (bf16[128,1024]{1,0:T(8,128)(2,1)S(1)}, bf16[128,1024]{1,0:T(8,128)(2,1)S(1)}, u32[]{:S(2)}, u32[]{:S(2)}) collective-permute-start(bf16[128,1024]{1,0:T(8,128)(2,1)S(1)} %collective-permute-done.26), channel_id=1, source_target_pairs={{0,4},{1,5},{2,6},{3,7},{4,0},{5,1},{6,2},{7,3},{8,12},{9,13},{10,... | collective-permute-start | bytes 786440 | tf_op jit(solution)/shard_map/ppermute | solution.py:133
  284.1 59.3 %collective-permute-start.85 = (bf16[4,128,1024]{2,1,0:T(8,128)(2,1)}, bf16[4,128,1024]{2,1,0:T(8,128)(2,1)}, u32[]{:S(2)}, u32[]{:S(2)}) collective-permute-start(bf16[4,128,1024]{2,1,0:T(8,128)(2,1)} %dynamic-slice_bitcast_fusion), channel_id=1, source_target_pairs={{0,4},{1,5},{2,6},{3,7},{4,0},{5,1},{6,2},{7,3},{8,12},{9,13},{10,... | collective-permute-start | bytes 3145736 | tf_op jit(solution)/shard_map/ppermute | solution.py:133
  311.2 37.2 %collective-permute-start.79 = (bf16[4,128,1024]{1,2,0:T(8,128)(2,1)}, bf16[4,128,1024]{1,2,0:T(8,128)(2,1)}, u32[]{:S(2)}, u32[]{:S(2)}) collective-permute-start(bf16[4,128,1024]{1,2,0:T(8,128)(2,1)} %bitcast.425), channel_id=1, source_target_pairs={{0,4},{1,5},{2,6},{3,7},{4,0},{5,1},{6,2},{7,3},{8,12},{9,13},{10,... | collective-permute-start | bytes 3145736 | tf_op jit(solution)/shard_map/ppermute | solution.py:133
  312.3 44.8 %collective-permute-start.73 = (bf16[4,128,1024]{1,2,0:T(8,128)(2,1)}, bf16[4,128,1024]{1,2,0:T(8,128)(2,1)}, u32[]{:S(2)}, u32[]{:S(2)}) collective-permute-start(bf16[4,128,1024]{1,2,0:T(8,128)(2,1)} %bitcast.424), channel_id=1, source_target_pairs={{0,4},{1,5},{2,6},{3,7},{4,0},{5,1},{6,2},{7,3},{8,12},{9,13},{10,... | collective-permute-start | bytes 3145736 | tf_op jit(solution)/shard_map/ppermute | solution.py:133
  330.2 98.1 %collective-permute-start.46 = (bf16[1024,1024]{1,0:T(8,128)(2,1)}, bf16[1024,1024]{1,0:T(8,128)(2,1)}, u32[]{:S(2)}, u32[]{:S(2)}) collective-permute-start(bf16[1024,1024]{1,0:T(8,128)(2,1)} %slice.245), channel_id=1, source_target_pairs={{0,1},{1,0},{2,3},{3,2},{4,5},{5,4},{6,7},{7,6},{8,9},{9,8},{10,11... | collective-permute-start | bytes 6291464 | tf_op jit(solution)/shard_map/ppermute | solution.py:133
  345.1 14.7 %collective-permute-start.86 = (bf16[128,1024]{1,0:T(8,128)(2,1)S(1)}, bf16[128,1024]{1,0:T(8,128)(2,1)S(1)}, u32[]{:S(2)}, u32[]{:S(2)}) collective-permute-start(bf16[128,1024]{1,0:T(8,128)(2,1)S(1)} %get-tuple-element.68), channel_id=1, source_target_pairs={{0,8},{1,9},{2,10},{3,11},{4,12},{5,13},{6,14},{7,15},{8,0},{9,1},... | collective-permute-start | bytes 786440 | tf_op jit(solution)/shard_map/ppermute | solution.py:133
  348.0 20.5 %collective-permute-start.88 = (bf16[128,1024]{1,0:T(8,128)(2,1)S(1)}, bf16[128,1024]{1,0:T(8,128)(2,1)S(1)}, u32[]{:S(2)}, u32[]{:S(2)}) collective-permute-start(bf16[128,1024]{1,0:T(8,128)(2,1)S(1)} %get-tuple-element.69), channel_id=1, source_target_pairs={{0,24},{1,25},{2,26},{3,27},{4,28},{5,29},{6,30},{7,31},{8,16},{9,... | collective-permute-start | bytes 786440 | tf_op jit(solution)/shard_map/ppermute | solution.py:133
  348.4 58.3 %collective-permute-start.87 = (bf16[128,1024]{1,0:T(8,128)(2,1)S(1)}, bf16[128,1024]{1,0:T(8,128)(2,1)S(1)}, u32[]{:S(2)}, u32[]{:S(2)}) collective-permute-start(bf16[128,1024]{1,0:T(8,128)(2,1)S(1)} %get-tuple-element.70), channel_id=1, source_target_pairs={{0,16},{1,17},{2,18},{3,19},{4,20},{5,21},{6,22},{7,23},{8,24},{9,... | collective-permute-start | bytes 786440 | tf_op jit(solution)/shard_map/ppermute | solution.py:133
  357.1 15.0 %collective-permute-start.80 = (bf16[128,1024]{0,1:T(8,128)(2,1)S(1)}, bf16[128,1024]{0,1:T(8,128)(2,1)S(1)}, u32[]{:S(2)}, u32[]{:S(2)}) collective-permute-start(bf16[128,1024]{0,1:T(8,128)(2,1)S(1)} %get-tuple-element.101), channel_id=1, source_target_pairs={{0,8},{1,9},{2,10},{3,11},{4,12},{5,13},{6,14},{7,15},{8,0},{9,1},... | collective-permute-start | bytes 786440 | tf_op jit(solution)/shard_map/ppermute | solution.py:133
  359.9 35.3 %collective-permute-start.82 = (bf16[128,1024]{0,1:T(8,128)(2,1)S(1)}, bf16[128,1024]{0,1:T(8,128)(2,1)S(1)}, u32[]{:S(2)}, u32[]{:S(2)}) collective-permute-start(bf16[128,1024]{0,1:T(8,128)(2,1)S(1)} %get-tuple-element.102), channel_id=1, source_target_pairs={{0,24},{1,25},{2,26},{3,27},{4,28},{5,29},{6,30},{7,31},{8,16},{9,... | collective-permute-start | bytes 786440 | tf_op jit(solution)/shard_map/ppermute | solution.py:133
  368.5 33.7 %collective-permute-start.81 = (bf16[128,1024]{0,1:T(8,128)(2,1)S(1)}, bf16[128,1024]{0,1:T(8,128)(2,1)S(1)}, u32[]{:S(2)}, u32[]{:S(2)}) collective-permute-start(bf16[128,1024]{0,1:T(8,128)(2,1)S(1)} %get-tuple-element.103), channel_id=1, source_target_pairs={{0,16},{1,17},{2,18},{3,19},{4,20},{5,21},{6,22},{7,23},{8,24},{9,... | collective-permute-start | bytes 786440 | tf_op jit(solution)/shard_map/ppermute | solution.py:133
  372.1 36.0 %collective-permute-start.74 = (bf16[128,1024]{0,1:T(8,128)(2,1)S(1)}, bf16[128,1024]{0,1:T(8,128)(2,1)S(1)}, u32[]{:S(2)}, u32[]{:S(2)}) collective-permute-start(bf16[128,1024]{0,1:T(8,128)(2,1)S(1)} %get-tuple-element.108), channel_id=1, source_target_pairs={{0,8},{1,9},{2,10},{3,11},{4,12},{5,13},{6,14},{7,15},{8,0},{9,1},... | collective-permute-start | bytes 786440 | tf_op jit(solution)/shard_map/ppermute | solution.py:133
  395.2 16.9 %collective-permute-start.76 = (bf16[128,1024]{0,1:T(8,128)(2,1)S(1)}, bf16[128,1024]{0,1:T(8,128)(2,1)S(1)}, u32[]{:S(2)}, u32[]{:S(2)}) collective-permute-start(bf16[128,1024]{0,1:T(8,128)(2,1)S(1)} %get-tuple-element.109), channel_id=1, source_target_pairs={{0,24},{1,25},{2,26},{3,27},{4,28},{5,29},{6,30},{7,31},{8,16},{9,... | collective-permute-start | bytes 786440 | tf_op jit(solution)/shard_map/ppermute | solution.py:133
  406.7 25.9 %collective-permute-start.42 = (bf16[1024,1024]{1,0:T(8,128)(2,1)S(1)}, bf16[1024,1024]{1,0:T(8,128)(2,1)S(1)}, u32[]{:S(2)}, u32[]{:S(2)}) collective-permute-start(bf16[1024,1024]{1,0:T(8,128)(2,1)S(1)} %copy-done.35), channel_id=1, source_target_pairs={{0,1},{1,0},{2,3},{3,2},{4,5},{5,4},{6,7},{7,6},{8,9},{9,8},{10,11... | collective-permute-start | bytes 6291464 | tf_op jit(solution)/shard_map/ppermute | solution.py:133
  417.3 15.1 %collective-permute-start.90 = (bf16[2,128,1024]{2,1,0:T(8,128)(2,1)S(1)}, bf16[2,128,1024]{2,1,0:T(8,128)(2,1)S(1)}, u32[]{:S(2)}, u32[]{:S(2)}) collective-permute-start(bf16[2,128,1024]{2,1,0:T(8,128)(2,1)S(1)} %pad_maximum_fusion.17), channel_id=1, source_target_pairs={{0,1},{1,0},{2,3},{3,2},{4,5},{5,4},{6,7},{7,6},{8,9},{9,8},{10,11... | collective-permute-start | bytes 1572872 | tf_op jit(solution)/shard_map/ppermute | solution.py:133
  430.9 26.0 %collective-permute-start.47 = (bf16[512,1024]{1,0:T(8,128)(2,1)S(1)}, bf16[512,1024]{1,0:T(8,128)(2,1)S(1)}, u32[]{:S(2)}, u32[]{:S(2)}) collective-permute-start(bf16[512,1024]{1,0:T(8,128)(2,1)S(1)} %slice.321), channel_id=1, source_target_pairs={{0,2},{1,3},{2,0},{3,1},{4,6},{5,7},{6,4},{7,5},{8,10},{9,11},{10,... | collective-permute-start | bytes 3145736 | tf_op jit(solution)/shard_map/ppermute | solution.py:133
  434.5 44.5 %collective-permute-start.43 = (bf16[512,1024]{1,0:T(8,128)(2,1)S(1)}, bf16[512,1024]{1,0:T(8,128)(2,1)S(1)}, u32[]{:S(2)}, u32[]{:S(2)}) collective-permute-start(bf16[512,1024]{1,0:T(8,128)(2,1)S(1)} %slice.322), channel_id=1, source_target_pairs={{0,2},{1,3},{2,0},{3,1},{4,6},{5,7},{6,4},{7,5},{8,10},{9,11},{10,... | collective-permute-start | bytes 3145736 | tf_op jit(solution)/shard_map/ppermute | solution.py:133
  541.4 42.9 %collective-permute-start.63 = (bf16[1024,512]{1,0:T(8,128)(2,1)}, bf16[1024,512]{1,0:T(8,128)(2,1)}, u32[]{:S(2)}, u32[]{:S(2)}) collective-permute-start(bf16[1024,512]{1,0:T(8,128)(2,1)} %constant_dynamic-slice_fusion.32), channel_id=1, source_target_pairs={{0,1},{1,0},{2,3},{3,2},{4,5},{5,4},{6,7},{7,6},{8,9},{9,8},{10,11... | collective-permute-start | bytes 3145736 | tf_op jit(solution)/shard_map/ppermute | solution.py:133
  555.6 47.7 %collective-permute-start.53 = (bf16[1024,1536]{1,0:T(8,128)(2,1)}, bf16[1024,1536]{1,0:T(8,128)(2,1)}, u32[]{:S(2)}, u32[]{:S(2)}) collective-permute-start(bf16[1024,1536]{1,0:T(8,128)(2,1)} %constant_dynamic-slice_fusion.42), channel_id=1, source_target_pairs={{0,1},{1,0},{2,3},{3,2},{4,5},{5,4},{6,7},{7,6},{8,9},{9,8},{10,11... | collective-permute-start | bytes 9437192 | tf_op jit(solution)/shard_map/ppermute | solution.py:133
  596.8 31.0 %collective-permute-start.67 = (bf16[4,128,128]{2,1,0:T(8,128)(2,1)}, bf16[4,128,128]{2,1,0:T(8,128)(2,1)S(1)}, u32[]{:S(2)}, u32[]{:S(2)}) collective-permute-start(bf16[4,128,128]{2,1,0:T(8,128)(2,1)} %dynamic-slice_bitcast_fusion.2), channel_id=1, source_target_pairs={{0,4},{1,5},{2,6},{3,7},{4,0},{5,1},{6,2},{7,3},{8,12},{9,13},{10,... | collective-permute-start | bytes 393224 | tf_op jit(solution)/shard_map/ppermute | solution.py:133
  601.9 25.9 %collective-permute-start.65 = (bf16[4,128,128]{2,1,0:T(8,128)(2,1)}, bf16[4,128,128]{2,1,0:T(8,128)(2,1)}, u32[]{:S(2)}, u32[]{:S(2)}) collective-permute-start(bf16[4,128,128]{2,1,0:T(8,128)(2,1)} %constant_dynamic-slice_fusion.29), channel_id=1, source_target_pairs={{0,2},{1,3},{2,0},{3,1},{4,6},{5,7},{6,4},{7,5},{8,10},{9,11},{10,... | collective-permute-start | bytes 393224 | tf_op jit(solution)/shard_map/ppermute | solution.py:133
  622.4 14.8 %collective-permute-start.56 = (bf16[4,2,128,384]{3,2,1,0:T(8,128)(2,1)S(1)}, bf16[4,2,128,384]{3,2,1,0:T(8,128)(2,1)S(1)}, u32[]{:S(2)}, u32[]{:S(2)}) collective-permute-start(bf16[4,2,128,384]{3,2,1,0:T(8,128)(2,1)S(1)} %bitcast.445), channel_id=1, source_target_pairs={{0,2},{1,3},{2,0},{3,1},{4,6},{5,7},{6,4},{7,5},{8,10},{9,11},{10,... | collective-permute-start | bytes 2359304 | tf_op jit(solution)/shard_map/ppermute | solution.py:133
  626.5 18.8 %collective-permute-start.54 = (bf16[4,128,768]{2,1,0:T(8,128)(2,1)S(1)}, bf16[4,128,768]{2,1,0:T(8,128)(2,1)S(1)}, u32[]{:S(2)}, u32[]{:S(2)}) collective-permute-start(bf16[4,128,768]{2,1,0:T(8,128)(2,1)S(1)} %bitcast.444), channel_id=1, source_target_pairs={{0,4},{1,5},{2,6},{3,7},{4,0},{5,1},{6,2},{7,3},{8,12},{9,13},{10,... | collective-permute-start | bytes 2359304 | tf_op jit(solution)/shard_map/ppermute | solution.py:133
  628.8 18.1 %collective-permute-start.68 = (bf16[128,2,128]{2,0,1:T(8,128)(2,1)S(1)}, bf16[128,2,128]{2,0,1:T(8,128)(2,1)S(1)}, u32[]{:S(2)}, u32[]{:S(2)}) collective-permute-start(bf16[128,2,128]{2,0,1:T(8,128)(2,1)S(1)} %get-tuple-element.146), channel_id=1, source_target_pairs={{0,8},{1,9},{2,10},{3,11},{4,12},{5,13},{6,14},{7,15},{8,0},{9,1},... | collective-permute-start | bytes 196616 | tf_op jit(solution)/shard_map/ppermute | solution.py:133
  630.6 16.3 %collective-permute-start.69 = (bf16[128,2,128]{2,0,1:T(8,128)(2,1)S(1)}, bf16[128,2,128]{2,0,1:T(8,128)(2,1)S(1)}, u32[]{:S(2)}, u32[]{:S(2)}) collective-permute-start(bf16[128,2,128]{2,0,1:T(8,128)(2,1)S(1)} %get-tuple-element.147), channel_id=1, source_target_pairs={{0,16},{1,17},{2,18},{3,19},{4,20},{5,21},{6,22},{7,23},{8,24},{9,... | collective-permute-start | bytes 196616 | tf_op jit(solution)/shard_map/ppermute | solution.py:133
  631.4 15.5 %collective-permute-start.70 = (bf16[128,2,128]{2,0,1:T(8,128)(2,1)S(1)}, bf16[128,2,128]{2,0,1:T(8,128)(2,1)S(1)}, u32[]{:S(2)}, u32[]{:S(2)}) collective-permute-start(bf16[128,2,128]{2,0,1:T(8,128)(2,1)S(1)} %get-tuple-element.148), channel_id=1, source_target_pairs={{0,24},{1,25},{2,26},{3,27},{4,28},{5,29},{6,30},{7,31},{8,16},{9,... | collective-permute-start | bytes 196616 | tf_op jit(solution)/shard_map/ppermute | solution.py:133
  (133 other events, 1464.2 us)

commit v2 on v1

--- a/solution.py
+++ b/solution.py
@@ -3,6 +3,8 @@
 import jax
 import jax.numpy as jnp
 from jax import lax
+from jax.experimental import pallas as pl
+from jax.experimental.pallas import tpu as pltpu
 from jax.sharding import PartitionSpec as P
 
 HEADS = 16
@@ -139,42 +141,909 @@
     return lax.dynamic_index_in_dim(stacked, index, 0, keepdims=False)
 
 
-def solution(mesh):
+BITS = {"z1": (2, 0), "z2": (4, 0), "z3": (6, 0), "x": (1, 0), "y": (0, 2), "core": (0, 1)}
+CONTRACT = {
+    "nn": (((1,), (0,)), ((), ())),
+    "nt": (((1,), (1,)), ((), ())),
+    "tn": (((0,), (0,)), ((), ())),
+}
+BIG = pltpu.CompilerParams(vmem_limit_bytes=56 << 20)
+
+
+def work(flops):
+    return pl.CostEstimate(flops=int(flops), bytes_accessed=0, transcendentals=0)
+
+
+ANY = pl.BlockSpec(memory_space=pl.ANY)
+SMEM = pl.BlockSpec(memory_space=pltpu.SMEM)
+
+
+def dot(a, b, form="nn"):
+    return lax.dot_general(a, b, CONTRACT[form], preferred_element_type=F32)
+
+
+def after(value, *done):
+    return lax.optimization_barrier((value,) + done)[0]
+
+
+def window(*values):
+    return lax.optimization_barrier(values)
+
+
+def lane_tables(position, width):
+    lane = jnp.arange(2 * width, dtype=jnp.int32)
+    index = (lane % (width // 2)).astype(F32)
+    freqs = jnp.power(10000.0, -index * (2.0 / width))
+    angles = position.astype(F32)[:, None] * freqs[None, :]
+    sign = jnp.where(lane % width < width // 2, -1.0, 1.0)
+    return jnp.cos(angles), jnp.sin(angles) * sign[None, :]
+
+
+def sds(shape, dtype):
+    return jax.ShapeDtypeStruct(shape, dtype)
+
+
+def whole(shape):
+    return pl.BlockSpec(shape, lambda *_: (0,) * len(shape))
+
+
+def rotate_lanes(u, cosine, signed_sine, first):
+    turned = jnp.where(first, pltpu.roll(u, 96, 1), pltpu.roll(u, 32, 1))
+    return u * cosine + turned * signed_sine
+
+
+PIECES = (
+    ((0, 0, 0),),
+    ((1, 0, 0), (2, 0, 0), (3, 0, 0)),
+    ((0, 1, 0), (0, 0, 1), (0, 1, 1)),
+    ((1, 1, 0), (2, 1, 0), (3, 1, 0)),
+    ((1, 0, 1), (2, 0, 1), (3, 0, 1)),
+    ((1, 1, 1),),
+    ((2, 1, 1), (3, 1, 1)),
+)
+
+
+def project_kernel(*refs):
+    n = len(PIECES)
+    idx, own, came = refs[0], refs[1 : 1 + n], refs[1 + n : 1 + 2 * n]
+    x_ref, cos_ref, sin_ref = refs[1 + 2 * n : 4 + 2 * n]
+    qkv_ref, normed_ref, w_ref, vec_ref, weights, sems, out_sem = refs[4 + 2 * n :]
+    j, steps = pl.program_id(0), pl.num_programs(0)
+    block = qkv_ref.shape[1]
+
+    def copies():
+        out, count = [], 0
+        for core_bit, group in ((0, own), (1, came)):
+            for ref, owners in zip(group, PIECES):
+                for i, (k, dx, dy) in enumerate(owners):
+                    owner = (((idx[0] ^ k) * 2 + (idx[1] ^ dx)) * 2 + (idx[2] ^ dy)) * 2
+                    row = pl.multiple_of((owner + (idx[3] ^ core_bit)) * 32, 32)
+                    out.append(
+                        pltpu.make_async_copy(
+                            ref.at[i], weights.at[pl.ds(row, 32), :], sems.at[count]
+                        )
+                    )
+                    count += 1
+        return out
+
+    def save():
+        return pltpu.make_async_copy(weights, w_ref, out_sem)
+
+    @pl.when(j == 0)
+    def _():
+        pieces = copies()
+        for c in pieces:
+            c.start()
+        x = x_ref[...].astype(F32)
+        centered = x - jnp.mean(x, axis=1, keepdims=True)
+        unit = centered * lax.rsqrt(jnp.mean(centered * centered, axis=1, keepdims=True) + EPS)
+        for c in pieces:
+            c.wait()
+        save().start()
+        vecs = weights[:, weights.shape[1] - 128 :].astype(F32).T
+        vec_ref[...] = vecs[:8]
+        normed_ref[...] = (unit * vecs[0:1] + vecs[1:2]).astype(BF)
+
+    p = dot(normed_ref[...], weights[:, pl.ds(pl.multiple_of(j * block, block), block)])
+    lane = lax.broadcasted_iota(jnp.int32, (1, 128), 1)
+    first = (lane % 64) < 32
+
+    @pl.when(j * 3 < 2 * steps)
+    def _():
+        for c in range(0, block, 128):
+            cols = slice(c, c + 128)
+            qkv_ref[:, cols] = rotate_lanes(p[:, cols], cos_ref[...], sin_ref[...], first).astype(BF)
+
+    @pl.when(j * 3 >= 2 * steps)
+    def _():
+        qkv_ref[...] = p.astype(BF)
+
+    @pl.when(j == steps - 1)
+    def _():
+        save().wait()
+
+
+def project(idx, own, came, x, cosine, signed_sine, block=512):
+    rows, width = x.shape
+    cols = own[0].shape[-1]
+    return pl.pallas_call(
+        project_kernel,
+        grid=(3 * width // block,),
+        in_specs=[SMEM] + [ANY] * (2 * len(PIECES)) + [whole((rows, width))] + [whole((rows, 128))] * 2,
+        out_specs=[
+            pl.BlockSpec((rows, block), lambda j: (0, j)),
+            whole((rows, width)),
+            ANY,
+            whole((8, width)),
+        ],
+        out_shape=[
+            sds((rows, 3 * width), BF),
+            sds((rows, width), BF),
+            sds((width, cols), BF),
+            sds((8, width), F32),
+        ],
+        scratch_shapes=[
+            pltpu.VMEM((width, cols), BF),
+            pltpu.SemaphoreType.DMA((32,)),
+            pltpu.SemaphoreType.DMA,
+        ],
+        compiler_params=BIG,
+        cost_estimate=work(1e9),
+        name="project",
+    )(idx, *own, *came, x, cosine, signed_sine)
+
+
+def set_bias(bias_ref, pos_ref, rows):
+    for b in range(rows // WINDOW):
+        keys = WINDOW if b == 0 else 2 * WINDOW
+        offset = (
+            lax.broadcasted_iota(jnp.int32, (WINDOW, keys), 0)
+            - lax.broadcasted_iota(jnp.int32, (WINDOW, keys), 1)
+            + (keys - WINDOW)
+        )
+        reach = jnp.minimum(pos_ref[b * WINDOW : (b + 1) * WINDOW, :], WINDOW - 1)
+        seen = (offset >= 0) & (offset <= reach)
+        bias_ref[b, :, 2 * WINDOW - keys :] = jnp.where(seen, 0.0, -1e30)
+
+
+def split_heads(u, low):
+    zero = jnp.zeros_like(u)
+    return jnp.concatenate([jnp.where(low, u, zero), jnp.where(low, zero, u)], axis=0)
+
+
+def pair_probs(q, k, bias, low):
+    q = split_heads(q, low) * jnp.asarray(0.125, BF)
+    scores = dot(q, k, "nt") + jnp.concatenate([bias, bias], axis=0)
+    e = jnp.exp(scores - jnp.max(scores, axis=1, keepdims=True))
+    return q, e * (1.0 / jnp.sum(e, axis=1, keepdims=True))
+
+
+def attend_kernel(q_ref, k_ref, v_ref, pos_ref, o_ref, bias_ref):
+    rows = q_ref.shape[0]
+
+    @pl.when(pl.program_id(0) == 0)
+    def _():
+        set_bias(bias_ref, pos_ref, rows)
+
+    low = lax.broadcasted_iota(jnp.int32, (1, 128), 1) < 64
+    for b in range(rows // WINDOW):
+        here = slice(b * WINDOW, (b + 1) * WINDOW)
+        keys = slice(max(b - 1, 0) * WINDOW, (b + 1) * WINDOW)
+        bias = bias_ref[b, :, 2 * WINDOW - (keys.stop - keys.start) :]
+        _, probs = pair_probs(q_ref[here, :], k_ref[keys, :], bias, low)
+        out = dot(probs.astype(BF), v_ref[keys, :])
+        o_ref[here, :] = jnp.where(low, out[:WINDOW], out[WINDOW:]).astype(BF)
+
+
+def attend(qkv, position):
+    rows, width = qkv.shape[0], qkv.shape[1] // 3
+    pairs = width // 128
+    cols = lambda part: pl.BlockSpec((rows, 128), lambda j: (0, j + part * pairs))
+    return pl.pallas_call(
+        attend_kernel,
+        grid=(pairs,),
+        in_specs=[cols(0), cols(1), cols(2), whole((rows, 1))],
+        out_specs=cols(0),
+        out_shape=sds((rows, width), BF),
+        scratch_shapes=[pltpu.VMEM((rows // WINDOW, WINDOW, 2 * WINDOW), F32)],
+        compiler_params=BIG,
+        cost_estimate=work(1e9),
+        name="attend",
+    )(qkv, qkv, qkv, position)
+
+
+def attend_back_kernel(
+    q_ref, k_ref, v_ref, do_ref, pos_ref, cos_ref, sin_ref, dq_ref, dk_ref, dv_ref, bias_ref
+):
+    rows = q_ref.shape[0]
+    blocks = rows // WINDOW
+
+    @pl.when(pl.program_id(0) == 0)
+    def _():
+        set_bias(bias_ref, pos_ref, rows)
+
+    lane = lax.broadcasted_iota(jnp.int32, (1, 128), 1)
+    low, first = lane < 64, (lane % 64) < 32
+
+    def turn_back(u, here):
+        return rotate_lanes(u, cos_ref[here, :], -sin_ref[here, :], first).astype(BF)
+
+    dk, dv = [None] * blocks, [None] * blocks
+    for b in range(blocks):
+        here = slice(b * WINDOW, (b + 1) * WINDOW)
+        keys = slice(max(b - 1, 0) * WINDOW, (b + 1) * WINDOW)
+        bias = bias_ref[b, :, 2 * WINDOW - (keys.stop - keys.start) :]
+        q, probs = pair_probs(q_ref[here, :], k_ref[keys, :], bias, low)
+        do = split_heads(do_ref[here, :], low)
+        dp = dot(do, v_ref[keys, :], "nt")
+        delta = jnp.sum(probs * dp, axis=1, keepdims=True)
+        ds = (probs * (dp - delta)).astype(BF)
+        dq = dot(ds, k_ref[keys, :]) * 0.125
+        dq_ref[here, :] = turn_back(jnp.where(low, dq[:WINDOW], dq[WINDOW:]), here)
+        k_part = dot(ds, q, "tn")
+        v_part = dot(probs.astype(BF), do, "tn")
+        for i, kb in enumerate(range(max(b - 1, 0), b + 1)):
+            part = slice(i * WINDOW, (i + 1) * WINDOW)
+            dk[kb] = k_part[part] if dk[kb] is None else dk[kb] + k_part[part]
+            dv[kb] = v_part[part] if dv[kb] is None else dv[kb] + v_part[part]
+    for kb in range(blocks):
+        here = slice(kb * WINDOW, (kb + 1) * WINDOW)
+        dk_ref[here, :] = turn_back(dk[kb], here)
+        dv_ref[here, :] = dv[kb].astype(BF)
+
+
+def attend_back(qkv, grad, position, cosine, signed_sine):
+    rows, width = qkv.shape[0], qkv.shape[1] // 3
+    pairs = width // 128
+    cols = lambda part: pl.BlockSpec((rows, 128), lambda j: (0, j + part * pairs))
+    return pl.pallas_call(
+        attend_back_kernel,
+        grid=(pairs,),
+        in_specs=[cols(0), cols(1), cols(2), cols(0), whole((rows, 1))] + [whole((rows, 128))] * 2,
+        out_specs=[cols(0)] * 3,
+        out_shape=[sds((rows, width), BF)] * 3,
+        scratch_shapes=[pltpu.VMEM((rows // WINDOW, WINDOW, 2 * WINDOW), F32)],
+        compiler_params=BIG,
+        cost_estimate=work(1e9),
+        name="attend_back",
+    )(qkv, qkv, qkv, grad, position, cosine, signed_sine)
+
+
+def mlp_copies(idx, pieces, downs, gate, up, down, sems):
+    first, second, last = [], [], []
+    half = gate.shape[1] // 2
+
+    def copy(src, dst, group):
+        n = len(first) + len(second) + len(last)
+        group.append(pltpu.make_async_copy(src, dst, sems.at[n]))
+
+    for i, ref in enumerate(pieces):
+        rows = ref.shape[1]
+        here = pl.ds(pl.multiple_of(((idx[0] * 2 + idx[1]) ^ i) * rows, rows), rows)
+        for c, group in ((0, first), (half, second)):
+            cols = pl.ds(c, half)
+            for m, target in ((0, gate), (1, up)):
+                copy(ref.at[m, :, cols], target.at[here, cols], group)
+    for i, ref in enumerate(downs):
+        rows = ref.shape[0]
+        here = pl.ds(pl.multiple_of(((idx[0] * 2 + idx[1]) ^ i) * rows, rows), rows)
+        copy(ref, down.at[here, :], last)
+    return first, second, last
+
+
+def store_split(idx, total, send_ref, keep_ref):
+    rows = send_ref.shape[1]
+    for k in range(send_ref.shape[0]):
+        for ref, x in ((send_ref, 1 - idx[1]), (keep_ref, idx[1])):
+            at = pl.multiple_of((2 * k + x) * rows, rows)
+            ref[k] = total[pl.ds(at, rows), :].astype(BF)
+
+
+def mlp_kernel(last_half, *refs):
+    idx, pieces, downs = refs[0], refs[1:9], refs[9:17]
+    n_parts, g_parts, scale_ref = refs[17:19], refs[19:21], refs[21]
+    refs = refs[22:]
+    if last_half:
+        before_ref, refs = refs[0], refs[1:]
+    gg_ref, gu_ref = refs[:2]
+    gn_parts, mlp_parts = refs[2:4], refs[4:6]
+    refs = refs[6:]
+    if last_half:
+        send_ref, keep_ref, refs = refs[0], refs[1], refs[2:]
+    else:
+        total_ref, refs = refs[0], refs[1:]
+    w_gate, w_up, w_down, total, n_buf, g_buf, sems = refs
+    i, last = pl.program_id(0), pl.num_programs(0) - 1
+    block, half = gg_ref.shape[0], pl.num_programs(0) // 2
+    first, second, down = mlp_copies(idx, pieces, downs, w_gate, w_up, w_down, sems)
+
+    def wait(copies):
+        @pl.when(i == 0)
+        def _():
+            for c in copies:
+                c.wait()
+
+    @pl.when(i == 0)
+    def _():
+        for c in first + second + down:
+            c.start()
+
+    here = pl.ds(pl.multiple_of((i % half) * block, block), block)
+
+    def load(which):
+        n_buf[...] = n_parts[which][here, :]
+        g_buf[...] = (scale_ref[...] * g_parts[which][here, :].astype(F32)).astype(BF)
+
+    pl.when(i < half)(lambda: load(0))
+    pl.when(i >= half)(lambda: load(1))
+    n, gm = n_buf[...], g_buf[...]
+    width = w_gate.shape[1]
+    kept = []
+    wait(first)
+    for c in range(0, width, width // 2):
+        cols = slice(c, c + width // 2)
+        gate, up = dot(n, w_gate[:, cols]), dot(n, w_up[:, cols])
+        if c == 0:
+            wait(second)
+        s = 0.5 * jnp.tanh(0.5 * gate) + 0.5
+        silu = gate * s
+        hidden = (silu * up).astype(BF)
+        part = dot(hidden, gm, "tn")
+
+        @pl.when(i == 0)
+        def _():
+            if last_half:
+                total[cols, :] = before_ref[cols, :].astype(F32) + part
+            else:
+                total[cols, :] = part
+
+        @pl.when(i > 0)
+        def _():
+            total[cols, :] += part
+
+        kept.append((cols, silu, up * (s + silu * (1.0 - s)), hidden))
+    wait(down)
+    gn = mlp = None
+    for cols, silu, slope, hidden in kept:
+        gh = dot(gm, w_down[cols, :], "nt")
+        gg = (gh * slope).astype(BF)
+        gu = (gh * silu).astype(BF)
+        gg_ref[:, cols], gu_ref[:, cols] = gg, gu
+        gn_c = dot(gg, w_gate[:, cols], "nt") + dot(gu, w_up[:, cols], "nt")
+        mlp_c = dot(hidden, w_down[cols, :])
+        gn = gn_c if gn is None else gn + gn_c
+        mlp = mlp_c if mlp is None else mlp + mlp_c
+
+    def store(which):
+        gn_parts[which][here, :] = gn.astype(BF)
+        mlp_parts[which][here, :] = mlp.astype(BF)
+
+    pl.when(i < half)(lambda: store(0))
+    pl.when(i >= half)(lambda: store(1))
+
+    @pl.when(i == last)
+    def _():
+        if last_half:
+            store_split(idx, total, send_ref, keep_ref)
+        else:
+            total_ref[...] = total[...].astype(BF)
+
+
+def mlp_both(idx, pieces, downs, n_parts, g_parts, scale, before=None, block=512):
+    rows, width = n_parts[0].shape
+    part = pieces[0].shape[2]
+    last_half = before is not None
+    row = pl.BlockSpec((block, part), lambda i: (i, 0))
+    part_spec, part_shape = whole((rows, width)), sds((rows, width), BF)
+    split, total = (4, part // 8, width), (part, width)
+    in_specs = [SMEM] + [ANY] * 16 + [part_spec] * 4 + [whole((1, width))]
+    out_specs = [row, row] + [part_spec] * 4
+    out_shape = [sds((2 * rows, part), BF)] * 2 + [part_shape] * 4
+    args = (idx, *pieces, *downs, *n_parts, *g_parts, scale)
+    if last_half:
+        in_specs.append(whole(total))
+        args += (before,)
+        out_specs += [whole(split)] * 2
+        out_shape += [sds(split, BF)] * 2
+    else:
+        out_specs.append(whole(total))
+        out_shape.append(sds(total, BF))
+    return pl.pallas_call(
+        lambda *refs: mlp_kernel(last_half, *refs),
+        grid=(2 * rows // block,),
+        in_specs=in_specs,
+        out_specs=out_specs,
+        out_shape=out_shape,
+        scratch_shapes=[
+            pltpu.VMEM((width, part), BF),
+            pltpu.VMEM((width, part), BF),
+            pltpu.VMEM((part, width), BF),
+            pltpu.VMEM(total, F32),
+            pltpu.VMEM((block, width), BF),
+            pltpu.VMEM((block, width), BF),
+            pltpu.SemaphoreType.DMA((40,)),
+        ],
+        compiler_params=BIG,
+        cost_estimate=work(1e9),
+        name="mlp_both",
+    )(*args)
+
+
+def weight_grad_kernel(idx, *refs):
+    a_refs, b_refs, send_ref, keep_ref = refs[:8], refs[8:10], refs[10], refs[11]
+    total = None
+    for p in range(4):
+        a = jnp.concatenate([a_refs[2 * p][...], a_refs[2 * p + 1][...]], axis=1)
+        rows = a.shape[0]
+        part = dot(a, b_refs[p // 2][pl.ds((p % 2) * rows, rows), :], "tn")
+        total = part if total is None else total + part
+    total = total.astype(BF).reshape((2,) + send_ref.shape[1:])
+    half = pl.num_programs(0) // 2
+
+    @pl.when(pl.program_id(0) < half)
+    def _():
+        send_ref[...] = total
+
+    @pl.when(pl.program_id(0) >= half)
+    def _():
+        keep_ref[...] = total
+
+
+def weight_grad(idx, a_parts, b_parts):
+    tokens, width = a_parts[0].shape
+    part = b_parts[0].shape[1]
+    rows = width // 8
+    split = (4, rows, part)
+
+    def column(which):
+        def place(i, s):
+            mine = jnp.where(i < 2, 1 - s[1], s[1])
+            return (0, 2 * (2 * (i % 2) + which) + mine)
+
+        return pl.BlockSpec((tokens, rows), place)
+
+    return pl.pallas_call(
+        weight_grad_kernel,
+        grid_spec=pltpu.PrefetchScalarGridSpec(
+            num_scalar_prefetch=1,
+            grid=(4,),
+            in_specs=[column(0), column(1)] * 4
+            + [pl.BlockSpec((2 * tokens, part), lambda i, s: (0, 0))] * 2,
+            out_specs=[
+                pl.BlockSpec((2, rows, part), lambda i, s: (jnp.minimum(i, 1), 0, 0)),
+                pl.BlockSpec((2, rows, part), lambda i, s: (jnp.maximum(i - 2, 0), 0, 0)),
+            ],
+        ),
+        out_shape=[sds(split, BF)] * 2,
+        compiler_params=BIG,
+        cost_estimate=work(1e9),
+        name="weight_grad",
+    )(idx, *[p for p in a_parts for _ in range(2)], *b_parts)
+
+
+def attn_grad_kernel(idx, q_in, o_in, dq, dk, dv, do, *refs):
+    outs, total = refs[:8], refs[8]
+    core = idx[3]
+    half = dq.shape[1]
+    for n, parts in enumerate((((q_in, dq), (q_in, dk)), ((q_in, dv), (o_in, do)))):
+        side = idx[1 + n]
+        for c, (a, b) in enumerate(parts):
+            product = dot(a[...], b[...], "tn").astype(BF)
+            total[:, :, :, :, :, c * half : (c + 1) * half] = product.reshape(4, 2, 2, 2, 32, half)
+        for m in range(4):
+            to_core = (1 - core) if m < 2 else core
+            to_side = (1 - side) if m % 2 == 0 else side
+            for k in range(4):
+                for other in range(2):
+                    x, y = (to_side, other) if n == 0 else (other, to_side)
+                    outs[4 * n + m][k, other] = total[k, x, y, to_core]
+
+
+def attn_grad(idx, q_in, o_in, dq, dk, dv, do):
+    width = q_in.shape[1]
+    vmem = pl.BlockSpec(memory_space=pltpu.VMEM)
+    return pl.pallas_call(
+        attn_grad_kernel,
+        in_specs=[SMEM] + [vmem] * 6,
+        out_specs=[vmem] * 8,
+        out_shape=[sds((4, 2, 32, 2 * width), BF)] * 8,
+        scratch_shapes=[pltpu.VMEM((4, 2, 2, 2, 32, 2 * width), BF)],
+        compiler_params=BIG,
+        cost_estimate=work(1e9),
+        name="attn_grad",
+    )(idx, q_in, o_in, dq, dk, dv, do)
+
+
+def place_kernel(idx, own, y_ref, core_ref, *outs):
+    rep = idx[2] * 2 + idx[3]
+    for ref, d in ((own, 0), (y_ref, 2), (core_ref.at[0], 1), (core_ref.at[1], 3)):
+        low = 0
+        for out in outs:
+            cols = out.shape[2]
+            out[pl.ds(rep ^ d, 1)] = ref[:, low : low + cols].astype(F32)[None]
+            low += cols
+
+
+def place_rows(idx, own, other_y, other_core, widths):
+    rows = own.shape[0]
+    vmem = pl.BlockSpec(memory_space=pltpu.VMEM)
+    outs = pl.pallas_call(
+        place_kernel,
+        in_specs=[SMEM, vmem, vmem, vmem],
+        out_specs=[vmem] * len(widths),
+        out_shape=[sds((4, rows, w), F32) for w in widths],
+        compiler_params=BIG,
+        cost_estimate=work(1e9),
+        name="place_rows",
+    )(idx, own, other_y, other_core)
+    return [out.reshape(4 * rows, -1) for out in outs]
+
+
+def place_columns_kernel(idx, up_ref, gate_ref, y_ref, core_ref, up_out, gate_out):
+    rep = idx[2] * 2 + idx[3]
+    for m, (own, out) in enumerate(((up_ref, up_out), (gate_ref, gate_out))):
+        parts = ((own, 0), (y_ref.at[m], 2), (core_ref.at[0, m], 1), (core_ref.at[1, m], 3))
+        for ref, d in parts:
+            for g in range(own.shape[1] // 128):
+                at = pl.multiple_of((g * 4 + (rep ^ d)) * 128, 128)
+                out[:, pl.ds(at, 128)] = ref[:, g * 128 : (g + 1) * 128].astype(F32)
+
+
+def place_columns(idx, up, gate, other_y, other_core):
+    rows, cols = up.shape
+    vmem = pl.BlockSpec(memory_space=pltpu.VMEM)
+    return pl.pallas_call(
+        place_columns_kernel,
+        in_specs=[SMEM] + [vmem] * 4,
+        out_specs=[vmem] * 2,
+        out_shape=[sds((rows, 4 * cols), F32)] * 2,
+        compiler_params=BIG,
+        cost_estimate=work(1e9),
+        name="place_columns",
+    )(idx, up, gate, other_y, other_core)
+
+
+def share_kernel(idx, gate_ref, up_ref, here_ref, there_ref):
+    rep = idx[2] * 2 + idx[3]
+    for d in range(4):
+        out = (here_ref, there_ref)[d // 2]
+        for m, ref in enumerate((gate_ref, up_ref)):
+            for g in range(out.shape[3] // 128):
+                at = pl.multiple_of((g * 4 + (rep ^ d)) * 128, 128)
+                out[d % 2, m, :, g * 128 : (g + 1) * 128] = ref[:, pl.ds(at, 128)]
+
+
+def share(idx, w_gate, w_up):
+    rows, ff = w_gate.shape
+    vmem = pl.BlockSpec(memory_space=pltpu.VMEM)
+    return pl.pallas_call(
+        share_kernel,
+        in_specs=[SMEM, vmem, vmem],
+        out_specs=[vmem] * 2,
+        out_shape=[sds((2, 2, rows, ff // 4), BF)] * 2,
+        compiler_params=BIG,
+        cost_estimate=work(1e9),
+        name="share",
+    )(idx, w_gate, w_up)
+
+
+def join_kernel(idx, own, y_ref, core_ref, out_ref):
+    rep = idx[2] * 2 + idx[3]
+    rows = own.shape[2]
+    parts = ((own.at[0], 0), (y_ref.at[0], 2), (core_ref.at[0], 1), (core_ref.at[1], 3))
+    for ref, d in parts:
+        at = pl.multiple_of((rep ^ d) * rows, rows)
+        out_ref[:, pl.ds(at, rows), :] = ref[...]
+
+
+def join(idx, own, other_y, other_core):
+    rows, part = own.shape[2:]
+    vmem = pl.BlockSpec(memory_space=pltpu.VMEM)
+    return pl.pallas_call(
+        join_kernel,
+        in_specs=[SMEM] + [vmem] * 3,
+        out_specs=vmem,
+        out_shape=sds((2, 4 * rows, part), BF),
+        compiler_params=BIG,
+        cost_estimate=work(1e9),
+        name="join",
+    )(idx, own, other_y, other_core)
+
+
+def tuned(mesh):
+    swap_bits = make_links(8, 4)
+
+    def swap(value, name):
+        return swap_bits(value, *BITS[name])
+
+    def add(a, b):
+        return (a.astype(F32) + b.astype(F32)).astype(BF)
+
+    def along(value, index, axis):
+        return lax.dynamic_index_in_dim(value, index, axis, keepdims=False)
+
+    def shards(
+        inputs,
+        lengths,
+        ln1_gain,
+        ln1_bias,
+        w_qkv,
+        w_out,
+        scale_attn,
+        ln2_gain,
+        ln2_bias,
+        w_gate,
+        w_up,
+        w_down,
+        scale_mlp,
+        grad_out,
+    ):
+        count, width = inputs.shape
+        head_width = width // HEADS
+        group, rep = lax.axis_index("group"), lax.axis_index("rep")
+        z, x, y, core = group // 2, group % 2, rep // 2, rep % 2
+        idx = jnp.stack([z, x, y, core]).astype(jnp.int32)
+
+        vectors = jnp.stack([ln1_gain, ln1_bias, scale_attn, ln2_gain, ln2_bias, scale_mlp], axis=1)
+        vectors = jnp.pad(vectors, ((0, 0), (0, 122)))
+        bundle = jnp.concatenate([w_qkv, w_out, vectors], axis=1)[None]
+        share_here, share_there = share(idx, w_gate, w_up)
+        bundle, share_there = window(bundle, share_there)
+        from_z = [swap(bundle, "z1"), swap(bundle, "z2")]
+        x_own, share_y = swap(bundle, "x"), swap(share_there, "y")
+        y_own = swap(bundle, "y")
+
+        segment, position = clip_layout(lengths[0], count)
+        cosine, sine = lane_tables(position, head_width)
+        position = position[:, None]
+
+        *from_z, x_own, y_own, share_y, share_here, bundle, w_down = window(
+            *from_z, x_own, y_own, share_y, share_here, bundle, w_down
+        )
+        from_z.append(swap(bundle, "z3"))
+        share_core = swap(jnp.stack([share_here[1], share_y[1]]), "core")
+        gu0 = join(idx, share_here, share_y, share_core)
+        both_own, dnx0, came_own = swap(x_own, "y"), swap(w_down, "x"), swap(bundle, "core")
+        *from_z, gu0, both_own, x_own, y_own, dnx0, came_own, cosine, sine, position = window(
+            *from_z, gu0, both_own, x_own, y_own, dnx0, came_own, cosine, sine, position
+        )
+        rest = jnp.concatenate(from_z)
+        owns = jnp.concatenate([x_own, y_own, both_own])
+        rest, owns = window(rest, owns)
+        x_rest, y_rest = swap(rest, "x"), swap(rest, "y")
+        gu1, gu2, gux0 = swap(gu0, "z1"), swap(gu0, "z2"), swap(gu0, "x")
+
+        x_rest, y_rest, gu1, gu2, gux0, w_down = window(x_rest, y_rest, gu1, gu2, gux0, w_down)
+        y_one, x_two, w_down, rest = window(x_rest[:1], y_rest[1:], w_down, rest)
+        both_one, both_two = swap(y_one, "y"), swap(x_two, "x")
+        dn1, dn2 = swap(w_down, "z1"), swap(w_down, "z2")
+        came_rest = swap(rest, "core")
+
+        have = [bundle, rest, owns, x_rest, y_rest, both_one, both_two]
+        gu0, gu1, gu2, dn1, dn2, grad_out, came_rest, *have = window(
+            gu0, gu1, gu2, dn1, dn2, grad_out, came_rest, *have
+        )
+        came = [came_own, came_rest] + [swap(p, "core") for p in have[2:]]
+        gu3, gux1, go_y = swap(gu0, "z3"), swap(gu1, "x"), swap(grad_out, "y")
+        dnx1, dnx2 = swap(dn1, "x"), swap(dn2, "x")
+        *came, cosine, sine, position = window(*came, cosine, sine, position)
+
+        qkv, normed, w_attn, vecs = project(idx, have, came, inputs, cosine, sine)
+        qkv, gux1, gu2, dnx1, dnx2, gu3, w_down = window(
+            qkv, gux1, gu2, dnx1, dnx2, gu3, w_down
+        )
+        gux2, dn3 = swap(gu2, "x"), swap(w_down, "z3")
+        gux3 = swap(gu3, "x")
+        attended = attend(qkv, position)
+        attended, gux2, go_y, dn3 = window(attended, gux2, go_y, dn3)
+        gain_one, bias_one, attn_scale, gain_two, bias_two, mlp_scale = [vecs[i] for i in range(6)]
+        out_full = w_attn[:, 3 * width : 4 * width]
+        dnx3 = swap(dn3, "x")
+        frames = inputs.astype(F32)
+        branch = jnp.dot(attended, out_full, preferred_element_type=F32)
+        middle = frames + attn_scale * branch
+        unit_two, inverse_two = norm_parts(middle)
+        n_own = (unit_two * gain_two + bias_two).astype(BF)
+        n_own, gux3, dnx3, grad_out, go_y = window(n_own, gux3, dnx3, grad_out, go_y)
+
+        n_y, n_core = swap(n_own, "y"), swap(n_own, "core")
+        go_core = swap(grad_out, "core")
+        n_core, go_core = window(n_core, go_core)
+        go_yc = swap(go_y, "core")
+        pieces = (gu0, gux0, gu1, gux1, gu2, gux2, gu3, gux3)
+        downs = (w_down, dnx0, dn1, dnx1, dn2, dnx2, dn3, dnx3)
+        scale = mlp_scale[None]
+        gg_a, gu_a, gn_own, gn_core, mlp_own, mlp_core, total = mlp_both(
+            idx, pieces, downs, (n_own, n_core), (grad_out, go_core), scale
+        )
+        n_y, go_y, go_yc, gn_core = window(n_y, go_y, go_yc, gn_core)
+        n_yc = swap(n_y, "core")
+        n_y, n_yc = window(n_y, n_yc)
+        gn_core, mlp_core = swap(gn_core, "core"), swap(mlp_core, "core")
+        gg_b, gu_b, gn_y, gn_yc, mlp_y, mlp_yc, down_send, down_keep = mlp_both(
+            idx, pieces, downs, (n_y, n_yc), (go_y, go_yc), scale, total
+        )
+        gn_y, gn_yc, gn_core, mlp_core, down_send = window(gn_y, gn_yc, gn_core, mlp_core, down_send)
+        down_x = swap(down_send, "x")
+        gn_yc = swap(gn_yc, "core")
+        gn_y, gn_yc = window(gn_y, gn_yc)
+        gn_send, gu_b, mlp_yc = window(add(gn_y, gn_yc), gu_b, mlp_yc)
+        gn_y = swap(gn_send, "y")
+        mlp_yc = swap(mlp_yc, "core")
+
+        def z_pairs(keep, came, bit):
+            shape = (2, 2) + keep.shape[1:]
+            keep, came = along(keep.reshape(shape), bit, 1), along(came.reshape(shape), bit, 1)
+            return keep.astype(F32) + came.astype(F32)
+
+        def z_near(keep, came):
+            return z_pairs(keep, came, 1 - z % 2).astype(BF)
+
+        def z_far(keep, came, near):
+            return (
+                pick(z_pairs(keep, came, z % 2), 1 - z // 2)
+                + pick(near, 1 - z // 2).astype(F32)
+            ).astype(BF)
+
+        def z_total(keep, came, near, far):
+            mine = pick(z_pairs(keep, came, z % 2), z // 2) + pick(near, z // 2).astype(F32)
+            return (mine + far.astype(F32)).astype(BF)
+
+        n_all = (n_own, n_core, n_y, n_yc)
+        up_send, up_keep = weight_grad(idx, n_all, (gu_a, gu_b))
+        gate_send, gate_keep = weight_grad(idx, n_all, (after(gg_a, up_send), gg_b))
+        down_x, gate_send, up_send, mlp_yc = window(down_x, gate_send, up_send, mlp_yc)
+        down_near = z_near(down_keep, down_x)
+        mlp_send = add(mlp_y, mlp_yc)
+        down_near, gn_y, mlp_send, up_send = window(down_near, gn_y, mlp_send, up_send)
+        up_x, mlp_y, down_near = swap(up_send, "x"), swap(mlp_send, "y"), swap(down_near, "z1")
+
+        cotangent = grad_out.astype(F32)
+        grad_normed_two = gn_own.astype(F32) + gn_core.astype(F32) + gn_y.astype(F32)
+        ln2_gain_grad = jnp.sum(grad_normed_two * unit_two, axis=0)
+        ln2_bias_grad = jnp.sum(grad_normed_two, axis=0)
+        grad_middle = cotangent + norm_back(grad_normed_two, unit_two, inverse_two, gain_two)
+        scale_attn_grad = jnp.sum(grad_middle * branch, axis=0)
+        grad_branch = (attn_scale * grad_middle).astype(BF)
+        grad_attended = dot(grad_branch, out_full, "nt").astype(BF)
+        grad_attended, gate_send = window(grad_attended, gate_send)
+        gate_x = swap(gate_send, "x")
+
+        dq, dk, dv = attend_back(qkv, grad_attended, position, cosine, sine)
+        dq, mlp_y, up_x, down_near = window(dq, mlp_y, up_x, down_near)
+        up_near, down_far = z_near(up_keep, up_x), z_far(down_keep, down_x, down_near)
+        up_near, down_far, dq = window(up_near, down_far, dq)
+        up_near, down_far = swap(up_near, "z1"), swap(down_far, "z2")
+        grads = attn_grad(idx, normed, attended, dq, dk, dv, grad_branch)
+        dq, dk, dv, gate_x, up_near, down_far, *grads = window(
+            dq, dk, dv, gate_x, up_near, down_far, *grads
+        )
+        a_send, a_send_here, a_keep, a_keep_here, b_send, b_send_here, b_keep, b_keep_here = grads
+
+        a_core, b_core = swap(a_send, "core"), swap(b_send, "core")
+        gate_near = z_near(gate_keep, gate_x)
+        down_mine = z_total(down_keep, down_x, down_near, down_far)
+        up_far = z_far(up_keep, up_x, up_near)
+        a_core, b_core, gate_near, up_far, down_mine, a_send_here, b_send_here = window(
+            a_core, b_core, gate_near, up_far, down_mine, a_send_here, b_send_here
+        )
+        a_core_here, b_core_here = swap(a_send_here, "core"), swap(b_send_here, "core")
+        a_away, b_away, a_core_here, b_core_here, dq, dk, dv, gate_near, up_far = window(
+            add(a_keep, a_core),
+            add(b_keep, b_core),
+            a_core_here,
+            b_core_here,
+            dq,
+            dk,
+            dv,
+            gate_near,
+            up_far,
+        )
+        a_x, b_y = swap(a_away, "x"), swap(b_away, "y")
+        gate_near, up_far = swap(gate_near, "z1"), swap(up_far, "z2")
+        w_qkv_full = w_attn[:, : 3 * width]
+        grad_normed = (
+            dot(dq, w_qkv_full[:, :width], "nt")
+            + dot(dk, w_qkv_full[:, width : 2 * width], "nt")
+            + dot(dv, w_qkv_full[:, 2 * width :], "nt")
+        )
+        grad_normed, gate_near, up_far = window(grad_normed, gate_near, up_far)
+        gate_far = swap(z_far(gate_keep, gate_x, gate_near), "z2")
+        up_mine = z_total(up_keep, up_x, up_near, up_far)
+        unit_one, inverse_one = norm_parts(frames)
+        ln1_gain_grad = jnp.sum(grad_normed * unit_one, axis=0)
+        ln1_bias_grad = jnp.sum(grad_normed, axis=0)
+        input_grad = grad_middle + norm_back(grad_normed, unit_one, inverse_one, gain_one)
+        mlp = mlp_own.astype(F32) + mlp_core.astype(F32) + mlp_y.astype(F32)
+        block_out = (middle + mlp_scale * mlp).astype(BF)
+        scale_mlp_grad = jnp.sum(cotangent * mlp, axis=0)
+        small = jnp.stack(
+            [
+                ln1_gain_grad,
+                ln1_bias_grad,
+                scale_attn_grad,
+                ln2_gain_grad,
+                ln2_bias_grad,
+                scale_mlp_grad,
+            ]
+        )
+        small = small + swap(small, "core")
+        a_x, b_y, small, up_mine, gate_far = window(a_x, b_y, small, up_mine, gate_far)
+        a_half, b_half = (a_keep_here, a_core_here, a_x), (b_keep_here, b_core_here, b_y)
+
+        def add_three(parts, index):
+            p = [along(v, index, 1).astype(F32) for v in parts]
+            return p[0] + p[1] + p[2]
+
+        a_away, b_away = add_three(a_half, y ^ 1).astype(BF), add_three(b_half, x ^ 1).astype(BF)
+        a_away, b_away, small, down_mine = window(a_away, b_away, small, down_mine)
+        a_y, b_x, down_y = swap(a_away, "y"), swap(b_away, "x"), swap(down_mine, "y")
+        small = small + swap(small, "x")
+        gate_mine = z_total(gate_keep, gate_x, gate_near, gate_far)
+        both_mine = jnp.stack([up_mine, gate_mine])
+        a_y, b_x, small, down_y, down_mine, both_mine = window(
+            a_y, b_x, small, down_y, down_mine, both_mine
+        )
+        column = jnp.concatenate(
+            [
+                (add_three(a_half, y) + a_y.astype(F32)).astype(BF),
+                (add_three(b_half, x) + b_x.astype(F32)).astype(BF),
+            ],
+            axis=-1,
+        )
+        sends = [pick(column, z ^ k) for k in (1, 2, 3)]
+        *sends, small = window(*sends, small)
+        got = [swap(v, n) for v, n in zip(sends, ("z1", "z2", "z3"))]
+        both_y = swap(both_mine, "y")
+        small = small + swap(small, "z1")
+        down_both = jnp.stack([down_mine, down_y])
+        *got, small, both_y, down_both = window(*got, small, both_y, down_both)
+        mine = (
+            pick(column, z).astype(F32)
+            + (got[0].astype(F32) + got[1].astype(F32) + got[2].astype(F32))
+        ).astype(BF)
+        mine, small, both_y, down_both = window(mine, small, both_y, down_both)
+        other, down_core = swap(mine, "y"), swap(down_both, "core")
+        both_pair = jnp.stack([both_mine, both_y])
+        small = small + swap(small, "z2")
+        other, small, both_pair, down_core = window(other, small, both_pair, down_core)
+        mine_core = swap(jnp.stack([mine, other]), "core")
+        both_core = swap(both_pair, "core")
+        small = small + swap(small, "y")
+        (w_down_grad,) = place_rows(idx, down_mine, down_y, down_core, (width,))
+        w_up_grad, w_gate_grad = place_columns(
+            idx, both_mine[0], both_mine[1], both_y, both_core
+        )
+        w_qkv_grad, w_out_grad = place_rows(idx, mine, other, mine_core, (3 * width, width))
+        small = lax.dynamic_slice_in_dim(small, group * (width // 8), width // 8, 1)
+        return (
+            block_out,
+            input_grad,
+            small[0],
+            small[1],
+            w_qkv_grad,
+            w_out_grad,
+            small[2],
+            small[3],
+            small[4],
+            w_gate_grad,
+            w_up_grad,
+            w_down_grad,
+            small[5],
+        )
+
+    return shards
+
+
+def plain(mesh):
     n_group, n_rep = mesh.shape["group"], mesh.shape["rep"]
     swap = make_links(n_group, n_rep)
-    tuned = n_group == 8 and n_rep == 4
 
     def gather_group(piece, group):
-        if not tuned:
-            return lax.all_gather(piece, "group", axis=0)
-        own = [piece] + [swap(piece, 2 * k, 0) for k in (1, 2, 3)]
-        other = [swap(p, 1, 0) for p in own]
-        full = jnp.zeros((8,) + piece.shape, piece.dtype)
-        for k in range(4):
-            for d, p in ((0, own[k]), (1, other[k])):
-                at = group ^ (2 * k + d)
-                full = lax.dynamic_update_index_in_dim(full, p, at, 0)
-        return full
-
+        return lax.all_gather(piece, "group", axis=0)
     def gather_all(piece, group, rep):
-        if not tuned:
-            full = lax.all_gather(piece, AXES, axis=0)
-            return full.reshape((n_group, n_rep) + piece.shape)
-        base = [piece] + [swap(piece, 2 * k, 0) for k in (1, 2, 3)]
-        along_x = [swap(p, 1, 0) for p in base]
-        along_y = [swap(p, 0, 2) for p in base]
-        both = [swap(along_x[k], 0, 2) if k < 2 else swap(along_y[k], 1, 0) for k in range(4)]
-        y = rep // 2
-        half = jnp.zeros((8, 2) + piece.shape, piece.dtype)
-        zeros = (0,) * piece.ndim
-        for k in range(4):
-            for dx, dy, p in ((0, 0, base[k]), (1, 0, along_x[k]), (0, 1, along_y[k]), (1, 1, both[k])):
-                at = (group ^ (2 * k + dx), y ^ dy) + zeros
-                half = lax.dynamic_update_slice(half, p[None, None], at)
-        other = swap(half, 0, 1)
-        even = rep % 2 == 0
-        full = jnp.stack([jnp.where(even, half, other), jnp.where(even, other, half)], axis=2)
-        return full.reshape((8, 4) + piece.shape)
+        full = lax.all_gather(piece, AXES, axis=0)
+        return full.reshape((n_group, n_rep) + piece.shape)
 
     def gather_rep(piece):
         low = jnp.concatenate([piece, swap(piece, 0, 2)], axis=0)
@@ -187,75 +1056,18 @@
         return low[:quarter] + swap(low[quarter:].astype(BF), 0, 2).astype(F32)
 
     def scatter_group(grads, group):
-        if not tuned:
-            return lax.psum_scatter(grads, "group", scatter_dimension=0, tiled=False).astype(F32)
-        z, x = group // 2, group % 2
-        blocks = grads.reshape((4, 2) + grads.shape[1:])
-        there = lax.dynamic_index_in_dim(blocks, x ^ 1, 1, keepdims=False)
-        here = lax.dynamic_index_in_dim(blocks, x, 1, keepdims=False)
-        came = swap(there, 1, 0)
-
-        def part(k):
-            return pick(here, z ^ k).astype(F32) + pick(came, z ^ k).astype(F32)
-
-        arrived = [swap(part(k).astype(BF), 2 * k, 0) for k in (1, 2, 3)]
-        return part(0) + (
-            arrived[0].astype(F32) + arrived[1].astype(F32) + arrived[2].astype(F32)
-        )
+        return lax.psum_scatter(grads, "group", scatter_dimension=0, tiled=False).astype(F32)
 
     def whole_rep(piece, rep):
         piece = piece.astype(BF)
-        if not tuned:
-            return lax.all_gather(piece, "rep", axis=0).astype(F32)
-        low = jnp.stack([piece, swap(piece, 0, 2)])
-        high = swap(low, 0, 1)
-        rel = jnp.stack([low[0], high[0], low[1], high[1]])
-        return jnp.stack([pick(rel, rep ^ j) for j in range(4)]).astype(F32)
+        return lax.all_gather(piece, "rep", axis=0).astype(F32)
 
     def scatter_attn(grads, group, rep):
-        rows, cols = grads.shape
-        if not tuned:
-            part = lax.psum_scatter(grads, "group", scatter_dimension=0, tiled=True)
-            return lax.psum(part, "rep").astype(F32)
-        x, y, core = group % 2, rep // 2, rep % 2
-        z = group // 2
-        half = cols // 2
-        there = lax.dynamic_slice_in_dim(grads, (core ^ 1) * half, half, 1)
-        here = lax.dynamic_slice_in_dim(grads, core * half, half, 1)
-        chip = (here.astype(F32) + swap(there, 0, 1).astype(F32)).astype(BF)
-        chip = chip.reshape(4, 2, rows // 8, 2, half // 2)
-        quarter = half // 4
-
-        def add(a, b):
-            return (a.astype(F32) + b.astype(F32)).astype(BF)
-
-        def over_x(v):
-            return add(
-                lax.dynamic_index_in_dim(v, x, 1, keepdims=False),
-                swap(lax.dynamic_index_in_dim(v, x ^ 1, 1, keepdims=False), 1, 0),
-            )
-
-        def over_y(v):
-            return add(
-                lax.dynamic_slice_in_dim(v, y * quarter, quarter, v.ndim - 1),
-                swap(lax.dynamic_slice_in_dim(v, (y ^ 1) * quarter, quarter, v.ndim - 1), 0, 2),
-            )
-
-        first = over_y(over_x(chip[:, :, :, 0]))
-        second = over_x(over_y(chip[:, :, :, 1]))
-        column = jnp.stack([first, second], axis=2)
-        arrived = [swap(pick(column, z ^ k), 2 * k, 0).astype(F32) for k in (1, 2, 3)]
-        mine = pick(column, z).astype(F32) + (arrived[0] + arrived[1] + arrived[2])
-        full = whole_rep(mine, rep)
-        full = full.reshape(2, 2, rows // 8, 2, quarter)
-        return full.transpose(2, 1, 3, 0, 4).reshape(rows // 8, cols)
+        part = lax.psum_scatter(grads, "group", scatter_dimension=0, tiled=True)
+        return lax.psum(part, "rep").astype(F32)
 
     def sum_all(value):
-        if not tuned:
-            return lax.psum(value, AXES)
-        for bits in ((0, 1), (0, 2), (1, 0), (2, 0), (4, 0)):
-            value = value + swap(value, *bits)
-        return value
+        return lax.psum(value, AXES)
 
     def shards(
         inputs,
@@ -429,6 +1241,12 @@
             small[5],
         )
 
+    return shards
+
+
+def solution(mesh):
+    n_group, n_rep = mesh.shape["group"], mesh.shape["rep"]
+    shards = tuned(mesh) if n_group == 8 and n_rep == 4 else plain(mesh)
     rowed, flat = P(AXES, None), P(AXES)
     in_specs = (
         rowed, rowed, flat, flat, rowed, rowed, flat, flat, flat, rowed, rowed, rowed, flat, rowed,

time: 688 us -> 448 us (0.65)
  Pallas kernels: 0 us -> 146 us
  matrix products: 158 us -> 18.4 us
  local copies, waits for them, and re-layouts: 113 us -> 14.1 us
  waiting for transfers between devices: 233 us -> 149 us
  other arithmetic: 83.2 us -> 46.7 us
  starting transfers between devices: 89.1 us -> 63.5 us
    pallas_call x0 -> x13, Pallas kernels: none -> 146 us  [the longest x2 57.4 us: mlp_both(): pl.pallas_call(lambda *refs: mlp_kernel(last_half, *refs), grid=(2 * rows...]
    dot_general x20 -> x4, matrix products: 153 us -> 13.5 us  [dot(): return lax.dot_general(a, b, CONTRACT[form], preferred_element_type=F32)]
    ppermute x91 -> x76, waiting for transfers between devices: 233 us -> 149 us  [swap(): return lax.ppermute(value, AXES, pairs)]
    ppermute x91 -> x76, starting transfers between devices: 89.1 us -> 63.5 us  [swap(): return lax.ppermute(value, AXES, pairs)]
    dynamic_update_slice x38 -> x0, local copies, waits for them, and re-layouts: 20 us -> none  [the longest x15 10.9 us: gather_all(): half = lax.dynamic_update_slice(half, p[None, None], at)]
    unnamed x196 -> x168, local copies, waits for them, and re-layouts: 27.9 us -> 8.25 us
    dynamic_slice x20 -> x0, local copies, waits for them, and re-layouts: 18.8 us -> none  [the longest x2 4.5 us: scatter_attn(): there = lax.dynamic_slice_in_dim(grads, (core ^ 1) * half, half, 1)]
    slice x18 -> x4, local copies, waits for them, and re-layouts: 19.8 us -> 1.06 us  [the longest x2 1.01 us: shards(): share_core = swap(jnp.stack([share_here[1], share_y[1]]), 'core')]
  transfers between devices with their start and end apart: 91 -> 76, of which waited for: 43 -> 28; matrix products, arithmetic and copies ran while one was open for 35% -> 12% of each run, Pallas kernels for 0% -> 32%
where the time goes in v2:
time: 448 us; the launch traced here: 440 us
  waiting for transfers between devices  149 us (33%)
  Pallas kernels  146 us (33%)
  starting transfers between devices  63.5 us (14%)
  other arithmetic  46.7 us (10%)
  matrix products  18.4 us (4%)
  local copies, waits for them, and re-layouts  14.1 us (3%)
    ppermute x76, waiting for transfers between devices, swap(): return lax.ppermute(value, AXES, pairs)  149 us
    ppermute x76, starting transfers between devices, swap(): return lax.ppermute(value, AXES, pairs)  63.5 us
    pallas_call x2, Pallas kernels, mlp_both(): pl.pallas_call(lambda *refs: mlp_kernel(last_half, *refs), grid=(2 * rows...  57.4 us
    pallas_call x2, Pallas kernels, weight_grad(): pl.pallas_call(weight_grad_kernel, grid_spec=pltpu.PrefetchScalarGridSpec...  21 us
    pallas_call x1, Pallas kernels, attend_back(): pl.pallas_call(attend_back_kernel, grid=(pairs,), in_specs=[cols(0), cols...  20.1 us
    pallas_call x1, Pallas kernels, project(): pl.pallas_call(project_kernel, grid=(3 * width // block,), in_specs=[SMEM...  14.2 us
    dot_general x4, matrix products, dot(): return lax.dot_general(a, b, CONTRACT[form], preferred_element_type=F32)  13.5 us
    pallas_call x1, Pallas kernels, attend(): pl.pallas_call(attend_kernel, grid=(pairs,), in_specs=[cols(0), cols(1),...  10.7 us
  transfers between devices with their start and end apart: 76, of which 28 were waited for; matrix products, arithmetic and copies ran while one was open for 12% of the time, Pallas kernels for 32%

profile of v2, /device:TPU:10, one launch (start us, length us, event | category | flops | bytes accessed | tf_op | source)
XLA Modules:
  0.0 439.9 jit_solution(7561887908493779415)
XLA Ops:
  4.9 2.6 collective-permute-start.1
  10.4 10.6 %collective-permute-done.4.y_ref = bf16[2,2,32,1024]{3,2,1,0:T(8,128)(2,1)S(1)} collective-permute-done((bf16[2,2,32,1024]{3,2,1,0:T(8,128)(2,1)}, bf16[2,2,32,1024]{3,2,1,0:T(8,128)(2,1)S(1)}, u32[]{:S(2)}, u32[]{:S(2)}) %collective-permute-start.4) | collective-permute-done | bytes 262176 | tf_op jit(solution)/shard_map/ppermute | solution.py:135
  30.6 4.0 collective-permute-done.8.refs_10_
  34.6 4.2 collective-permute-done.5
  44.7 18.3 %collective-permute-done.12.refs_3_ = bf16[2,128,1024]{2,1,0:T(8,128)(2,1)S(1)} collective-permute-done((bf16[2,128,1024]{2,1,0:T(8,128)(2,1)S(1)}, bf16[2,128,1024]{2,1,0:T(8,128)(2,1)S(1)}, u32[]{:S(2)}, u32[]{:S(2)}) %collective-permute-start.12) | collective-permute-done | bytes 524320 | tf_op jit(solution)/shard_map/ppermute | solution.py:135
  63.0 3.4 collective-permute-done.13.refs_5_
  66.4 3.7 collective-permute-done.14.refs_2_
  76.0 8.4 %collective-permute-done.15.refs_11_ = bf16[128,1024]{1,0:T(8,128)(2,1)S(1)} collective-permute-done((bf16[128,1024]{1,0:T(8,128)(2,1)S(1)}, bf16[128,1024]{1,0:T(8,128)(2,1)S(1)}, u32[]{:S(2)}, u32[]{:S(2)}) %collective-permute-start.15) | collective-permute-done | bytes 262176 | tf_op jit(solution)/shard_map/ppermute | solution.py:135
  84.4 3.5 collective-permute-done.16.refs_13_
  89.1 4.7 %collective-permute-done.23.refs_13_ = bf16[1,32,4224]{2,1,0:T(8,128)(2,1)S(1)} collective-permute-done((bf16[1,32,4224]{2,1,0:T(8,128)(2,1)S(1)}, bf16[1,32,4224]{2,1,0:T(8,128)(2,1)S(1)}, u32[]{:S(2)}, u32[]{:S(2)}) %collective-permute-start.23) | collective-permute-done | bytes 270368 | tf_op jit(solution)/shard_map/ppermute | solution.py:135
  100.1 14.2 %project.1 = (bf16[512,3072]{1,0:T(8,128)(2,1)}, bf16[512,1024]{1,0:T(8,128)(2,1)}, bf16[1024,4224]{1,0:T(8,128)(2,1)}, f32[8,1024]{1,0:T(8,128)}) custom-call(s32[4]{0:T(128)} %pad_add_fusion.idx.refs_0_, bf16[1,32,4224]{2,1,0:T(8,128)(2,1)} %copy-done.31, bf16[3,32,4224]{2,1,0:T(8,128)(2,1)} %copy-done.20, bf16[3,32,4224]{2,1,0:T(8,128)(2,1)} %copy-done.19, ...), custom_call_target="tpu_custom_call" | custom-call | flops 1000000000 | tf_op jit(solution)/shard_map/project/pallas_call | solution.py:269
  114.3 4.8 %collective-permute-done.27.refs_14_ = bf16[128,1024]{1,0:T(8,128)(2,1)} collective-permute-done((bf16[128,1024]{1,0:T(8,128)(2,1)}, bf16[128,1024]{1,0:T(8,128)(2,1)}, u32[]{:S(2)}, u32[]{:S(2)}) %collective-permute-start.27) | collective-permute-done | bytes 262176 | tf_op jit(solution)/shard_map/ppermute | solution.py:135
  123.0 10.7 %attend.1.o_in = bf16[512,1024]{1,0:T(8,128)(2,1)} custom-call(bf16[512,3072]{1,0:T(8,128)(2,1)} %get-tuple-element.287.q_ref.k_ref.v_ref, bf16[512,3072]{1,0:T(8,128)(2,1)} %get-tuple-element.287.q_ref.k_ref.v_ref, bf16[512,3072]{1,0:T(8,128)(2,1)} %get-tuple-element.287.q_ref.k_ref.v_ref, s32[512,1]{1,0:T(8,128)} %iota_subtract_fusion.pos_ref), custom_call_target="tpu_custom_call" | custom-call | flops 1000000000 | tf_op jit(solution)/shard_map/attend/pallas_call | solution.py:342
  134.4 4.9 %fusion.62 = (f32[512]{0:T(512)S(1)}, f32[512,1024]{1,0:T(8,128)S(1)}, f32[512]{0:T(512)S(1)}, f32[512,1024]{1,0:T(8,128)}) fusion(f32[1024]{0:T(1024)S(1)} %bitcast.188, bf16[512,1024]{1,0:T(8,128)(2,1)S(1)} %copy-done.7, f32[512]{0:T(512)S(1)} %broadcast_multiply_fusion.2, bf16[512,1024]{1,0:T(8,128)(2,1)} %attend.1.o_in, ...), kind=kOutput, calls=%fused_computation.149 | convolution fusion | flops 1077410816 | bytes 8398848 | tf_op jit(solution)/shard_map/dot_general | solution.py:843
  141.7 3.8 collective-permute-done.32.refs_8_
  145.5 3.7 collective-permute-done.33.refs_16_
  151.9 3.0 collective-permute-done.35.refs_20_
  155.9 28.2 %mlp_both.2 = (bf16[1024,1024]{1,0:T(8,128)(2,1)}, bf16[1024,1024]{1,0:T(8,128)(2,1)}, bf16[512,1024]{1,0:T(8,128)(2,1)}, bf16[512,1024]{1,0:T(8,128)(2,1)}, bf1...) custom-call(s32[4]{0:T(128)} %pad_add_fusion.idx.refs_0_, ...), custom_call_target="tpu_custom_call" | custom-call | flops 1000000000 | tf_op jit(solution)/shard_map/mlp_both/pallas_call | solution.py:551
  184.8 2.1 collective-permute-done.38.refs_18_.refs_6_.refs_7_
  187.9 29.2 %mlp_both.3 = (bf16[1024,1024]{1,0:T(8,128)(2,1)}, bf16[1024,1024]{1,0:T(8,128)(2,1)}, bf16[512,1024]{1,0:T(8,128)(2,1)}, bf16[512,1024]{1,0:T(8,128)(2,1)}, bf1...) custom-call(s32[4]{0:T(128)} %pad_add_fusion.idx.refs_0_, ...), custom_call_target="tpu_custom_call" | custom-call | flops 1000000000 | tf_op jit(solution)/shard_map/mlp_both/pallas_call | solution.py:551
  221.9 10.4 %weight_grad.2 = (bf16[4,128,1024]{2,1,0:T(8,128)(2,1)}, bf16[4,128,1024]{2,1,0:T(8,128)(2,1)}) custom-call(s32[4]{0:T(128)} %pad_add_fusion.idx.refs_0_, bf16[512,1024]{1,0:T(8,128)(2,1)} %copy-done, bf16[512,1024]{1,0:T(8,128)(2,1)} %copy-done, bf16[512,1024]{1,0:T(8,128)(2,1)} %copy-done.1, bf16[512,1024]{1,0:T(8,128)(2,1)} %copy-done.1, ...), custom_call_target="tpu_custom_call" | custom-call | flops 1000000000 | tf_op jit(solution)/shard_map/weight_grad/pallas_call | solution.py:605
  232.3 10.6 %weight_grad.3 = (bf16[4,128,1024]{2,1,0:T(8,128)(2,1)}, bf16[4,128,1024]{2,1,0:T(8,128)(2,1)}) custom-call(s32[4]{0:T(128)} %pad_add_fusion.idx.refs_0_, bf16[512,1024]{1,0:T(8,128)(2,1)} %copy-done, bf16[512,1024]{1,0:T(8,128)(2,1)} %copy-done, bf16[512,1024]{1,0:T(8,128)(2,1)} %copy-done.1, bf16[512,1024]{1,0:T(8,128)(2,1)} %copy-done.1, ...), custom_call_target="tpu_custom_call" | custom-call | flops 1000000000 | tf_op jit(solution)/shard_map/weight_grad/pallas_call | solution.py:605
  243.1 2.2 fusion.28
  245.3 2.6 add_convert_fusion.3
  247.9 2.9 multiply_reduce_fusion
  256.1 2.6 multiply_reduce_fusion.1
  258.9 4.7 %fusion.22.do_ref = bf16[512,1024]{1,0:T(8,128)(2,1)} fusion(bf16[512,1024]{1,0:T(8,128)(2,1)S(1)} %multiply_convert_fusion.do, bf16[1024,4224]{1,0:T(8,128)(2,1)} %get-tuple-element.293), kind=kOutput, calls=%fused_computation.44 | convolution fusion | flops 1074266112 | bytes 4194304 | tf_op jit(solution)/shard_map/dot_general | solution.py:162
  265.2 20.1 %attend_back.1 = (bf16[512,1024]{1,0:T(8,128)(2,1)}, bf16[512,1024]{1,0:T(8,128)(2,1)}, bf16[512,1024]{1,0:T(8,128)(2,1)}) custom-call(bf16[512,3072]{1,0:T(8,128)(2,1)} %get-tuple-element.287.q_ref.k_ref.v_ref, bf16[512,3072]{1,0:T(8,128)(2,1)} %get-tuple-element.287.q_ref.k_ref.v_ref, bf16[512,3072]{1,0:T(8,128)(2,1)} %get-tuple-element.287.q_ref.k_ref.v_ref, ...), custom_call_target="tpu_custom_call" | custom-call | flops 1000000000 | tf_op jit(solution)/shard_map/attend_back/pallas_call | solution.py:399
  288.6 2.0 fusion.29
  292.6 9.6 %attn_grad.1 = (bf16[4,2,32,2048]{3,2,1,0:T(8,128)(2,1)}, bf16[4,2,32,2048]{3,2,1,0:T(8,128)(2,1)}, bf16[4,2,32,2048]{3,2,1,0:T(8,128)(2,1)}, bf16[4,2,32,2048]{...) custom-call(s32[4]{0:T(128)} %pad_add_fusion.idx.refs_0_, ...), custom_call_target="tpu_custom_call" | custom-call | flops 1000000000 | tf_op jit(solution)/shard_map/attn_grad/pallas_call | solution.py:645
  302.2 7.0 %collective-permute-done.50 = bf16[128,1024]{1,0:T(8,128)(2,1)S(1)} collective-permute-done((bf16[128,1024]{1,0:T(8,128)(2,1)S(1)}, bf16[128,1024]{1,0:T(8,128)(2,1)S(1)}, u32[]{:S(2)}, u32[]{:S(2)}) %collective-permute-start.50) | collective-permute-done | bytes 262176 | tf_op jit(solution)/shard_map/ppermute | solution.py:135
  312.6 3.6 fusion.11
  326.4 2.9 fusion.14
  329.3 3.0 fusion.16
  332.9 2.5 collective-permute-start.56
  336.2 2.9 add_add_fusion
  339.2 13.7 %collective-permute-done.56 = bf16[128,1024]{1,0:T(8,128)(2,1)S(1)} collective-permute-done((bf16[128,1024]{1,0:T(8,128)(2,1)S(1)}, bf16[128,1024]{1,0:T(8,128)(2,1)S(1)}, u32[]{:S(2)}, u32[]{:S(2)}) %collective-permute-start.56) | collective-permute-done | bytes 262176 | tf_op jit(solution)/shard_map/ppermute | solution.py:135
  356.8 8.5 %collective-permute-done.60 = bf16[128,1024]{1,0:T(8,128)(2,1)} collective-permute-done((bf16[128,1024]{1,0:T(8,128)(2,1)}, bf16[128,1024]{1,0:T(8,128)(2,1)}, u32[]{:S(2)}, u32[]{:S(2)}) %collective-permute-start.60) | collective-permute-done | bytes 262176 | tf_op jit(solution)/shard_map/ppermute | solution.py:135
  373.5 8.7 %collective-permute-done.63 = f32[6,1024]{1,0:T(8,128)S(1)} collective-permute-done((f32[6,1024]{1,0:T(8,128)S(1)}, f32[6,1024]{1,0:T(8,128)S(1)}, u32[]{:S(2)}, u32[]{:S(2)}) %collective-permute-start.63) | collective-permute-done | bytes 24608 | tf_op jit(solution)/shard_map/ppermute | solution.py:135
  382.3 4.8 %collective-permute-done.64.y_ref = bf16[128,1024]{1,0:T(8,128)(2,1)S(1)} collective-permute-done((bf16[128,1024]{1,0:T(8,128)(2,1)S(1)}, bf16[128,1024]{1,0:T(8,128)(2,1)S(1)}, u32[]{:S(2)}, u32[]{:S(2)}) %collective-permute-start.64) | collective-permute-done | bytes 262176 | tf_op jit(solution)/shard_map/ppermute | solution.py:135
  391.9 2.1 collective-permute-start.66
  396.4 12.6 %collective-permute-done.68 = f32[6,1024]{1,0:T(8,128)S(1)} collective-permute-done((f32[6,1024]{1,0:T(8,128)S(1)}, f32[6,1024]{1,0:T(8,128)S(1)}, u32[]{:S(2)}, u32[]{:S(2)}) %collective-permute-start.68) | collective-permute-done | bytes 24608 | tf_op jit(solution)/shard_map/ppermute | solution.py:135
  409.0 2.2 collective-permute-done.66
  411.2 4.5 %collective-permute-done.67 = bf16[32,4096]{1,0:T(8,128)(2,1)S(1)} collective-permute-done((bf16[32,4096]{1,0:T(8,128)(2,1)S(1)}, bf16[32,4096]{1,0:T(8,128)(2,1)S(1)}, u32[]{:S(2)}, u32[]{:S(2)}) %collective-permute-start.67) | collective-permute-done | bytes 262176 | tf_op jit(solution)/shard_map/ppermute | solution.py:135
  419.8 4.7 %collective-permute-done.71 = f32[6,1024]{1,0:T(8,128)S(1)} collective-permute-done((f32[6,1024]{1,0:T(8,128)S(1)}, f32[6,1024]{1,0:T(8,128)S(1)}, u32[]{:S(2)}, u32[]{:S(2)}) %collective-permute-start.71) | collective-permute-done | bytes 24608 | tf_op jit(solution)/shard_map/ppermute | solution.py:135
  427.9 2.7 place_rows.3
  431.9 2.7 place_rows.2
  435.5 4.2 place_columns.1
  (366 shorter events, 108.8 us)
Async XLA Ops:
  4.3 16.6 %collective-permute-start = (bf16[1,32,4224]{2,1,0:T(8,128)(2,1)S(1)}, bf16[1,32,4224]{2,1,0:T(8,128)(2,1)S(1)}, u32[]{:S(2)}, u32[]{:S(2)}) collective-permute-start(bf16[1,32,4224]{2,1,0:T(8,128)(2,1)S(1)} %fusion.41.refs_1_), channel_id=1, source_target_pairs={{0,8},{1,9},{2,10},{3,11},{4,12},{5,13},{6,14},{7,15},{8,0},{9,1},... | collective-permute-start | bytes 811016 | tf_op jit(solution)/shard_map/ppermute | solution.py:135
  4.9 16.1 %collective-permute-start.1 = (bf16[1,32,4224]{2,1,0:T(8,128)(2,1)S(1)}, bf16[1,32,4224]{2,1,0:T(8,128)(2,1)S(1)}, u32[]{:S(2)}, u32[]{:S(2)}) collective-permute-start(bf16[1,32,4224]{2,1,0:T(8,128)(2,1)S(1)} %fusion.41.refs_1_), channel_id=1, source_target_pairs={{0,16},{1,17},{2,18},{3,19},{4,20},{5,21},{6,22},{7,23},{8,24},{9,... | collective-permute-start | bytes 811016 | tf_op jit(solution)/shard_map/ppermute | solution.py:135
  7.4 13.5 %collective-permute-start.2 = (bf16[1,32,4224]{2,1,0:T(8,128)(2,1)S(1)}, bf16[1,32,4224]{2,1,0:T(8,128)(2,1)S(1)}, u32[]{:S(2)}, u32[]{:S(2)}) collective-permute-start(bf16[1,32,4224]{2,1,0:T(8,128)(2,1)S(1)} %fusion.41.refs_1_), channel_id=1, source_target_pairs={{0,4},{1,5},{2,6},{3,7},{4,0},{5,1},{6,2},{7,3},{8,12},{9,13},{10,... | collective-permute-start | bytes 811016 | tf_op jit(solution)/shard_map/ppermute | solution.py:135
  24.1 14.7 %collective-permute-start.5 = (bf16[1,32,4224]{2,1,0:T(8,128)(2,1)S(1)}, bf16[1,32,4224]{2,1,0:T(8,128)(2,1)S(1)}, u32[]{:S(2)}, u32[]{:S(2)}) collective-permute-start(bf16[1,32,4224]{2,1,0:T(8,128)(2,1)S(1)} %fusion.41.refs_1_), channel_id=1, source_target_pairs={{0,24},{1,25},{2,26},{3,27},{4,28},{5,29},{6,30},{7,31},{8,16},{9,... | collective-permute-start | bytes 811016 | tf_op jit(solution)/shard_map/ppermute | solution.py:135
  24.6 14.2 %collective-permute-start.9 = (bf16[1,32,4224]{2,1,0:T(8,128)(2,1)S(1)}, bf16[1,32,4224]{2,1,0:T(8,128)(2,1)S(1)}, u32[]{:S(2)}, u32[]{:S(2)}) collective-permute-start(bf16[1,32,4224]{2,1,0:T(8,128)(2,1)S(1)} %fusion.41.refs_1_), channel_id=1, source_target_pairs={{0,1},{1,0},{2,3},{3,2},{4,5},{5,4},{6,7},{7,6},{8,9},{9,8},{10,11... | collective-permute-start | bytes 811016 | tf_op jit(solution)/shard_map/ppermute | solution.py:135
  24.8 14.0 %collective-permute-start.7 = (bf16[1,32,4224]{2,1,0:T(8,128)(2,1)S(1)}, bf16[1,32,4224]{2,1,0:T(8,128)(2,1)S(1)}, u32[]{:S(2)}, u32[]{:S(2)}) collective-permute-start(bf16[1,32,4224]{2,1,0:T(8,128)(2,1)S(1)} %collective-permute-done.2), channel_id=1, source_target_pairs={{0,2},{1,3},{2,0},{3,1},{4,6},{5,7},{6,4},{7,5},{8,10},{9,11},{10,... | collective-permute-start | bytes 811016 | tf_op jit(solution)/shard_map/ppermute | solution.py:135
  39.1 31.0 %collective-permute-start.10 = (bf16[3,32,4224]{2,1,0:T(8,128)(2,1)S(1)}, bf16[3,32,4224]{2,1,0:T(8,128)(2,1)S(1)}, u32[]{:S(2)}, u32[]{:S(2)}) collective-permute-start(bf16[3,32,4224]{2,1,0:T(8,128)(2,1)S(1)} %pad_maximum_fusion.1.refs_2_), channel_id=1, source_target_pairs={{0,4},{1,5},{2,6},{3,7},{4,0},{5,1},{6,2},{7,3},{8,12},{9,13},{10,... | collective-permute-start | bytes 2433032 | tf_op jit(solution)/shard_map/ppermute | solution.py:135
  40.7 30.2 %collective-permute-start.11 = (bf16[3,32,4224]{2,1,0:T(8,128)(2,1)S(1)}, bf16[3,32,4224]{2,1,0:T(8,128)(2,1)S(1)}, u32[]{:S(2)}, u32[]{:S(2)}) collective-permute-start(bf16[3,32,4224]{2,1,0:T(8,128)(2,1)S(1)} %pad_maximum_fusion.1.refs_2_), channel_id=1, source_target_pairs={{0,2},{1,3},{2,0},{3,1},{4,6},{5,7},{6,4},{7,5},{8,10},{9,11},{10,... | collective-permute-start | bytes 2433032 | tf_op jit(solution)/shard_map/ppermute | solution.py:135
  42.2 20.7 %collective-permute-start.12 = (bf16[2,128,1024]{2,1,0:T(8,128)(2,1)S(1)}, bf16[2,128,1024]{2,1,0:T(8,128)(2,1)S(1)}, u32[]{:S(2)}, u32[]{:S(2)}) collective-permute-start(bf16[2,128,1024]{2,1,0:T(8,128)(2,1)S(1)} %copy-done.23), channel_id=1, source_target_pairs={{0,8},{1,9},{2,10},{3,11},{4,12},{5,13},{6,14},{7,15},{8,0},{9,1},... | collective-permute-start | bytes 1572872 | tf_op jit(solution)/shard_map/ppermute | solution.py:135
  42.2 24.2 %collective-permute-start.13 = (bf16[2,128,1024]{2,1,0:T(8,128)(2,1)S(1)}, bf16[2,128,1024]{2,1,0:T(8,128)(2,1)S(1)}, u32[]{:S(2)}, u32[]{:S(2)}) collective-permute-start(bf16[2,128,1024]{2,1,0:T(8,128)(2,1)S(1)} %copy-done.23), channel_id=1, source_target_pairs={{0,16},{1,17},{2,18},{3,19},{4,20},{5,21},{6,22},{7,23},{8,24},{9,... | collective-permute-start | bytes 1572872 | tf_op jit(solution)/shard_map/ppermute | solution.py:135
  44.1 26.0 %collective-permute-start.14 = (bf16[2,128,1024]{2,1,0:T(8,128)(2,1)S(1)}, bf16[2,128,1024]{2,1,0:T(8,128)(2,1)S(1)}, u32[]{:S(2)}, u32[]{:S(2)}) collective-permute-start(bf16[2,128,1024]{2,1,0:T(8,128)(2,1)S(1)} %copy-done.23), channel_id=1, source_target_pairs={{0,4},{1,5},{2,6},{3,7},{4,0},{5,1},{6,2},{7,3},{8,12},{9,13},{10,... | collective-permute-start | bytes 1572872 | tf_op jit(solution)/shard_map/ppermute | solution.py:135
  71.0 17.0 %collective-permute-start.17 = (bf16[3,32,4224]{2,1,0:T(8,128)(2,1)S(1)}, bf16[3,32,4224]{2,1,0:T(8,128)(2,1)S(1)}, u32[]{:S(2)}, u32[]{:S(2)}) collective-permute-start(bf16[3,32,4224]{2,1,0:T(8,128)(2,1)S(1)} %pad_maximum_fusion.1.refs_2_), channel_id=1, source_target_pairs={{0,1},{1,0},{2,3},{3,2},{4,5},{5,4},{6,7},{7,6},{8,9},{9,8},{10,11... | collective-permute-start | bytes 2433032 | tf_op jit(solution)/shard_map/ppermute | solution.py:135
  71.1 16.9 %collective-permute-start.19 = (bf16[2,32,4224]{2,1,0:T(8,128)(2,1)S(1)}, bf16[2,32,4224]{2,1,0:T(8,128)(2,1)S(1)}, u32[]{:S(2)}, u32[]{:S(2)}) collective-permute-start(bf16[2,32,4224]{2,1,0:T(8,128)(2,1)S(1)} %slice.70), channel_id=1, source_target_pairs={{0,4},{1,5},{2,6},{3,7},{4,0},{5,1},{6,2},{7,3},{8,12},{9,13},{10,... | collective-permute-start | bytes 1622024 | tf_op jit(solution)/shard_map/ppermute | solution.py:135
  72.6 15.3 %collective-permute-start.18 = (bf16[1,32,4224]{2,1,0:T(8,128)(2,1)S(1)}, bf16[1,32,4224]{2,1,0:T(8,128)(2,1)S(1)}, u32[]{:S(2)}, u32[]{:S(2)}) collective-permute-start(bf16[1,32,4224]{2,1,0:T(8,128)(2,1)S(1)} %slice.69), channel_id=1, source_target_pairs={{0,2},{1,3},{2,0},{3,1},{4,6},{5,7},{6,4},{7,5},{8,10},{9,11},{10,... | collective-permute-start | bytes 811016 | tf_op jit(solution)/shard_map/ppermute | solution.py:135
  74.1 13.8 %collective-permute-start.16 = (bf16[128,1024]{1,0:T(8,128)(2,1)S(1)}, bf16[128,1024]{1,0:T(8,128)(2,1)}, u32[]{:S(2)}, u32[]{:S(2)}) collective-permute-start(bf16[128,1024]{1,0:T(8,128)(2,1)S(1)} %copy-done.38), channel_id=1, source_target_pairs={{0,16},{1,17},{2,18},{3,19},{4,20},{5,21},{6,22},{7,23},{8,24},{9,... | collective-permute-start | bytes 786440 | tf_op jit(solution)/shard_map/ppermute | solution.py:135
  93.8 25.3 %collective-permute-start.25 = (bf16[2,128,1024]{2,1,0:T(8,128)(2,1)S(1)}, bf16[2,128,1024]{2,1,0:T(8,128)(2,1)S(1)}, u32[]{:S(2)}, u32[]{:S(2)}) collective-permute-start(bf16[2,128,1024]{2,1,0:T(8,128)(2,1)S(1)} %collective-permute-done.12.refs_3_), channel_id=1, source_target_pairs={{0,4},{1,5},{2,6},{3,7},{4,0},{5,1},{6,2},{7,3},{8,12},{9,13},{10,... | collective-permute-start | bytes 1572872 | tf_op jit(solution)/shard_map/ppermute | solution.py:135
  94.4 25.0 %collective-permute-start.28 = (bf16[2,128,1024]{2,1,0:T(8,128)(2,1)S(1)}, bf16[2,128,1024]{2,1,0:T(8,128)(2,1)}, u32[]{:S(2)}, u32[]{:S(2)}) collective-permute-start(bf16[2,128,1024]{2,1,0:T(8,128)(2,1)S(1)} %copy-done.23), channel_id=1, source_target_pairs={{0,24},{1,25},{2,26},{3,27},{4,28},{5,29},{6,30},{7,31},{8,16},{9,... | collective-permute-start | bytes 1572872 | tf_op jit(solution)/shard_map/ppermute | solution.py:135
  96.0 38.4 %collective-permute-start.30 = (bf16[512,1024]{1,0:T(8,128)(2,1)S(1)}, bf16[512,1024]{1,0:T(8,128)(2,1)}, u32[]{:S(2)}, u32[]{:S(2)}) collective-permute-start(bf16[512,1024]{1,0:T(8,128)(2,1)S(1)} %copy-done.9), channel_id=1, source_target_pairs={{0,2},{1,3},{2,0},{3,1},{4,6},{5,7},{6,4},{7,5},{8,10},{9,11},{10,... | collective-permute-start | bytes 3145736 | tf_op jit(solution)/shard_map/ppermute | solution.py:135
  96.5 17.8 %collective-permute-start.26 = (bf16[128,1024]{1,0:T(8,128)(2,1)S(1)}, bf16[128,1024]{1,0:T(8,128)(2,1)}, u32[]{:S(2)}, u32[]{:S(2)}) collective-permute-start(bf16[128,1024]{1,0:T(8,128)(2,1)S(1)} %collective-permute-done.15.refs_11_), channel_id=1, source_target_pairs={{0,4},{1,5},{2,6},{3,7},{4,0},{5,1},{6,2},{7,3},{8,12},{9,13},{10,... | collective-permute-start | bytes 786440 | tf_op jit(solution)/shard_map/ppermute | solution.py:135
  99.0 20.2 %collective-permute-start.27 = (bf16[128,1024]{1,0:T(8,128)(2,1)}, bf16[128,1024]{1,0:T(8,128)(2,1)}, u32[]{:S(2)}, u32[]{:S(2)}) collective-permute-start(bf16[128,1024]{1,0:T(8,128)(2,1)} %collective-permute-done.16.refs_13_), channel_id=1, source_target_pairs={{0,4},{1,5},{2,6},{3,7},{4,0},{5,1},{6,2},{7,3},{8,12},{9,13},{10,... | collective-permute-start | bytes 786440 | tf_op jit(solution)/shard_map/ppermute | solution.py:135
  119.4 15.0 %collective-permute-start.29 = (bf16[2,128,1024]{2,1,0:T(8,128)(2,1)S(1)}, bf16[2,128,1024]{2,1,0:T(8,128)(2,1)S(1)}, u32[]{:S(2)}, u32[]{:S(2)}) collective-permute-start(bf16[2,128,1024]{2,1,0:T(8,128)(2,1)S(1)} %collective-permute-done.13.refs_5_), channel_id=1, source_target_pairs={{0,4},{1,5},{2,6},{3,7},{4,0},{5,1},{6,2},{7,3},{8,12},{9,13},{10,... | collective-permute-start | bytes 1572872 | tf_op jit(solution)/shard_map/ppermute | solution.py:135
  120.9 13.5 %collective-permute-start.31 = (bf16[128,1024]{1,0:T(8,128)(2,1)S(1)}, bf16[128,1024]{1,0:T(8,128)(2,1)S(1)}, u32[]{:S(2)}, u32[]{:S(2)}) collective-permute-start(bf16[128,1024]{1,0:T(8,128)(2,1)S(1)} %copy-done.38), channel_id=1, source_target_pairs={{0,24},{1,25},{2,26},{3,27},{4,28},{5,29},{6,30},{7,31},{8,16},{9,... | collective-permute-start | bytes 786440 | tf_op jit(solution)/shard_map/ppermute | solution.py:135
  122.5 23.0 %collective-permute-start.32 = (bf16[2,128,1024]{2,1,0:T(8,128)(2,1)}, bf16[2,128,1024]{2,1,0:T(8,128)(2,1)S(1)}, u32[]{:S(2)}, u32[]{:S(2)}) collective-permute-start(bf16[2,128,1024]{2,1,0:T(8,128)(2,1)} %collective-permute-done.28.refs_7_), channel_id=1, source_target_pairs={{0,4},{1,5},{2,6},{3,7},{4,0},{5,1},{6,2},{7,3},{8,12},{9,13},{10,... | collective-permute-start | bytes 1572872 | tf_op jit(solution)/shard_map/ppermute | solution.py:135
  149.7 34.3 %collective-permute-start.36 = (bf16[512,1024]{1,0:T(8,128)(2,1)S(1)}, bf16[512,1024]{1,0:T(8,128)(2,1)S(1)}, u32[]{:S(2)}, u32[]{:S(2)}) collective-permute-start(bf16[512,1024]{1,0:T(8,128)(2,1)S(1)} %add_convert_fusion.5.refs_17_.refs_0_.refs_1_), channel_id=1, source_target_pairs={{0,2},{1,3},{2,0},{3,1},{4,6},{5,7},{6,4},{7,5},{8,10},{9,11},{10,... | collective-permute-start | bytes 3145736 | tf_op jit(solution)/shard_map/ppermute | solution.py:135
  150.3 33.8 %collective-permute-start.37 = (bf16[512,1024]{1,0:T(8,128)(2,1)}, bf16[512,1024]{1,0:T(8,128)(2,1)}, u32[]{:S(2)}, u32[]{:S(2)}) collective-permute-start(bf16[512,1024]{1,0:T(8,128)(2,1)} %collective-permute-done.30.refs_19_), channel_id=1, source_target_pairs={{0,1},{1,0},{2,3},{3,2},{4,5},{5,4},{6,7},{7,6},{8,9},{9,8},{10,11... | collective-permute-start | bytes 3145736 | tf_op jit(solution)/shard_map/ppermute | solution.py:135
  184.3 32.8 %collective-permute-start.39 = (bf16[512,1024]{1,0:T(8,128)(2,1)}, bf16[512,1024]{1,0:T(8,128)(2,1)}, u32[]{:S(2)}, u32[]{:S(2)}) collective-permute-start(bf16[512,1024]{1,0:T(8,128)(2,1)} %get-tuple-element.320), channel_id=1, source_target_pairs={{0,1},{1,0},{2,3},{3,2},{4,5},{5,4},{6,7},{7,6},{8,9},{9,8},{10,11... | collective-permute-start | bytes 3145736 | tf_op jit(solution)/shard_map/ppermute | solution.py:135
  184.7 32.5 %collective-permute-start.40 = (bf16[512,1024]{1,0:T(8,128)(2,1)}, bf16[512,1024]{1,0:T(8,128)(2,1)S(1)}, u32[]{:S(2)}, u32[]{:S(2)}) collective-permute-start(bf16[512,1024]{1,0:T(8,128)(2,1)} %get-tuple-element.321), channel_id=1, source_target_pairs={{0,1},{1,0},{2,3},{3,2},{4,5},{5,4},{6,7},{7,6},{8,9},{9,8},{10,11... | collective-permute-start | bytes 3145736 | tf_op jit(solution)/shard_map/ppermute | solution.py:135
  217.4 25.8 %collective-permute-start.41 = (bf16[4,128,1024]{2,1,0:T(8,128)(2,1)}, bf16[4,128,1024]{2,1,0:T(8,128)(2,1)}, u32[]{:S(2)}, u32[]{:S(2)}) collective-permute-start(bf16[4,128,1024]{2,1,0:T(8,128)(2,1)} %get-tuple-element.327), channel_id=1, source_target_pairs={{0,4},{1,5},{2,6},{3,7},{4,0},{5,1},{6,2},{7,3},{8,12},{9,13},{10,... | collective-permute-start | bytes 3145736 | tf_op jit(solution)/shard_map/ppermute | solution.py:135
  221.7 21.4 %collective-permute-start.43 = (bf16[512,1024]{1,0:T(8,128)(2,1)}, bf16[512,1024]{1,0:T(8,128)(2,1)}, u32[]{:S(2)}, u32[]{:S(2)}) collective-permute-start(bf16[512,1024]{1,0:T(8,128)(2,1)} %get-tuple-element.341), channel_id=1, source_target_pairs={{0,1},{1,0},{2,3},{3,2},{4,5},{5,4},{6,7},{7,6},{8,9},{9,8},{10,11... | collective-permute-start | bytes 3145736 | tf_op jit(solution)/shard_map/ppermute | solution.py:135
  221.9 25.9 %collective-permute-start.44 = (bf16[512,1024]{1,0:T(8,128)(2,1)S(1)}, bf16[512,1024]{1,0:T(8,128)(2,1)}, u32[]{:S(2)}, u32[]{:S(2)}) collective-permute-start(bf16[512,1024]{1,0:T(8,128)(2,1)S(1)} %add_convert_fusion.4), channel_id=1, source_target_pairs={{0,2},{1,3},{2,0},{3,1},{4,6},{5,7},{6,4},{7,5},{8,10},{9,11},{10,... | collective-permute-start | bytes 3145736 | tf_op jit(solution)/shard_map/ppermute | solution.py:135
  250.8 35.8 %collective-permute-start.45 = (bf16[512,1024]{1,0:T(8,128)(2,1)}, bf16[512,1024]{1,0:T(8,128)(2,1)}, u32[]{:S(2)}, u32[]{:S(2)}) collective-permute-start(bf16[512,1024]{1,0:T(8,128)(2,1)} %add_convert_fusion.3), channel_id=1, source_target_pairs={{0,2},{1,3},{2,0},{3,1},{4,6},{5,7},{6,4},{7,5},{8,10},{9,11},{10,... | collective-permute-start | bytes 3145736 | tf_op jit(solution)/shard_map/ppermute | solution.py:135
  252.8 33.8 %collective-permute-start.46 = (bf16[4,128,1024]{2,1,0:T(8,128)(2,1)}, bf16[4,128,1024]{2,1,0:T(8,128)(2,1)}, u32[]{:S(2)}, u32[]{:S(2)}) collective-permute-start(bf16[4,128,1024]{2,1,0:T(8,128)(2,1)} %get-tuple-element.352), channel_id=1, source_target_pairs={{0,4},{1,5},{2,6},{3,7},{4,0},{5,1},{6,2},{7,3},{8,12},{9,13},{10,... | collective-permute-start | bytes 3145736 | tf_op jit(solution)/shard_map/ppermute | solution.py:135
  254.3 32.4 %collective-permute-start.47 = (bf16[2,128,1024]{2,1,0:T(8,128)(2,1)}, bf16[2,128,1024]{2,1,0:T(8,128)(2,1)}, u32[]{:S(2)}, u32[]{:S(2)}) collective-permute-start(bf16[2,128,1024]{2,1,0:T(8,128)(2,1)} %fusion.28), channel_id=1, source_target_pairs={{0,8},{1,9},{2,10},{3,11},{4,12},{5,13},{6,14},{7,15},{8,0},{9,1},... | collective-permute-start | bytes 1572872 | tf_op jit(solution)/shard_map/ppermute | solution.py:135
  263.6 38.6 %collective-permute-start.48 = (bf16[4,128,1024]{2,1,0:T(8,128)(2,1)}, bf16[4,128,1024]{2,1,0:T(8,128)(2,1)}, u32[]{:S(2)}, u32[]{:S(2)}) collective-permute-start(bf16[4,128,1024]{2,1,0:T(8,128)(2,1)} %get-tuple-element.362), channel_id=1, source_target_pairs={{0,4},{1,5},{2,6},{3,7},{4,0},{5,1},{6,2},{7,3},{8,12},{9,13},{10,... | collective-permute-start | bytes 3145736 | tf_op jit(solution)/shard_map/ppermute | solution.py:135
  290.7 18.5 %collective-permute-start.49 = (bf16[2,128,1024]{2,1,0:T(8,128)(2,1)}, bf16[2,128,1024]{2,1,0:T(8,128)(2,1)}, u32[]{:S(2)}, u32[]{:S(2)}) collective-permute-start(bf16[2,128,1024]{2,1,0:T(8,128)(2,1)} %fusion.29), channel_id=1, source_target_pairs={{0,8},{1,9},{2,10},{3,11},{4,12},{5,13},{6,14},{7,15},{8,0},{9,1},... | collective-permute-start | bytes 1572872 | tf_op jit(solution)/shard_map/ppermute | solution.py:135
  290.7 18.5 %collective-permute-start.50 = (bf16[128,1024]{1,0:T(8,128)(2,1)S(1)}, bf16[128,1024]{1,0:T(8,128)(2,1)S(1)}, u32[]{:S(2)}, u32[]{:S(2)}) collective-permute-start(bf16[128,1024]{1,0:T(8,128)(2,1)S(1)} %fusion.43), channel_id=1, source_target_pairs={{0,16},{1,17},{2,18},{3,19},{4,20},{5,21},{6,22},{7,23},{8,24},{9,... | collective-permute-start | bytes 786440 | tf_op jit(solution)/shard_map/ppermute | solution.py:135
  332.3 20.6 %collective-permute-start.55 = (bf16[2,128,1024]{2,1,0:T(8,128)(2,1)S(1)}, bf16[2,128,1024]{2,1,0:T(8,128)(2,1)S(1)}, u32[]{:S(2)}, u32[]{:S(2)}) collective-permute-start(bf16[2,128,1024]{2,1,0:T(8,128)(2,1)S(1)} %fusion.30), channel_id=1, source_target_pairs={{0,8},{1,9},{2,10},{3,11},{4,12},{5,13},{6,14},{7,15},{8,0},{9,1},... | collective-permute-start | bytes 1572872 | tf_op jit(solution)/shard_map/ppermute | solution.py:135
  332.9 20.0 %collective-permute-start.56 = (bf16[128,1024]{1,0:T(8,128)(2,1)S(1)}, bf16[128,1024]{1,0:T(8,128)(2,1)S(1)}, u32[]{:S(2)}, u32[]{:S(2)}) collective-permute-start(bf16[128,1024]{1,0:T(8,128)(2,1)S(1)} %fusion.44), channel_id=1, source_target_pairs={{0,16},{1,17},{2,18},{3,19},{4,20},{5,21},{6,22},{7,23},{8,24},{9,... | collective-permute-start | bytes 786440 | tf_op jit(solution)/shard_map/ppermute | solution.py:135
  335.4 29.9 %collective-permute-start.57 = (bf16[4,2,32,2048]{3,2,0,1:T(8,128)(2,1)}, bf16[4,2,32,2048]{3,2,0,1:T(8,128)(2,1)}, u32[]{:S(2)}, u32[]{:S(2)}) collective-permute-start(bf16[4,2,32,2048]{3,2,0,1:T(8,128)(2,1)} %add_convert_fusion.1), channel_id=1, source_target_pairs={{0,4},{1,5},{2,6},{3,7},{4,0},{5,1},{6,2},{7,3},{8,12},{9,13},{10,... | collective-permute-start | bytes 3145736 | tf_op jit(solution)/shard_map/ppermute | solution.py:135
  335.9 29.4 %collective-permute-start.58 = (bf16[4,2,32,2048]{3,2,0,1:T(8,128)(2,1)}, bf16[4,2,32,2048]{3,2,0,1:T(8,128)(2,1)}, u32[]{:S(2)}, u32[]{:S(2)}) collective-permute-start(bf16[4,2,32,2048]{3,2,0,1:T(8,128)(2,1)} %add_convert_fusion), channel_id=1, source_target_pairs={{0,2},{1,3},{2,0},{3,1},{4,6},{5,7},{6,4},{7,5},{8,10},{9,11},{10,... | collective-permute-start | bytes 3145736 | tf_op jit(solution)/shard_map/ppermute | solution.py:135
  368.3 18.8 %collective-permute-start.61 = (bf16[4,32,2048]{2,1,0:T(8,128)(2,1)S(1)}, bf16[4,32,2048]{2,1,0:T(8,128)(2,1)S(1)}, u32[]{:S(2)}, u32[]{:S(2)}) collective-permute-start(bf16[4,32,2048]{2,1,0:T(8,128)(2,1)S(1)} %fusion.31), channel_id=1, source_target_pairs={{0,2},{1,3},{2,0},{3,1},{4,6},{5,7},{6,4},{7,5},{8,10},{9,11},{10,... | collective-permute-start | bytes 1572872 | tf_op jit(solution)/shard_map/ppermute | solution.py:135
  368.7 18.4 %collective-permute-start.62 = (bf16[4,32,2048]{2,1,0:T(8,128)(2,1)S(1)}, bf16[4,32,2048]{2,1,0:T(8,128)(2,1)S(1)}, u32[]{:S(2)}, u32[]{:S(2)}) collective-permute-start(bf16[4,32,2048]{2,1,0:T(8,128)(2,1)S(1)} %fusion.32), channel_id=1, source_target_pairs={{0,4},{1,5},{2,6},{3,7},{4,0},{5,1},{6,2},{7,3},{8,12},{9,13},{10,... | collective-permute-start | bytes 1572872 | tf_op jit(solution)/shard_map/ppermute | solution.py:135
  370.7 16.3 %collective-permute-start.64 = (bf16[128,1024]{1,0:T(8,128)(2,1)S(1)}, bf16[128,1024]{1,0:T(8,128)(2,1)S(1)}, u32[]{:S(2)}, u32[]{:S(2)}) collective-permute-start(bf16[128,1024]{1,0:T(8,128)(2,1)S(1)} %fusion.37.own), channel_id=1, source_target_pairs={{0,2},{1,3},{2,0},{3,1},{4,6},{5,7},{6,4},{7,5},{8,10},{9,11},{10,... | collective-permute-start | bytes 786440 | tf_op jit(solution)/shard_map/ppermute | solution.py:135
  387.1 28.6 %collective-permute-start.69 = (bf16[2,128,1024]{2,1,0:T(8,128)(2,1)S(1)}, bf16[2,128,1024]{2,1,0:T(8,128)(2,1)S(1)}, u32[]{:S(2)}, u32[]{:S(2)}) collective-permute-start(bf16[2,128,1024]{2,1,0:T(8,128)(2,1)S(1)} %pad_maximum_fusion.3), channel_id=1, source_target_pairs={{0,2},{1,3},{2,0},{3,1},{4,6},{5,7},{6,4},{7,5},{8,10},{9,11},{10,... | collective-permute-start | bytes 1572872 | tf_op jit(solution)/shard_map/ppermute | solution.py:135
  390.5 18.4 %collective-permute-start.65 = (bf16[32,4096]{1,0:T(8,128)(2,1)S(1)}, bf16[32,4096]{1,0:T(8,128)(2,1)S(1)}, u32[]{:S(2)}, u32[]{:S(2)}) collective-permute-start(bf16[32,4096]{1,0:T(8,128)(2,1)S(1)} %get-tuple-element.420), channel_id=1, source_target_pairs={{0,8},{1,9},{2,10},{3,11},{4,12},{5,13},{6,14},{7,15},{8,0},{9,1},... | collective-permute-start | bytes 786440 | tf_op jit(solution)/shard_map/ppermute | solution.py:135
  391.9 19.2 %collective-permute-start.66 = (bf16[32,4096]{1,0:T(8,128)(2,1)S(1)}, bf16[32,4096]{1,0:T(8,128)(2,1)S(1)}, u32[]{:S(2)}, u32[]{:S(2)}) collective-permute-start(bf16[32,4096]{1,0:T(8,128)(2,1)S(1)} %get-tuple-element.421), channel_id=1, source_target_pairs={{0,16},{1,17},{2,18},{3,19},{4,20},{5,21},{6,22},{7,23},{8,24},{9,... | collective-permute-start | bytes 786440 | tf_op jit(solution)/shard_map/ppermute | solution.py:135
  394.1 21.7 %collective-permute-start.67 = (bf16[32,4096]{1,0:T(8,128)(2,1)S(1)}, bf16[32,4096]{1,0:T(8,128)(2,1)S(1)}, u32[]{:S(2)}, u32[]{:S(2)}) collective-permute-start(bf16[32,4096]{1,0:T(8,128)(2,1)S(1)} %get-tuple-element.422), channel_id=1, source_target_pairs={{0,24},{1,25},{2,26},{3,27},{4,28},{5,29},{6,30},{7,31},{8,16},{9,... | collective-permute-start | bytes 786440 | tf_op jit(solution)/shard_map/ppermute | solution.py:135
  394.5 14.4 %collective-permute-start.68 = (f32[6,1024]{1,0:T(8,128)S(1)}, f32[6,1024]{1,0:T(8,128)S(1)}, u32[]{:S(2)}, u32[]{:S(2)}) collective-permute-start(f32[6,1024]{1,0:T(8,128)S(1)} %add.375), channel_id=1, source_target_pairs={{0,8},{1,9},{2,10},{3,11},{4,12},{5,13},{6,14},{7,15},{8,0},{9,1},... | collective-permute-start | bytes 73736 | tf_op jit(solution)/shard_map/ppermute | solution.py:135
  (112 other events, 1250.6 us)

commit v3 on v2

--- a/solution.py
+++ b/solution.py
@@ -193,13 +193,11 @@
 
 
 PIECES = (
-    ((0, 0, 0),),
-    ((1, 0, 0), (2, 0, 0), (3, 0, 0)),
-    ((0, 1, 0), (0, 0, 1), (0, 1, 1)),
-    ((1, 1, 0), (2, 1, 0), (3, 1, 0)),
-    ((1, 0, 1), (2, 0, 1), (3, 0, 1)),
-    ((1, 1, 1),),
-    ((2, 1, 1), (3, 1, 1)),
+    ((0, 0, 0), (1, 0, 0), (2, 0, 0), (3, 0, 0)),
+    ((0, 1, 0), (1, 1, 0), (2, 1, 0), (3, 1, 0)),
+    ((0, 0, 1), (1, 0, 1), (2, 0, 1), (3, 0, 1)),
+    ((0, 1, 1), (1, 1, 1), (2, 1, 1)),
+    ((3, 1, 1),),
 )
 
 
@@ -293,6 +291,131 @@
     )(idx, *own, *came, x, cosine, signed_sine)
 
 
+def unit_of(values):
+    centered = values - jnp.mean(values, axis=1, keepdims=True)
+    inverse = lax.rsqrt(jnp.mean(centered * centered, axis=1, keepdims=True) + EPS)
+    return centered * inverse, inverse
+
+
+def unit_back(grad, unit, inverse, gain):
+    scaled = grad * gain
+    return inverse * (
+        scaled
+        - jnp.mean(scaled, axis=1, keepdims=True)
+        - unit * jnp.mean(scaled * unit, axis=1, keepdims=True)
+    )
+
+
+def add_rows(ref, row, values):
+    total = jnp.sum(values, axis=0, keepdims=True)
+
+    @pl.when(pl.program_id(0) == 0)
+    def _():
+        ref[row : row + 1, :] = total
+
+    @pl.when(pl.program_id(0) > 0)
+    def _():
+        ref[row : row + 1, :] += total
+
+
+def leave_kernel(attended_ref, w_ref, x_ref, vec_ref, branch_ref, n_ref):
+    branch = dot(attended_ref[...], w_ref[...])
+    branch_ref[...] = branch
+    unit, _ = unit_of(x_ref[...].astype(F32) + vec_ref[2:3] * branch)
+    n_ref[...] = (unit * vec_ref[3:4] + vec_ref[4:5]).astype(BF)
+
+
+def leave(attended, w_attn, x, vecs, block=256):
+    rows, width = x.shape
+    row = pl.BlockSpec((block, width), lambda i: (i, 0))
+    return pl.pallas_call(
+        leave_kernel,
+        grid=(rows // block,),
+        in_specs=[row, pl.BlockSpec((width, width), lambda i: (0, 3)), row, whole((8, width))],
+        out_specs=[row, row],
+        out_shape=[sds((rows, width), F32), sds((rows, width), BF)],
+        compiler_params=BIG,
+        cost_estimate=work(1e9),
+        name="leave",
+    )(attended, w_attn, x, vecs)
+
+
+def back_kernel(
+    a_ref, b_ref, c_ref, go_ref, branch_ref, x_ref, vec_ref, w_ref, gm_ref, gb_ref, ga_ref, sum_ref
+):
+    grad = a_ref[...].astype(F32) + b_ref[...].astype(F32) + c_ref[...].astype(F32)
+    branch = branch_ref[...]
+    unit, inverse = unit_of(x_ref[...].astype(F32) + vec_ref[2:3] * branch)
+
+    @pl.when(pl.program_id(0) == 0)
+    def _():
+        sum_ref[...] = jnp.zeros_like(sum_ref)
+
+    add_rows(sum_ref, 3, grad * unit)
+    add_rows(sum_ref, 4, grad)
+    grad_middle = go_ref[...].astype(F32) + unit_back(grad, unit, inverse, vec_ref[3:4])
+    gm_ref[...] = grad_middle
+    add_rows(sum_ref, 2, grad_middle * branch)
+    grad_branch = (vec_ref[2:3] * grad_middle).astype(BF)
+    gb_ref[...] = grad_branch
+    ga_ref[...] = dot(grad_branch, w_ref[...], "nt").astype(BF)
+
+
+def back(parts, grad_out, branch, x, vecs, w_attn, block=256):
+    rows, width = x.shape
+    row = pl.BlockSpec((block, width), lambda i: (i, 0))
+    return pl.pallas_call(
+        back_kernel,
+        grid=(rows // block,),
+        in_specs=[row] * 6
+        + [whole((8, width)), pl.BlockSpec((width, width), lambda i: (0, 3))],
+        out_specs=[row, row, row, whole((8, width))],
+        out_shape=[sds((rows, width), F32)] + [sds((rows, width), BF)] * 2 + [sds((8, width), F32)],
+        compiler_params=BIG,
+        cost_estimate=work(1e9),
+        name="back",
+    )(*parts, grad_out, branch, x, vecs, w_attn)
+
+
+def last_kernel(*refs):
+    dq, dk, dv, wq, wk, wv, x_ref, vec_ref, gm_ref, m0, m1, m2, go_ref, branch_ref, mid_ref = refs[:15]
+    ig_ref, out_ref, sum_ref = refs[15:]
+    grad = dot(dq[...], wq[...], "nt") + dot(dk[...], wk[...], "nt") + dot(dv[...], wv[...], "nt")
+    x = x_ref[...].astype(F32)
+    unit, inverse = unit_of(x)
+
+    @pl.when(pl.program_id(0) == 0)
+    def _():
+        sum_ref[...] = mid_ref[...]
+
+    add_rows(sum_ref, 0, grad * unit)
+    add_rows(sum_ref, 1, grad)
+    ig_ref[...] = gm_ref[...] + unit_back(grad, unit, inverse, vec_ref[0:1])
+    mlp = m0[...].astype(F32) + m1[...].astype(F32) + m2[...].astype(F32)
+    out_ref[...] = (x + vec_ref[2:3] * branch_ref[...] + vec_ref[5:6] * mlp).astype(BF)
+    add_rows(sum_ref, 5, go_ref[...].astype(F32) * mlp)
+
+
+def last(grads, w_attn, x, vecs, grad_middle, mlp_parts, grad_out, branch, mid_sums, block=256):
+    rows, width = x.shape
+    row = pl.BlockSpec((block, width), lambda i: (i, 0))
+    columns = [pl.BlockSpec((width, width), lambda i, n=n: (0, n)) for n in range(3)]
+    return pl.pallas_call(
+        last_kernel,
+        grid=(rows // block,),
+        in_specs=[row] * 3
+        + columns
+        + [row, whole((8, width))]
+        + [row] * 6
+        + [whole((8, width))],
+        out_specs=[row, row, whole((8, width))],
+        out_shape=[sds((rows, width), F32), sds((rows, width), BF), sds((8, width), F32)],
+        compiler_params=BIG,
+        cost_estimate=work(1e9),
+        name="last",
+    )(*grads, w_attn, w_attn, w_attn, x, vecs, grad_middle, *mlp_parts, grad_out, branch, mid_sums)
+
+
 def set_bias(bias_ref, pos_ref, rows):
     for b in range(rows // WINDOW):
         keys = WINDOW if b == 0 else 2 * WINDOW
@@ -431,137 +554,124 @@
     return first, second, last
 
 
-def store_split(idx, total, send_ref, keep_ref):
-    rows = send_ref.shape[1]
-    for k in range(send_ref.shape[0]):
-        for ref, x in ((send_ref, 1 - idx[1]), (keep_ref, idx[1])):
-            at = pl.multiple_of((2 * k + x) * rows, rows)
-            ref[k] = total[pl.ds(at, rows), :].astype(BF)
-
-
 def mlp_kernel(last_half, *refs):
     idx, pieces, downs = refs[0], refs[1:9], refs[9:17]
     n_parts, g_parts, scale_ref = refs[17:19], refs[19:21], refs[21]
     refs = refs[22:]
     if last_half:
         before_ref, refs = refs[0], refs[1:]
-    gg_ref, gu_ref = refs[:2]
+    gg_out, gu_out = refs[:2]
     gn_parts, mlp_parts = refs[2:4], refs[4:6]
     refs = refs[6:]
     if last_half:
         send_ref, keep_ref, refs = refs[0], refs[1], refs[2:]
     else:
-        total_ref, refs = refs[0], refs[1:]
-    w_gate, w_up, w_down, total, n_buf, g_buf, sems = refs
-    i, last = pl.program_id(0), pl.num_programs(0) - 1
-    block, half = gg_ref.shape[0], pl.num_programs(0) // 2
+        total_out, refs = refs[0], refs[1:]
+    (w_gate, w_up, w_down, n, gm, silu, slope, hidden, gg, gu, gn, mlp, total) = refs[:13]
+    sems, n_sems, out_sems = refs[13:]
+    rows, width = n.shape
+    half, part = rows // 2, w_gate.shape[1]
     first, second, down = mlp_copies(idx, pieces, downs, w_gate, w_up, w_down, sems)
-
-    def wait(copies):
-        @pl.when(i == 0)
-        def _():
-            for c in copies:
+    n_copies, g_copies = [], []
+    for k in range(2):
+        here = pl.ds(k * half, half)
+        n_copies.append(pltpu.make_async_copy(n_parts[k], n.at[here, :], n_sems.at[k]))
+        g_copies.append(pltpu.make_async_copy(g_parts[k], gm.at[here, :], n_sems.at[2 + k]))
+    before = [pltpu.make_async_copy(before_ref, total, n_sems.at[4])] if last_half else []
+    for c in n_copies + first + second + g_copies + down + before:
+        c.start()
+    outs = []
+
+    def send(src, dst):
+        outs.append(pltpu.make_async_copy(src, dst, out_sems.at[len(outs)]))
+        outs[-1].start()
+
+    for c in n_copies + first:
+        c.wait()
+    chunks = [slice(c, c + part // 2) for c in (0, part // 2)]
+    for k, cols in enumerate(chunks):
+        if k == 1:
+            for c in second:
                 c.wait()
-
-    @pl.when(i == 0)
-    def _():
-        for c in first + second + down:
-            c.start()
-
-    here = pl.ds(pl.multiple_of((i % half) * block, block), block)
-
-    def load(which):
-        n_buf[...] = n_parts[which][here, :]
-        g_buf[...] = (scale_ref[...] * g_parts[which][here, :].astype(F32)).astype(BF)
-
-    pl.when(i < half)(lambda: load(0))
-    pl.when(i >= half)(lambda: load(1))
-    n, gm = n_buf[...], g_buf[...]
-    width = w_gate.shape[1]
-    kept = []
-    wait(first)
-    for c in range(0, width, width // 2):
-        cols = slice(c, c + width // 2)
-        gate, up = dot(n, w_gate[:, cols]), dot(n, w_up[:, cols])
-        if c == 0:
-            wait(second)
+        gate, up = dot(n[...], w_gate[:, cols]), dot(n[...], w_up[:, cols])
         s = 0.5 * jnp.tanh(0.5 * gate) + 0.5
-        silu = gate * s
-        hidden = (silu * up).astype(BF)
-        part = dot(hidden, gm, "tn")
-
-        @pl.when(i == 0)
-        def _():
-            if last_half:
-                total[cols, :] = before_ref[cols, :].astype(F32) + part
-            else:
-                total[cols, :] = part
-
-        @pl.when(i > 0)
-        def _():
-            total[cols, :] += part
-
-        kept.append((cols, silu, up * (s + silu * (1.0 - s)), hidden))
-    wait(down)
-    gn = mlp = None
-    for cols, silu, slope, hidden in kept:
-        gh = dot(gm, w_down[cols, :], "nt")
-        gg = (gh * slope).astype(BF)
-        gu = (gh * silu).astype(BF)
-        gg_ref[:, cols], gu_ref[:, cols] = gg, gu
-        gn_c = dot(gg, w_gate[:, cols], "nt") + dot(gu, w_up[:, cols], "nt")
-        mlp_c = dot(hidden, w_down[cols, :])
-        gn = gn_c if gn is None else gn + gn_c
-        mlp = mlp_c if mlp is None else mlp + mlp_c
-
-    def store(which):
-        gn_parts[which][here, :] = gn.astype(BF)
-        mlp_parts[which][here, :] = mlp.astype(BF)
-
-    pl.when(i < half)(lambda: store(0))
-    pl.when(i >= half)(lambda: store(1))
-
-    @pl.when(i == last)
-    def _():
+        act = gate * s
+        silu[:, cols] = act
+        slope[:, cols] = up * (s + act * (1.0 - s))
+        hidden[:, cols] = (act * up).astype(BF)
+    for c in g_copies + before:
+        c.wait()
+    gm[...] = (scale_ref[5:6] * gm[...].astype(F32)).astype(BF)
+    for cols in chunks:
+        product = dot(hidden[:, cols], gm[...], "tn")
         if last_half:
-            store_split(idx, total, send_ref, keep_ref)
-        else:
-            total_ref[...] = total[...].astype(BF)
-
-
-def mlp_both(idx, pieces, downs, n_parts, g_parts, scale, before=None, block=512):
+            product = product + total[cols, :].astype(F32)
+        total[cols, :] = product.astype(BF)
+    if last_half:
+        block = send_ref.shape[1]
+        for k in range(send_ref.shape[0]):
+            for ref, x in ((send_ref, 1 - idx[1]), (keep_ref, idx[1])):
+                at = pl.multiple_of((2 * k + x) * block, block)
+                send(total.at[pl.ds(at, block), :], ref.at[k])
+    else:
+        send(total, total_out)
+    for c in down:
+        c.wait()
+    for cols in chunks:
+        gh = dot(gm[...], w_down[cols, :], "nt")
+        gg[:, cols] = (gh * slope[:, cols]).astype(BF)
+        gu[:, cols] = (gh * silu[:, cols]).astype(BF)
+    send(gg, gg_out)
+    send(gu, gu_out)
+    for k in range(2):
+        here = pl.ds(k * half, half)
+        product = dot(gg[here, :], w_gate[...], "nt") + dot(gu[here, :], w_up[...], "nt")
+        gn[here, :] = product.astype(BF)
+        send(gn.at[here, :], gn_parts[k])
+        mlp[here, :] = dot(hidden[here, :], w_down[...]).astype(BF)
+        send(mlp.at[here, :], mlp_parts[k])
+    for c in outs:
+        c.wait()
+
+
+def mlp_both(idx, pieces, downs, n_parts, g_parts, scale, before=None):
     rows, width = n_parts[0].shape
     part = pieces[0].shape[2]
     last_half = before is not None
-    row = pl.BlockSpec((block, part), lambda i: (i, 0))
-    part_spec, part_shape = whole((rows, width)), sds((rows, width), BF)
     split, total = (4, part // 8, width), (part, width)
-    in_specs = [SMEM] + [ANY] * 16 + [part_spec] * 4 + [whole((1, width))]
-    out_specs = [row, row] + [part_spec] * 4
-    out_shape = [sds((2 * rows, part), BF)] * 2 + [part_shape] * 4
+    in_specs = [SMEM] + [ANY] * 20 + [pl.BlockSpec(memory_space=pltpu.VMEM)]
+    out_shape = [sds((2 * rows, part), BF)] * 2 + [sds((rows, width), BF)] * 4
     args = (idx, *pieces, *downs, *n_parts, *g_parts, scale)
     if last_half:
-        in_specs.append(whole(total))
+        in_specs.append(ANY)
         args += (before,)
-        out_specs += [whole(split)] * 2
         out_shape += [sds(split, BF)] * 2
     else:
-        out_specs.append(whole(total))
         out_shape.append(sds(total, BF))
+    tokens = (2 * rows, width)
+    inner = (2 * rows, part)
     return pl.pallas_call(
         lambda *refs: mlp_kernel(last_half, *refs),
-        grid=(2 * rows // block,),
         in_specs=in_specs,
-        out_specs=out_specs,
+        out_specs=[ANY] * len(out_shape),
         out_shape=out_shape,
         scratch_shapes=[
             pltpu.VMEM((width, part), BF),
             pltpu.VMEM((width, part), BF),
-            pltpu.VMEM((part, width), BF),
-            pltpu.VMEM(total, F32),
-            pltpu.VMEM((block, width), BF),
-            pltpu.VMEM((block, width), BF),
+            pltpu.VMEM(total, BF),
+            pltpu.VMEM(tokens, BF),
+            pltpu.VMEM(tokens, BF),
+            pltpu.VMEM(inner, F32),
+            pltpu.VMEM(inner, F32),
+            pltpu.VMEM(inner, BF),
+            pltpu.VMEM(inner, BF),
+            pltpu.VMEM(inner, BF),
+            pltpu.VMEM(tokens, BF),
+            pltpu.VMEM(tokens, BF),
+            pltpu.VMEM(total, BF),
             pltpu.SemaphoreType.DMA((40,)),
+            pltpu.SemaphoreType.DMA((5,)),
+            pltpu.SemaphoreType.DMA((14,)),
         ],
         compiler_params=BIG,
         cost_estimate=work(1e9),
@@ -622,109 +732,353 @@
 
 
 def attn_grad_kernel(idx, q_in, o_in, dq, dk, dv, do, *refs):
-    outs, total = refs[:8], refs[8]
+    outs, totals, sems = refs[:10], refs[10:12], refs[12]
     core = idx[3]
     half = dq.shape[1]
+    copies = []
     for n, parts in enumerate((((q_in, dq), (q_in, dk)), ((q_in, dv), (o_in, do)))):
-        side = idx[1 + n]
+        side, total = idx[1 + n], totals[n]
         for c, (a, b) in enumerate(parts):
             product = dot(a[...], b[...], "tn").astype(BF)
             total[:, :, :, :, :, c * half : (c + 1) * half] = product.reshape(4, 2, 2, 2, 32, half)
-        for m in range(4):
-            to_core = (1 - core) if m < 2 else core
-            to_side = (1 - side) if m % 2 == 0 else side
-            for k in range(4):
-                for other in range(2):
+        for m in range(5):
+            to_core = (1 - core) if m < 3 else core
+            to_side = (1 - side) if m in (0, 1, 3) else side
+            cols = pl.ds(m * half, half) if m < 2 else pl.ds(0, 2 * half)
+            for other in range(2):
+                for k in range(4):
                     x, y = (to_side, other) if n == 0 else (other, to_side)
-                    outs[4 * n + m][k, other] = total[k, x, y, to_core]
+                    copy = pltpu.make_async_copy(
+                        total.at[k, x, y, to_core, :, cols],
+                        outs[5 * n + m].at[other, k],
+                        sems.at[len(copies)],
+                    )
+                    copy.start()
+                    copies.append(copy)
+    for copy in copies:
+        copy.wait()
 
 
 def attn_grad(idx, q_in, o_in, dq, dk, dv, do):
     width = q_in.shape[1]
     vmem = pl.BlockSpec(memory_space=pltpu.VMEM)
+    one, two = sds((2, 4, 32, width), BF), sds((2, 4, 32, 2 * width), BF)
     return pl.pallas_call(
         attn_grad_kernel,
         in_specs=[SMEM] + [vmem] * 6,
-        out_specs=[vmem] * 8,
-        out_shape=[sds((4, 2, 32, 2 * width), BF)] * 8,
-        scratch_shapes=[pltpu.VMEM((4, 2, 2, 2, 32, 2 * width), BF)],
+        out_specs=[ANY] * 10,
+        out_shape=[one, one, two, two, two] * 2,
+        scratch_shapes=[pltpu.VMEM((4, 2, 2, 2, 32, 2 * width), BF)] * 2
+        + [pltpu.SemaphoreType.DMA((80,))],
         compiler_params=BIG,
         cost_estimate=work(1e9),
         name="attn_grad",
     )(idx, q_in, o_in, dq, dk, dv, do)
 
 
-def place_kernel(idx, own, y_ref, core_ref, *outs):
+def z_blocks(step, z):
+    if step == "near":
+        return [1 - z % 2, 3 - z % 2]
+    return [2 * (1 - z // 2) + z % 2] if step == "far" else [z]
+
+
+def z_copies(idx, jobs, buf, sems):
+    copies = []
+    for step, pairs in jobs:
+        for pair in pairs:
+            for b in z_blocks(step, idx[0]):
+                for ref in pair:
+                    at = len(copies)
+                    copies.append(pltpu.make_async_copy(ref.at[b], buf.at[at], sems.at[at]))
+    return copies
+
+
+def z_count(jobs):
+    return sum(2 * n * (2 if step == "near" else 1) for step, n in jobs)
+
+
+def z_scratch(jobs, block):
+    count = z_count(jobs)
+    return [pltpu.VMEM((count,) + block, BF), pltpu.SemaphoreType.DMA((count,))]
+
+
+def z_near(buf, at, out):
+    for k in range(2):
+        total = buf[at + 2 * k].astype(F32) + buf[at + 2 * k + 1].astype(F32)
+        out[k] = total.astype(BF)
+
+
+def z_add(buf, at, *more):
+    total = buf[at].astype(F32) + buf[at + 1].astype(F32)
+    for part in more:
+        total = total + part.astype(F32)
+    return total.astype(BF)
+
+
+def near_sum_kernel(n, idx, *refs):
+    pairs, (out, buf, sems) = refs[: 2 * n], refs[2 * n :]
+    pairs = [pairs[2 * m : 2 * m + 2] for m in range(n)]
+    copies = z_copies(idx, [("near", pairs)], buf, sems)
+    for copy in copies:
+        copy.start()
+    for copy in copies:
+        copy.wait()
+    for m in range(n):
+        z_near(buf, 4 * m, out.at[m])
+
+
+def near_sum(idx, pairs):
+    n = len(pairs)
+    block = pairs[0][0].shape[1:]
+    return pl.pallas_call(
+        lambda *refs: near_sum_kernel(n, *refs),
+        in_specs=[SMEM] + [ANY] * (2 * n),
+        out_specs=pl.BlockSpec(memory_space=pltpu.VMEM),
+        out_shape=sds((n, 2) + block, BF),
+        scratch_shapes=z_scratch([("near", n)], block),
+        compiler_params=BIG,
+        cost_estimate=work(1e9),
+        name="near_sum",
+    )(idx, *[p for pair in pairs for p in pair])
+
+
+def first_sum_kernel(idx, a_ref, q_ref, k_ref, b_ref, v_ref, o_ref, near, *refs):
+    z_refs, (a_out, b_out, far, gate_near, buf, sems) = refs[:6], refs[6:]
+    down, up, gate = z_refs[:2], z_refs[2:4], z_refs[4:6]
+    copies = z_copies(idx, [("far", [down, up]), ("near", [gate])], buf, sems)
+    for copy in copies:
+        copy.start()
+    half = q_ref.shape[3]
+    for keep, left, right, out in ((a_ref, q_ref, k_ref, a_out), (b_ref, v_ref, o_ref, b_out)):
+        for ref, cols in ((left, slice(0, half)), (right, slice(half, 2 * half))):
+            total = keep[:, :, :, cols].astype(F32) + ref[...].astype(F32)
+            out[:, :, :, cols] = total.astype(BF)
+    for copy in copies:
+        copy.wait()
+    high = idx[0] // 2
+    for m in range(2):
+        far[m] = z_add(buf, 2 * m, near[m, 1 - high])
+    z_near(buf, 4, gate_near)
+
+
+def first_sum(idx, parts, near, pairs):
+    block = near.shape[2:]
+    vmem = pl.BlockSpec(memory_space=pltpu.VMEM)
+    shape = sds(parts[0].shape, BF)
+    return pl.pallas_call(
+        first_sum_kernel,
+        in_specs=[SMEM] + [vmem] * 7 + [ANY] * 6,
+        out_specs=[vmem] * 4,
+        out_shape=[shape, shape, sds((2,) + block, BF), sds((2,) + block, BF)],
+        scratch_shapes=z_scratch([("far", 2), ("near", 1)], block),
+        compiler_params=BIG,
+        cost_estimate=work(1e9),
+        name="first_sum",
+    )(idx, *parts, near, *[p for pair in pairs for p in pair])
+
+
+def second_sum_kernel(idx, a0, a1, a2, b0, b1, b2, gate_near, *refs):
+    gate, (a_away, b_away, gate_far, buf, sems) = refs[:2], refs[2:]
+    copies = z_copies(idx, [("far", [gate])], buf, sems)
+    i = pl.program_id(0)
+
+    @pl.when(i == 0)
+    def _():
+        for copy in copies:
+            copy.start()
+
+    for p0, p1, p2, out in ((a0, a1, a2, a_away), (b0, b1, b2, b_away)):
+        out[...] = (p0[...].astype(F32) + p1[...].astype(F32) + p2[...].astype(F32)).astype(BF)
+
+    @pl.when(i == pl.num_programs(0) - 1)
+    def _():
+        for copy in copies:
+            copy.wait()
+        gate_far[...] = z_add(buf, 0, gate_near[1 - idx[0] // 2])
+
+
+def stay_sum_kernel(idx, a0, a1, a2, b0, b1, b2, near, far, *refs):
+    pairs, (a_stay, b_stay, own, buf, sems) = refs[:4], refs[4:]
+    copies = z_copies(idx, [("total", [pairs[:2], pairs[2:]])], buf, sems)
+    i = pl.program_id(0)
+
+    @pl.when(i == 0)
+    def _():
+        for copy in copies:
+            copy.start()
+
+    for p0, p1, p2, out in ((a0, a1, a2, a_stay), (b0, b1, b2, b_stay)):
+        out[...] = p0[...].astype(F32) + p1[...].astype(F32) + p2[...].astype(F32)
+
+    @pl.when(i == pl.num_programs(0) - 1)
+    def _():
+        for copy in copies:
+            copy.wait()
+        for m in range(2):
+            own[m] = z_add(buf, 2 * m, near[m, idx[0] // 2], far[m])
+
+
+def half_sum(kernel, idx, parts, away, more, pairs, outs, jobs, dtype, name):
+    _, blocks, rows, cols = parts[0].shape
+    block = pairs[0][0].shape[1:]
+    side = lambda at: pl.BlockSpec(
+        (None, 2, rows, cols), lambda i, s: (1 - s[at] if away else s[at], i, 0, 0)
+    )
+    out = pl.BlockSpec((2, rows, cols), lambda i, s: (i, 0, 0))
+    return pl.pallas_call(
+        kernel,
+        grid_spec=pltpu.PrefetchScalarGridSpec(
+            num_scalar_prefetch=1,
+            grid=(blocks // 2,),
+            in_specs=[side(2)] * 3
+            + [side(1)] * 3
+            + [pl.BlockSpec(p.shape, lambda i, s, n=p.ndim: (0,) * n) for p in more]
+            + [ANY] * (2 * len(pairs)),
+            out_specs=[out, out]
+            + [pl.BlockSpec(shape, lambda i, s, n=len(shape): (0,) * n) for shape in outs],
+            scratch_shapes=z_scratch(jobs, block),
+        ),
+        out_shape=[sds((blocks, rows, cols), dtype)] * 2 + [sds(shape, BF) for shape in outs],
+        compiler_params=BIG,
+        cost_estimate=work(1e9),
+        name=name,
+    )(idx, *parts, *more, *[p for pair in pairs for p in pair])
+
+
+def second_sum(idx, parts, gate_near, pair):
+    block = gate_near.shape[1:]
+    return half_sum(
+        second_sum_kernel, idx, parts, True, [gate_near], [pair], [block], [("far", 1)], BF, "second_sum"
+    )
+
+
+def stay_sum(idx, parts, near, far, pairs):
+    return half_sum(
+        stay_sum_kernel, idx, parts, False, [near, far], pairs, [far.shape], [("total", 2)], F32, "stay_sum"
+    )
+
+
+def third_sum_kernel(idx, a0, a1, b0, b1, small, own, gate_near, gate_far, *refs):
+    gate, (own_out, mine, s1, s2, s3, buf, sems) = refs[:2], refs[2:]
+    copies = z_copies(idx, [("total", [gate])], buf, sems)
+    for copy in copies:
+        copy.start()
+    half, width = a0.shape[2], 2 * a0.shape[2]
+    for k, out in enumerate((mine, s1, s2, s3)):
+        z = idx[0] ^ k
+        for p0, p1, low in ((a0, a1, 0), (b0, b1, half)):
+            total = p0[z].astype(F32) + p1[z].astype(F32)
+            out[:, low : low + half] = total.astype(out.dtype)
+        out[:, width:] = small[z].astype(out.dtype)
+    for copy in copies:
+        copy.wait()
+    own_out[pl.ds(0, 2)] = own[...]
+    own_out[2] = z_add(buf, 0, gate_near[idx[0] // 2], gate_far[...])
+
+
+def third_sum(idx, a_stay, a_y, b_stay, b_x, small, own, gate_near, gate_far, pair):
+    vmem = pl.BlockSpec(memory_space=pltpu.VMEM)
+    _, rows, half = a_stay.shape
+    cols = 2 * half + small.shape[2]
+    block = gate_far.shape
+    return pl.pallas_call(
+        third_sum_kernel,
+        in_specs=[SMEM] + [vmem] * 8 + [ANY] * 2,
+        out_specs=[vmem] * 5,
+        out_shape=[sds((3,) + block, BF), sds((rows, cols), F32)] + [sds((rows, cols), BF)] * 3,
+        scratch_shapes=z_scratch([("total", 1)], block),
+        compiler_params=BIG,
+        cost_estimate=work(1e9),
+        name="third_sum",
+    )(idx, a_stay, a_y, b_stay, b_x, small, own, gate_near, gate_far, *pair)
+
+
+def place_kernel(n_small, idx, own, y_ref, core_ref, both_ref, *outs):
     rep = idx[2] * 2 + idx[3]
-    for ref, d in ((own, 0), (y_ref, 2), (core_ref.at[0], 1), (core_ref.at[1], 3)):
+    rows = own.shape[0]
+    wide, narrow = outs, ()
+    if n_small:
+        wide, narrow, tall = outs[: -1 - n_small], outs[-1 - n_small : -1], outs[-1]
+    for ref, d in ((own, 0), (y_ref, 2), (core_ref, 1), (both_ref, 3)):
         low = 0
-        for out in outs:
+        for out in wide:
             cols = out.shape[2]
             out[pl.ds(rep ^ d, 1)] = ref[:, low : low + cols].astype(F32)[None]
             low += cols
-
-
-def place_rows(idx, own, other_y, other_core, widths):
+        if n_small:
+            at = pl.multiple_of((rep ^ d) * rows, rows)
+            tall[pl.ds(at, rows), :] = ref[:, low : low + 128].astype(F32)
+    if n_small:
+        turned = tall[...].T
+        for k, out in enumerate(narrow):
+            out[...] = turned[k : k + 1]
+
+
+def place_rows(idx, own, other_y, other_core, other_both, widths, n_small=0):
     rows = own.shape[0]
     vmem = pl.BlockSpec(memory_space=pltpu.VMEM)
     outs = pl.pallas_call(
-        place_kernel,
-        in_specs=[SMEM, vmem, vmem, vmem],
-        out_specs=[vmem] * len(widths),
-        out_shape=[sds((4, rows, w), F32) for w in widths],
+        lambda *refs: place_kernel(n_small, *refs),
+        in_specs=[SMEM] + [vmem] * 4,
+        out_specs=[vmem] * (len(widths) + n_small),
+        out_shape=[sds((4, rows, w), F32) for w in widths] + [sds((1, 4 * rows), F32)] * n_small,
+        scratch_shapes=[pltpu.VMEM((4 * rows, 128), F32)] if n_small else [],
         compiler_params=BIG,
         cost_estimate=work(1e9),
         name="place_rows",
-    )(idx, own, other_y, other_core)
-    return [out.reshape(4 * rows, -1) for out in outs]
-
-
-def place_columns_kernel(idx, up_ref, gate_ref, y_ref, core_ref, up_out, gate_out):
+    )(idx, own, other_y, other_core, other_both)
+    n = len(widths)
+    return [out.reshape(4 * rows, -1) for out in outs[:n]] + [out[0] for out in outs[n:]]
+
+
+def place_mlp_kernel(idx, own_ref, y_ref, core_ref, both_ref, down_out, up_out, gate_out):
     rep = idx[2] * 2 + idx[3]
-    for m, (own, out) in enumerate(((up_ref, up_out), (gate_ref, gate_out))):
-        parts = ((own, 0), (y_ref.at[m], 2), (core_ref.at[0, m], 1), (core_ref.at[1, m], 3))
+    parts = ((own_ref, 0), (y_ref, 2), (core_ref, 1), (both_ref, 3))
+    for ref, d in parts:
+        down_out[pl.ds(rep ^ d, 1)] = ref[0].astype(F32)[None]
+    for m, out in ((1, up_out), (2, gate_out)):
         for ref, d in parts:
-            for g in range(own.shape[1] // 128):
+            for g in range(own_ref.shape[2] // 128):
                 at = pl.multiple_of((g * 4 + (rep ^ d)) * 128, 128)
-                out[:, pl.ds(at, 128)] = ref[:, g * 128 : (g + 1) * 128].astype(F32)
-
-
-def place_columns(idx, up, gate, other_y, other_core):
-    rows, cols = up.shape
+                out[:, pl.ds(at, 128)] = ref[m, :, g * 128 : (g + 1) * 128].astype(F32)
+
+
+def place_mlp(idx, own, other_y, other_core, other_both):
+    _, rows, cols = own.shape
     vmem = pl.BlockSpec(memory_space=pltpu.VMEM)
-    return pl.pallas_call(
-        place_columns_kernel,
+    down, up, gate = pl.pallas_call(
+        place_mlp_kernel,
         in_specs=[SMEM] + [vmem] * 4,
-        out_specs=[vmem] * 2,
-        out_shape=[sds((rows, 4 * cols), F32)] * 2,
-        compiler_params=BIG,
-        cost_estimate=work(1e9),
-        name="place_columns",
-    )(idx, up, gate, other_y, other_core)
-
-
-def share_kernel(idx, gate_ref, up_ref, here_ref, there_ref):
+        out_specs=[vmem] * 3,
+        out_shape=[sds((4, rows, cols), F32)] + [sds((rows, 4 * cols), F32)] * 2,
+        compiler_params=BIG,
+        cost_estimate=work(1e9),
+        name="place_mlp",
+    )(idx, own, other_y, other_core, other_both)
+    return down.reshape(4 * rows, cols), up, gate
+
+
+def share_kernel(idx, raw_ref, here_ref, there_ref):
     rep = idx[2] * 2 + idx[3]
     for d in range(4):
         out = (here_ref, there_ref)[d // 2]
-        for m, ref in enumerate((gate_ref, up_ref)):
-            for g in range(out.shape[3] // 128):
-                at = pl.multiple_of((g * 4 + (rep ^ d)) * 128, 128)
-                out[d % 2, m, :, g * 128 : (g + 1) * 128] = ref[:, pl.ds(at, 128)]
-
-
-def share(idx, w_gate, w_up):
-    rows, ff = w_gate.shape
+        for g in range(out.shape[3] // 128):
+            at = pl.multiple_of((g * 4 + (rep ^ d)) * 128, 128)
+            out[d % 2, :, :, g * 128 : (g + 1) * 128] = raw_ref[:, :, pl.ds(at, 128)]
+
+
+def share(idx, raw):
+    _, rows, ff = raw.shape
     vmem = pl.BlockSpec(memory_space=pltpu.VMEM)
     return pl.pallas_call(
         share_kernel,
-        in_specs=[SMEM, vmem, vmem],
+        in_specs=[SMEM, vmem],
         out_specs=[vmem] * 2,
         out_shape=[sds((2, 2, rows, ff // 4), BF)] * 2,
         compiler_params=BIG,
         cost_estimate=work(1e9),
         name="share",
-    )(idx, w_gate, w_up)
+    )(idx, raw)
 
 
 def join_kernel(idx, own, y_ref, core_ref, out_ref):
@@ -787,64 +1141,58 @@
         vectors = jnp.stack([ln1_gain, ln1_bias, scale_attn, ln2_gain, ln2_bias, scale_mlp], axis=1)
         vectors = jnp.pad(vectors, ((0, 0), (0, 122)))
         bundle = jnp.concatenate([w_qkv, w_out, vectors], axis=1)[None]
-        share_here, share_there = share(idx, w_gate, w_up)
-        bundle, share_there = window(bundle, share_there)
-        from_z = [swap(bundle, "z1"), swap(bundle, "z2")]
-        x_own, share_y = swap(bundle, "x"), swap(share_there, "y")
-        y_own = swap(bundle, "y")
+        from_z = [swap(bundle, n) for n in ("z1", "z2", "z3")]
+        raw = jnp.stack([w_gate, w_up])
+        raw_x = swap(raw, "x")
+        share_here, share_there = share(idx, raw)
+        share_y = swap(share_there, "y")
 
         segment, position = clip_layout(lengths[0], count)
         cosine, sine = lane_tables(position, head_width)
         position = position[:, None]
 
-        *from_z, x_own, y_own, share_y, share_here, bundle, w_down = window(
-            *from_z, x_own, y_own, share_y, share_here, bundle, w_down
-        )
-        from_z.append(swap(bundle, "z3"))
         share_core = swap(jnp.stack([share_here[1], share_y[1]]), "core")
         gu0 = join(idx, share_here, share_y, share_core)
-        both_own, dnx0, came_own = swap(x_own, "y"), swap(w_down, "x"), swap(bundle, "core")
-        *from_z, gu0, both_own, x_own, y_own, dnx0, came_own, cosine, sine, position = window(
-            *from_z, gu0, both_own, x_own, y_own, dnx0, came_own, cosine, sine, position
-        )
-        rest = jnp.concatenate(from_z)
-        owns = jnp.concatenate([x_own, y_own, both_own])
-        rest, owns = window(rest, owns)
-        x_rest, y_rest = swap(rest, "x"), swap(rest, "y")
-        gu1, gu2, gux0 = swap(gu0, "z1"), swap(gu0, "z2"), swap(gu0, "x")
-
-        x_rest, y_rest, gu1, gu2, gux0, w_down = window(x_rest, y_rest, gu1, gu2, gux0, w_down)
-        y_one, x_two, w_down, rest = window(x_rest[:1], y_rest[1:], w_down, rest)
-        both_one, both_two = swap(y_one, "y"), swap(x_two, "x")
+        dnx0 = swap(w_down, "x")
+        share_here, share_there = share(idx, raw_x)
+        *from_z, gu0, dnx0, cosine, sine, position, share_here, share_there = window(
+            *from_z, gu0, dnx0, cosine, sine, position, share_here, share_there
+        )
+        near = jnp.concatenate([bundle] + from_z)
+        near, gu0, share_here, share_there = window(near, gu0, share_here, share_there)
+        far_x, far_y = swap(near, "x"), swap(near, "y")
+        gu1, gu2 = swap(gu0, "z1"), swap(gu0, "z2")
+        share_y = swap(share_there, "y")
+        far_x, far_y, gu1, gu2, share_y, share_here, w_down = window(
+            far_x, far_y, gu1, gu2, share_y, share_here, w_down
+        )
+        by_y, by_x, w_down, near = window(far_x[:3], far_y[3:], w_down, near)
+        both_y, both_x = swap(by_y, "y"), swap(by_x, "x")
         dn1, dn2 = swap(w_down, "z1"), swap(w_down, "z2")
-        came_rest = swap(rest, "core")
-
-        have = [bundle, rest, owns, x_rest, y_rest, both_one, both_two]
-        gu0, gu1, gu2, dn1, dn2, grad_out, came_rest, *have = window(
-            gu0, gu1, gu2, dn1, dn2, grad_out, came_rest, *have
-        )
-        came = [came_own, came_rest] + [swap(p, "core") for p in have[2:]]
-        gu3, gux1, go_y = swap(gu0, "z3"), swap(gu1, "x"), swap(grad_out, "y")
-        dnx1, dnx2 = swap(dn1, "x"), swap(dn2, "x")
+        came_near = swap(near, "core")
+
+        have = [near, far_x, far_y, both_y, both_x]
+        gu0, gu1, gu2, dn1, dn2, grad_out, came_near, *have = window(
+            gu0, gu1, gu2, dn1, dn2, grad_out, came_near, *have
+        )
+        came = [came_near] + [swap(p, "core") for p in have[1:]]
+        gu3, go_y = swap(gu0, "z3"), swap(grad_out, "y")
+        gux1, dnx1, dnx2 = swap(gu1, "x"), swap(dn1, "x"), swap(dn2, "x")
         *came, cosine, sine, position = window(*came, cosine, sine, position)
 
         qkv, normed, w_attn, vecs = project(idx, have, came, inputs, cosine, sine)
-        qkv, gux1, gu2, dnx1, dnx2, gu3, w_down = window(
-            qkv, gux1, gu2, dnx1, dnx2, gu3, w_down
-        )
+        qkv, gu2, dnx1, dnx2, gux1, gu3, w_down, share_here, share_y = window(
+            qkv, gu2, dnx1, dnx2, gux1, gu3, w_down, share_here, share_y
+        )
+        share_core = swap(jnp.stack([share_here[1], share_y[1]]), "core")
         gux2, dn3 = swap(gu2, "x"), swap(w_down, "z3")
         gux3 = swap(gu3, "x")
         attended = attend(qkv, position)
-        attended, gux2, go_y, dn3 = window(attended, gux2, go_y, dn3)
-        gain_one, bias_one, attn_scale, gain_two, bias_two, mlp_scale = [vecs[i] for i in range(6)]
-        out_full = w_attn[:, 3 * width : 4 * width]
+        attended, gux2, go_y, dn3, share_core = window(attended, gux2, go_y, dn3, share_core)
+        gux0 = join(idx, share_here, share_y, share_core)
         dnx3 = swap(dn3, "x")
-        frames = inputs.astype(F32)
-        branch = jnp.dot(attended, out_full, preferred_element_type=F32)
-        middle = frames + attn_scale * branch
-        unit_two, inverse_two = norm_parts(middle)
-        n_own = (unit_two * gain_two + bias_two).astype(BF)
-        n_own, gux3, dnx3, grad_out, go_y = window(n_own, gux3, dnx3, grad_out, go_y)
+        branch, n_own = leave(attended, w_attn, inputs, vecs)
+        n_own, gux0, gux3, dnx3, grad_out, go_y = window(n_own, gux0, gux3, dnx3, grad_out, go_y)
 
         n_y, n_core = swap(n_own, "y"), swap(n_own, "core")
         go_core = swap(grad_out, "core")
@@ -852,16 +1200,15 @@
         go_yc = swap(go_y, "core")
         pieces = (gu0, gux0, gu1, gux1, gu2, gux2, gu3, gux3)
         downs = (w_down, dnx0, dn1, dnx1, dn2, dnx2, dn3, dnx3)
-        scale = mlp_scale[None]
         gg_a, gu_a, gn_own, gn_core, mlp_own, mlp_core, total = mlp_both(
-            idx, pieces, downs, (n_own, n_core), (grad_out, go_core), scale
+            idx, pieces, downs, (n_own, n_core), (grad_out, go_core), vecs
         )
         n_y, go_y, go_yc, gn_core = window(n_y, go_y, go_yc, gn_core)
         n_yc = swap(n_y, "core")
         n_y, n_yc = window(n_y, n_yc)
         gn_core, mlp_core = swap(gn_core, "core"), swap(mlp_core, "core")
         gg_b, gu_b, gn_y, gn_yc, mlp_y, mlp_yc, down_send, down_keep = mlp_both(
-            idx, pieces, downs, (n_y, n_yc), (go_y, go_yc), scale, total
+            idx, pieces, downs, (n_y, n_yc), (go_y, go_yc), vecs, total
         )
         gn_y, gn_yc, gn_core, mlp_core, down_send = window(gn_y, gn_yc, gn_core, mlp_core, down_send)
         down_x = swap(down_send, "x")
@@ -871,151 +1218,87 @@
         gn_y = swap(gn_send, "y")
         mlp_yc = swap(mlp_yc, "core")
 
-        def z_pairs(keep, came, bit):
-            shape = (2, 2) + keep.shape[1:]
-            keep, came = along(keep.reshape(shape), bit, 1), along(came.reshape(shape), bit, 1)
-            return keep.astype(F32) + came.astype(F32)
-
-        def z_near(keep, came):
-            return z_pairs(keep, came, 1 - z % 2).astype(BF)
-
-        def z_far(keep, came, near):
-            return (
-                pick(z_pairs(keep, came, z % 2), 1 - z // 2)
-                + pick(near, 1 - z // 2).astype(F32)
-            ).astype(BF)
-
-        def z_total(keep, came, near, far):
-            mine = pick(z_pairs(keep, came, z % 2), z // 2) + pick(near, z // 2).astype(F32)
-            return (mine + far.astype(F32)).astype(BF)
-
         n_all = (n_own, n_core, n_y, n_yc)
         up_send, up_keep = weight_grad(idx, n_all, (gu_a, gu_b))
         gate_send, gate_keep = weight_grad(idx, n_all, (after(gg_a, up_send), gg_b))
-        down_x, gate_send, up_send, mlp_yc = window(down_x, gate_send, up_send, mlp_yc)
-        down_near = z_near(down_keep, down_x)
-        mlp_send = add(mlp_y, mlp_yc)
-        down_near, gn_y, mlp_send, up_send = window(down_near, gn_y, mlp_send, up_send)
+        gate_send, up_send, mlp_yc, down_x = window(gate_send, up_send, mlp_yc, down_x)
+        down_near = near_sum(idx, [(down_keep, down_x)])
+        gn_y, mlp_send, up_send, down_near = window(
+            gn_y, add(mlp_y, mlp_yc), up_send, down_near
+        )
         up_x, mlp_y, down_near = swap(up_send, "x"), swap(mlp_send, "y"), swap(down_near, "z1")
 
-        cotangent = grad_out.astype(F32)
-        grad_normed_two = gn_own.astype(F32) + gn_core.astype(F32) + gn_y.astype(F32)
-        ln2_gain_grad = jnp.sum(grad_normed_two * unit_two, axis=0)
-        ln2_bias_grad = jnp.sum(grad_normed_two, axis=0)
-        grad_middle = cotangent + norm_back(grad_normed_two, unit_two, inverse_two, gain_two)
-        scale_attn_grad = jnp.sum(grad_middle * branch, axis=0)
-        grad_branch = (attn_scale * grad_middle).astype(BF)
-        grad_attended = dot(grad_branch, out_full, "nt").astype(BF)
+        grad_middle, grad_branch, grad_attended, mid_sums = back(
+            (gn_own, gn_core, gn_y), grad_out, branch, inputs, vecs, w_attn
+        )
         grad_attended, gate_send = window(grad_attended, gate_send)
         gate_x = swap(gate_send, "x")
 
         dq, dk, dv = attend_back(qkv, grad_attended, position, cosine, sine)
         dq, mlp_y, up_x, down_near = window(dq, mlp_y, up_x, down_near)
-        up_near, down_far = z_near(up_keep, up_x), z_far(down_keep, down_x, down_near)
-        up_near, down_far, dq = window(up_near, down_far, dq)
-        up_near, down_far = swap(up_near, "z1"), swap(down_far, "z2")
+        up_near, dq = window(near_sum(idx, [(up_keep, up_x)]), dq)
+        up_near = swap(up_near, "z1")
         grads = attn_grad(idx, normed, attended, dq, dk, dv, grad_branch)
-        dq, dk, dv, gate_x, up_near, down_far, *grads = window(
-            dq, dk, dv, gate_x, up_near, down_far, *grads
-        )
-        a_send, a_send_here, a_keep, a_keep_here, b_send, b_send_here, b_keep, b_keep_here = grads
-
+        gate_x, up_near, *grads = window(gate_x, up_near, *grads)
+        near = jnp.concatenate([down_near, up_near])
+        pairs = [(down_keep, down_x), (up_keep, up_x), (gate_keep, gate_x)]
+        q_send, k_send, a_send, a_keep, a_keep_here = grads[:5]
+        v_send, o_send, b_send, b_keep, b_keep_here = grads[5:]
+
+        away = [swap(v, "core") for v in (q_send, k_send, v_send, o_send)]
+        late = (near, dq, dk, dv, mlp_y, a_send, b_send)
+        *away, near, dq, dk, dv, mlp_y, a_send, b_send = window(*away, *late)
         a_core, b_core = swap(a_send, "core"), swap(b_send, "core")
-        gate_near = z_near(gate_keep, gate_x)
-        down_mine = z_total(down_keep, down_x, down_near, down_far)
-        up_far = z_far(up_keep, up_x, up_near)
-        a_core, b_core, gate_near, up_far, down_mine, a_send_here, b_send_here = window(
-            a_core, b_core, gate_near, up_far, down_mine, a_send_here, b_send_here
-        )
-        a_core_here, b_core_here = swap(a_send_here, "core"), swap(b_send_here, "core")
-        a_away, b_away, a_core_here, b_core_here, dq, dk, dv, gate_near, up_far = window(
-            add(a_keep, a_core),
-            add(b_keep, b_core),
-            a_core_here,
-            b_core_here,
-            dq,
-            dk,
-            dv,
-            gate_near,
-            up_far,
-        )
+        a_away, b_away, far, gate_near = first_sum(
+            idx, (a_keep, *away[:2], b_keep, *away[2:]), near, pairs
+        )
+        late = (a_core, b_core, dq, dk, dv, mlp_y)
+        a_away, b_away, far, gate_near, *late = window(a_away, b_away, far, gate_near, *late)
+        a_core, b_core, dq, dk, dv, mlp_y = late
         a_x, b_y = swap(a_away, "x"), swap(b_away, "y")
-        gate_near, up_far = swap(gate_near, "z1"), swap(up_far, "z2")
-        w_qkv_full = w_attn[:, : 3 * width]
-        grad_normed = (
-            dot(dq, w_qkv_full[:, :width], "nt")
-            + dot(dk, w_qkv_full[:, width : 2 * width], "nt")
-            + dot(dv, w_qkv_full[:, 2 * width :], "nt")
-        )
-        grad_normed, gate_near, up_far = window(grad_normed, gate_near, up_far)
-        gate_far = swap(z_far(gate_keep, gate_x, gate_near), "z2")
-        up_mine = z_total(up_keep, up_x, up_near, up_far)
-        unit_one, inverse_one = norm_parts(frames)
-        ln1_gain_grad = jnp.sum(grad_normed * unit_one, axis=0)
-        ln1_bias_grad = jnp.sum(grad_normed, axis=0)
-        input_grad = grad_middle + norm_back(grad_normed, unit_one, inverse_one, gain_one)
-        mlp = mlp_own.astype(F32) + mlp_core.astype(F32) + mlp_y.astype(F32)
-        block_out = (middle + mlp_scale * mlp).astype(BF)
-        scale_mlp_grad = jnp.sum(cotangent * mlp, axis=0)
-        small = jnp.stack(
-            [
-                ln1_gain_grad,
-                ln1_bias_grad,
-                scale_attn_grad,
-                ln2_gain_grad,
-                ln2_bias_grad,
-                scale_mlp_grad,
-            ]
+        far, gate_near = swap(far, "z2"), swap(gate_near, "z1")
+        input_grad, block_out, small = last(
+            (dq, dk, dv),
+            w_attn,
+            inputs,
+            vecs,
+            grad_middle,
+            (mlp_own, mlp_core, mlp_y),
+            grad_out,
+            branch,
+            mid_sums,
         )
         small = small + swap(small, "core")
-        a_x, b_y, small, up_mine, gate_far = window(a_x, b_y, small, up_mine, gate_far)
-        a_half, b_half = (a_keep_here, a_core_here, a_x), (b_keep_here, b_core_here, b_y)
-
-        def add_three(parts, index):
-            p = [along(v, index, 1).astype(F32) for v in parts]
-            return p[0] + p[1] + p[2]
-
-        a_away, b_away = add_three(a_half, y ^ 1).astype(BF), add_three(b_half, x ^ 1).astype(BF)
-        a_away, b_away, small, down_mine = window(a_away, b_away, small, down_mine)
-        a_y, b_x, down_y = swap(a_away, "y"), swap(b_away, "x"), swap(down_mine, "y")
         small = small + swap(small, "x")
-        gate_mine = z_total(gate_keep, gate_x, gate_near, gate_far)
-        both_mine = jnp.stack([up_mine, gate_mine])
-        a_y, b_x, small, down_y, down_mine, both_mine = window(
-            a_y, b_x, small, down_y, down_mine, both_mine
-        )
-        column = jnp.concatenate(
-            [
-                (add_three(a_half, y) + a_y.astype(F32)).astype(BF),
-                (add_three(b_half, x) + b_x.astype(F32)).astype(BF),
-            ],
-            axis=-1,
-        )
-        sends = [pick(column, z ^ k) for k in (1, 2, 3)]
-        *sends, small = window(*sends, small)
+        a_x, b_y, small, gate_near, far = window(a_x, b_y, small, gate_near, far)
+        parts = (a_keep_here, a_core, a_x, b_keep_here, b_core, b_y)
+        a_away, b_away, gate_far = second_sum(idx, parts, gate_near, pairs[2])
+        a_away, b_away, gate_far, small, *parts = window(a_away, b_away, gate_far, small, *parts)
+        a_y, b_x, gate_far = swap(a_away, "y"), swap(b_away, "x"), swap(gate_far, "z2")
+        a_stay, b_stay, own = stay_sum(idx, parts, near, far, pairs[:2])
+        small = small + swap(small, "y")
+        rows_of = small[:6].reshape(6, 4, 2, 2, 2, 32)
+        rows_of = along(along(along(rows_of, x, 2), y, 2), core, 2)
+        rows_of = jnp.pad(rows_of.transpose(1, 2, 0), ((0, 0), (0, 0), (0, 122))).astype(BF)
+        a_y, b_x, rows_of, gate_far = window(a_y, b_x, rows_of, gate_far)
+        own, mine, *sends = third_sum(
+            idx, a_stay, a_y, b_stay, b_x, rows_of, own, gate_near, gate_far, pairs[2]
+        )
+        *sends, own, mine = window(*sends, own, mine)
         got = [swap(v, n) for v, n in zip(sends, ("z1", "z2", "z3"))]
-        both_y = swap(both_mine, "y")
-        small = small + swap(small, "z1")
-        down_both = jnp.stack([down_mine, down_y])
-        *got, small, both_y, down_both = window(*got, small, both_y, down_both)
-        mine = (
-            pick(column, z).astype(F32)
-            + (got[0].astype(F32) + got[1].astype(F32) + got[2].astype(F32))
-        ).astype(BF)
-        mine, small, both_y, down_both = window(mine, small, both_y, down_both)
-        other, down_core = swap(mine, "y"), swap(down_both, "core")
-        both_pair = jnp.stack([both_mine, both_y])
-        small = small + swap(small, "z2")
-        other, small, both_pair, down_core = window(other, small, both_pair, down_core)
-        mine_core = swap(jnp.stack([mine, other]), "core")
-        both_core = swap(both_pair, "core")
-        small = small + swap(small, "y")
-        (w_down_grad,) = place_rows(idx, down_mine, down_y, down_core, (width,))
-        w_up_grad, w_gate_grad = place_columns(
-            idx, both_mine[0], both_mine[1], both_y, both_core
-        )
-        w_qkv_grad, w_out_grad = place_rows(idx, mine, other, mine_core, (3 * width, width))
-        small = lax.dynamic_slice_in_dim(small, group * (width // 8), width // 8, 1)
+        own_y, own_core = swap(own, "y"), swap(own, "core")
+        *got, own, own_y, own_core = window(*got, own, own_y, own_core)
+        mine = mine + (got[0].astype(F32) + got[1].astype(F32) + got[2].astype(F32))
+        mine, own, own_y, own_core = window(mine.astype(BF), own, own_y, own_core)
+        other, mine_core, own_both = swap(mine, "y"), swap(mine, "core"), swap(own_y, "core")
+        w_down_grad, w_up_grad, w_gate_grad = place_mlp(idx, own, own_y, own_core, own_both)
+        other, mine_core, w_down_grad, w_up_grad, w_gate_grad = window(
+            other, mine_core, w_down_grad, w_up_grad, w_gate_grad
+        )
+        other_core = swap(other, "core")
+        w_qkv_grad, w_out_grad, *small = place_rows(
+            idx, mine, other, mine_core, other_core, (3 * width, width), 6
+        )
         return (
             block_out,
             input_grad,

time: 448 us -> 397 us (0.89)
  Pallas kernels: 146 us -> 189 us
  waiting for transfers between devices: 149 us -> 108 us
  other arithmetic: 46.7 us -> 11.3 us
  matrix products: 18.4 us -> 0 us
    ppermute x76 -> x72, waiting for transfers between devices: 149 us -> 108 us  [swap(): return lax.ppermute(value, AXES, pairs)]
    pallas_call x6 -> x15, Pallas kernels: 68.9 us -> 109 us  [the longest x2 43.8 us: mlp_both(): pl.pallas_call(lambda *refs: mlp_kernel(last_half, *refs), in_specs=in_sp...]
    dot_general x5 -> x0, matrix products: 18.4 us -> none  [the longest x4 13.5 us: dot(): return lax.dot_general(a, b, CONTRACT[form], preferred_element_type=F32)]
    convert_element_type x15 -> x1, other arithmetic: 17.8 us -> 1.58 us  [shards(): mine, own, own_y, own_core = window(mine.astype(BF), own, own_y, own_core)]
    reduce_sum x6 -> x0, other arithmetic: 10.8 us -> none  [the longest x1 3.6 us: shards(): scale_mlp_grad = jnp.sum(cotangent * mlp, axis=0)]
    add x6 -> x0, other arithmetic: 5.87 us -> none  [the longest x3 3.83 us: z_pairs(): return keep.astype(F32) + came.astype(F32)]
    convert_element_type x4 -> x2, other arithmetic: 6.94 us -> 2.02 us  [add(): return (a.astype(F32) + b.astype(F32)).astype(BF)]
    unnamed x168 -> x143, local copies, waits for them, and re-layouts: 8.25 us -> 13.1 us
  transfers between devices with their start and end apart: 76 -> 72, of which waited for: 28 -> 31; matrix products, arithmetic and copies ran while one was open for 12% -> 3% of each run, Pallas kernels for 32% -> 45%
where the time goes in v3:
time: 397 us; the launch traced here: 390 us
  Pallas kernels  189 us (48%)
  waiting for transfers between devices  108 us (27%)
  starting transfers between devices  63 us (16%)
  local copies, waits for them, and re-layouts  16.7 us (4%)
  other arithmetic  11.3 us (3%)
    ppermute x72, waiting for transfers between devices, swap(): return lax.ppermute(value, AXES, pairs)  108 us
    ppermute x72, starting transfers between devices, swap(): return lax.ppermute(value, AXES, pairs)  63 us
    pallas_call x2, Pallas kernels, mlp_both(): pl.pallas_call(lambda *refs: mlp_kernel(last_half, *refs), in_specs=in_sp...  43.8 us
    pallas_call x2, Pallas kernels, weight_grad(): pl.pallas_call(weight_grad_kernel, grid_spec=pltpu.PrefetchScalarGridSpec...  20.6 us
    pallas_call x1, Pallas kernels, attend_back(): pl.pallas_call(attend_back_kernel, grid=(pairs,), in_specs=[cols(0), cols...  20.2 us
    pallas_call x1, Pallas kernels, project(): pl.pallas_call(project_kernel, grid=(3 * width // block,), in_specs=[SMEM...  14.3 us
    pallas_call x1, Pallas kernels, last(): pl.pallas_call(last_kernel, grid=(rows // block,), in_specs=[row] * 3 + c...  13.5 us
    unnamed x143, local copies, waits for them, and re-layouts  13.1 us
  transfers between devices with their start and end apart: 72, of which 31 were waited for; matrix products, arithmetic and copies ran while one was open for 3% of the time, Pallas kernels for 45%

profile of v3, /device:TPU:10, one launch (start us, length us, event | category | flops | bytes accessed | tf_op | source)
XLA Modules:
  0.0 389.9 jit_solution(17570138711280396259)
XLA Ops:
  2.5 1.6 collective-permute-start.2
  9.0 2.0 share.2
  13.8 4.6 %collective-permute-done.3.y_ref = bf16[2,2,32,1024]{3,2,1,0:T(8,128)(2,1)S(1)} collective-permute-done((bf16[2,2,32,1024]{3,2,1,0:T(8,128)(2,1)}, bf16[2,2,32,1024]{3,2,1,0:T(8,128)(2,1)S(1)}, u32[]{:S(2)}, u32[]{:S(2)}) %collective-permute-start.3) | collective-permute-done | bytes 262176 | tf_op jit(solution)/shard_map/ppermute | solution.py:135
  18.7 1.8 fusion.3
  22.9 1.9 join.2.refs_1_
  25.6 2.0 share.3
  27.6 1.8 collective-permute-done.5.refs_10_
  32.7 2.6 collective-permute-start.10
  36.1 24.6 %collective-permute-done.11.y_ref = bf16[2,2,32,1024]{3,2,1,0:T(8,128)(2,1)S(1)} collective-permute-done((bf16[2,2,32,1024]{3,2,1,0:T(8,128)(2,1)S(1)}, bf16[2,2,32,1024]{3,2,1,0:T(8,128)(2,1)S(1)}, u32[]{:S(2)}, u32[]{:S(2)}) %collective-permute-start.11) | collective-permute-done | bytes 262176 | tf_op jit(solution)/shard_map/ppermute | solution.py:135
  64.7 2.6 collective-permute-start.13
  67.7 10.7 %collective-permute-done.13.refs_13_ = bf16[128,1024]{1,0:T(8,128)(2,1)S(1)} collective-permute-done((bf16[128,1024]{1,0:T(8,128)(2,1)S(1)}, bf16[128,1024]{1,0:T(8,128)(2,1)S(1)}, u32[]{:S(2)}, u32[]{:S(2)}) %collective-permute-start.13) | collective-permute-done | bytes 262176 | tf_op jit(solution)/shard_map/ppermute | solution.py:135
  79.4 2.7 collective-permute-done.15.refs_4_
  84.7 3.3 collective-permute-done.20.refs_10_
  94.1 14.3 %project.1 = (bf16[512,3072]{1,0:T(8,128)(2,1)}, bf16[512,1024]{1,0:T(8,128)(2,1)}, bf16[1024,4224]{1,0:T(8,128)(2,1)}, f32[8,1024]{1,0:T(8,128)}) custom-call(s32[4]{0:T(128)} %pad_add_fusion.idx.refs_0_, bf16[4,32,4224]{2,1,0:T(8,128)(2,1)} %copy-done.5, bf16[4,32,4224]{2,1,0:T(8,128)(2,1)} %copy-done.12, bf16[4,32,4224]{2,1,0:T(8,128)(2,1)} %copy-done.21, ...), custom_call_target="tpu_custom_call" | custom-call | flops 1000000000 | tf_op jit(solution)/shard_map/project/pallas_call | solution.py:267
  108.4 4.9 %collective-permute-done.22.refs_14_ = bf16[128,1024]{1,0:T(8,128)(2,1)} collective-permute-done((bf16[128,1024]{1,0:T(8,128)(2,1)S(1)}, bf16[128,1024]{1,0:T(8,128)(2,1)}, u32[]{:S(2)}, u32[]{:S(2)}) %collective-permute-start.22) | collective-permute-done | bytes 262176 | tf_op jit(solution)/shard_map/ppermute | solution.py:135
  118.0 10.7 %attend.1.attended_ref.o_in = bf16[512,1024]{1,0:T(8,128)(2,1)} custom-call(bf16[512,3072]{1,0:T(8,128)(2,1)} %get-tuple-element.307.q_ref.k_ref.v_ref, bf16[512,3072]{1,0:T(8,128)(2,1)} %get-tuple-element.307.q_ref.k_ref.v_ref, bf16[512,3072]{1,0:T(8,128)(2,1)} %get-tuple-element.307.q_ref.k_ref.v_ref, s32[512,1]{1,0:T(8,128)} %iota_subtract_fusion.pos_ref), custom_call_target="tpu_custom_call" | custom-call | flops 1000000000 | tf_op jit(solution)/shard_map/attend/pallas_call | solution.py:465
  130.9 1.9 join.3.refs_2_
  132.8 5.3 %leave.1 = (f32[512,1024]{1,0:T(8,128)}, bf16[512,1024]{1,0:T(8,128)(2,1)}) custom-call(bf16[512,1024]{1,0:T(8,128)(2,1)} %attend.1.attended_ref.o_in, bf16[1024,4224]{1,0:T(8,128)(2,1)} %get-tuple-element.315.w_ref.refs_3_.refs_4_.refs_5_, bf16[512,1024]{1,0:T(8,128)(2,1)} %refs_6_.1, f32[8,1024]{1,0:T(8,128)} %get-tuple-element.316.vec_ref.refs_21_.refs_7_), custom_call_target="tpu_custom_call" | custom-call | flops 1000000000 | tf_op jit(solution)/shard_map/leave/pallas_call | solution.py:331
  139.5 3.9 collective-permute-done.30.refs_16_
  145.4 2.1 collective-permute-done.32.refs_20_
  149.5 21.9 %mlp_both.2 = (bf16[1024,1024]{1,0:T(8,128)(2,1)}, bf16[1024,1024]{1,0:T(8,128)(2,1)}, bf16[512,1024]{1,0:T(8,128)(2,1)}, bf16[512,1024]{1,0:T(8,128)(2,1)}, bf1...) custom-call(s32[4]{0:T(128)} %pad_add_fusion.idx.refs_0_, ...), custom_call_target="tpu_custom_call" | custom-call | flops 1000000000 | tf_op jit(solution)/shard_map/mlp_both/pallas_call | solution.py:653
  172.2 2.1 collective-permute-done.35.refs_18_.refs_6_.refs_7_
  175.3 21.9 %mlp_both.3 = (bf16[1024,1024]{1,0:T(8,128)(2,1)}, bf16[1024,1024]{1,0:T(8,128)(2,1)}, bf16[512,1024]{1,0:T(8,128)(2,1)}, bf16[512,1024]{1,0:T(8,128)(2,1)}, bf1...) custom-call(s32[4]{0:T(128)} %pad_add_fusion.idx.refs_0_, ...), custom_call_target="tpu_custom_call" | custom-call | flops 1000000000 | tf_op jit(solution)/shard_map/mlp_both/pallas_call | solution.py:653
  200.2 1.6 add_convert_fusion.1
  202.0 1.6 collective-permute-start.39
  203.6 10.3 %weight_grad.2 = (bf16[4,128,1024]{2,1,0:T(8,128)(2,1)}, bf16[4,128,1024]{2,1,0:T(8,128)(2,1)}) custom-call(s32[4]{0:T(128)} %pad_add_fusion.idx.refs_0_, bf16[512,1024]{1,0:T(8,128)(2,1)} %get-tuple-element.330.refs_17_.refs_0_.refs_1_, bf16[512,1024]{1,0:T(8,128)(2,1)} %get-tuple-element.330.refs_17_.refs_0_.refs_1_, bf16[512,1024]{1,0:T(8,128)(2,1)} %copy-done.2, ...), custom_call_target="tpu_custom_call" | custom-call | flops 1000000000 | tf_op jit(solution)/shard_map/weight_grad/pallas_call | solution.py:715
  214.0 10.3 %weight_grad.3 = (bf16[4,128,1024]{2,1,0:T(8,128)(2,1)}, bf16[4,128,1024]{2,1,0:T(8,128)(2,1)}) custom-call(s32[4]{0:T(128)} %pad_add_fusion.idx.refs_0_, bf16[512,1024]{1,0:T(8,128)(2,1)} %get-tuple-element.330.refs_17_.refs_0_.refs_1_, bf16[512,1024]{1,0:T(8,128)(2,1)} %get-tuple-element.330.refs_17_.refs_0_.refs_1_, bf16[512,1024]{1,0:T(8,128)(2,1)} %copy-done.2, ...), custom_call_target="tpu_custom_call" | custom-call | flops 1000000000 | tf_op jit(solution)/shard_map/weight_grad/pallas_call | solution.py:715
  225.3 2.8 near_sum.2
  231.5 8.3 %back.1 = (f32[512,1024]{1,0:T(8,128)}, bf16[512,1024]{1,0:T(8,128)(2,1)}, bf16[512,1024]{1,0:T(8,128)(2,1)}, f32[8,1024]{1,0:T(8,128)}) custom-call(bf16[512,1024]{1,0:T(8,128)(2,1)} %get-tuple-element.334.a_ref, bf16[512,1024]{1,0:T(8,128)(2,1)} %copy-done.30, bf16[512,1024]{1,0:T(8,128)(2,1)} %copy-done.31, bf16[512,1024]{1,0:T(8,128)(2,1)} %refs_12_, ...), custom_call_target="tpu_custom_call" | custom-call | flops 1000000000 | tf_op jit(solution)/shard_map/back/pallas_call | solution.py:367
  240.5 20.2 %attend_back.1 = (bf16[512,1024]{1,0:T(8,128)(2,1)}, bf16[512,1024]{1,0:T(8,128)(2,1)}, bf16[512,1024]{1,0:T(8,128)(2,1)}) custom-call(bf16[512,3072]{1,0:T(8,128)(2,1)} %get-tuple-element.307.q_ref.k_ref.v_ref, bf16[512,3072]{1,0:T(8,128)(2,1)} %get-tuple-element.307.q_ref.k_ref.v_ref, bf16[512,3072]{1,0:T(8,128)(2,1)} %get-tuple-element.307.q_ref.k_ref.v_ref, ...), custom_call_target="tpu_custom_call" | custom-call | flops 1000000000 | tf_op jit(solution)/shard_map/attend_back/pallas_call | solution.py:522
  261.8 2.8 near_sum.3
  266.0 10.1 %attn_grad.1 = (bf16[2,4,32,1024]{3,2,1,0:T(8,128)(2,1)}, bf16[2,4,32,1024]{3,2,1,0:T(8,128)(2,1)}, bf16[2,4,32,2048]{3,2,1,0:T(8,128)(2,1)}, bf16[2,4,32,2048]{...) custom-call(s32[4]{0:T(128)} %pad_add_fusion.idx.refs_0_, ...), custom_call_target="tpu_custom_call" | custom-call | flops 1000000000 | tf_op jit(solution)/shard_map/attn_grad/pallas_call | solution.py:766
  283.2 5.8 %first_sum.1 = (bf16[2,4,32,2048]{3,2,1,0:T(8,128)(2,1)}, bf16[2,4,32,2048]{3,2,1,0:T(8,128)(2,1)}, bf16[2,128,1024]{2,1,0:T(8,128)(2,1)}, bf16[2,128,1024]{2,1,0:T(8,128)(2,1)}) custom-call(s32[4]{0:T(128)} %pad_add_fusion.idx.refs_0_, bf16[2,4,32,2048]{3,2,1,0:T(8,128)(2,1)} %get-tuple-element.399.a_ref, bf16[2,4,32,1024]{3,2,1,0:T(8,128)(2,1)} %copy-done.42, ...), custom_call_target="tpu_custom_call" | custom-call | flops 1000000000 | tf_op jit(solution)/shard_map/first_sum/pallas_call | solution.py:868
  292.9 2.6 collective-permute-start.58
  295.5 13.5 %last.1 = (f32[512,1024]{1,0:T(8,128)}, bf16[512,1024]{1,0:T(8,128)(2,1)}, f32[8,1024]{1,0:T(8,128)}) custom-call(bf16[512,1024]{1,0:T(8,128)(2,1)} %get-tuple-element.427.dq.refs_0_, bf16[512,1024]{1,0:T(8,128)(2,1)} %get-tuple-element.428.dk.refs_1_, bf16[512,1024]{1,0:T(8,128)(2,1)} %get-tuple-element.429.dv.refs_2_, ...), custom_call_target="tpu_custom_call" | custom-call | flops 1000000000 | tf_op jit(solution)/shard_map/last/pallas_call | solution.py:403
  311.7 3.5 collective-permute-done.56
  315.4 2.9 collective-permute-done.58.far
  320.3 4.6 %second_sum.1 = (bf16[4,32,2048]{2,1,0:T(8,128)(2,1)}, bf16[4,32,2048]{2,1,0:T(8,128)(2,1)}, bf16[128,1024]{1,0:T(8,128)(2,1)}) custom-call(s32[4]{0:T(128)} %pad_add_fusion.idx.refs_0_, bf16[2,4,32,2048]{3,2,1,0:T(8,128)(2,1)} %get-tuple-element.453.a0, bf16[2,4,32,2048]{3,2,1,0:T(8,128)(2,1)} %copy-done.8, bf16[2,4,32,2048]{3,2,1,0:T(8,128)(2,1)} %copy-done.10, ...), custom_call_target="tpu_custom_call" | custom-call | flops 1000000000 | tf_op jit(solution)/shard_map/second_sum/pallas_call | solution.py:928
  327.5 2.7 collective-permute-start.62
  330.2 5.8 %stay_sum.1 = (f32[4,32,2048]{2,1,0:T(8,128)}, f32[4,32,2048]{2,1,0:T(8,128)}, bf16[2,128,1024]{2,1,0:T(8,128)(2,1)}) custom-call(s32[4]{0:T(128)} %pad_add_fusion.idx.refs_0_, bf16[2,4,32,2048]{3,2,1,0:T(8,128)(2,1)} %get-tuple-element.453.a0, bf16[2,4,32,2048]{3,2,1,0:T(8,128)(2,1)} %copy-done.8, bf16[2,4,32,2048]{3,2,1,0:T(8,128)(2,1)} %copy-done.10, ...), custom_call_target="tpu_custom_call" | custom-call | flops 1000000000 | tf_op jit(solution)/shard_map/stay_sum/pallas_call | solution.py:928
  336.0 2.5 collective-permute-done.61
  340.4 4.6 %third_sum.1 = (bf16[3,128,1024]{2,1,0:T(8,128)(2,1)}, f32[32,4224]{1,0:T(8,128)}, bf16[32,4224]{1,0:T(8,128)(2,1)}, bf16[32,4224]{1,0:T(8,128)(2,1)}, bf16[32,4224]{1,0:T(8,128)(2,1)}) custom-call(s32[4]{0:T(128)} %pad_add_fusion.idx.refs_0_, f32[4,32,2048]{2,1,0:T(8,128)} %get-tuple-element.460.a0, bf16[4,32,2048]{2,1,0:T(8,128)(2,1)} %copy-done.48, ...), custom_call_target="tpu_custom_call" | custom-call | flops 1000000000 | tf_op jit(solution)/shard_map/third_sum/pallas_call | solution.py:984
  347.2 2.0 collective-permute-start.64
  349.8 9.1 %collective-permute-done.63 = bf16[32,4224]{1,0:T(8,128)(2,1)S(1)} collective-permute-done((bf16[32,4224]{1,0:T(8,128)(2,1)}, bf16[32,4224]{1,0:T(8,128)(2,1)S(1)}, u32[]{:S(2)}, u32[]{:S(2)}) %collective-permute-start.63) | collective-permute-done | bytes 270368 | tf_op jit(solution)/shard_map/ppermute | solution.py:135
  358.8 9.1 %collective-permute-done.64 = bf16[32,4224]{1,0:T(8,128)(2,1)S(1)} collective-permute-done((bf16[32,4224]{1,0:T(8,128)(2,1)}, bf16[32,4224]{1,0:T(8,128)(2,1)S(1)}, u32[]{:S(2)}, u32[]{:S(2)}) %collective-permute-start.64) | collective-permute-done | bytes 270368 | tf_op jit(solution)/shard_map/ppermute | solution.py:135
  368.0 5.9 %collective-permute-done.65 = bf16[32,4224]{1,0:T(8,128)(2,1)S(1)} collective-permute-done((bf16[32,4224]{1,0:T(8,128)(2,1)}, bf16[32,4224]{1,0:T(8,128)(2,1)S(1)}, u32[]{:S(2)}, u32[]{:S(2)}) %collective-permute-start.65) | collective-permute-done | bytes 270368 | tf_op jit(solution)/shard_map/ppermute | solution.py:135
  378.8 5.2 %place_mlp.1 = (f32[4,128,1024]{2,1,0:T(8,128)}, f32[128,4096]{1,0:T(8,128)}, f32[128,4096]{1,0:T(8,128)}) custom-call(s32[4]{0:T(128)} %pad_add_fusion.idx.refs_0_, bf16[3,128,1024]{2,1,0:T(8,128)(2,1)} %get-tuple-element.488.own_ref, bf16[3,128,1024]{2,1,0:T(8,128)(2,1)} %copy-done.60, bf16[3,128,1024]{2,1,0:T(8,128)(2,1)} %copy-done.59, ...), custom_call_target="tpu_custom_call" | custom-call | flops 1000000000 | tf_op jit(solution)/shard_map/place_mlp/pallas_call | solution.py:1049
  386.9 2.6 place_rows.1
  (296 shorter events, 85.9 us)
Async XLA Ops:
  2.5 26.9 %collective-permute-start.2 = (bf16[1,32,4224]{2,1,0:T(8,128)(2,1)S(1)}, bf16[1,32,4224]{2,1,0:T(8,128)(2,1)S(1)}, u32[]{:S(2)}, u32[]{:S(2)}) collective-permute-start(bf16[1,32,4224]{2,1,0:T(8,128)(2,1)S(1)} %fusion.2), channel_id=1, source_target_pairs={{0,24},{1,25},{2,26},{3,27},{4,28},{5,29},{6,30},{7,31},{8,16},{9,... | collective-permute-start | bytes 811016 | tf_op jit(solution)/shard_map/ppermute | solution.py:135
  4.1 25.2 %collective-permute-start.1 = (bf16[1,32,4224]{2,1,0:T(8,128)(2,1)S(1)}, bf16[1,32,4224]{2,1,0:T(8,128)(2,1)S(1)}, u32[]{:S(2)}, u32[]{:S(2)}) collective-permute-start(bf16[1,32,4224]{2,1,0:T(8,128)(2,1)S(1)} %fusion.2), channel_id=1, source_target_pairs={{0,16},{1,17},{2,18},{3,19},{4,20},{5,21},{6,22},{7,23},{8,24},{9,... | collective-permute-start | bytes 811016 | tf_op jit(solution)/shard_map/ppermute | solution.py:135
  5.4 24.0 %collective-permute-start = (bf16[1,32,4224]{2,1,0:T(8,128)(2,1)S(1)}, bf16[1,32,4224]{2,1,0:T(8,128)(2,1)S(1)}, u32[]{:S(2)}, u32[]{:S(2)}) collective-permute-start(bf16[1,32,4224]{2,1,0:T(8,128)(2,1)S(1)} %fusion.2), channel_id=1, source_target_pairs={{0,8},{1,9},{2,10},{3,11},{4,12},{5,13},{6,14},{7,15},{8,0},{9,1},... | collective-permute-start | bytes 811016 | tf_op jit(solution)/shard_map/ppermute | solution.py:135
  7.7 17.1 %collective-permute-start.6 = (bf16[2,32,4096]{2,1,0:T(8,128)(2,1)S(1)}, bf16[2,32,4096]{2,1,0:T(8,128)(2,1)S(1)}, u32[]{:S(2)}, u32[]{:S(2)}) collective-permute-start(bf16[2,32,4096]{2,1,0:T(8,128)(2,1)S(1)} %pad_maximum_fusion.2.raw_ref), channel_id=1, source_target_pairs={{0,4},{1,5},{2,6},{3,7},{4,0},{5,1},{6,2},{7,3},{8,12},{9,13},{10,... | collective-permute-start | bytes 1572872 | tf_op jit(solution)/shard_map/ppermute | solution.py:135
  29.6 31.2 %collective-permute-start.8 = (bf16[4,32,4224]{2,1,0:T(8,128)(2,1)S(1)}, bf16[4,32,4224]{2,1,0:T(8,128)(2,1)S(1)}, u32[]{:S(2)}, u32[]{:S(2)}) collective-permute-start(bf16[4,32,4224]{2,1,0:T(8,128)(2,1)S(1)} %pad_maximum_fusion.refs_1_), channel_id=1, source_target_pairs={{0,2},{1,3},{2,0},{3,1},{4,6},{5,7},{6,4},{7,5},{8,10},{9,11},{10,... | collective-permute-start | bytes 3244040 | tf_op jit(solution)/shard_map/ppermute | solution.py:135
  31.2 30.3 %collective-permute-start.7 = (bf16[4,32,4224]{2,1,0:T(8,128)(2,1)S(1)}, bf16[4,32,4224]{2,1,0:T(8,128)(2,1)S(1)}, u32[]{:S(2)}, u32[]{:S(2)}) collective-permute-start(bf16[4,32,4224]{2,1,0:T(8,128)(2,1)S(1)} %pad_maximum_fusion.refs_1_), channel_id=1, source_target_pairs={{0,4},{1,5},{2,6},{3,7},{4,0},{5,1},{6,2},{7,3},{8,12},{9,13},{10,... | collective-permute-start | bytes 3244040 | tf_op jit(solution)/shard_map/ppermute | solution.py:135
  32.7 28.1 %collective-permute-start.10 = (bf16[2,128,1024]{2,1,0:T(8,128)(2,1)S(1)}, bf16[2,128,1024]{2,1,0:T(8,128)(2,1)S(1)}, u32[]{:S(2)}, u32[]{:S(2)}) collective-permute-start(bf16[2,128,1024]{2,1,0:T(8,128)(2,1)S(1)} %copy-done.14), channel_id=1, source_target_pairs={{0,16},{1,17},{2,18},{3,19},{4,20},{5,21},{6,22},{7,23},{8,24},{9,... | collective-permute-start | bytes 1572872 | tf_op jit(solution)/shard_map/ppermute | solution.py:135
  35.3 25.4 %collective-permute-start.9 = (bf16[2,128,1024]{2,1,0:T(8,128)(2,1)S(1)}, bf16[2,128,1024]{2,1,0:T(8,128)(2,1)S(1)}, u32[]{:S(2)}, u32[]{:S(2)}) collective-permute-start(bf16[2,128,1024]{2,1,0:T(8,128)(2,1)S(1)} %copy-done.14), channel_id=1, source_target_pairs={{0,8},{1,9},{2,10},{3,11},{4,12},{5,13},{6,14},{7,15},{8,0},{9,1},... | collective-permute-start | bytes 1572872 | tf_op jit(solution)/shard_map/ppermute | solution.py:135
  35.6 25.2 %collective-permute-start.11 = (bf16[2,2,32,1024]{3,2,1,0:T(8,128)(2,1)S(1)}, bf16[2,2,32,1024]{3,2,1,0:T(8,128)(2,1)S(1)}, u32[]{:S(2)}, u32[]{:S(2)}) collective-permute-start(bf16[2,2,32,1024]{3,2,1,0:T(8,128)(2,1)S(1)} %copy-done.67), channel_id=1, source_target_pairs={{0,2},{1,3},{2,0},{3,1},{4,6},{5,7},{6,4},{7,5},{8,10},{9,11},{10,... | collective-permute-start | bytes 786440 | tf_op jit(solution)/shard_map/ppermute | solution.py:135
  61.6 20.6 %collective-permute-start.14 = (bf16[4,32,4224]{2,1,0:T(8,128)(2,1)S(1)}, bf16[4,32,4224]{2,1,0:T(8,128)(2,1)S(1)}, u32[]{:S(2)}, u32[]{:S(2)}) collective-permute-start(bf16[4,32,4224]{2,1,0:T(8,128)(2,1)S(1)} %pad_maximum_fusion.refs_1_), channel_id=1, source_target_pairs={{0,1},{1,0},{2,3},{3,2},{4,5},{5,4},{6,7},{7,6},{8,9},{9,8},{10,11... | collective-permute-start | bytes 3244040 | tf_op jit(solution)/shard_map/ppermute | solution.py:135
  61.7 20.5 %collective-permute-start.15 = (bf16[3,32,4224]{2,1,0:T(8,128)(2,1)S(1)}, bf16[3,32,4224]{2,1,0:T(8,128)(2,1)S(1)}, u32[]{:S(2)}, u32[]{:S(2)}) collective-permute-start(bf16[3,32,4224]{2,1,0:T(8,128)(2,1)S(1)} %slice.23), channel_id=1, source_target_pairs={{0,2},{1,3},{2,0},{3,1},{4,6},{5,7},{6,4},{7,5},{8,10},{9,11},{10,... | collective-permute-start | bytes 2433032 | tf_op jit(solution)/shard_map/ppermute | solution.py:135
  63.2 16.2 %collective-permute-start.16 = (bf16[1,32,4224]{2,1,0:T(8,128)(2,1)S(1)}, bf16[1,32,4224]{2,1,0:T(8,128)(2,1)S(1)}, u32[]{:S(2)}, u32[]{:S(2)}) collective-permute-start(bf16[1,32,4224]{2,1,0:T(8,128)(2,1)S(1)} %slice.24), channel_id=1, source_target_pairs={{0,4},{1,5},{2,6},{3,7},{4,0},{5,1},{6,2},{7,3},{8,12},{9,13},{10,... | collective-permute-start | bytes 811016 | tf_op jit(solution)/shard_map/ppermute | solution.py:135
  64.7 13.6 %collective-permute-start.13 = (bf16[128,1024]{1,0:T(8,128)(2,1)S(1)}, bf16[128,1024]{1,0:T(8,128)(2,1)S(1)}, u32[]{:S(2)}, u32[]{:S(2)}) collective-permute-start(bf16[128,1024]{1,0:T(8,128)(2,1)S(1)} %copy-done.32), channel_id=1, source_target_pairs={{0,16},{1,17},{2,18},{3,19},{4,20},{5,21},{6,22},{7,23},{8,24},{9,... | collective-permute-start | bytes 786440 | tf_op jit(solution)/shard_map/ppermute | solution.py:135
  67.4 12.0 %collective-permute-start.12 = (bf16[128,1024]{1,0:T(8,128)(2,1)S(1)}, bf16[128,1024]{1,0:T(8,128)(2,1)S(1)}, u32[]{:S(2)}, u32[]{:S(2)}) collective-permute-start(bf16[128,1024]{1,0:T(8,128)(2,1)S(1)} %copy-done.32), channel_id=1, source_target_pairs={{0,8},{1,9},{2,10},{3,11},{4,12},{5,13},{6,14},{7,15},{8,0},{9,1},... | collective-permute-start | bytes 786440 | tf_op jit(solution)/shard_map/ppermute | solution.py:135
  83.2 30.1 %collective-permute-start.24 = (bf16[2,128,1024]{2,1,0:T(8,128)(2,1)S(1)}, bf16[2,128,1024]{2,1,0:T(8,128)(2,1)S(1)}, u32[]{:S(2)}, u32[]{:S(2)}) collective-permute-start(bf16[2,128,1024]{2,1,0:T(8,128)(2,1)S(1)} %copy-done.14), channel_id=1, source_target_pairs={{0,24},{1,25},{2,26},{3,27},{4,28},{5,29},{6,30},{7,31},{8,16},{9,... | collective-permute-start | bytes 1572872 | tf_op jit(solution)/shard_map/ppermute | solution.py:135
  88.0 25.3 %collective-permute-start.23 = (bf16[2,128,1024]{2,1,0:T(8,128)(2,1)S(1)}, bf16[2,128,1024]{2,1,0:T(8,128)(2,1)S(1)}, u32[]{:S(2)}, u32[]{:S(2)}) collective-permute-start(bf16[2,128,1024]{2,1,0:T(8,128)(2,1)S(1)} %collective-permute-done.9.refs_3_), channel_id=1, source_target_pairs={{0,4},{1,5},{2,6},{3,7},{4,0},{5,1},{6,2},{7,3},{8,12},{9,13},{10,... | collective-permute-start | bytes 1572872 | tf_op jit(solution)/shard_map/ppermute | solution.py:135
  89.5 39.3 %collective-permute-start.26 = (bf16[512,1024]{1,0:T(8,128)(2,1)S(1)}, bf16[512,1024]{1,0:T(8,128)(2,1)}, u32[]{:S(2)}, u32[]{:S(2)}) collective-permute-start(bf16[512,1024]{1,0:T(8,128)(2,1)S(1)} %copy-done.4), channel_id=1, source_target_pairs={{0,2},{1,3},{2,0},{3,1},{4,6},{5,7},{6,4},{7,5},{8,10},{9,11},{10,... | collective-permute-start | bytes 3145736 | tf_op jit(solution)/shard_map/ppermute | solution.py:135
  91.1 17.3 %collective-permute-start.21 = (bf16[128,1024]{1,0:T(8,128)(2,1)S(1)}, bf16[128,1024]{1,0:T(8,128)(2,1)S(1)}, u32[]{:S(2)}, u32[]{:S(2)}) collective-permute-start(bf16[128,1024]{1,0:T(8,128)(2,1)S(1)} %collective-permute-done.12.refs_11_), channel_id=1, source_target_pairs={{0,4},{1,5},{2,6},{3,7},{4,0},{5,1},{6,2},{7,3},{8,12},{9,13},{10,... | collective-permute-start | bytes 786440 | tf_op jit(solution)/shard_map/ppermute | solution.py:135
  93.0 20.3 %collective-permute-start.22 = (bf16[128,1024]{1,0:T(8,128)(2,1)S(1)}, bf16[128,1024]{1,0:T(8,128)(2,1)}, u32[]{:S(2)}, u32[]{:S(2)}) collective-permute-start(bf16[128,1024]{1,0:T(8,128)(2,1)S(1)} %collective-permute-done.13.refs_13_), channel_id=1, source_target_pairs={{0,4},{1,5},{2,6},{3,7},{4,0},{5,1},{6,2},{7,3},{8,12},{9,13},{10,... | collective-permute-start | bytes 786440 | tf_op jit(solution)/shard_map/ppermute | solution.py:135
  113.3 17.0 %collective-permute-start.25 = (bf16[2,128,1024]{2,1,0:T(8,128)(2,1)S(1)}, bf16[2,128,1024]{2,1,0:T(8,128)(2,1)S(1)}, u32[]{:S(2)}, u32[]{:S(2)}) collective-permute-start(bf16[2,128,1024]{2,1,0:T(8,128)(2,1)S(1)} %collective-permute-done.10.refs_5_), channel_id=1, source_target_pairs={{0,4},{1,5},{2,6},{3,7},{4,0},{5,1},{6,2},{7,3},{8,12},{9,13},{10,... | collective-permute-start | bytes 1572872 | tf_op jit(solution)/shard_map/ppermute | solution.py:135
  115.9 12.9 %collective-permute-start.28 = (bf16[2,2,32,1024]{3,2,1,0:T(8,128)(2,1)S(1)}, bf16[2,2,32,1024]{3,2,1,0:T(8,128)(2,1)S(1)}, u32[]{:S(2)}, u32[]{:S(2)}) collective-permute-start(bf16[2,2,32,1024]{3,2,1,0:T(8,128)(2,1)S(1)} %pad_maximum_fusion.4), channel_id=1, source_target_pairs={{0,1},{1,0},{2,3},{3,2},{4,5},{5,4},{6,7},{7,6},{8,9},{9,8},{10,11... | collective-permute-start | bytes 786440 | tf_op jit(solution)/shard_map/ppermute | solution.py:135
  116.0 14.3 %collective-permute-start.27 = (bf16[128,1024]{1,0:T(8,128)(2,1)S(1)}, bf16[128,1024]{1,0:T(8,128)(2,1)S(1)}, u32[]{:S(2)}, u32[]{:S(2)}) collective-permute-start(bf16[128,1024]{1,0:T(8,128)(2,1)S(1)} %copy-done.32), channel_id=1, source_target_pairs={{0,24},{1,25},{2,26},{3,27},{4,28},{5,29},{6,30},{7,31},{8,16},{9,... | collective-permute-start | bytes 786440 | tf_op jit(solution)/shard_map/ppermute | solution.py:135
  117.5 22.0 %collective-permute-start.29 = (bf16[2,128,1024]{2,1,0:T(8,128)(2,1)S(1)}, bf16[2,128,1024]{2,1,0:T(8,128)(2,1)S(1)}, u32[]{:S(2)}, u32[]{:S(2)}) collective-permute-start(bf16[2,128,1024]{2,1,0:T(8,128)(2,1)S(1)} %collective-permute-done.24.refs_7_), channel_id=1, source_target_pairs={{0,4},{1,5},{2,6},{3,7},{4,0},{5,1},{6,2},{7,3},{8,12},{9,13},{10,... | collective-permute-start | bytes 1572872 | tf_op jit(solution)/shard_map/ppermute | solution.py:135
  130.3 13.1 %collective-permute-start.30 = (bf16[128,1024]{1,0:T(8,128)(2,1)S(1)}, bf16[128,1024]{1,0:T(8,128)(2,1)S(1)}, u32[]{:S(2)}, u32[]{:S(2)}) collective-permute-start(bf16[128,1024]{1,0:T(8,128)(2,1)S(1)} %collective-permute-done.27.refs_15_), channel_id=1, source_target_pairs={{0,4},{1,5},{2,6},{3,7},{4,0},{5,1},{6,2},{7,3},{8,12},{9,13},{10,... | collective-permute-start | bytes 786440 | tf_op jit(solution)/shard_map/ppermute | solution.py:135
  143.9 27.5 %collective-permute-start.34 = (bf16[512,1024]{1,0:T(8,128)(2,1)}, bf16[512,1024]{1,0:T(8,128)(2,1)S(1)}, u32[]{:S(2)}, u32[]{:S(2)}) collective-permute-start(bf16[512,1024]{1,0:T(8,128)(2,1)} %collective-permute-done.26.refs_19_), channel_id=1, source_target_pairs={{0,1},{1,0},{2,3},{3,2},{4,5},{5,4},{6,7},{7,6},{8,9},{9,8},{10,11... | collective-permute-start | bytes 3145736 | tf_op jit(solution)/shard_map/ppermute | solution.py:135
  143.9 27.6 %collective-permute-start.33 = (bf16[512,1024]{1,0:T(8,128)(2,1)}, bf16[512,1024]{1,0:T(8,128)(2,1)S(1)}, u32[]{:S(2)}, u32[]{:S(2)}) collective-permute-start(bf16[512,1024]{1,0:T(8,128)(2,1)} %get-tuple-element.330.refs_17_.refs_0_.refs_1_), channel_id=1, source_target_pairs={{0,2},{1,3},{2,0},{3,1},{4,6},{5,7},{6,4},{7,5},{8,10},{9,11},{10,... | collective-permute-start | bytes 3145736 | tf_op jit(solution)/shard_map/ppermute | solution.py:135
  171.7 25.5 %collective-permute-start.36 = (bf16[512,1024]{1,0:T(8,128)(2,1)}, bf16[512,1024]{1,0:T(8,128)(2,1)S(1)}, u32[]{:S(2)}, u32[]{:S(2)}) collective-permute-start(bf16[512,1024]{1,0:T(8,128)(2,1)} %get-tuple-element.345), channel_id=1, source_target_pairs={{0,1},{1,0},{2,3},{3,2},{4,5},{5,4},{6,7},{7,6},{8,9},{9,8},{10,11... | collective-permute-start | bytes 3145736 | tf_op jit(solution)/shard_map/ppermute | solution.py:135
  172.1 25.2 %collective-permute-start.37 = (bf16[512,1024]{1,0:T(8,128)(2,1)}, bf16[512,1024]{1,0:T(8,128)(2,1)S(1)}, u32[]{:S(2)}, u32[]{:S(2)}) collective-permute-start(bf16[512,1024]{1,0:T(8,128)(2,1)} %get-tuple-element.346), channel_id=1, source_target_pairs={{0,1},{1,0},{2,3},{3,2},{4,5},{5,4},{6,7},{7,6},{8,9},{9,8},{10,11... | collective-permute-start | bytes 3145736 | tf_op jit(solution)/shard_map/ppermute | solution.py:135
  197.5 26.8 %collective-permute-start.41 = (bf16[4,128,1024]{2,1,0:T(8,128)(2,1)}, bf16[4,128,1024]{2,1,0:T(8,128)(2,1)S(1)}, u32[]{:S(2)}, u32[]{:S(2)}) collective-permute-start(bf16[4,128,1024]{2,1,0:T(8,128)(2,1)} %get-tuple-element.365), channel_id=1, source_target_pairs={{0,4},{1,5},{2,6},{3,7},{4,0},{5,1},{6,2},{7,3},{8,12},{9,13},{10,... | collective-permute-start | bytes 3145736 | tf_op jit(solution)/shard_map/ppermute | solution.py:135
  201.8 22.5 %collective-permute-start.40 = (bf16[512,1024]{1,0:T(8,128)(2,1)S(1)}, bf16[512,1024]{1,0:T(8,128)(2,1)S(1)}, u32[]{:S(2)}, u32[]{:S(2)}) collective-permute-start(bf16[512,1024]{1,0:T(8,128)(2,1)S(1)} %copy-done.58), channel_id=1, source_target_pairs={{0,1},{1,0},{2,3},{3,2},{4,5},{5,4},{6,7},{7,6},{8,9},{9,8},{10,11... | collective-permute-start | bytes 3145736 | tf_op jit(solution)/shard_map/ppermute | solution.py:135
  202.0 26.5 %collective-permute-start.39 = (bf16[512,1024]{1,0:T(8,128)(2,1)S(1)}, bf16[512,1024]{1,0:T(8,128)(2,1)S(1)}, u32[]{:S(2)}, u32[]{:S(2)}) collective-permute-start(bf16[512,1024]{1,0:T(8,128)(2,1)S(1)} %add_convert_fusion.1), channel_id=1, source_target_pairs={{0,2},{1,3},{2,0},{3,1},{4,6},{5,7},{6,4},{7,5},{8,10},{9,11},{10,... | collective-permute-start | bytes 3145736 | tf_op jit(solution)/shard_map/ppermute | solution.py:135
  228.6 32.1 %collective-permute-start.43 = (bf16[512,1024]{1,0:T(8,128)(2,1)S(1)}, bf16[512,1024]{1,0:T(8,128)(2,1)S(1)}, u32[]{:S(2)}, u32[]{:S(2)}) collective-permute-start(bf16[512,1024]{1,0:T(8,128)(2,1)S(1)} %add_convert_fusion), channel_id=1, source_target_pairs={{0,2},{1,3},{2,0},{3,1},{4,6},{5,7},{6,4},{7,5},{8,10},{9,11},{10,... | collective-permute-start | bytes 3145736 | tf_op jit(solution)/shard_map/ppermute | solution.py:135
  229.3 31.4 %collective-permute-start.44 = (bf16[4,128,1024]{2,1,0:T(8,128)(2,1)S(1)}, bf16[4,128,1024]{2,1,0:T(8,128)(2,1)S(1)}, u32[]{:S(2)}, u32[]{:S(2)}) collective-permute-start(bf16[4,128,1024]{2,1,0:T(8,128)(2,1)S(1)} %copy-done.57), channel_id=1, source_target_pairs={{0,4},{1,5},{2,6},{3,7},{4,0},{5,1},{6,2},{7,3},{8,12},{9,13},{10,... | collective-permute-start | bytes 3145736 | tf_op jit(solution)/shard_map/ppermute | solution.py:135
  230.8 29.9 %collective-permute-start.45 = (bf16[1,2,128,1024]{3,2,1,0:T(8,128)(2,1)S(1)}, bf16[1,2,128,1024]{3,2,1,0:T(8,128)(2,1)S(1)}, u32[]{:S(2)}, u32[]{:S(2)}) collective-permute-start(bf16[1,2,128,1024]{3,2,1,0:T(8,128)(2,1)S(1)} %copy-done.63), channel_id=1, source_target_pairs={{0,8},{1,9},{2,10},{3,11},{4,12},{5,13},{6,14},{7,15},{8,0},{9,1},... | collective-permute-start | bytes 1572872 | tf_op jit(solution)/shard_map/ppermute | solution.py:135
  239.8 37.1 %collective-permute-start.42 = (bf16[4,128,1024]{2,1,0:T(8,128)(2,1)S(1)}, bf16[4,128,1024]{2,1,0:T(8,128)(2,1)S(1)}, u32[]{:S(2)}, u32[]{:S(2)}) collective-permute-start(bf16[4,128,1024]{2,1,0:T(8,128)(2,1)S(1)} %copy-done.55), channel_id=1, source_target_pairs={{0,4},{1,5},{2,6},{3,7},{4,0},{5,1},{6,2},{7,3},{8,12},{9,13},{10,... | collective-permute-start | bytes 3145736 | tf_op jit(solution)/shard_map/ppermute | solution.py:135
  264.6 13.4 %collective-permute-start.46 = (bf16[1,2,128,1024]{3,2,1,0:T(8,128)(2,1)}, bf16[1,2,128,1024]{3,2,1,0:T(8,128)(2,1)S(1)}, u32[]{:S(2)}, u32[]{:S(2)}) collective-permute-start(bf16[1,2,128,1024]{3,2,1,0:T(8,128)(2,1)} %near_sum.3), channel_id=1, source_target_pairs={{0,8},{1,9},{2,10},{3,11},{4,12},{5,13},{6,14},{7,15},{8,0},{9,1},... | collective-permute-start | bytes 1572872 | tf_op jit(solution)/shard_map/ppermute | solution.py:135
  289.0 29.3 %collective-permute-start.53 = (bf16[2,4,32,2048]{3,2,1,0:T(8,128)(2,1)}, bf16[2,4,32,2048]{3,2,1,0:T(8,128)(2,1)S(1)}, u32[]{:S(2)}, u32[]{:S(2)}) collective-permute-start(bf16[2,4,32,2048]{3,2,1,0:T(8,128)(2,1)} %get-tuple-element.439), channel_id=1, source_target_pairs={{0,4},{1,5},{2,6},{3,7},{4,0},{5,1},{6,2},{7,3},{8,12},{9,13},{10,... | collective-permute-start | bytes 3145736 | tf_op jit(solution)/shard_map/ppermute | solution.py:135
  290.5 27.9 %collective-permute-start.54 = (bf16[2,4,32,2048]{3,2,1,0:T(8,128)(2,1)}, bf16[2,4,32,2048]{3,2,1,0:T(8,128)(2,1)S(1)}, u32[]{:S(2)}, u32[]{:S(2)}) collective-permute-start(bf16[2,4,32,2048]{3,2,1,0:T(8,128)(2,1)} %get-tuple-element.440), channel_id=1, source_target_pairs={{0,2},{1,3},{2,0},{3,1},{4,6},{5,7},{6,4},{7,5},{8,10},{9,11},{10,... | collective-permute-start | bytes 3145736 | tf_op jit(solution)/shard_map/ppermute | solution.py:135
  291.6 23.8 %collective-permute-start.57 = (bf16[2,128,1024]{2,1,0:T(8,128)(2,1)}, bf16[2,128,1024]{2,1,0:T(8,128)(2,1)S(1)}, u32[]{:S(2)}, u32[]{:S(2)}) collective-permute-start(bf16[2,128,1024]{2,1,0:T(8,128)(2,1)} %get-tuple-element.442), channel_id=1, source_target_pairs={{0,8},{1,9},{2,10},{3,11},{4,12},{5,13},{6,14},{7,15},{8,0},{9,1},... | collective-permute-start | bytes 1572872 | tf_op jit(solution)/shard_map/ppermute | solution.py:135
  292.9 25.4 %collective-permute-start.58 = (bf16[2,128,1024]{2,1,0:T(8,128)(2,1)}, bf16[2,128,1024]{2,1,0:T(8,128)(2,1)S(1)}, u32[]{:S(2)}, u32[]{:S(2)}) collective-permute-start(bf16[2,128,1024]{2,1,0:T(8,128)(2,1)} %get-tuple-element.443), channel_id=1, source_target_pairs={{0,16},{1,17},{2,18},{3,19},{4,20},{5,21},{6,22},{7,23},{8,24},{9,... | collective-permute-start | bytes 1572872 | tf_op jit(solution)/shard_map/ppermute | solution.py:135
  325.0 14.4 %collective-permute-start.59 = (bf16[4,32,2048]{2,1,0:T(8,128)(2,1)}, bf16[4,32,2048]{2,1,0:T(8,128)(2,1)S(1)}, u32[]{:S(2)}, u32[]{:S(2)}) collective-permute-start(bf16[4,32,2048]{2,1,0:T(8,128)(2,1)} %get-tuple-element.461), channel_id=1, source_target_pairs={{0,2},{1,3},{2,0},{3,1},{4,6},{5,7},{6,4},{7,5},{8,10},{9,11},{10,... | collective-permute-start | bytes 1572872 | tf_op jit(solution)/shard_map/ppermute | solution.py:135
  326.0 13.3 %collective-permute-start.60 = (bf16[4,32,2048]{2,1,0:T(8,128)(2,1)}, bf16[4,32,2048]{2,1,0:T(8,128)(2,1)S(1)}, u32[]{:S(2)}, u32[]{:S(2)}) collective-permute-start(bf16[4,32,2048]{2,1,0:T(8,128)(2,1)} %get-tuple-element.462), channel_id=1, source_target_pairs={{0,4},{1,5},{2,6},{3,7},{4,0},{5,1},{6,2},{7,3},{8,12},{9,13},{10,... | collective-permute-start | bytes 1572872 | tf_op jit(solution)/shard_map/ppermute | solution.py:135
  326.5 12.0 %collective-permute-start.61 = (f32[8,1024]{1,0:T(8,128)S(1)}, f32[8,1024]{1,0:T(8,128)S(1)}, u32[]{:S(2)}, u32[]{:S(2)}) collective-permute-start(f32[8,1024]{1,0:T(8,128)S(1)} %add.86), channel_id=1, source_target_pairs={{0,2},{1,3},{2,0},{3,1},{4,6},{5,7},{6,4},{7,5},{8,10},{9,11},{10,... | collective-permute-start | bytes 98312 | tf_op jit(solution)/shard_map/ppermute | solution.py:135
  345.0 28.9 %collective-permute-start.67 = (bf16[3,128,1024]{2,1,0:T(8,128)(2,1)}, bf16[3,128,1024]{2,1,0:T(8,128)(2,1)S(1)}, u32[]{:S(2)}, u32[]{:S(2)}) collective-permute-start(bf16[3,128,1024]{2,1,0:T(8,128)(2,1)} %get-tuple-element.488.own_ref), channel_id=1, source_target_pairs={{0,1},{1,0},{2,3},{3,2},{4,5},{5,4},{6,7},{7,6},{8,9},{9,8},{10,11... | collective-permute-start | bytes 2359304 | tf_op jit(solution)/shard_map/ppermute | solution.py:135
  345.1 28.9 %collective-permute-start.66 = (bf16[3,128,1024]{2,1,0:T(8,128)(2,1)}, bf16[3,128,1024]{2,1,0:T(8,128)(2,1)S(1)}, u32[]{:S(2)}, u32[]{:S(2)}) collective-permute-start(bf16[3,128,1024]{2,1,0:T(8,128)(2,1)} %get-tuple-element.488.own_ref), channel_id=1, source_target_pairs={{0,2},{1,3},{2,0},{3,1},{4,6},{5,7},{6,4},{7,5},{8,10},{9,11},{10,... | collective-permute-start | bytes 2359304 | tf_op jit(solution)/shard_map/ppermute | solution.py:135
  346.1 12.7 %collective-permute-start.63 = (bf16[32,4224]{1,0:T(8,128)(2,1)}, bf16[32,4224]{1,0:T(8,128)(2,1)S(1)}, u32[]{:S(2)}, u32[]{:S(2)}) collective-permute-start(bf16[32,4224]{1,0:T(8,128)(2,1)} %get-tuple-element.477), channel_id=1, source_target_pairs={{0,8},{1,9},{2,10},{3,11},{4,12},{5,13},{6,14},{7,15},{8,0},{9,1},... | collective-permute-start | bytes 811016 | tf_op jit(solution)/shard_map/ppermute | solution.py:135
  347.2 20.8 %collective-permute-start.64 = (bf16[32,4224]{1,0:T(8,128)(2,1)}, bf16[32,4224]{1,0:T(8,128)(2,1)S(1)}, u32[]{:S(2)}, u32[]{:S(2)}) collective-permute-start(bf16[32,4224]{1,0:T(8,128)(2,1)} %get-tuple-element.478), channel_id=1, source_target_pairs={{0,16},{1,17},{2,18},{3,19},{4,20},{5,21},{6,22},{7,23},{8,24},{9,... | collective-permute-start | bytes 811016 | tf_op jit(solution)/shard_map/ppermute | solution.py:135
  349.2 24.7 %collective-permute-start.65 = (bf16[32,4224]{1,0:T(8,128)(2,1)}, bf16[32,4224]{1,0:T(8,128)(2,1)S(1)}, u32[]{:S(2)}, u32[]{:S(2)}) collective-permute-start(bf16[32,4224]{1,0:T(8,128)(2,1)} %get-tuple-element.479), channel_id=1, source_target_pairs={{0,24},{1,25},{2,26},{3,27},{4,28},{5,29},{6,30},{7,31},{8,16},{9,... | collective-permute-start | bytes 811016 | tf_op jit(solution)/shard_map/ppermute | solution.py:135
  (96 other events, 939.2 us)

commit v4 on v3

--- a/solution.py
+++ b/solution.py
@@ -147,7 +147,10 @@
     "nt": (((1,), (1,)), ((), ())),
     "tn": (((0,), (0,)), ((), ())),
 }
-BIG = pltpu.CompilerParams(vmem_limit_bytes=56 << 20)
+
+
+def vmem_of(mib):
+    return pltpu.CompilerParams(vmem_limit_bytes=mib << 20)
 
 
 def work(flops):
@@ -196,8 +199,7 @@
     ((0, 0, 0), (1, 0, 0), (2, 0, 0), (3, 0, 0)),
     ((0, 1, 0), (1, 1, 0), (2, 1, 0), (3, 1, 0)),
     ((0, 0, 1), (1, 0, 1), (2, 0, 1), (3, 0, 1)),
-    ((0, 1, 1), (1, 1, 1), (2, 1, 1)),
-    ((3, 1, 1),),
+    ((0, 1, 1), (1, 1, 1), (2, 1, 1), (3, 1, 1)),
 )
 
 
@@ -261,7 +263,7 @@
         save().wait()
 
 
-def project(idx, own, came, x, cosine, signed_sine, block=512):
+def project(idx, own, came, x, cosine, signed_sine, block=1024):
     rows, width = x.shape
     cols = own[0].shape[-1]
     return pl.pallas_call(
@@ -285,7 +287,7 @@
             pltpu.SemaphoreType.DMA((32,)),
             pltpu.SemaphoreType.DMA,
         ],
-        compiler_params=BIG,
+        compiler_params=vmem_of(28),
         cost_estimate=work(1e9),
         name="project",
     )(idx, *own, *came, x, cosine, signed_sine)
@@ -334,7 +336,7 @@
         in_specs=[row, pl.BlockSpec((width, width), lambda i: (0, 3)), row, whole((8, width))],
         out_specs=[row, row],
         out_shape=[sds((rows, width), F32), sds((rows, width), BF)],
-        compiler_params=BIG,
+        compiler_params=vmem_of(20),
         cost_estimate=work(1e9),
         name="leave",
     )(attended, w_attn, x, vecs)
@@ -371,7 +373,7 @@
         + [whole((8, width)), pl.BlockSpec((width, width), lambda i: (0, 3))],
         out_specs=[row, row, row, whole((8, width))],
         out_shape=[sds((rows, width), F32)] + [sds((rows, width), BF)] * 2 + [sds((8, width), F32)],
-        compiler_params=BIG,
+        compiler_params=vmem_of(28),
         cost_estimate=work(1e9),
         name="back",
     )(*parts, grad_out, branch, x, vecs, w_attn)
@@ -410,7 +412,7 @@
         + [whole((8, width))],
         out_specs=[row, row, whole((8, width))],
         out_shape=[sds((rows, width), F32), sds((rows, width), BF), sds((8, width), F32)],
-        compiler_params=BIG,
+        compiler_params=vmem_of(36),
         cost_estimate=work(1e9),
         name="last",
     )(*grads, w_attn, w_attn, w_attn, x, vecs, grad_middle, *mlp_parts, grad_out, branch, mid_sums)
@@ -420,13 +422,14 @@
     for b in range(rows // WINDOW):
         keys = WINDOW if b == 0 else 2 * WINDOW
         offset = (
-            lax.broadcasted_iota(jnp.int32, (WINDOW, keys), 0)
-            - lax.broadcasted_iota(jnp.int32, (WINDOW, keys), 1)
+            lax.broadcasted_iota(jnp.int32, (keys, WINDOW), 1)
+            - lax.broadcasted_iota(jnp.int32, (keys, WINDOW), 0)
             + (keys - WINDOW)
         )
-        reach = jnp.minimum(pos_ref[b * WINDOW : (b + 1) * WINDOW, :], WINDOW - 1)
-        seen = (offset >= 0) & (offset <= reach)
-        bias_ref[b, :, 2 * WINDOW - keys :] = jnp.where(seen, 0.0, -1e30)
+        reach = jnp.minimum(pos_ref[:, b * WINDOW : (b + 1) * WINDOW], WINDOW - 1)
+        bias = jnp.where((offset >= 0) & (offset <= reach), 0.0, -1e30)
+        bias_ref[b, 2 * WINDOW - keys :, :WINDOW] = bias
+        bias_ref[b, 2 * WINDOW - keys :, WINDOW:] = bias
 
 
 def split_heads(u, low):
@@ -436,9 +439,9 @@
 
 def pair_probs(q, k, bias, low):
     q = split_heads(q, low) * jnp.asarray(0.125, BF)
-    scores = dot(q, k, "nt") + jnp.concatenate([bias, bias], axis=0)
-    e = jnp.exp(scores - jnp.max(scores, axis=1, keepdims=True))
-    return q, e * (1.0 / jnp.sum(e, axis=1, keepdims=True))
+    scores = dot(k, q, "nt") + bias
+    e = jnp.exp(scores - jnp.max(scores, axis=0, keepdims=True))
+    return q, e * (1.0 / jnp.sum(e, axis=0, keepdims=True))
 
 
 def attend_kernel(q_ref, k_ref, v_ref, pos_ref, o_ref, bias_ref):
@@ -449,27 +452,29 @@
         set_bias(bias_ref, pos_ref, rows)
 
     low = lax.broadcasted_iota(jnp.int32, (1, 128), 1) < 64
-    for b in range(rows // WINDOW):
-        here = slice(b * WINDOW, (b + 1) * WINDOW)
-        keys = slice(max(b - 1, 0) * WINDOW, (b + 1) * WINDOW)
-        bias = bias_ref[b, :, 2 * WINDOW - (keys.stop - keys.start) :]
-        _, probs = pair_probs(q_ref[here, :], k_ref[keys, :], bias, low)
-        out = dot(probs.astype(BF), v_ref[keys, :])
-        o_ref[here, :] = jnp.where(low, out[:WINDOW], out[WINDOW:]).astype(BF)
-
-
-def attend(qkv, position):
+    for c in range(0, q_ref.shape[1], 128):
+        pair = slice(c, c + 128)
+        for b in range(rows // WINDOW):
+            here = slice(b * WINDOW, (b + 1) * WINDOW)
+            keys = slice(max(b - 1, 0) * WINDOW, (b + 1) * WINDOW)
+            bias = bias_ref[b, 2 * WINDOW - (keys.stop - keys.start) :, :]
+            _, probs = pair_probs(q_ref[here, pair], k_ref[keys, pair], bias, low)
+            out = dot(probs.astype(BF), v_ref[keys, pair], "tn")
+            o_ref[here, pair] = jnp.where(low, out[:WINDOW], out[WINDOW:]).astype(BF)
+
+
+def attend(qkv, position, pairs=4):
     rows, width = qkv.shape[0], qkv.shape[1] // 3
-    pairs = width // 128
-    cols = lambda part: pl.BlockSpec((rows, 128), lambda j: (0, j + part * pairs))
+    steps = width // 128 // pairs
+    cols = lambda part: pl.BlockSpec((rows, 128 * pairs), lambda j: (0, j + part * steps))
     return pl.pallas_call(
         attend_kernel,
-        grid=(pairs,),
-        in_specs=[cols(0), cols(1), cols(2), whole((rows, 1))],
+        grid=(steps,),
+        in_specs=[cols(0), cols(1), cols(2), whole((1, rows))],
         out_specs=cols(0),
         out_shape=sds((rows, width), BF),
-        scratch_shapes=[pltpu.VMEM((rows // WINDOW, WINDOW, 2 * WINDOW), F32)],
-        compiler_params=BIG,
+        scratch_shapes=[pltpu.VMEM((rows // WINDOW, 2 * WINDOW, 2 * WINDOW), F32)],
+        compiler_params=vmem_of(16),
         cost_estimate=work(1e9),
         name="attend",
     )(qkv, qkv, qkv, position)
@@ -491,42 +496,45 @@
     def turn_back(u, here):
         return rotate_lanes(u, cos_ref[here, :], -sin_ref[here, :], first).astype(BF)
 
-    dk, dv = [None] * blocks, [None] * blocks
-    for b in range(blocks):
-        here = slice(b * WINDOW, (b + 1) * WINDOW)
-        keys = slice(max(b - 1, 0) * WINDOW, (b + 1) * WINDOW)
-        bias = bias_ref[b, :, 2 * WINDOW - (keys.stop - keys.start) :]
-        q, probs = pair_probs(q_ref[here, :], k_ref[keys, :], bias, low)
-        do = split_heads(do_ref[here, :], low)
-        dp = dot(do, v_ref[keys, :], "nt")
-        delta = jnp.sum(probs * dp, axis=1, keepdims=True)
-        ds = (probs * (dp - delta)).astype(BF)
-        dq = dot(ds, k_ref[keys, :]) * 0.125
-        dq_ref[here, :] = turn_back(jnp.where(low, dq[:WINDOW], dq[WINDOW:]), here)
-        k_part = dot(ds, q, "tn")
-        v_part = dot(probs.astype(BF), do, "tn")
-        for i, kb in enumerate(range(max(b - 1, 0), b + 1)):
-            part = slice(i * WINDOW, (i + 1) * WINDOW)
-            dk[kb] = k_part[part] if dk[kb] is None else dk[kb] + k_part[part]
-            dv[kb] = v_part[part] if dv[kb] is None else dv[kb] + v_part[part]
-    for kb in range(blocks):
-        here = slice(kb * WINDOW, (kb + 1) * WINDOW)
-        dk_ref[here, :] = turn_back(dk[kb], here)
-        dv_ref[here, :] = dv[kb].astype(BF)
-
-
-def attend_back(qkv, grad, position, cosine, signed_sine):
+    for c in range(0, q_ref.shape[1], 128):
+        pair = slice(c, c + 128)
+        dk, dv = [None] * blocks, [None] * blocks
+        for b in range(blocks):
+            here = slice(b * WINDOW, (b + 1) * WINDOW)
+            keys = slice(max(b - 1, 0) * WINDOW, (b + 1) * WINDOW)
+            bias = bias_ref[b, 2 * WINDOW - (keys.stop - keys.start) :, :]
+            k = k_ref[keys, pair]
+            q, probs = pair_probs(q_ref[here, pair], k, bias, low)
+            do = split_heads(do_ref[here, pair], low)
+            dp = dot(v_ref[keys, pair], do, "nt")
+            delta = jnp.sum(probs * dp, axis=0, keepdims=True)
+            ds = (probs * (dp - delta)).astype(BF)
+            dq = dot(ds, k, "tn") * 0.125
+            dq_ref[here, pair] = turn_back(jnp.where(low, dq[:WINDOW], dq[WINDOW:]), here)
+            k_part = dot(ds, q)
+            v_part = dot(probs.astype(BF), do)
+            for i, kb in enumerate(range(max(b - 1, 0), b + 1)):
+                part = slice(i * WINDOW, (i + 1) * WINDOW)
+                dk[kb] = k_part[part] if dk[kb] is None else dk[kb] + k_part[part]
+                dv[kb] = v_part[part] if dv[kb] is None else dv[kb] + v_part[part]
+        for kb in range(blocks):
+            here = slice(kb * WINDOW, (kb + 1) * WINDOW)
+            dk_ref[here, pair] = turn_back(dk[kb], here)
+            dv_ref[here, pair] = dv[kb].astype(BF)
+
+
+def attend_back(qkv, grad, position, cosine, signed_sine, pairs=2):
     rows, width = qkv.shape[0], qkv.shape[1] // 3
-    pairs = width // 128
-    cols = lambda part: pl.BlockSpec((rows, 128), lambda j: (0, j + part * pairs))
+    steps = width // 128 // pairs
+    cols = lambda part: pl.BlockSpec((rows, 128 * pairs), lambda j: (0, j + part * steps))
     return pl.pallas_call(
         attend_back_kernel,
-        grid=(pairs,),
-        in_specs=[cols(0), cols(1), cols(2), cols(0), whole((rows, 1))] + [whole((rows, 128))] * 2,
+        grid=(steps,),
+        in_specs=[cols(0), cols(1), cols(2), cols(0), whole((1, rows))] + [whole((rows, 128))] * 2,
         out_specs=[cols(0)] * 3,
         out_shape=[sds((rows, width), BF)] * 3,
-        scratch_shapes=[pltpu.VMEM((rows // WINDOW, WINDOW, 2 * WINDOW), F32)],
-        compiler_params=BIG,
+        scratch_shapes=[pltpu.VMEM((rows // WINDOW, 2 * WINDOW, 2 * WINDOW), F32)],
+        compiler_params=vmem_of(20),
         cost_estimate=work(1e9),
         name="attend_back",
     )(qkv, qkv, qkv, grad, position, cosine, signed_sine)
@@ -673,7 +681,7 @@
             pltpu.SemaphoreType.DMA((5,)),
             pltpu.SemaphoreType.DMA((14,)),
         ],
-        compiler_params=BIG,
+        compiler_params=vmem_of(46),
         cost_estimate=work(1e9),
         name="mlp_both",
     )(*args)
@@ -725,38 +733,33 @@
             ],
         ),
         out_shape=[sds(split, BF)] * 2,
-        compiler_params=BIG,
+        compiler_params=vmem_of(22),
         cost_estimate=work(1e9),
         name="weight_grad",
     )(idx, *[p for p in a_parts for _ in range(2)], *b_parts)
 
 
 def attn_grad_kernel(idx, q_in, o_in, dq, dk, dv, do, *refs):
-    outs, totals, sems = refs[:10], refs[10:12], refs[12]
+    outs, total = refs[:10], refs[10]
     core = idx[3]
     half = dq.shape[1]
-    copies = []
     for n, parts in enumerate((((q_in, dq), (q_in, dk)), ((q_in, dv), (o_in, do)))):
-        side, total = idx[1 + n], totals[n]
+        side = idx[1 + n]
         for c, (a, b) in enumerate(parts):
+            cols = slice(c * half, (c + 1) * half)
             product = dot(a[...], b[...], "tn").astype(BF)
-            total[:, :, :, :, :, c * half : (c + 1) * half] = product.reshape(4, 2, 2, 2, 32, half)
-        for m in range(5):
-            to_core = (1 - core) if m < 3 else core
-            to_side = (1 - side) if m in (0, 1, 3) else side
-            cols = pl.ds(m * half, half) if m < 2 else pl.ds(0, 2 * half)
-            for other in range(2):
-                for k in range(4):
-                    x, y = (to_side, other) if n == 0 else (other, to_side)
-                    copy = pltpu.make_async_copy(
-                        total.at[k, x, y, to_core, :, cols],
-                        outs[5 * n + m].at[other, k],
-                        sems.at[len(copies)],
-                    )
-                    copy.start()
-                    copies.append(copy)
-    for copy in copies:
-        copy.wait()
+            total[:, :, :, :, :, cols] = product.reshape(4, 2, 2, 2, 32, half)
+            for m in (c, 2, 3, 4):
+                to_core = (1 - core) if m < 3 else core
+                to_side = (1 - side) if m in (0, 1, 3) else side
+                for other in range(2):
+                    for k in range(4):
+                        x, y = (to_side, other) if n == 0 else (other, to_side)
+                        block = total[k, x, y, to_core, :, cols]
+                        if m < 2:
+                            outs[5 * n + m][other, k] = block
+                        else:
+                            outs[5 * n + m][other, k, :, cols] = block
 
 
 def attn_grad(idx, q_in, o_in, dq, dk, dv, do):
@@ -766,11 +769,10 @@
     return pl.pallas_call(
         attn_grad_kernel,
         in_specs=[SMEM] + [vmem] * 6,
-        out_specs=[ANY] * 10,
+        out_specs=[vmem] * 10,
         out_shape=[one, one, two, two, two] * 2,
-        scratch_shapes=[pltpu.VMEM((4, 2, 2, 2, 32, 2 * width), BF)] * 2
-        + [pltpu.SemaphoreType.DMA((80,))],
-        compiler_params=BIG,
+        scratch_shapes=[pltpu.VMEM((4, 2, 2, 2, 32, 2 * width), BF)],
+        compiler_params=vmem_of(30),
         cost_estimate=work(1e9),
         name="attn_grad",
     )(idx, q_in, o_in, dq, dk, dv, do)
@@ -836,7 +838,7 @@
         out_specs=pl.BlockSpec(memory_space=pltpu.VMEM),
         out_shape=sds((n, 2) + block, BF),
         scratch_shapes=z_scratch([("near", n)], block),
-        compiler_params=BIG,
+        compiler_params=vmem_of(10),
         cost_estimate=work(1e9),
         name="near_sum",
     )(idx, *[p for pair in pairs for p in pair])
@@ -871,7 +873,7 @@
         out_specs=[vmem] * 4,
         out_shape=[shape, shape, sds((2,) + block, BF), sds((2,) + block, BF)],
         scratch_shapes=z_scratch([("far", 2), ("near", 1)], block),
-        compiler_params=BIG,
+        compiler_params=vmem_of(22),
         cost_estimate=work(1e9),
         name="first_sum",
     )(idx, *parts, near, *[p for pair in pairs for p in pair])
@@ -908,7 +910,7 @@
             copy.start()
 
     for p0, p1, p2, out in ((a0, a1, a2, a_stay), (b0, b1, b2, b_stay)):
-        out[...] = p0[...].astype(F32) + p1[...].astype(F32) + p2[...].astype(F32)
+        out[...] = (p0[...].astype(F32) + p1[...].astype(F32) + p2[...].astype(F32)).astype(BF)
 
     @pl.when(i == pl.num_programs(0) - 1)
     def _():
@@ -918,7 +920,7 @@
             own[m] = z_add(buf, 2 * m, near[m, idx[0] // 2], far[m])
 
 
-def half_sum(kernel, idx, parts, away, more, pairs, outs, jobs, dtype, name):
+def half_sum(kernel, idx, parts, away, more, pairs, outs, jobs, mib, name):
     _, blocks, rows, cols = parts[0].shape
     block = pairs[0][0].shape[1:]
     side = lambda at: pl.BlockSpec(
@@ -938,8 +940,8 @@
             + [pl.BlockSpec(shape, lambda i, s, n=len(shape): (0,) * n) for shape in outs],
             scratch_shapes=z_scratch(jobs, block),
         ),
-        out_shape=[sds((blocks, rows, cols), dtype)] * 2 + [sds(shape, BF) for shape in outs],
-        compiler_params=BIG,
+        out_shape=[sds((blocks, rows, cols), BF)] * 2 + [sds(shape, BF) for shape in outs],
+        compiler_params=vmem_of(mib),
         cost_estimate=work(1e9),
         name=name,
     )(idx, *parts, *more, *[p for pair in pairs for p in pair])
@@ -948,13 +950,13 @@
 def second_sum(idx, parts, gate_near, pair):
     block = gate_near.shape[1:]
     return half_sum(
-        second_sum_kernel, idx, parts, True, [gate_near], [pair], [block], [("far", 1)], BF, "second_sum"
+        second_sum_kernel, idx, parts, True, [gate_near], [pair], [block], [("far", 1)], 14, "second_sum"
     )
 
 
 def stay_sum(idx, parts, near, far, pairs):
     return half_sum(
-        stay_sum_kernel, idx, parts, False, [near, far], pairs, [far.shape], [("total", 2)], F32, "stay_sum"
+        stay_sum_kernel, idx, parts, False, [near, far], pairs, [far.shape], [("total", 2)], 56, "stay_sum"
     )
 
 
@@ -987,7 +989,7 @@
         out_specs=[vmem] * 5,
         out_shape=[sds((3,) + block, BF), sds((rows, cols), F32)] + [sds((rows, cols), BF)] * 3,
         scratch_shapes=z_scratch([("total", 1)], block),
-        compiler_params=BIG,
+        compiler_params=vmem_of(16),
         cost_estimate=work(1e9),
         name="third_sum",
     )(idx, a_stay, a_y, b_stay, b_x, small, own, gate_near, gate_far, *pair)
@@ -1023,7 +1025,7 @@
         out_specs=[vmem] * (len(widths) + n_small),
         out_shape=[sds((4, rows, w), F32) for w in widths] + [sds((1, 4 * rows), F32)] * n_small,
         scratch_shapes=[pltpu.VMEM((4 * rows, 128), F32)] if n_small else [],
-        compiler_params=BIG,
+        compiler_params=vmem_of(16),
         cost_estimate=work(1e9),
         name="place_rows",
     )(idx, own, other_y, other_core, other_both)
@@ -1051,7 +1053,7 @@
         in_specs=[SMEM] + [vmem] * 4,
         out_specs=[vmem] * 3,
         out_shape=[sds((4, rows, cols), F32)] + [sds((rows, 4 * cols), F32)] * 2,
-        compiler_params=BIG,
+        compiler_params=vmem_of(16),
         cost_estimate=work(1e9),
         name="place_mlp",
     )(idx, own, other_y, other_core, other_both)
@@ -1075,7 +1077,7 @@
         in_specs=[SMEM, vmem],
         out_specs=[vmem] * 2,
         out_shape=[sds((2, 2, rows, ff // 4), BF)] * 2,
-        compiler_params=BIG,
+        compiler_params=vmem_of(8),
         cost_estimate=work(1e9),
         name="share",
     )(idx, raw)
@@ -1098,7 +1100,7 @@
         in_specs=[SMEM] + [vmem] * 3,
         out_specs=vmem,
         out_shape=sds((2, 4 * rows, part), BF),
-        compiler_params=BIG,
+        compiler_params=vmem_of(8),
         cost_estimate=work(1e9),
         name="join",
     )(idx, own, other_y, other_core)
@@ -1149,7 +1151,7 @@
 
         segment, position = clip_layout(lengths[0], count)
         cosine, sine = lane_tables(position, head_width)
-        position = position[:, None]
+        position = position[None, :]
 
         share_core = swap(jnp.stack([share_here[1], share_y[1]]), "core")
         gu0 = join(idx, share_here, share_y, share_core)
@@ -1161,42 +1163,38 @@
         near = jnp.concatenate([bundle] + from_z)
         near, gu0, share_here, share_there = window(near, gu0, share_here, share_there)
         far_x, far_y = swap(near, "x"), swap(near, "y")
-        gu1, gu2 = swap(gu0, "z1"), swap(gu0, "z2")
-        share_y = swap(share_there, "y")
-        far_x, far_y, gu1, gu2, share_y, share_here, w_down = window(
-            far_x, far_y, gu1, gu2, share_y, share_here, w_down
-        )
-        by_y, by_x, w_down, near = window(far_x[:3], far_y[3:], w_down, near)
-        both_y, both_x = swap(by_y, "y"), swap(by_x, "x")
-        dn1, dn2 = swap(w_down, "z1"), swap(w_down, "z2")
-        came_near = swap(near, "core")
-
-        have = [near, far_x, far_y, both_y, both_x]
-        gu0, gu1, gu2, dn1, dn2, grad_out, came_near, *have = window(
-            gu0, gu1, gu2, dn1, dn2, grad_out, came_near, *have
+        gu1, dn1, dn2 = swap(gu0, "z1"), swap(w_down, "z1"), swap(w_down, "z2")
+
+        far_x, far_y, gu0, gu1, dn1, dn2, near = window(far_x, far_y, gu0, gu1, dn1, dn2, near)
+        both, came_near = swap(far_x, "y"), swap(near, "core")
+        gu2, gux1, dnx1 = swap(gu0, "z2"), swap(gu1, "x"), swap(dn1, "x")
+
+        have = [near, far_x, far_y, both]
+        gu0, gu2, gux1, dnx1, dn2, grad_out, came_near, *have = window(
+            gu0, gu2, gux1, dnx1, dn2, grad_out, came_near, *have
         )
         came = [came_near] + [swap(p, "core") for p in have[1:]]
         gu3, go_y = swap(gu0, "z3"), swap(grad_out, "y")
-        gux1, dnx1, dnx2 = swap(gu1, "x"), swap(dn1, "x"), swap(dn2, "x")
+        gux2, dnx2 = swap(gu2, "x"), swap(dn2, "x")
         *came, cosine, sine, position = window(*came, cosine, sine, position)
 
         qkv, normed, w_attn, vecs = project(idx, have, came, inputs, cosine, sine)
-        qkv, gu2, dnx1, dnx2, gux1, gu3, w_down, share_here, share_y = window(
-            qkv, gu2, dnx1, dnx2, gux1, gu3, w_down, share_here, share_y
+        qkv, gux2, dnx2, gu3, w_down, share_there = window(
+            qkv, gux2, dnx2, gu3, w_down, share_there
+        )
+        gux3, dn3, share_y = swap(gu3, "x"), swap(w_down, "z3"), swap(share_there, "y")
+        attended = attend(qkv, position)
+        attended, go_y, gux3, dn3, share_y, share_here, grad_out = window(
+            attended, go_y, gux3, dn3, share_y, share_here, grad_out
         )
         share_core = swap(jnp.stack([share_here[1], share_y[1]]), "core")
-        gux2, dn3 = swap(gu2, "x"), swap(w_down, "z3")
-        gux3 = swap(gu3, "x")
-        attended = attend(qkv, position)
-        attended, gux2, go_y, dn3, share_core = window(attended, gux2, go_y, dn3, share_core)
         gux0 = join(idx, share_here, share_y, share_core)
-        dnx3 = swap(dn3, "x")
+        dnx3, go_core = swap(dn3, "x"), swap(grad_out, "core")
         branch, n_own = leave(attended, w_attn, inputs, vecs)
-        n_own, gux0, gux3, dnx3, grad_out, go_y = window(n_own, gux0, gux3, dnx3, grad_out, go_y)
+        n_own, gux0, dnx3, go_core, go_y = window(n_own, gux0, dnx3, go_core, go_y)
 
         n_y, n_core = swap(n_own, "y"), swap(n_own, "core")
-        go_core = swap(grad_out, "core")
-        n_core, go_core = window(n_core, go_core)
+        n_core, go_y = window(n_core, go_y)
         go_yc = swap(go_y, "core")
         pieces = (gu0, gux0, gu1, gux1, gu2, gux2, gu3, gux3)
         downs = (w_down, dnx0, dn1, dnx1, dn2, dnx2, dn3, dnx3)
@@ -1222,11 +1220,10 @@
         up_send, up_keep = weight_grad(idx, n_all, (gu_a, gu_b))
         gate_send, gate_keep = weight_grad(idx, n_all, (after(gg_a, up_send), gg_b))
         gate_send, up_send, mlp_yc, down_x = window(gate_send, up_send, mlp_yc, down_x)
+        up_x = swap(up_send, "x")
         down_near = near_sum(idx, [(down_keep, down_x)])
-        gn_y, mlp_send, up_send, down_near = window(
-            gn_y, add(mlp_y, mlp_yc), up_send, down_near
-        )
-        up_x, mlp_y, down_near = swap(up_send, "x"), swap(mlp_send, "y"), swap(down_near, "z1")
+        gn_y, mlp_send, down_near = window(gn_y, add(mlp_y, mlp_yc), down_near)
+        mlp_y, down_near = swap(mlp_send, "y"), swap(down_near, "z1")
 
         grad_middle, grad_branch, grad_attended, mid_sums = back(
             (gn_own, gn_core, gn_y), grad_out, branch, inputs, vecs, w_attn
@@ -1235,11 +1232,11 @@
         gate_x = swap(gate_send, "x")
 
         dq, dk, dv = attend_back(qkv, grad_attended, position, cosine, sine)
-        dq, mlp_y, up_x, down_near = window(dq, mlp_y, up_x, down_near)
+        dq, up_x, down_near = window(dq, up_x, down_near)
         up_near, dq = window(near_sum(idx, [(up_keep, up_x)]), dq)
         up_near = swap(up_near, "z1")
         grads = attn_grad(idx, normed, attended, dq, dk, dv, grad_branch)
-        gate_x, up_near, *grads = window(gate_x, up_near, *grads)
+        gate_x, up_near, mlp_y, *grads = window(gate_x, up_near, mlp_y, *grads)
         near = jnp.concatenate([down_near, up_near])
         pairs = [(down_keep, down_x), (up_keep, up_x), (gate_keep, gate_x)]
         q_send, k_send, a_send, a_keep, a_keep_here = grads[:5]

time: 397 us -> 356 us (0.90)
  Pallas kernels: 189 us -> 133 us
  waiting for transfers between devices: 108 us -> 134 us
  other arithmetic: 11.3 us -> 4.78 us
  starting transfers between devices: 63 us -> 56.9 us
    ppermute x72 -> x70, waiting for transfers between devices: 108 us -> 134 us  [swap(): return lax.ppermute(value, AXES, pairs)]
    pallas_call x2, Pallas kernels: 30.9 us -> 19.4 us  [the longest x1 14.9 us: attend_back(): pl.pallas_call(attend_back_kernel, grid=(steps,), in_specs=[cols(0), cols...]
    ppermute x72 -> x70, starting transfers between devices: 63 us -> 56.9 us  [swap(): return lax.ppermute(value, AXES, pairs)]
    pallas_call x2, Pallas kernels: 20.6 us -> 14.9 us  [weight_grad(): pl.pallas_call(weight_grad_kernel, grid_spec=pltpu.PrefetchScalarGridSpec...]
    unnamed x143 -> x179, local copies, waits for them, and re-layouts: 13.1 us -> 18.7 us
    pallas_call x2, Pallas kernels: 5.61 us -> 1.57 us  [near_sum(): pl.pallas_call(lambda *refs: near_sum_kernel(n, *refs), in_specs=[SMEM] +...]
  transfers between devices with their start and end apart: 72 -> 70, of which waited for: 31 -> 40; matrix products, arithmetic and copies ran while one was open for 3% -> 1% of each run, Pallas kernels for 45% -> 36%
where the time goes in v4:
time: 356 us; the launch traced here: 351 us
  waiting for transfers between devices  134 us (38%)
  Pallas kernels  133 us (37%)
  starting transfers between devices  56.9 us (16%)
  local copies, waits for them, and re-layouts  19.7 us (6%)
  other arithmetic  4.78 us (1%)
    ppermute x70, waiting for transfers between devices, swap(): return lax.ppermute(value, AXES, pairs)  134 us
    ppermute x70, starting transfers between devices, swap(): return lax.ppermute(value, AXES, pairs)  56.9 us
    pallas_call x2, Pallas kernels, mlp_both(): pl.pallas_call(lambda *refs: mlp_kernel(last_half, *refs), in_specs=in_sp...  40 us
    unnamed x179, local copies, waits for them, and re-layouts  18.7 us
    pallas_call x1, Pallas kernels, attend_back(): pl.pallas_call(attend_back_kernel, grid=(steps,), in_specs=[cols(0), cols...  14.9 us
    pallas_call x2, Pallas kernels, weight_grad(): pl.pallas_call(weight_grad_kernel, grid_spec=pltpu.PrefetchScalarGridSpec...  14.9 us
    pallas_call x1, Pallas kernels, last(): pl.pallas_call(last_kernel, grid=(rows // block,), in_specs=[row] * 3 + c...  11.5 us
    pallas_call x1, Pallas kernels, project(): pl.pallas_call(project_kernel, grid=(3 * width // block,), in_specs=[SMEM...  10.7 us
  transfers between devices with their start and end apart: 70, of which 40 were waited for; matrix products, arithmetic and copies ran while one was open for 1% of the time, Pallas kernels for 36%

profile of v4, /device:TPU:10, one launch (start us, length us, event | category | flops | bytes accessed | tf_op | source)
XLA Modules:
  0.0 350.6 jit_solution(6123513036137132322)
XLA Ops:
  2.5 1.6 collective-permute-start.2
  9.1 1.6 collective-permute-start.3
  11.1 5.3 %collective-permute-done.3.y_ref = bf16[2,2,32,1024]{3,2,1,0:T(8,128)(2,1)S(1)} collective-permute-done((bf16[2,2,32,1024]{3,2,1,0:T(8,128)(2,1)S(1)}, bf16[2,2,32,1024]{3,2,1,0:T(8,128)(2,1)S(1)}, u32[]{:S(2)}, u32[]{:S(2)}) %collective-permute-start.3) | collective-permute-done | bytes 262176 | tf_op jit(solution)/shard_map/ppermute | solution.py:135
  22.3 4.2 %collective-permute-done.5.refs_10_ = bf16[128,1024]{1,0:T(8,128)(2,1)S(1)} collective-permute-done((bf16[128,1024]{1,0:T(8,128)(2,1)S(1)}, bf16[128,1024]{1,0:T(8,128)(2,1)S(1)}, u32[]{:S(2)}, u32[]{:S(2)}) %collective-permute-start.5) | collective-permute-done | bytes 262176 | tf_op jit(solution)/shard_map/ppermute | solution.py:135
  29.6 2.3 collective-permute-start.9
  32.0 3.0 collective-permute-start.11
  35.0 18.1 %collective-permute-done.10.refs_11_ = bf16[128,1024]{1,0:T(8,128)(2,1)S(1)} collective-permute-done((bf16[128,1024]{1,0:T(8,128)(2,1)S(1)}, bf16[128,1024]{1,0:T(8,128)(2,1)S(1)}, u32[]{:S(2)}, u32[]{:S(2)}) %collective-permute-start.10) | collective-permute-done | bytes 262176 | tf_op jit(solution)/shard_map/ppermute | solution.py:135
  55.3 2.0 collective-permute-start.12
  60.1 16.7 %collective-permute-done.14.refs_12_ = bf16[128,1024]{1,0:T(8,128)(2,1)S(1)} collective-permute-done((bf16[128,1024]{1,0:T(8,128)(2,1)S(1)}, bf16[128,1024]{1,0:T(8,128)(2,1)S(1)}, u32[]{:S(2)}, u32[]{:S(2)}) %collective-permute-start.14) | collective-permute-done | bytes 262176 | tf_op jit(solution)/shard_map/ppermute | solution.py:135
  77.5 2.2 collective-permute-done.12.refs_5_
  87.5 10.7 %project.1 = (bf16[512,3072]{1,0:T(8,128)(2,1)S(1)}, bf16[512,1024]{1,0:T(8,128)(2,1)S(1)}, bf16[1024,4224]{1,0:T(8,128)(2,1)S(1)}, f32[8,1024]{1,0:T(8,128)S(1)}) custom-call(s32[4]{0:T(128)S(1)} %pad_add_fusion.idx.refs_0_, bf16[4,32,4224]{2,1,0:T(8,128)(2,1)S(1)} %pad_maximum_fusion.refs_1_, bf16[4,32,4224]{2,1,0:T(8,128)(2,1)S(1)} %collective-permute-done.7.refs_2_, ...), custom_call_target="tpu_custom_call" | custom-call | flops 1000000000 | tf_op jit(solution)/shard_map/project/pallas_call | solution.py:269
  99.2 2.7 collective-permute-done.21.refs_14_
  101.9 5.3 %collective-permute-done.22.refs_7_ = bf16[2,128,1024]{2,1,0:T(8,128)(2,1)S(1)} collective-permute-done((bf16[2,128,1024]{2,1,0:T(8,128)(2,1)S(1)}, bf16[2,128,1024]{2,1,0:T(8,128)(2,1)S(1)}, u32[]{:S(2)}, u32[]{:S(2)}) %collective-permute-start.22) | collective-permute-done | bytes 524320 | tf_op jit(solution)/shard_map/ppermute | solution.py:135
  109.8 4.5 %attend.1.attended_ref.o_in = bf16[512,1024]{1,0:T(8,128)(2,1)S(1)} custom-call(bf16[512,3072]{1,0:T(8,128)(2,1)S(1)} %get-tuple-element.289.q_ref.k_ref.v_ref, bf16[512,3072]{1,0:T(8,128)(2,1)S(1)} %get-tuple-element.289.q_ref.k_ref.v_ref, bf16[512,3072]{1,0:T(8,128)(2,1)S(1)} %get-tuple-element.289.q_ref.k_ref.v_ref, s32[1,512]{1,0:T(1,128)S(1)} %iota_subtract_fusion.pos_ref), custom_call_target="tpu_custom_call" | custom-call | flops 1000000000 | tf_op jit(solution)/shard_map/attend/pallas_call | solution.py:470
  114.4 1.7 copy-done.1
  116.4 4.5 %collective-permute-done.25.refs_15_ = bf16[128,1024]{1,0:T(8,128)(2,1)S(1)} collective-permute-done((bf16[128,1024]{1,0:T(8,128)(2,1)S(1)}, bf16[128,1024]{1,0:T(8,128)(2,1)S(1)}, u32[]{:S(2)}, u32[]{:S(2)}) %collective-permute-start.25) | collective-permute-done | bytes 262176 | tf_op jit(solution)/shard_map/ppermute | solution.py:135
  123.0 2.2 leave.1
  126.0 3.9 %collective-permute-done.28.refs_16_ = bf16[128,1024]{1,0:T(8,128)(2,1)S(1)} collective-permute-done((bf16[128,1024]{1,0:T(8,128)(2,1)S(1)}, bf16[128,1024]{1,0:T(8,128)(2,1)S(1)}, u32[]{:S(2)}, u32[]{:S(2)}) %collective-permute-start.28) | collective-permute-done | bytes 262176 | tf_op jit(solution)/shard_map/ppermute | solution.py:135
  130.5 2.1 collective-permute-done.30.refs_18_.refs_2_.refs_3_
  134.7 20.0 %mlp_both.2 = (bf16[1024,1024]{1,0:T(8,128)(2,1)}, bf16[1024,1024]{1,0:T(8,128)(2,1)}, bf16[512,1024]{1,0:T(8,128)(2,1)S(1)}, bf16[512,1024]{1,0:T(8,128)(2,1)},...) custom-call(s32[4]{0:T(128)S(1)} %pad_add_fusion.idx.refs_0_, ...), custom_call_target="tpu_custom_call" | custom-call | flops 1000000000 | tf_op jit(solution)/shard_map/mlp_both/pallas_call | solution.py:661
  156.6 1.8 collective-permute-done.33.refs_18_.refs_6_.refs_7_
  159.4 20.1 %mlp_both.3 = (bf16[1024,1024]{1,0:T(8,128)(2,1)}, bf16[1024,1024]{1,0:T(8,128)(2,1)}, bf16[512,1024]{1,0:T(8,128)(2,1)S(1)}, bf16[512,1024]{1,0:T(8,128)(2,1)},...) custom-call(s32[4]{0:T(128)S(1)} %pad_add_fusion.idx.refs_0_, ...), custom_call_target="tpu_custom_call" | custom-call | flops 1000000000 | tf_op jit(solution)/shard_map/mlp_both/pallas_call | solution.py:661
  185.2 1.6 copy-done.40
  186.8 1.6 copy-done.42
  188.4 7.4 %weight_grad.2 = (bf16[4,128,1024]{2,1,0:T(8,128)(2,1)S(1)}, bf16[4,128,1024]{2,1,0:T(8,128)(2,1)S(1)}) custom-call(s32[4]{0:T(128)S(1)} %pad_add_fusion.idx.refs_0_, bf16[512,1024]{1,0:T(8,128)(2,1)S(1)} %copy-done.8, bf16[512,1024]{1,0:T(8,128)(2,1)S(1)} %copy-done.8, bf16[512,1024]{1,0:T(8,128)(2,1)S(1)} %copy-done.10, bf16[512,1024]{1,0:T(8,128)(2,1)S(1)} %copy-done.10, ...), custom_call_target="tpu_custom_call" | custom-call | flops 1000000000 | tf_op jit(solution)/shard_map/weight_grad/pallas_call | solution.py:723
  195.8 7.4 %weight_grad.3 = (bf16[4,128,1024]{2,1,0:T(8,128)(2,1)S(1)}, bf16[4,128,1024]{2,1,0:T(8,128)(2,1)S(1)}) custom-call(s32[4]{0:T(128)S(1)} %pad_add_fusion.idx.refs_0_, bf16[512,1024]{1,0:T(8,128)(2,1)S(1)} %copy-done.8, bf16[512,1024]{1,0:T(8,128)(2,1)S(1)} %copy-done.8, bf16[512,1024]{1,0:T(8,128)(2,1)S(1)} %copy-done.10, bf16[512,1024]{1,0:T(8,128)(2,1)S(1)} %copy-done.10, ...), custom_call_target="tpu_custom_call" | custom-call | flops 1000000000 | tf_op jit(solution)/shard_map/weight_grad/pallas_call | solution.py:723
  203.3 2.1 collective-permute-done.39.refs_2_.refs_1_
  209.6 5.6 %back.1 = (f32[512,1024]{1,0:T(8,128)S(1)}, bf16[512,1024]{1,0:T(8,128)(2,1)S(1)}, bf16[512,1024]{1,0:T(8,128)(2,1)S(1)}, f32[8,1024]{1,0:T(8,128)S(1)}) custom-call(bf16[512,1024]{1,0:T(8,128)(2,1)S(1)} %copy-done.65, bf16[512,1024]{1,0:T(8,128)(2,1)} %collective-permute-done.34.b_ref, bf16[512,1024]{1,0:T(8,128)(2,1)S(1)} %collective-permute-done.37.c_ref, ...), custom_call_target="tpu_custom_call" | custom-call | flops 1000000000 | tf_op jit(solution)/shard_map/back/pallas_call | solution.py:369
  216.3 14.9 %attend_back.1 = (bf16[512,1024]{1,0:T(8,128)(2,1)S(1)}, bf16[512,1024]{1,0:T(8,128)(2,1)S(1)}, bf16[512,1024]{1,0:T(8,128)(2,1)S(1)}) custom-call(bf16[512,3072]{1,0:T(8,128)(2,1)S(1)} %copy-done.2, bf16[512,3072]{1,0:T(8,128)(2,1)S(1)} %copy-done.2, bf16[512,3072]{1,0:T(8,128)(2,1)S(1)} %copy-done.2, bf16[512,1024]{1,0:T(8,128)(2,1)S(1)} %get-tuple-element.358.do_ref, ...), custom_call_target="tpu_custom_call" | custom-call | flops 1000000000 | tf_op jit(solution)/shard_map/attend_back/pallas_call | solution.py:530
  232.3 1.9 collective-permute-start.43
  234.2 6.5 %attn_grad.1 = (bf16[2,4,32,1024]{3,2,1,0:T(8,128)(2,1)S(1)}, bf16[2,4,32,1024]{3,2,1,0:T(8,128)(2,1)S(1)}, bf16[2,4,32,2048]{3,2,1,0:T(8,128)(2,1)}, bf16[2,4,3...) custom-call(s32[4]{0:T(128)S(1)} %pad_add_fusion.idx.refs_0_, ...), custom_call_target="tpu_custom_call" | custom-call | flops 1000000000 | tf_op jit(solution)/shard_map/attn_grad/pallas_call | solution.py:769
  241.7 10.5 %collective-permute-done.40.refs_5_.refs_1_ = bf16[4,128,1024]{2,1,0:T(8,128)(2,1)S(1)} collective-permute-done((bf16[4,128,1024]{2,1,0:T(8,128)(2,1)S(1)}, bf16[4,128,1024]{2,1,0:T(8,128)(2,1)S(1)}, u32[]{:S(2)}, u32[]{:S(2)}) %collective-permute-start.40) | collective-permute-done | bytes 1048608 | tf_op jit(solution)/shard_map/ppermute | solution.py:135
  257.0 2.5 first_sum.1
  262.5 2.0 collective-permute-start.56
  264.6 11.5 %last.1 = (f32[512,1024]{1,0:T(8,128)}, bf16[512,1024]{1,0:T(8,128)(2,1)}, f32[8,1024]{1,0:T(8,128)S(1)}) custom-call(bf16[512,1024]{1,0:T(8,128)(2,1)S(1)} %get-tuple-element.409.dq.refs_0_, bf16[512,1024]{1,0:T(8,128)(2,1)S(1)} %get-tuple-element.410.dk.refs_1_, bf16[512,1024]{1,0:T(8,128)(2,1)S(1)} %get-tuple-element.411.dv.refs_2_, ...), custom_call_target="tpu_custom_call" | custom-call | flops 1000000000 | tf_op jit(solution)/shard_map/last/pallas_call | solution.py:405
  278.1 8.3 %collective-permute-done.54 = f32[8,1024]{1,0:T(8,128)S(1)} collective-permute-done((f32[8,1024]{1,0:T(8,128)S(1)}, f32[8,1024]{1,0:T(8,128)S(1)}, u32[]{:S(2)}, u32[]{:S(2)}) %collective-permute-start.54) | collective-permute-done | bytes 32800 | tf_op jit(solution)/shard_map/ppermute | solution.py:135
  287.6 2.0 second_sum.1
  290.3 1.6 collective-permute-start.57
  293.2 2.6 collective-permute-start.60
  295.8 5.5 %stay_sum.1 = (bf16[4,32,2048]{2,1,0:T(8,128)(2,1)}, bf16[4,32,2048]{2,1,0:T(8,128)(2,1)}, bf16[2,128,1024]{2,1,0:T(8,128)(2,1)}) custom-call(s32[4]{0:T(128)} %copy-done.82, bf16[2,4,32,2048]{3,2,1,0:T(8,128)(2,1)} %copy-done.29, bf16[2,4,32,2048]{3,2,1,0:T(8,128)(2,1)} %copy-done.31, bf16[2,4,32,2048]{3,2,1,0:T(8,128)(2,1)} %copy-done.33, ...), custom_call_target="tpu_custom_call" | custom-call | flops 1000000000 | tf_op jit(solution)/shard_map/stay_sum/pallas_call | solution.py:930
  301.2 2.4 collective-permute-done.59
  310.4 1.8 collective-permute-start.61
  313.9 9.4 %collective-permute-done.61 = bf16[32,4224]{1,0:T(8,128)(2,1)S(1)} collective-permute-done((bf16[32,4224]{1,0:T(8,128)(2,1)S(1)}, bf16[32,4224]{1,0:T(8,128)(2,1)S(1)}, u32[]{:S(2)}, u32[]{:S(2)}) %collective-permute-start.61) | collective-permute-done | bytes 270368 | tf_op jit(solution)/shard_map/ppermute | solution.py:135
  323.4 8.3 %collective-permute-done.62 = bf16[32,4224]{1,0:T(8,128)(2,1)S(1)} collective-permute-done((bf16[32,4224]{1,0:T(8,128)(2,1)S(1)}, bf16[32,4224]{1,0:T(8,128)(2,1)S(1)}, u32[]{:S(2)}, u32[]{:S(2)}) %collective-permute-start.62) | collective-permute-done | bytes 270368 | tf_op jit(solution)/shard_map/ppermute | solution.py:135
  331.6 6.0 %collective-permute-done.63 = bf16[32,4224]{1,0:T(8,128)(2,1)S(1)} collective-permute-done((bf16[32,4224]{1,0:T(8,128)(2,1)S(1)}, bf16[32,4224]{1,0:T(8,128)(2,1)S(1)}, u32[]{:S(2)}, u32[]{:S(2)}) %collective-permute-start.63) | collective-permute-done | bytes 270368 | tf_op jit(solution)/shard_map/ppermute | solution.py:135
  340.1 3.9 %place_mlp.1 = (f32[4,128,1024]{2,1,0:T(8,128)}, f32[128,4096]{1,0:T(8,128)}, f32[128,4096]{1,0:T(8,128)}) custom-call(s32[4]{0:T(128)S(1)} %copy-done.83, bf16[3,128,1024]{2,1,0:T(8,128)(2,1)S(1)} %get-tuple-element.470.own_ref, bf16[3,128,1024]{2,1,0:T(8,128)(2,1)S(1)} %collective-permute-done.64.y_ref, ...), custom_call_target="tpu_custom_call" | custom-call | flops 1000000000 | tf_op jit(solution)/shard_map/place_mlp/pallas_call | solution.py:1051
  344.1 2.8 collective-permute-done.66.refs_2_
  348.4 1.9 place_rows.1
  (324 shorter events, 80.0 us)
Async XLA Ops:
  2.5 24.0 %collective-permute-start.2 = (bf16[1,32,4224]{2,1,0:T(8,128)(2,1)S(1)}, bf16[1,32,4224]{2,1,0:T(8,128)(2,1)S(1)}, u32[]{:S(2)}, u32[]{:S(2)}) collective-permute-start(bf16[1,32,4224]{2,1,0:T(8,128)(2,1)S(1)} %fusion.2), channel_id=1, source_target_pairs={{0,24},{1,25},{2,26},{3,27},{4,28},{5,29},{6,30},{7,31},{8,16},{9,... | collective-permute-start | bytes 811016 | tf_op jit(solution)/shard_map/ppermute | solution.py:135
  4.1 23.1 %collective-permute-start.1 = (bf16[1,32,4224]{2,1,0:T(8,128)(2,1)S(1)}, bf16[1,32,4224]{2,1,0:T(8,128)(2,1)S(1)}, u32[]{:S(2)}, u32[]{:S(2)}) collective-permute-start(bf16[1,32,4224]{2,1,0:T(8,128)(2,1)S(1)} %fusion.2), channel_id=1, source_target_pairs={{0,16},{1,17},{2,18},{3,19},{4,20},{5,21},{6,22},{7,23},{8,24},{9,... | collective-permute-start | bytes 811016 | tf_op jit(solution)/shard_map/ppermute | solution.py:135
  5.4 21.9 %collective-permute-start = (bf16[1,32,4224]{2,1,0:T(8,128)(2,1)S(1)}, bf16[1,32,4224]{2,1,0:T(8,128)(2,1)S(1)}, u32[]{:S(2)}, u32[]{:S(2)}) collective-permute-start(bf16[1,32,4224]{2,1,0:T(8,128)(2,1)S(1)} %fusion.2), channel_id=1, source_target_pairs={{0,8},{1,9},{2,10},{3,11},{4,12},{5,13},{6,14},{7,15},{8,0},{9,1},... | collective-permute-start | bytes 811016 | tf_op jit(solution)/shard_map/ppermute | solution.py:135
  7.7 13.3 %collective-permute-start.6 = (bf16[2,32,4096]{2,1,0:T(8,128)(2,1)S(1)}, bf16[2,32,4096]{2,1,0:T(8,128)(2,1)}, u32[]{:S(2)}, u32[]{:S(2)}) collective-permute-start(bf16[2,32,4096]{2,1,0:T(8,128)(2,1)S(1)} %pad_maximum_fusion.2.raw_ref), channel_id=1, source_target_pairs={{0,4},{1,5},{2,6},{3,7},{4,0},{5,1},{6,2},{7,3},{8,12},{9,13},{10,... | collective-permute-start | bytes 1572872 | tf_op jit(solution)/shard_map/ppermute | solution.py:135
  18.0 8.5 %collective-permute-start.5 = (bf16[128,1024]{1,0:T(8,128)(2,1)S(1)}, bf16[128,1024]{1,0:T(8,128)(2,1)S(1)}, u32[]{:S(2)}, u32[]{:S(2)}) collective-permute-start(bf16[128,1024]{1,0:T(8,128)(2,1)S(1)} %copy-done.66), channel_id=1, source_target_pairs={{0,4},{1,5},{2,6},{3,7},{4,0},{5,1},{6,2},{7,3},{8,12},{9,13},{10,... | collective-permute-start | bytes 786440 | tf_op jit(solution)/shard_map/ppermute | solution.py:135
  27.4 27.2 %collective-permute-start.8 = (bf16[4,32,4224]{2,1,0:T(8,128)(2,1)S(1)}, bf16[4,32,4224]{2,1,0:T(8,128)(2,1)S(1)}, u32[]{:S(2)}, u32[]{:S(2)}) collective-permute-start(bf16[4,32,4224]{2,1,0:T(8,128)(2,1)S(1)} %pad_maximum_fusion.refs_1_), channel_id=1, source_target_pairs={{0,2},{1,3},{2,0},{3,1},{4,6},{5,7},{6,4},{7,5},{8,10},{9,11},{10,... | collective-permute-start | bytes 3244040 | tf_op jit(solution)/shard_map/ppermute | solution.py:135
  29.0 25.7 %collective-permute-start.7 = (bf16[4,32,4224]{2,1,0:T(8,128)(2,1)S(1)}, bf16[4,32,4224]{2,1,0:T(8,128)(2,1)S(1)}, u32[]{:S(2)}, u32[]{:S(2)}) collective-permute-start(bf16[4,32,4224]{2,1,0:T(8,128)(2,1)S(1)} %pad_maximum_fusion.refs_1_), channel_id=1, source_target_pairs={{0,4},{1,5},{2,6},{3,7},{4,0},{5,1},{6,2},{7,3},{8,12},{9,13},{10,... | collective-permute-start | bytes 3244040 | tf_op jit(solution)/shard_map/ppermute | solution.py:135
  29.6 25.0 %collective-permute-start.9 = (bf16[2,128,1024]{2,1,0:T(8,128)(2,1)S(1)}, bf16[2,128,1024]{2,1,0:T(8,128)(2,1)S(1)}, u32[]{:S(2)}, u32[]{:S(2)}) collective-permute-start(bf16[2,128,1024]{2,1,0:T(8,128)(2,1)S(1)} %join.2.refs_1_), channel_id=1, source_target_pairs={{0,8},{1,9},{2,10},{3,11},{4,12},{5,13},{6,14},{7,15},{8,0},{9,1},... | collective-permute-start | bytes 1572872 | tf_op jit(solution)/shard_map/ppermute | solution.py:135
  31.9 21.2 %collective-permute-start.10 = (bf16[128,1024]{1,0:T(8,128)(2,1)S(1)}, bf16[128,1024]{1,0:T(8,128)(2,1)S(1)}, u32[]{:S(2)}, u32[]{:S(2)}) collective-permute-start(bf16[128,1024]{1,0:T(8,128)(2,1)S(1)} %copy-done.66), channel_id=1, source_target_pairs={{0,8},{1,9},{2,10},{3,11},{4,12},{5,13},{6,14},{7,15},{8,0},{9,1},... | collective-permute-start | bytes 786440 | tf_op jit(solution)/shard_map/ppermute | solution.py:135
  32.0 22.7 %collective-permute-start.11 = (bf16[128,1024]{1,0:T(8,128)(2,1)S(1)}, bf16[128,1024]{1,0:T(8,128)(2,1)S(1)}, u32[]{:S(2)}, u32[]{:S(2)}) collective-permute-start(bf16[128,1024]{1,0:T(8,128)(2,1)S(1)} %copy-done.66), channel_id=1, source_target_pairs={{0,16},{1,17},{2,18},{3,19},{4,20},{5,21},{6,22},{7,23},{8,24},{9,... | collective-permute-start | bytes 786440 | tf_op jit(solution)/shard_map/ppermute | solution.py:135
  54.7 24.9 %collective-permute-start.15 = (bf16[4,32,4224]{2,1,0:T(8,128)(2,1)S(1)}, bf16[4,32,4224]{2,1,0:T(8,128)(2,1)S(1)}, u32[]{:S(2)}, u32[]{:S(2)}) collective-permute-start(bf16[4,32,4224]{2,1,0:T(8,128)(2,1)S(1)} %pad_maximum_fusion.refs_1_), channel_id=1, source_target_pairs={{0,1},{1,0},{2,3},{3,2},{4,5},{5,4},{6,7},{7,6},{8,9},{9,8},{10,11... | collective-permute-start | bytes 3244040 | tf_op jit(solution)/shard_map/ppermute | solution.py:135
  54.8 26.3 %collective-permute-start.16 = (bf16[4,32,4224]{2,1,0:T(8,128)(2,1)S(1)}, bf16[4,32,4224]{2,1,0:T(8,128)(2,1)S(1)}, u32[]{:S(2)}, u32[]{:S(2)}) collective-permute-start(bf16[4,32,4224]{2,1,0:T(8,128)(2,1)S(1)} %collective-permute-done.7.refs_2_), channel_id=1, source_target_pairs={{0,2},{1,3},{2,0},{3,1},{4,6},{5,7},{6,4},{7,5},{8,10},{9,11},{10,... | collective-permute-start | bytes 3244040 | tf_op jit(solution)/shard_map/ppermute | solution.py:135
  55.3 24.3 %collective-permute-start.12 = (bf16[2,128,1024]{2,1,0:T(8,128)(2,1)S(1)}, bf16[2,128,1024]{2,1,0:T(8,128)(2,1)S(1)}, u32[]{:S(2)}, u32[]{:S(2)}) collective-permute-start(bf16[2,128,1024]{2,1,0:T(8,128)(2,1)S(1)} %join.2.refs_1_), channel_id=1, source_target_pairs={{0,16},{1,17},{2,18},{3,19},{4,20},{5,21},{6,22},{7,23},{8,24},{9,... | collective-permute-start | bytes 1572872 | tf_op jit(solution)/shard_map/ppermute | solution.py:135
  57.4 22.3 %collective-permute-start.13 = (bf16[2,128,1024]{2,1,0:T(8,128)(2,1)S(1)}, bf16[2,128,1024]{2,1,0:T(8,128)(2,1)S(1)}, u32[]{:S(2)}, u32[]{:S(2)}) collective-permute-start(bf16[2,128,1024]{2,1,0:T(8,128)(2,1)S(1)} %collective-permute-done.9.refs_3_), channel_id=1, source_target_pairs={{0,4},{1,5},{2,6},{3,7},{4,0},{5,1},{6,2},{7,3},{8,12},{9,13},{10,... | collective-permute-start | bytes 1572872 | tf_op jit(solution)/shard_map/ppermute | solution.py:135
  58.6 18.2 %collective-permute-start.14 = (bf16[128,1024]{1,0:T(8,128)(2,1)S(1)}, bf16[128,1024]{1,0:T(8,128)(2,1)S(1)}, u32[]{:S(2)}, u32[]{:S(2)}) collective-permute-start(bf16[128,1024]{1,0:T(8,128)(2,1)S(1)} %collective-permute-done.10.refs_11_), channel_id=1, source_target_pairs={{0,4},{1,5},{2,6},{3,7},{4,0},{5,1},{6,2},{7,3},{8,12},{9,13},{10,... | collective-permute-start | bytes 786440 | tf_op jit(solution)/shard_map/ppermute | solution.py:135
  81.6 25.6 %collective-permute-start.22 = (bf16[2,128,1024]{2,1,0:T(8,128)(2,1)S(1)}, bf16[2,128,1024]{2,1,0:T(8,128)(2,1)S(1)}, u32[]{:S(2)}, u32[]{:S(2)}) collective-permute-start(bf16[2,128,1024]{2,1,0:T(8,128)(2,1)S(1)} %join.2.refs_1_), channel_id=1, source_target_pairs={{0,24},{1,25},{2,26},{3,27},{4,28},{5,29},{6,30},{7,31},{8,16},{9,... | collective-permute-start | bytes 1572872 | tf_op jit(solution)/shard_map/ppermute | solution.py:135
  82.2 24.9 %collective-permute-start.20 = (bf16[2,128,1024]{2,1,0:T(8,128)(2,1)S(1)}, bf16[2,128,1024]{2,1,0:T(8,128)(2,1)S(1)}, u32[]{:S(2)}, u32[]{:S(2)}) collective-permute-start(bf16[2,128,1024]{2,1,0:T(8,128)(2,1)S(1)} %collective-permute-done.12.refs_5_), channel_id=1, source_target_pairs={{0,4},{1,5},{2,6},{3,7},{4,0},{5,1},{6,2},{7,3},{8,12},{9,13},{10,... | collective-permute-start | bytes 1572872 | tf_op jit(solution)/shard_map/ppermute | solution.py:135
  83.7 32.3 %collective-permute-start.23 = (bf16[512,1024]{1,0:T(8,128)(2,1)S(1)}, bf16[512,1024]{1,0:T(8,128)(2,1)}, u32[]{:S(2)}, u32[]{:S(2)}) collective-permute-start(bf16[512,1024]{1,0:T(8,128)(2,1)S(1)} %copy-done.16), channel_id=1, source_target_pairs={{0,2},{1,3},{2,0},{3,1},{4,6},{5,7},{6,4},{7,5},{8,10},{9,11},{10,... | collective-permute-start | bytes 3145736 | tf_op jit(solution)/shard_map/ppermute | solution.py:135
  85.3 16.6 %collective-permute-start.21 = (bf16[128,1024]{1,0:T(8,128)(2,1)S(1)}, bf16[128,1024]{1,0:T(8,128)(2,1)S(1)}, u32[]{:S(2)}, u32[]{:S(2)}) collective-permute-start(bf16[128,1024]{1,0:T(8,128)(2,1)S(1)} %collective-permute-done.11.refs_13_), channel_id=1, source_target_pairs={{0,4},{1,5},{2,6},{3,7},{4,0},{5,1},{6,2},{7,3},{8,12},{9,13},{10,... | collective-permute-start | bytes 786440 | tf_op jit(solution)/shard_map/ppermute | solution.py:135
  107.1 13.8 %collective-permute-start.24 = (bf16[2,128,1024]{2,1,0:T(8,128)(2,1)S(1)}, bf16[2,128,1024]{2,1,0:T(8,128)(2,1)S(1)}, u32[]{:S(2)}, u32[]{:S(2)}) collective-permute-start(bf16[2,128,1024]{2,1,0:T(8,128)(2,1)S(1)} %collective-permute-done.22.refs_7_), channel_id=1, source_target_pairs={{0,4},{1,5},{2,6},{3,7},{4,0},{5,1},{6,2},{7,3},{8,12},{9,13},{10,... | collective-permute-start | bytes 1572872 | tf_op jit(solution)/shard_map/ppermute | solution.py:135
  109.2 11.7 %collective-permute-start.25 = (bf16[128,1024]{1,0:T(8,128)(2,1)S(1)}, bf16[128,1024]{1,0:T(8,128)(2,1)S(1)}, u32[]{:S(2)}, u32[]{:S(2)}) collective-permute-start(bf16[128,1024]{1,0:T(8,128)(2,1)S(1)} %copy-done.66), channel_id=1, source_target_pairs={{0,24},{1,25},{2,26},{3,27},{4,28},{5,29},{6,30},{7,31},{8,16},{9,... | collective-permute-start | bytes 786440 | tf_op jit(solution)/shard_map/ppermute | solution.py:135
  120.9 9.0 %collective-permute-start.29 = (bf16[512,1024]{1,0:T(8,128)(2,1)S(1)}, bf16[512,1024]{1,0:T(8,128)(2,1)S(1)}, u32[]{:S(2)}, u32[]{:S(2)}) collective-permute-start(bf16[512,1024]{1,0:T(8,128)(2,1)S(1)} %copy-done.16), channel_id=1, source_target_pairs={{0,1},{1,0},{2,3},{3,2},{4,5},{5,4},{6,7},{7,6},{8,9},{9,8},{10,11... | collective-permute-start | bytes 3145736 | tf_op jit(solution)/shard_map/ppermute | solution.py:135
  129.9 25.8 %collective-permute-start.31 = (bf16[512,1024]{1,0:T(8,128)(2,1)S(1)}, bf16[512,1024]{1,0:T(8,128)(2,1)S(1)}, u32[]{:S(2)}, u32[]{:S(2)}) collective-permute-start(bf16[512,1024]{1,0:T(8,128)(2,1)S(1)} %get-tuple-element.313.refs_17_.refs_0_.refs_1_), channel_id=1, source_target_pairs={{0,2},{1,3},{2,0},{3,1},{4,6},{5,7},{6,4},{7,5},{8,10},{9,11},{10,... | collective-permute-start | bytes 3145736 | tf_op jit(solution)/shard_map/ppermute | solution.py:135
  133.5 22.1 %collective-permute-start.32 = (bf16[512,1024]{1,0:T(8,128)(2,1)}, bf16[512,1024]{1,0:T(8,128)(2,1)}, u32[]{:S(2)}, u32[]{:S(2)}) collective-permute-start(bf16[512,1024]{1,0:T(8,128)(2,1)} %collective-permute-done.23.refs_19_), channel_id=1, source_target_pairs={{0,1},{1,0},{2,3},{3,2},{4,5},{5,4},{6,7},{7,6},{8,9},{9,8},{10,11... | collective-permute-start | bytes 3145736 | tf_op jit(solution)/shard_map/ppermute | solution.py:135
  156.1 23.4 %collective-permute-start.35 = (bf16[512,1024]{1,0:T(8,128)(2,1)}, bf16[512,1024]{1,0:T(8,128)(2,1)}, u32[]{:S(2)}, u32[]{:S(2)}) collective-permute-start(bf16[512,1024]{1,0:T(8,128)(2,1)} %get-tuple-element.329), channel_id=1, source_target_pairs={{0,1},{1,0},{2,3},{3,2},{4,5},{5,4},{6,7},{7,6},{8,9},{9,8},{10,11... | collective-permute-start | bytes 3145736 | tf_op jit(solution)/shard_map/ppermute | solution.py:135
  156.3 23.3 %collective-permute-start.34 = (bf16[512,1024]{1,0:T(8,128)(2,1)}, bf16[512,1024]{1,0:T(8,128)(2,1)}, u32[]{:S(2)}, u32[]{:S(2)}) collective-permute-start(bf16[512,1024]{1,0:T(8,128)(2,1)} %get-tuple-element.328), channel_id=1, source_target_pairs={{0,1},{1,0},{2,3},{3,2},{4,5},{5,4},{6,7},{7,6},{8,9},{9,8},{10,11... | collective-permute-start | bytes 3145736 | tf_op jit(solution)/shard_map/ppermute | solution.py:135
  180.0 25.4 %collective-permute-start.39 = (bf16[4,128,1024]{2,1,0:T(8,128)(2,1)}, bf16[4,128,1024]{2,1,0:T(8,128)(2,1)S(1)}, u32[]{:S(2)}, u32[]{:S(2)}) collective-permute-start(bf16[4,128,1024]{2,1,0:T(8,128)(2,1)} %get-tuple-element.348), channel_id=1, source_target_pairs={{0,4},{1,5},{2,6},{3,7},{4,0},{5,1},{6,2},{7,3},{8,12},{9,13},{10,... | collective-permute-start | bytes 3145736 | tf_op jit(solution)/shard_map/ppermute | solution.py:135
  182.9 22.5 %collective-permute-start.38 = (bf16[512,1024]{1,0:T(8,128)(2,1)}, bf16[512,1024]{1,0:T(8,128)(2,1)S(1)}, u32[]{:S(2)}, u32[]{:S(2)}) collective-permute-start(bf16[512,1024]{1,0:T(8,128)(2,1)} %get-tuple-element.347), channel_id=1, source_target_pairs={{0,1},{1,0},{2,3},{3,2},{4,5},{5,4},{6,7},{7,6},{8,9},{9,8},{10,11... | collective-permute-start | bytes 3145736 | tf_op jit(solution)/shard_map/ppermute | solution.py:135
  183.3 25.2 %collective-permute-start.37 = (bf16[512,1024]{1,0:T(8,128)(2,1)S(1)}, bf16[512,1024]{1,0:T(8,128)(2,1)S(1)}, u32[]{:S(2)}, u32[]{:S(2)}) collective-permute-start(bf16[512,1024]{1,0:T(8,128)(2,1)S(1)} %add_convert_fusion.1), channel_id=1, source_target_pairs={{0,2},{1,3},{2,0},{3,1},{4,6},{5,7},{6,4},{7,5},{8,10},{9,11},{10,... | collective-permute-start | bytes 3145736 | tf_op jit(solution)/shard_map/ppermute | solution.py:135
  205.4 26.1 %collective-permute-start.41 = (bf16[4,128,1024]{2,1,0:T(8,128)(2,1)S(1)}, bf16[4,128,1024]{2,1,0:T(8,128)(2,1)S(1)}, u32[]{:S(2)}, u32[]{:S(2)}) collective-permute-start(bf16[4,128,1024]{2,1,0:T(8,128)(2,1)S(1)} %get-tuple-element.360), channel_id=1, source_target_pairs={{0,4},{1,5},{2,6},{3,7},{4,0},{5,1},{6,2},{7,3},{8,12},{9,13},{10,... | collective-permute-start | bytes 3145736 | tf_op jit(solution)/shard_map/ppermute | solution.py:135
  208.5 22.7 %collective-permute-start.42 = (bf16[1,2,128,1024]{3,2,1,0:T(8,128)(2,1)S(1)}, bf16[1,2,128,1024]{3,2,1,0:T(8,128)(2,1)S(1)}, u32[]{:S(2)}, u32[]{:S(2)}) collective-permute-start(bf16[1,2,128,1024]{3,2,1,0:T(8,128)(2,1)S(1)} %near_sum.2), channel_id=1, source_target_pairs={{0,8},{1,9},{2,10},{3,11},{4,12},{5,13},{6,14},{7,15},{8,0},{9,1},... | collective-permute-start | bytes 1572872 | tf_op jit(solution)/shard_map/ppermute | solution.py:135
  208.5 32.2 %collective-permute-start.44 = (bf16[512,1024]{1,0:T(8,128)(2,1)S(1)}, bf16[512,1024]{1,0:T(8,128)(2,1)S(1)}, u32[]{:S(2)}, u32[]{:S(2)}) collective-permute-start(bf16[512,1024]{1,0:T(8,128)(2,1)S(1)} %add_convert_fusion), channel_id=1, source_target_pairs={{0,2},{1,3},{2,0},{3,1},{4,6},{5,7},{6,4},{7,5},{8,10},{9,11},{10,... | collective-permute-start | bytes 3145736 | tf_op jit(solution)/shard_map/ppermute | solution.py:135
  215.2 37.0 %collective-permute-start.40 = (bf16[4,128,1024]{2,1,0:T(8,128)(2,1)S(1)}, bf16[4,128,1024]{2,1,0:T(8,128)(2,1)S(1)}, u32[]{:S(2)}, u32[]{:S(2)}) collective-permute-start(bf16[4,128,1024]{2,1,0:T(8,128)(2,1)S(1)} %get-tuple-element.356), channel_id=1, source_target_pairs={{0,4},{1,5},{2,6},{3,7},{4,0},{5,1},{6,2},{7,3},{8,12},{9,13},{10,... | collective-permute-start | bytes 3145736 | tf_op jit(solution)/shard_map/ppermute | solution.py:135
  232.3 19.9 %collective-permute-start.43 = (bf16[1,2,128,1024]{3,2,1,0:T(8,128)(2,1)S(1)}, bf16[1,2,128,1024]{3,2,1,0:T(8,128)(2,1)S(1)}, u32[]{:S(2)}, u32[]{:S(2)}) collective-permute-start(bf16[1,2,128,1024]{3,2,1,0:T(8,128)(2,1)S(1)} %near_sum.3), channel_id=1, source_target_pairs={{0,8},{1,9},{2,10},{3,11},{4,12},{5,13},{6,14},{7,15},{8,0},{9,1},... | collective-permute-start | bytes 1572872 | tf_op jit(solution)/shard_map/ppermute | solution.py:135
  260.5 27.0 %collective-permute-start.51 = (bf16[2,4,32,2048]{3,2,1,0:T(8,128)(2,1)S(1)}, bf16[2,4,32,2048]{3,2,1,0:T(8,128)(2,1)S(1)}, u32[]{:S(2)}, u32[]{:S(2)}) collective-permute-start(bf16[2,4,32,2048]{3,2,1,0:T(8,128)(2,1)S(1)} %get-tuple-element.421), channel_id=1, source_target_pairs={{0,4},{1,5},{2,6},{3,7},{4,0},{5,1},{6,2},{7,3},{8,12},{9,13},{10,... | collective-permute-start | bytes 3145736 | tf_op jit(solution)/shard_map/ppermute | solution.py:135
  261.9 25.6 %collective-permute-start.52 = (bf16[2,4,32,2048]{3,2,1,0:T(8,128)(2,1)S(1)}, bf16[2,4,32,2048]{3,2,1,0:T(8,128)(2,1)S(1)}, u32[]{:S(2)}, u32[]{:S(2)}) collective-permute-start(bf16[2,4,32,2048]{3,2,1,0:T(8,128)(2,1)S(1)} %get-tuple-element.422), channel_id=1, source_target_pairs={{0,2},{1,3},{2,0},{3,1},{4,6},{5,7},{6,4},{7,5},{8,10},{9,11},{10,... | collective-permute-start | bytes 3145736 | tf_op jit(solution)/shard_map/ppermute | solution.py:135
  262.5 23.9 %collective-permute-start.55 = (bf16[2,128,1024]{2,1,0:T(8,128)(2,1)}, bf16[2,128,1024]{2,1,0:T(8,128)(2,1)S(1)}, u32[]{:S(2)}, u32[]{:S(2)}) collective-permute-start(bf16[2,128,1024]{2,1,0:T(8,128)(2,1)} %get-tuple-element.424), channel_id=1, source_target_pairs={{0,8},{1,9},{2,10},{3,11},{4,12},{5,13},{6,14},{7,15},{8,0},{9,1},... | collective-permute-start | bytes 1572872 | tf_op jit(solution)/shard_map/ppermute | solution.py:135
  262.5 25.0 %collective-permute-start.56 = (bf16[2,128,1024]{2,1,0:T(8,128)(2,1)}, bf16[2,128,1024]{2,1,0:T(8,128)(2,1)S(1)}, u32[]{:S(2)}, u32[]{:S(2)}) collective-permute-start(bf16[2,128,1024]{2,1,0:T(8,128)(2,1)} %get-tuple-element.425), channel_id=1, source_target_pairs={{0,16},{1,17},{2,18},{3,19},{4,20},{5,21},{6,22},{7,23},{8,24},{9,... | collective-permute-start | bytes 1572872 | tf_op jit(solution)/shard_map/ppermute | solution.py:135
  277.3 9.1 %collective-permute-start.54 = (f32[8,1024]{1,0:T(8,128)S(1)}, f32[8,1024]{1,0:T(8,128)S(1)}, u32[]{:S(2)}, u32[]{:S(2)}) collective-permute-start(f32[8,1024]{1,0:T(8,128)S(1)} %add.85), channel_id=1, source_target_pairs={{0,4},{1,5},{2,6},{3,7},{4,0},{5,1},{6,2},{7,3},{8,12},{9,13},{10,... | collective-permute-start | bytes 98312 | tf_op jit(solution)/shard_map/ppermute | solution.py:135
  290.3 13.6 %collective-permute-start.57 = (bf16[4,32,2048]{2,1,0:T(8,128)(2,1)}, bf16[4,32,2048]{2,1,0:T(8,128)(2,1)S(1)}, u32[]{:S(2)}, u32[]{:S(2)}) collective-permute-start(bf16[4,32,2048]{2,1,0:T(8,128)(2,1)} %get-tuple-element.443), channel_id=1, source_target_pairs={{0,2},{1,3},{2,0},{3,1},{4,6},{5,7},{6,4},{7,5},{8,10},{9,11},{10,... | collective-permute-start | bytes 1572872 | tf_op jit(solution)/shard_map/ppermute | solution.py:135
  291.9 12.5 %collective-permute-start.58 = (bf16[4,32,2048]{2,1,0:T(8,128)(2,1)}, bf16[4,32,2048]{2,1,0:T(8,128)(2,1)}, u32[]{:S(2)}, u32[]{:S(2)}) collective-permute-start(bf16[4,32,2048]{2,1,0:T(8,128)(2,1)} %get-tuple-element.444), channel_id=1, source_target_pairs={{0,4},{1,5},{2,6},{3,7},{4,0},{5,1},{6,2},{7,3},{8,12},{9,13},{10,... | collective-permute-start | bytes 1572872 | tf_op jit(solution)/shard_map/ppermute | solution.py:135
  292.8 10.9 %collective-permute-start.59 = (f32[8,1024]{1,0:T(8,128)S(1)}, f32[8,1024]{1,0:T(8,128)S(1)}, u32[]{:S(2)}, u32[]{:S(2)}) collective-permute-start(f32[8,1024]{1,0:T(8,128)S(1)} %add.86), channel_id=1, source_target_pairs={{0,2},{1,3},{2,0},{3,1},{4,6},{5,7},{6,4},{7,5},{8,10},{9,11},{10,... | collective-permute-start | bytes 98312 | tf_op jit(solution)/shard_map/ppermute | solution.py:135
  293.2 10.8 %collective-permute-start.60 = (bf16[128,1024]{1,0:T(8,128)(2,1)}, bf16[128,1024]{1,0:T(8,128)(2,1)S(1)}, u32[]{:S(2)}, u32[]{:S(2)}) collective-permute-start(bf16[128,1024]{1,0:T(8,128)(2,1)} %copy-done.84), channel_id=1, source_target_pairs={{0,16},{1,17},{2,18},{3,19},{4,20},{5,21},{6,22},{7,23},{8,24},{9,... | collective-permute-start | bytes 786440 | tf_op jit(solution)/shard_map/ppermute | solution.py:135
  309.1 28.6 %collective-permute-start.65 = (bf16[3,128,1024]{2,1,0:T(8,128)(2,1)S(1)}, bf16[3,128,1024]{2,1,0:T(8,128)(2,1)S(1)}, u32[]{:S(2)}, u32[]{:S(2)}) collective-permute-start(bf16[3,128,1024]{2,1,0:T(8,128)(2,1)S(1)} %get-tuple-element.470.own_ref), channel_id=1, source_target_pairs={{0,1},{1,0},{2,3},{3,2},{4,5},{5,4},{6,7},{7,6},{8,9},{9,8},{10,11... | collective-permute-start | bytes 2359304 | tf_op jit(solution)/shard_map/ppermute | solution.py:135
  309.2 28.5 %collective-permute-start.64 = (bf16[3,128,1024]{2,1,0:T(8,128)(2,1)S(1)}, bf16[3,128,1024]{2,1,0:T(8,128)(2,1)S(1)}, u32[]{:S(2)}, u32[]{:S(2)}) collective-permute-start(bf16[3,128,1024]{2,1,0:T(8,128)(2,1)S(1)} %get-tuple-element.470.own_ref), channel_id=1, source_target_pairs={{0,2},{1,3},{2,0},{3,1},{4,6},{5,7},{6,4},{7,5},{8,10},{9,11},{10,... | collective-permute-start | bytes 2359304 | tf_op jit(solution)/shard_map/ppermute | solution.py:135
  310.4 12.9 %collective-permute-start.61 = (bf16[32,4224]{1,0:T(8,128)(2,1)S(1)}, bf16[32,4224]{1,0:T(8,128)(2,1)S(1)}, u32[]{:S(2)}, u32[]{:S(2)}) collective-permute-start(bf16[32,4224]{1,0:T(8,128)(2,1)S(1)} %get-tuple-element.459), channel_id=1, source_target_pairs={{0,8},{1,9},{2,10},{3,11},{4,12},{5,13},{6,14},{7,15},{8,0},{9,1},... | collective-permute-start | bytes 811016 | tf_op jit(solution)/shard_map/ppermute | solution.py:135
  312.2 19.4 %collective-permute-start.62 = (bf16[32,4224]{1,0:T(8,128)(2,1)S(1)}, bf16[32,4224]{1,0:T(8,128)(2,1)S(1)}, u32[]{:S(2)}, u32[]{:S(2)}) collective-permute-start(bf16[32,4224]{1,0:T(8,128)(2,1)S(1)} %get-tuple-element.460), channel_id=1, source_target_pairs={{0,16},{1,17},{2,18},{3,19},{4,20},{5,21},{6,22},{7,23},{8,24},{9,... | collective-permute-start | bytes 811016 | tf_op jit(solution)/shard_map/ppermute | solution.py:135
  313.1 24.5 %collective-permute-start.63 = (bf16[32,4224]{1,0:T(8,128)(2,1)S(1)}, bf16[32,4224]{1,0:T(8,128)(2,1)S(1)}, u32[]{:S(2)}, u32[]{:S(2)}) collective-permute-start(bf16[32,4224]{1,0:T(8,128)(2,1)S(1)} %get-tuple-element.461), channel_id=1, source_target_pairs={{0,24},{1,25},{2,26},{3,27},{4,28},{5,29},{6,30},{7,31},{8,16},{9,... | collective-permute-start | bytes 811016 | tf_op jit(solution)/shard_map/ppermute | solution.py:135
  (111 other events, 1455.1 us)

commit v5 on v4

--- a/solution.py
+++ b/solution.py
@@ -1253,7 +1253,8 @@
         a_away, b_away, far, gate_near, *late = window(a_away, b_away, far, gate_near, *late)
         a_core, b_core, dq, dk, dv, mlp_y = late
         a_x, b_y = swap(a_away, "x"), swap(b_away, "y")
-        far, gate_near = swap(far, "z2"), swap(gate_near, "z1")
+        gate_near = swap(gate_near, "z1")
+        far = swap(far, "z2")
         input_grad, block_out, small = last(
             (dq, dk, dv),
             w_attn,
@@ -1267,7 +1268,7 @@
         )
         small = small + swap(small, "core")
         small = small + swap(small, "x")
-        a_x, b_y, small, gate_near, far = window(a_x, b_y, small, gate_near, far)
+        far, a_x, b_y, gate_near, small = window(far, a_x, b_y, gate_near, small)
         parts = (a_keep_here, a_core, a_x, b_keep_here, b_core, b_y)
         a_away, b_away, gate_far = second_sum(idx, parts, gate_near, pairs[2])
         a_away, b_away, gate_far, small, *parts = window(a_away, b_away, gate_far, small, *parts)

time: 356 us -> 356 us (level)
  no operation moved by 1% of the time
where the time goes in v5:
time: 356 us; the launch traced here: 351 us
  waiting for transfers between devices  137 us (38%)
  Pallas kernels  133 us (37%)
  starting transfers between devices  55.4 us (16%)
  local copies, waits for them, and re-layouts  19.7 us (6%)
  other arithmetic  4.78 us (1%)
    ppermute x70, waiting for transfers between devices, swap(): return lax.ppermute(value, AXES, pairs)  137 us
    ppermute x70, starting transfers between devices, swap(): return lax.ppermute(value, AXES, pairs)  55.4 us
    pallas_call x2, Pallas kernels, mlp_both(): pl.pallas_call(lambda *refs: mlp_kernel(last_half, *refs), in_specs=in_sp...  40 us
    unnamed x179, local copies, waits for them, and re-layouts  18.7 us
    pallas_call x1, Pallas kernels, attend_back(): pl.pallas_call(attend_back_kernel, grid=(steps,), in_specs=[cols(0), cols...  14.9 us
    pallas_call x2, Pallas kernels, weight_grad(): pl.pallas_call(weight_grad_kernel, grid_spec=pltpu.PrefetchScalarGridSpec...  14.9 us
    pallas_call x1, Pallas kernels, last(): pl.pallas_call(last_kernel, grid=(rows // block,), in_specs=[row] * 3 + c...  11.5 us
    pallas_call x1, Pallas kernels, project(): pl.pallas_call(project_kernel, grid=(3 * width // block,), in_specs=[SMEM...  10.7 us
  transfers between devices with their start and end apart: 70, of which 40 were waited for; matrix products, arithmetic and copies ran while one was open for 1% of the time, Pallas kernels for 36%

profile of v5, /device:TPU:10, one launch (start us, length us, event | category | flops | bytes accessed | tf_op | source)
XLA Modules:
  0.0 351.3 jit_solution(9913208010182681750)
XLA Ops:
  2.5 1.6 collective-permute-start.2
  9.1 1.6 collective-permute-start.3
  11.1 5.3 %collective-permute-done.3.y_ref = bf16[2,2,32,1024]{3,2,1,0:T(8,128)(2,1)S(1)} collective-permute-done((bf16[2,2,32,1024]{3,2,1,0:T(8,128)(2,1)S(1)}, bf16[2,2,32,1024]{3,2,1,0:T(8,128)(2,1)S(1)}, u32[]{:S(2)}, u32[]{:S(2)}) %collective-permute-start.3) | collective-permute-done | bytes 262176 | tf_op jit(solution)/shard_map/ppermute | solution.py:135
  22.3 4.2 %collective-permute-done.5.refs_10_ = bf16[128,1024]{1,0:T(8,128)(2,1)S(1)} collective-permute-done((bf16[128,1024]{1,0:T(8,128)(2,1)S(1)}, bf16[128,1024]{1,0:T(8,128)(2,1)S(1)}, u32[]{:S(2)}, u32[]{:S(2)}) %collective-permute-start.5) | collective-permute-done | bytes 262176 | tf_op jit(solution)/shard_map/ppermute | solution.py:135
  27.4 1.6 collective-permute-start.8
  29.6 2.3 collective-permute-start.9
  32.0 3.0 collective-permute-start.11
  35.0 18.1 %collective-permute-done.10.refs_11_ = bf16[128,1024]{1,0:T(8,128)(2,1)S(1)} collective-permute-done((bf16[128,1024]{1,0:T(8,128)(2,1)S(1)}, bf16[128,1024]{1,0:T(8,128)(2,1)S(1)}, u32[]{:S(2)}, u32[]{:S(2)}) %collective-permute-start.10) | collective-permute-done | bytes 262176 | tf_op jit(solution)/shard_map/ppermute | solution.py:135
  55.3 2.0 collective-permute-start.12
  60.1 16.7 %collective-permute-done.14.refs_12_ = bf16[128,1024]{1,0:T(8,128)(2,1)S(1)} collective-permute-done((bf16[128,1024]{1,0:T(8,128)(2,1)S(1)}, bf16[128,1024]{1,0:T(8,128)(2,1)S(1)}, u32[]{:S(2)}, u32[]{:S(2)}) %collective-permute-start.14) | collective-permute-done | bytes 262176 | tf_op jit(solution)/shard_map/ppermute | solution.py:135
  77.5 2.2 collective-permute-done.12.refs_5_
  87.5 10.7 %project.1 = (bf16[512,3072]{1,0:T(8,128)(2,1)S(1)}, bf16[512,1024]{1,0:T(8,128)(2,1)S(1)}, bf16[1024,4224]{1,0:T(8,128)(2,1)S(1)}, f32[8,1024]{1,0:T(8,128)S(1)}) custom-call(s32[4]{0:T(128)S(1)} %pad_add_fusion.idx.refs_0_, bf16[4,32,4224]{2,1,0:T(8,128)(2,1)S(1)} %pad_maximum_fusion.refs_1_, bf16[4,32,4224]{2,1,0:T(8,128)(2,1)S(1)} %collective-permute-done.7.refs_2_, ...), custom_call_target="tpu_custom_call" | custom-call | flops 1000000000 | tf_op jit(solution)/shard_map/project/pallas_call | solution.py:269
  99.2 2.7 collective-permute-done.21.refs_14_
  101.9 5.3 %collective-permute-done.22.refs_7_ = bf16[2,128,1024]{2,1,0:T(8,128)(2,1)S(1)} collective-permute-done((bf16[2,128,1024]{2,1,0:T(8,128)(2,1)S(1)}, bf16[2,128,1024]{2,1,0:T(8,128)(2,1)S(1)}, u32[]{:S(2)}, u32[]{:S(2)}) %collective-permute-start.22) | collective-permute-done | bytes 524320 | tf_op jit(solution)/shard_map/ppermute | solution.py:135
  109.8 4.5 %attend.1.attended_ref.o_in = bf16[512,1024]{1,0:T(8,128)(2,1)S(1)} custom-call(bf16[512,3072]{1,0:T(8,128)(2,1)S(1)} %get-tuple-element.289.q_ref.k_ref.v_ref, bf16[512,3072]{1,0:T(8,128)(2,1)S(1)} %get-tuple-element.289.q_ref.k_ref.v_ref, bf16[512,3072]{1,0:T(8,128)(2,1)S(1)} %get-tuple-element.289.q_ref.k_ref.v_ref, s32[1,512]{1,0:T(1,128)S(1)} %iota_subtract_fusion.pos_ref), custom_call_target="tpu_custom_call" | custom-call | flops 1000000000 | tf_op jit(solution)/shard_map/attend/pallas_call | solution.py:470
  114.4 1.7 copy-done.1
  116.4 4.5 %collective-permute-done.25.refs_15_ = bf16[128,1024]{1,0:T(8,128)(2,1)S(1)} collective-permute-done((bf16[128,1024]{1,0:T(8,128)(2,1)S(1)}, bf16[128,1024]{1,0:T(8,128)(2,1)S(1)}, u32[]{:S(2)}, u32[]{:S(2)}) %collective-permute-start.25) | collective-permute-done | bytes 262176 | tf_op jit(solution)/shard_map/ppermute | solution.py:135
  123.0 2.2 leave.1
  126.0 3.9 %collective-permute-done.28.refs_16_ = bf16[128,1024]{1,0:T(8,128)(2,1)S(1)} collective-permute-done((bf16[128,1024]{1,0:T(8,128)(2,1)S(1)}, bf16[128,1024]{1,0:T(8,128)(2,1)S(1)}, u32[]{:S(2)}, u32[]{:S(2)}) %collective-permute-start.28) | collective-permute-done | bytes 262176 | tf_op jit(solution)/shard_map/ppermute | solution.py:135
  130.5 2.1 collective-permute-done.30.refs_18_.refs_2_.refs_3_
  134.7 20.0 %mlp_both.2 = (bf16[1024,1024]{1,0:T(8,128)(2,1)}, bf16[1024,1024]{1,0:T(8,128)(2,1)}, bf16[512,1024]{1,0:T(8,128)(2,1)S(1)}, bf16[512,1024]{1,0:T(8,128)(2,1)},...) custom-call(s32[4]{0:T(128)S(1)} %pad_add_fusion.idx.refs_0_, ...), custom_call_target="tpu_custom_call" | custom-call | flops 1000000000 | tf_op jit(solution)/shard_map/mlp_both/pallas_call | solution.py:661
  156.6 1.8 collective-permute-done.33.refs_18_.refs_6_.refs_7_
  159.4 20.1 %mlp_both.3 = (bf16[1024,1024]{1,0:T(8,128)(2,1)}, bf16[1024,1024]{1,0:T(8,128)(2,1)}, bf16[512,1024]{1,0:T(8,128)(2,1)S(1)}, bf16[512,1024]{1,0:T(8,128)(2,1)},...) custom-call(s32[4]{0:T(128)S(1)} %pad_add_fusion.idx.refs_0_, ...), custom_call_target="tpu_custom_call" | custom-call | flops 1000000000 | tf_op jit(solution)/shard_map/mlp_both/pallas_call | solution.py:661
  185.2 1.6 copy-done.40
  186.8 1.6 copy-done.42
  188.4 7.4 %weight_grad.2 = (bf16[4,128,1024]{2,1,0:T(8,128)(2,1)S(1)}, bf16[4,128,1024]{2,1,0:T(8,128)(2,1)S(1)}) custom-call(s32[4]{0:T(128)S(1)} %pad_add_fusion.idx.refs_0_, bf16[512,1024]{1,0:T(8,128)(2,1)S(1)} %copy-done.8, bf16[512,1024]{1,0:T(8,128)(2,1)S(1)} %copy-done.8, bf16[512,1024]{1,0:T(8,128)(2,1)S(1)} %copy-done.10, bf16[512,1024]{1,0:T(8,128)(2,1)S(1)} %copy-done.10, ...), custom_call_target="tpu_custom_call" | custom-call | flops 1000000000 | tf_op jit(solution)/shard_map/weight_grad/pallas_call | solution.py:723
  195.8 7.4 %weight_grad.3 = (bf16[4,128,1024]{2,1,0:T(8,128)(2,1)S(1)}, bf16[4,128,1024]{2,1,0:T(8,128)(2,1)S(1)}) custom-call(s32[4]{0:T(128)S(1)} %pad_add_fusion.idx.refs_0_, bf16[512,1024]{1,0:T(8,128)(2,1)S(1)} %copy-done.8, bf16[512,1024]{1,0:T(8,128)(2,1)S(1)} %copy-done.8, bf16[512,1024]{1,0:T(8,128)(2,1)S(1)} %copy-done.10, bf16[512,1024]{1,0:T(8,128)(2,1)S(1)} %copy-done.10, ...), custom_call_target="tpu_custom_call" | custom-call | flops 1000000000 | tf_op jit(solution)/shard_map/weight_grad/pallas_call | solution.py:723
  203.3 2.1 collective-permute-done.39.refs_2_.refs_1_
  209.6 5.6 %back.1 = (f32[512,1024]{1,0:T(8,128)S(1)}, bf16[512,1024]{1,0:T(8,128)(2,1)S(1)}, bf16[512,1024]{1,0:T(8,128)(2,1)S(1)}, f32[8,1024]{1,0:T(8,128)S(1)}) custom-call(bf16[512,1024]{1,0:T(8,128)(2,1)S(1)} %copy-done.65, bf16[512,1024]{1,0:T(8,128)(2,1)} %collective-permute-done.34.b_ref, bf16[512,1024]{1,0:T(8,128)(2,1)S(1)} %collective-permute-done.37.c_ref, ...), custom_call_target="tpu_custom_call" | custom-call | flops 1000000000 | tf_op jit(solution)/shard_map/back/pallas_call | solution.py:369
  216.3 14.9 %attend_back.1 = (bf16[512,1024]{1,0:T(8,128)(2,1)S(1)}, bf16[512,1024]{1,0:T(8,128)(2,1)S(1)}, bf16[512,1024]{1,0:T(8,128)(2,1)S(1)}) custom-call(bf16[512,3072]{1,0:T(8,128)(2,1)S(1)} %copy-done.2, bf16[512,3072]{1,0:T(8,128)(2,1)S(1)} %copy-done.2, bf16[512,3072]{1,0:T(8,128)(2,1)S(1)} %copy-done.2, bf16[512,1024]{1,0:T(8,128)(2,1)S(1)} %get-tuple-element.358.do_ref, ...), custom_call_target="tpu_custom_call" | custom-call | flops 1000000000 | tf_op jit(solution)/shard_map/attend_back/pallas_call | solution.py:530
  232.3 1.9 collective-permute-start.43
  234.2 6.5 %attn_grad.1 = (bf16[2,4,32,1024]{3,2,1,0:T(8,128)(2,1)S(1)}, bf16[2,4,32,1024]{3,2,1,0:T(8,128)(2,1)S(1)}, bf16[2,4,32,2048]{3,2,1,0:T(8,128)(2,1)}, bf16[2,4,3...) custom-call(s32[4]{0:T(128)S(1)} %pad_add_fusion.idx.refs_0_, ...), custom_call_target="tpu_custom_call" | custom-call | flops 1000000000 | tf_op jit(solution)/shard_map/attn_grad/pallas_call | solution.py:769
  241.7 10.5 %collective-permute-done.40.refs_5_.refs_1_ = bf16[4,128,1024]{2,1,0:T(8,128)(2,1)S(1)} collective-permute-done((bf16[4,128,1024]{2,1,0:T(8,128)(2,1)S(1)}, bf16[4,128,1024]{2,1,0:T(8,128)(2,1)S(1)}, u32[]{:S(2)}, u32[]{:S(2)}) %collective-permute-start.40) | collective-permute-done | bytes 1048608 | tf_op jit(solution)/shard_map/ppermute | solution.py:135
  257.0 2.5 first_sum.1
  262.5 2.0 collective-permute-start.54
  264.6 11.5 %last.1 = (f32[512,1024]{1,0:T(8,128)}, bf16[512,1024]{1,0:T(8,128)(2,1)}, f32[8,1024]{1,0:T(8,128)S(1)}) custom-call(bf16[512,1024]{1,0:T(8,128)(2,1)S(1)} %get-tuple-element.409.dq.refs_0_, bf16[512,1024]{1,0:T(8,128)(2,1)S(1)} %get-tuple-element.410.dk.refs_1_, bf16[512,1024]{1,0:T(8,128)(2,1)S(1)} %get-tuple-element.411.dv.refs_2_, ...), custom_call_target="tpu_custom_call" | custom-call | flops 1000000000 | tf_op jit(solution)/shard_map/last/pallas_call | solution.py:405
  278.1 8.3 %collective-permute-done.56 = f32[8,1024]{1,0:T(8,128)S(1)} collective-permute-done((f32[8,1024]{1,0:T(8,128)S(1)}, f32[8,1024]{1,0:T(8,128)S(1)}, u32[]{:S(2)}, u32[]{:S(2)}) %collective-permute-start.56) | collective-permute-done | bytes 32800 | tf_op jit(solution)/shard_map/ppermute | solution.py:135
  287.5 2.0 second_sum.1
  290.3 1.6 collective-permute-start.57
  294.1 5.5 %stay_sum.1 = (bf16[4,32,2048]{2,1,0:T(8,128)(2,1)}, bf16[4,32,2048]{2,1,0:T(8,128)(2,1)}, bf16[2,128,1024]{2,1,0:T(8,128)(2,1)}) custom-call(s32[4]{0:T(128)} %copy-done.82, bf16[2,4,32,2048]{3,2,1,0:T(8,128)(2,1)} %copy-done.29, bf16[2,4,32,2048]{3,2,1,0:T(8,128)(2,1)} %copy-done.31, bf16[2,4,32,2048]{3,2,1,0:T(8,128)(2,1)} %copy-done.33, ...), custom_call_target="tpu_custom_call" | custom-call | flops 1000000000 | tf_op jit(solution)/shard_map/stay_sum/pallas_call | solution.py:930
  299.6 4.1 %collective-permute-done.59 = f32[8,1024]{1,0:T(8,128)S(1)} collective-permute-done((f32[8,1024]{1,0:T(8,128)S(1)}, f32[8,1024]{1,0:T(8,128)S(1)}, u32[]{:S(2)}, u32[]{:S(2)}) %collective-permute-start.59) | collective-permute-done | bytes 32800 | tf_op jit(solution)/shard_map/ppermute | solution.py:135
  310.5 2.5 collective-permute-start.61
  314.4 9.7 %collective-permute-done.61 = bf16[32,4224]{1,0:T(8,128)(2,1)S(1)} collective-permute-done((bf16[32,4224]{1,0:T(8,128)(2,1)S(1)}, bf16[32,4224]{1,0:T(8,128)(2,1)S(1)}, u32[]{:S(2)}, u32[]{:S(2)}) %collective-permute-start.61) | collective-permute-done | bytes 270368 | tf_op jit(solution)/shard_map/ppermute | solution.py:135
  324.1 7.8 %collective-permute-done.62 = bf16[32,4224]{1,0:T(8,128)(2,1)S(1)} collective-permute-done((bf16[32,4224]{1,0:T(8,128)(2,1)S(1)}, bf16[32,4224]{1,0:T(8,128)(2,1)S(1)}, u32[]{:S(2)}, u32[]{:S(2)}) %collective-permute-start.62) | collective-permute-done | bytes 270368 | tf_op jit(solution)/shard_map/ppermute | solution.py:135
  331.9 6.5 %collective-permute-done.63 = bf16[32,4224]{1,0:T(8,128)(2,1)S(1)} collective-permute-done((bf16[32,4224]{1,0:T(8,128)(2,1)S(1)}, bf16[32,4224]{1,0:T(8,128)(2,1)S(1)}, u32[]{:S(2)}, u32[]{:S(2)}) %collective-permute-start.63) | collective-permute-done | bytes 270368 | tf_op jit(solution)/shard_map/ppermute | solution.py:135
  340.9 3.9 %place_mlp.1 = (f32[4,128,1024]{2,1,0:T(8,128)}, f32[128,4096]{1,0:T(8,128)}, f32[128,4096]{1,0:T(8,128)}) custom-call(s32[4]{0:T(128)S(1)} %copy-done.83, bf16[3,128,1024]{2,1,0:T(8,128)(2,1)S(1)} %get-tuple-element.470.own_ref, bf16[3,128,1024]{2,1,0:T(8,128)(2,1)S(1)} %collective-permute-done.64.y_ref, ...), custom_call_target="tpu_custom_call" | custom-call | flops 1000000000 | tf_op jit(solution)/shard_map/place_mlp/pallas_call | solution.py:1051
  344.8 2.8 collective-permute-done.66.refs_2_
  349.1 1.9 place_rows.1
  (324 shorter events, 79.2 us)
Async XLA Ops:
  2.5 24.0 %collective-permute-start.2 = (bf16[1,32,4224]{2,1,0:T(8,128)(2,1)S(1)}, bf16[1,32,4224]{2,1,0:T(8,128)(2,1)S(1)}, u32[]{:S(2)}, u32[]{:S(2)}) collective-permute-start(bf16[1,32,4224]{2,1,0:T(8,128)(2,1)S(1)} %fusion.2), channel_id=1, source_target_pairs={{0,24},{1,25},{2,26},{3,27},{4,28},{5,29},{6,30},{7,31},{8,16},{9,... | collective-permute-start | bytes 811016 | tf_op jit(solution)/shard_map/ppermute | solution.py:135
  4.1 23.1 %collective-permute-start.1 = (bf16[1,32,4224]{2,1,0:T(8,128)(2,1)S(1)}, bf16[1,32,4224]{2,1,0:T(8,128)(2,1)S(1)}, u32[]{:S(2)}, u32[]{:S(2)}) collective-permute-start(bf16[1,32,4224]{2,1,0:T(8,128)(2,1)S(1)} %fusion.2), channel_id=1, source_target_pairs={{0,16},{1,17},{2,18},{3,19},{4,20},{5,21},{6,22},{7,23},{8,24},{9,... | collective-permute-start | bytes 811016 | tf_op jit(solution)/shard_map/ppermute | solution.py:135
  5.4 21.9 %collective-permute-start = (bf16[1,32,4224]{2,1,0:T(8,128)(2,1)S(1)}, bf16[1,32,4224]{2,1,0:T(8,128)(2,1)S(1)}, u32[]{:S(2)}, u32[]{:S(2)}) collective-permute-start(bf16[1,32,4224]{2,1,0:T(8,128)(2,1)S(1)} %fusion.2), channel_id=1, source_target_pairs={{0,8},{1,9},{2,10},{3,11},{4,12},{5,13},{6,14},{7,15},{8,0},{9,1},... | collective-permute-start | bytes 811016 | tf_op jit(solution)/shard_map/ppermute | solution.py:135
  7.7 13.3 %collective-permute-start.6 = (bf16[2,32,4096]{2,1,0:T(8,128)(2,1)S(1)}, bf16[2,32,4096]{2,1,0:T(8,128)(2,1)}, u32[]{:S(2)}, u32[]{:S(2)}) collective-permute-start(bf16[2,32,4096]{2,1,0:T(8,128)(2,1)S(1)} %pad_maximum_fusion.2.raw_ref), channel_id=1, source_target_pairs={{0,4},{1,5},{2,6},{3,7},{4,0},{5,1},{6,2},{7,3},{8,12},{9,13},{10,... | collective-permute-start | bytes 1572872 | tf_op jit(solution)/shard_map/ppermute | solution.py:135
  18.0 8.5 %collective-permute-start.5 = (bf16[128,1024]{1,0:T(8,128)(2,1)S(1)}, bf16[128,1024]{1,0:T(8,128)(2,1)S(1)}, u32[]{:S(2)}, u32[]{:S(2)}) collective-permute-start(bf16[128,1024]{1,0:T(8,128)(2,1)S(1)} %copy-done.66), channel_id=1, source_target_pairs={{0,4},{1,5},{2,6},{3,7},{4,0},{5,1},{6,2},{7,3},{8,12},{9,13},{10,... | collective-permute-start | bytes 786440 | tf_op jit(solution)/shard_map/ppermute | solution.py:135
  27.4 27.2 %collective-permute-start.8 = (bf16[4,32,4224]{2,1,0:T(8,128)(2,1)S(1)}, bf16[4,32,4224]{2,1,0:T(8,128)(2,1)S(1)}, u32[]{:S(2)}, u32[]{:S(2)}) collective-permute-start(bf16[4,32,4224]{2,1,0:T(8,128)(2,1)S(1)} %pad_maximum_fusion.refs_1_), channel_id=1, source_target_pairs={{0,2},{1,3},{2,0},{3,1},{4,6},{5,7},{6,4},{7,5},{8,10},{9,11},{10,... | collective-permute-start | bytes 3244040 | tf_op jit(solution)/shard_map/ppermute | solution.py:135
  29.0 25.7 %collective-permute-start.7 = (bf16[4,32,4224]{2,1,0:T(8,128)(2,1)S(1)}, bf16[4,32,4224]{2,1,0:T(8,128)(2,1)S(1)}, u32[]{:S(2)}, u32[]{:S(2)}) collective-permute-start(bf16[4,32,4224]{2,1,0:T(8,128)(2,1)S(1)} %pad_maximum_fusion.refs_1_), channel_id=1, source_target_pairs={{0,4},{1,5},{2,6},{3,7},{4,0},{5,1},{6,2},{7,3},{8,12},{9,13},{10,... | collective-permute-start | bytes 3244040 | tf_op jit(solution)/shard_map/ppermute | solution.py:135
  29.6 25.0 %collective-permute-start.9 = (bf16[2,128,1024]{2,1,0:T(8,128)(2,1)S(1)}, bf16[2,128,1024]{2,1,0:T(8,128)(2,1)S(1)}, u32[]{:S(2)}, u32[]{:S(2)}) collective-permute-start(bf16[2,128,1024]{2,1,0:T(8,128)(2,1)S(1)} %join.2.refs_1_), channel_id=1, source_target_pairs={{0,8},{1,9},{2,10},{3,11},{4,12},{5,13},{6,14},{7,15},{8,0},{9,1},... | collective-permute-start | bytes 1572872 | tf_op jit(solution)/shard_map/ppermute | solution.py:135
  31.9 21.2 %collective-permute-start.10 = (bf16[128,1024]{1,0:T(8,128)(2,1)S(1)}, bf16[128,1024]{1,0:T(8,128)(2,1)S(1)}, u32[]{:S(2)}, u32[]{:S(2)}) collective-permute-start(bf16[128,1024]{1,0:T(8,128)(2,1)S(1)} %copy-done.66), channel_id=1, source_target_pairs={{0,8},{1,9},{2,10},{3,11},{4,12},{5,13},{6,14},{7,15},{8,0},{9,1},... | collective-permute-start | bytes 786440 | tf_op jit(solution)/shard_map/ppermute | solution.py:135
  32.0 22.7 %collective-permute-start.11 = (bf16[128,1024]{1,0:T(8,128)(2,1)S(1)}, bf16[128,1024]{1,0:T(8,128)(2,1)S(1)}, u32[]{:S(2)}, u32[]{:S(2)}) collective-permute-start(bf16[128,1024]{1,0:T(8,128)(2,1)S(1)} %copy-done.66), channel_id=1, source_target_pairs={{0,16},{1,17},{2,18},{3,19},{4,20},{5,21},{6,22},{7,23},{8,24},{9,... | collective-permute-start | bytes 786440 | tf_op jit(solution)/shard_map/ppermute | solution.py:135
  54.7 24.9 %collective-permute-start.15 = (bf16[4,32,4224]{2,1,0:T(8,128)(2,1)S(1)}, bf16[4,32,4224]{2,1,0:T(8,128)(2,1)S(1)}, u32[]{:S(2)}, u32[]{:S(2)}) collective-permute-start(bf16[4,32,4224]{2,1,0:T(8,128)(2,1)S(1)} %pad_maximum_fusion.refs_1_), channel_id=1, source_target_pairs={{0,1},{1,0},{2,3},{3,2},{4,5},{5,4},{6,7},{7,6},{8,9},{9,8},{10,11... | collective-permute-start | bytes 3244040 | tf_op jit(solution)/shard_map/ppermute | solution.py:135
  54.8 26.3 %collective-permute-start.16 = (bf16[4,32,4224]{2,1,0:T(8,128)(2,1)S(1)}, bf16[4,32,4224]{2,1,0:T(8,128)(2,1)S(1)}, u32[]{:S(2)}, u32[]{:S(2)}) collective-permute-start(bf16[4,32,4224]{2,1,0:T(8,128)(2,1)S(1)} %collective-permute-done.7.refs_2_), channel_id=1, source_target_pairs={{0,2},{1,3},{2,0},{3,1},{4,6},{5,7},{6,4},{7,5},{8,10},{9,11},{10,... | collective-permute-start | bytes 3244040 | tf_op jit(solution)/shard_map/ppermute | solution.py:135
  55.3 24.3 %collective-permute-start.12 = (bf16[2,128,1024]{2,1,0:T(8,128)(2,1)S(1)}, bf16[2,128,1024]{2,1,0:T(8,128)(2,1)S(1)}, u32[]{:S(2)}, u32[]{:S(2)}) collective-permute-start(bf16[2,128,1024]{2,1,0:T(8,128)(2,1)S(1)} %join.2.refs_1_), channel_id=1, source_target_pairs={{0,16},{1,17},{2,18},{3,19},{4,20},{5,21},{6,22},{7,23},{8,24},{9,... | collective-permute-start | bytes 1572872 | tf_op jit(solution)/shard_map/ppermute | solution.py:135
  57.4 22.3 %collective-permute-start.13 = (bf16[2,128,1024]{2,1,0:T(8,128)(2,1)S(1)}, bf16[2,128,1024]{2,1,0:T(8,128)(2,1)S(1)}, u32[]{:S(2)}, u32[]{:S(2)}) collective-permute-start(bf16[2,128,1024]{2,1,0:T(8,128)(2,1)S(1)} %collective-permute-done.9.refs_3_), channel_id=1, source_target_pairs={{0,4},{1,5},{2,6},{3,7},{4,0},{5,1},{6,2},{7,3},{8,12},{9,13},{10,... | collective-permute-start | bytes 1572872 | tf_op jit(solution)/shard_map/ppermute | solution.py:135
  58.6 18.2 %collective-permute-start.14 = (bf16[128,1024]{1,0:T(8,128)(2,1)S(1)}, bf16[128,1024]{1,0:T(8,128)(2,1)S(1)}, u32[]{:S(2)}, u32[]{:S(2)}) collective-permute-start(bf16[128,1024]{1,0:T(8,128)(2,1)S(1)} %collective-permute-done.10.refs_11_), channel_id=1, source_target_pairs={{0,4},{1,5},{2,6},{3,7},{4,0},{5,1},{6,2},{7,3},{8,12},{9,13},{10,... | collective-permute-start | bytes 786440 | tf_op jit(solution)/shard_map/ppermute | solution.py:135
  81.6 25.6 %collective-permute-start.22 = (bf16[2,128,1024]{2,1,0:T(8,128)(2,1)S(1)}, bf16[2,128,1024]{2,1,0:T(8,128)(2,1)S(1)}, u32[]{:S(2)}, u32[]{:S(2)}) collective-permute-start(bf16[2,128,1024]{2,1,0:T(8,128)(2,1)S(1)} %join.2.refs_1_), channel_id=1, source_target_pairs={{0,24},{1,25},{2,26},{3,27},{4,28},{5,29},{6,30},{7,31},{8,16},{9,... | collective-permute-start | bytes 1572872 | tf_op jit(solution)/shard_map/ppermute | solution.py:135
  82.2 24.9 %collective-permute-start.20 = (bf16[2,128,1024]{2,1,0:T(8,128)(2,1)S(1)}, bf16[2,128,1024]{2,1,0:T(8,128)(2,1)S(1)}, u32[]{:S(2)}, u32[]{:S(2)}) collective-permute-start(bf16[2,128,1024]{2,1,0:T(8,128)(2,1)S(1)} %collective-permute-done.12.refs_5_), channel_id=1, source_target_pairs={{0,4},{1,5},{2,6},{3,7},{4,0},{5,1},{6,2},{7,3},{8,12},{9,13},{10,... | collective-permute-start | bytes 1572872 | tf_op jit(solution)/shard_map/ppermute | solution.py:135
  83.7 32.3 %collective-permute-start.23 = (bf16[512,1024]{1,0:T(8,128)(2,1)S(1)}, bf16[512,1024]{1,0:T(8,128)(2,1)}, u32[]{:S(2)}, u32[]{:S(2)}) collective-permute-start(bf16[512,1024]{1,0:T(8,128)(2,1)S(1)} %copy-done.16), channel_id=1, source_target_pairs={{0,2},{1,3},{2,0},{3,1},{4,6},{5,7},{6,4},{7,5},{8,10},{9,11},{10,... | collective-permute-start | bytes 3145736 | tf_op jit(solution)/shard_map/ppermute | solution.py:135
  85.3 16.6 %collective-permute-start.21 = (bf16[128,1024]{1,0:T(8,128)(2,1)S(1)}, bf16[128,1024]{1,0:T(8,128)(2,1)S(1)}, u32[]{:S(2)}, u32[]{:S(2)}) collective-permute-start(bf16[128,1024]{1,0:T(8,128)(2,1)S(1)} %collective-permute-done.11.refs_13_), channel_id=1, source_target_pairs={{0,4},{1,5},{2,6},{3,7},{4,0},{5,1},{6,2},{7,3},{8,12},{9,13},{10,... | collective-permute-start | bytes 786440 | tf_op jit(solution)/shard_map/ppermute | solution.py:135
  107.1 13.8 %collective-permute-start.24 = (bf16[2,128,1024]{2,1,0:T(8,128)(2,1)S(1)}, bf16[2,128,1024]{2,1,0:T(8,128)(2,1)S(1)}, u32[]{:S(2)}, u32[]{:S(2)}) collective-permute-start(bf16[2,128,1024]{2,1,0:T(8,128)(2,1)S(1)} %collective-permute-done.22.refs_7_), channel_id=1, source_target_pairs={{0,4},{1,5},{2,6},{3,7},{4,0},{5,1},{6,2},{7,3},{8,12},{9,13},{10,... | collective-permute-start | bytes 1572872 | tf_op jit(solution)/shard_map/ppermute | solution.py:135
  109.2 11.7 %collective-permute-start.25 = (bf16[128,1024]{1,0:T(8,128)(2,1)S(1)}, bf16[128,1024]{1,0:T(8,128)(2,1)S(1)}, u32[]{:S(2)}, u32[]{:S(2)}) collective-permute-start(bf16[128,1024]{1,0:T(8,128)(2,1)S(1)} %copy-done.66), channel_id=1, source_target_pairs={{0,24},{1,25},{2,26},{3,27},{4,28},{5,29},{6,30},{7,31},{8,16},{9,... | collective-permute-start | bytes 786440 | tf_op jit(solution)/shard_map/ppermute | solution.py:135
  120.9 9.0 %collective-permute-start.29 = (bf16[512,1024]{1,0:T(8,128)(2,1)S(1)}, bf16[512,1024]{1,0:T(8,128)(2,1)S(1)}, u32[]{:S(2)}, u32[]{:S(2)}) collective-permute-start(bf16[512,1024]{1,0:T(8,128)(2,1)S(1)} %copy-done.16), channel_id=1, source_target_pairs={{0,1},{1,0},{2,3},{3,2},{4,5},{5,4},{6,7},{7,6},{8,9},{9,8},{10,11... | collective-permute-start | bytes 3145736 | tf_op jit(solution)/shard_map/ppermute | solution.py:135
  129.9 25.8 %collective-permute-start.31 = (bf16[512,1024]{1,0:T(8,128)(2,1)S(1)}, bf16[512,1024]{1,0:T(8,128)(2,1)S(1)}, u32[]{:S(2)}, u32[]{:S(2)}) collective-permute-start(bf16[512,1024]{1,0:T(8,128)(2,1)S(1)} %get-tuple-element.313.refs_17_.refs_0_.refs_1_), channel_id=1, source_target_pairs={{0,2},{1,3},{2,0},{3,1},{4,6},{5,7},{6,4},{7,5},{8,10},{9,11},{10,... | collective-permute-start | bytes 3145736 | tf_op jit(solution)/shard_map/ppermute | solution.py:135
  133.5 22.1 %collective-permute-start.32 = (bf16[512,1024]{1,0:T(8,128)(2,1)}, bf16[512,1024]{1,0:T(8,128)(2,1)}, u32[]{:S(2)}, u32[]{:S(2)}) collective-permute-start(bf16[512,1024]{1,0:T(8,128)(2,1)} %collective-permute-done.23.refs_19_), channel_id=1, source_target_pairs={{0,1},{1,0},{2,3},{3,2},{4,5},{5,4},{6,7},{7,6},{8,9},{9,8},{10,11... | collective-permute-start | bytes 3145736 | tf_op jit(solution)/shard_map/ppermute | solution.py:135
  156.1 23.4 %collective-permute-start.35 = (bf16[512,1024]{1,0:T(8,128)(2,1)}, bf16[512,1024]{1,0:T(8,128)(2,1)}, u32[]{:S(2)}, u32[]{:S(2)}) collective-permute-start(bf16[512,1024]{1,0:T(8,128)(2,1)} %get-tuple-element.329), channel_id=1, source_target_pairs={{0,1},{1,0},{2,3},{3,2},{4,5},{5,4},{6,7},{7,6},{8,9},{9,8},{10,11... | collective-permute-start | bytes 3145736 | tf_op jit(solution)/shard_map/ppermute | solution.py:135
  156.3 23.3 %collective-permute-start.34 = (bf16[512,1024]{1,0:T(8,128)(2,1)}, bf16[512,1024]{1,0:T(8,128)(2,1)}, u32[]{:S(2)}, u32[]{:S(2)}) collective-permute-start(bf16[512,1024]{1,0:T(8,128)(2,1)} %get-tuple-element.328), channel_id=1, source_target_pairs={{0,1},{1,0},{2,3},{3,2},{4,5},{5,4},{6,7},{7,6},{8,9},{9,8},{10,11... | collective-permute-start | bytes 3145736 | tf_op jit(solution)/shard_map/ppermute | solution.py:135
  180.0 25.4 %collective-permute-start.39 = (bf16[4,128,1024]{2,1,0:T(8,128)(2,1)}, bf16[4,128,1024]{2,1,0:T(8,128)(2,1)S(1)}, u32[]{:S(2)}, u32[]{:S(2)}) collective-permute-start(bf16[4,128,1024]{2,1,0:T(8,128)(2,1)} %get-tuple-element.348), channel_id=1, source_target_pairs={{0,4},{1,5},{2,6},{3,7},{4,0},{5,1},{6,2},{7,3},{8,12},{9,13},{10,... | collective-permute-start | bytes 3145736 | tf_op jit(solution)/shard_map/ppermute | solution.py:135
  182.9 22.5 %collective-permute-start.38 = (bf16[512,1024]{1,0:T(8,128)(2,1)}, bf16[512,1024]{1,0:T(8,128)(2,1)S(1)}, u32[]{:S(2)}, u32[]{:S(2)}) collective-permute-start(bf16[512,1024]{1,0:T(8,128)(2,1)} %get-tuple-element.347), channel_id=1, source_target_pairs={{0,1},{1,0},{2,3},{3,2},{4,5},{5,4},{6,7},{7,6},{8,9},{9,8},{10,11... | collective-permute-start | bytes 3145736 | tf_op jit(solution)/shard_map/ppermute | solution.py:135
  183.3 25.2 %collective-permute-start.37 = (bf16[512,1024]{1,0:T(8,128)(2,1)S(1)}, bf16[512,1024]{1,0:T(8,128)(2,1)S(1)}, u32[]{:S(2)}, u32[]{:S(2)}) collective-permute-start(bf16[512,1024]{1,0:T(8,128)(2,1)S(1)} %add_convert_fusion.1), channel_id=1, source_target_pairs={{0,2},{1,3},{2,0},{3,1},{4,6},{5,7},{6,4},{7,5},{8,10},{9,11},{10,... | collective-permute-start | bytes 3145736 | tf_op jit(solution)/shard_map/ppermute | solution.py:135
  205.4 26.1 %collective-permute-start.41 = (bf16[4,128,1024]{2,1,0:T(8,128)(2,1)S(1)}, bf16[4,128,1024]{2,1,0:T(8,128)(2,1)S(1)}, u32[]{:S(2)}, u32[]{:S(2)}) collective-permute-start(bf16[4,128,1024]{2,1,0:T(8,128)(2,1)S(1)} %get-tuple-element.360), channel_id=1, source_target_pairs={{0,4},{1,5},{2,6},{3,7},{4,0},{5,1},{6,2},{7,3},{8,12},{9,13},{10,... | collective-permute-start | bytes 3145736 | tf_op jit(solution)/shard_map/ppermute | solution.py:135
  208.5 22.7 %collective-permute-start.42 = (bf16[1,2,128,1024]{3,2,1,0:T(8,128)(2,1)S(1)}, bf16[1,2,128,1024]{3,2,1,0:T(8,128)(2,1)S(1)}, u32[]{:S(2)}, u32[]{:S(2)}) collective-permute-start(bf16[1,2,128,1024]{3,2,1,0:T(8,128)(2,1)S(1)} %near_sum.2), channel_id=1, source_target_pairs={{0,8},{1,9},{2,10},{3,11},{4,12},{5,13},{6,14},{7,15},{8,0},{9,1},... | collective-permute-start | bytes 1572872 | tf_op jit(solution)/shard_map/ppermute | solution.py:135
  208.5 32.2 %collective-permute-start.44 = (bf16[512,1024]{1,0:T(8,128)(2,1)S(1)}, bf16[512,1024]{1,0:T(8,128)(2,1)S(1)}, u32[]{:S(2)}, u32[]{:S(2)}) collective-permute-start(bf16[512,1024]{1,0:T(8,128)(2,1)S(1)} %add_convert_fusion), channel_id=1, source_target_pairs={{0,2},{1,3},{2,0},{3,1},{4,6},{5,7},{6,4},{7,5},{8,10},{9,11},{10,... | collective-permute-start | bytes 3145736 | tf_op jit(solution)/shard_map/ppermute | solution.py:135
  215.2 37.0 %collective-permute-start.40 = (bf16[4,128,1024]{2,1,0:T(8,128)(2,1)S(1)}, bf16[4,128,1024]{2,1,0:T(8,128)(2,1)S(1)}, u32[]{:S(2)}, u32[]{:S(2)}) collective-permute-start(bf16[4,128,1024]{2,1,0:T(8,128)(2,1)S(1)} %get-tuple-element.356), channel_id=1, source_target_pairs={{0,4},{1,5},{2,6},{3,7},{4,0},{5,1},{6,2},{7,3},{8,12},{9,13},{10,... | collective-permute-start | bytes 3145736 | tf_op jit(solution)/shard_map/ppermute | solution.py:135
  232.3 19.9 %collective-permute-start.43 = (bf16[1,2,128,1024]{3,2,1,0:T(8,128)(2,1)S(1)}, bf16[1,2,128,1024]{3,2,1,0:T(8,128)(2,1)S(1)}, u32[]{:S(2)}, u32[]{:S(2)}) collective-permute-start(bf16[1,2,128,1024]{3,2,1,0:T(8,128)(2,1)S(1)} %near_sum.3), channel_id=1, source_target_pairs={{0,8},{1,9},{2,10},{3,11},{4,12},{5,13},{6,14},{7,15},{8,0},{9,1},... | collective-permute-start | bytes 1572872 | tf_op jit(solution)/shard_map/ppermute | solution.py:135
  260.5 26.9 %collective-permute-start.52 = (bf16[2,4,32,2048]{3,2,1,0:T(8,128)(2,1)S(1)}, bf16[2,4,32,2048]{3,2,1,0:T(8,128)(2,1)S(1)}, u32[]{:S(2)}, u32[]{:S(2)}) collective-permute-start(bf16[2,4,32,2048]{3,2,1,0:T(8,128)(2,1)S(1)} %get-tuple-element.422), channel_id=1, source_target_pairs={{0,4},{1,5},{2,6},{3,7},{4,0},{5,1},{6,2},{7,3},{8,12},{9,13},{10,... | collective-permute-start | bytes 3145736 | tf_op jit(solution)/shard_map/ppermute | solution.py:135
  261.9 25.5 %collective-permute-start.53 = (bf16[2,4,32,2048]{3,2,1,0:T(8,128)(2,1)S(1)}, bf16[2,4,32,2048]{3,2,1,0:T(8,128)(2,1)S(1)}, u32[]{:S(2)}, u32[]{:S(2)}) collective-permute-start(bf16[2,4,32,2048]{3,2,1,0:T(8,128)(2,1)S(1)} %get-tuple-element.423), channel_id=1, source_target_pairs={{0,2},{1,3},{2,0},{3,1},{4,6},{5,7},{6,4},{7,5},{8,10},{9,11},{10,... | collective-permute-start | bytes 3145736 | tf_op jit(solution)/shard_map/ppermute | solution.py:135
  262.5 23.9 %collective-permute-start.51 = (bf16[2,128,1024]{2,1,0:T(8,128)(2,1)}, bf16[2,128,1024]{2,1,0:T(8,128)(2,1)S(1)}, u32[]{:S(2)}, u32[]{:S(2)}) collective-permute-start(bf16[2,128,1024]{2,1,0:T(8,128)(2,1)} %get-tuple-element.421), channel_id=1, source_target_pairs={{0,16},{1,17},{2,18},{3,19},{4,20},{5,21},{6,22},{7,23},{8,24},{9,... | collective-permute-start | bytes 1572872 | tf_op jit(solution)/shard_map/ppermute | solution.py:135
  262.5 24.9 %collective-permute-start.54 = (bf16[2,128,1024]{2,1,0:T(8,128)(2,1)}, bf16[2,128,1024]{2,1,0:T(8,128)(2,1)S(1)}, u32[]{:S(2)}, u32[]{:S(2)}) collective-permute-start(bf16[2,128,1024]{2,1,0:T(8,128)(2,1)} %get-tuple-element.424), channel_id=1, source_target_pairs={{0,8},{1,9},{2,10},{3,11},{4,12},{5,13},{6,14},{7,15},{8,0},{9,1},... | collective-permute-start | bytes 1572872 | tf_op jit(solution)/shard_map/ppermute | solution.py:135
  277.3 9.1 %collective-permute-start.56 = (f32[8,1024]{1,0:T(8,128)S(1)}, f32[8,1024]{1,0:T(8,128)S(1)}, u32[]{:S(2)}, u32[]{:S(2)}) collective-permute-start(f32[8,1024]{1,0:T(8,128)S(1)} %add.85), channel_id=1, source_target_pairs={{0,4},{1,5},{2,6},{3,7},{4,0},{5,1},{6,2},{7,3},{8,12},{9,13},{10,... | collective-permute-start | bytes 98312 | tf_op jit(solution)/shard_map/ppermute | solution.py:135
  290.3 13.7 %collective-permute-start.57 = (bf16[4,32,2048]{2,1,0:T(8,128)(2,1)}, bf16[4,32,2048]{2,1,0:T(8,128)(2,1)S(1)}, u32[]{:S(2)}, u32[]{:S(2)}) collective-permute-start(bf16[4,32,2048]{2,1,0:T(8,128)(2,1)} %get-tuple-element.443), channel_id=1, source_target_pairs={{0,2},{1,3},{2,0},{3,1},{4,6},{5,7},{6,4},{7,5},{8,10},{9,11},{10,... | collective-permute-start | bytes 1572872 | tf_op jit(solution)/shard_map/ppermute | solution.py:135
  291.9 12.6 %collective-permute-start.58 = (bf16[4,32,2048]{2,1,0:T(8,128)(2,1)}, bf16[4,32,2048]{2,1,0:T(8,128)(2,1)}, u32[]{:S(2)}, u32[]{:S(2)}) collective-permute-start(bf16[4,32,2048]{2,1,0:T(8,128)(2,1)} %get-tuple-element.444), channel_id=1, source_target_pairs={{0,4},{1,5},{2,6},{3,7},{4,0},{5,1},{6,2},{7,3},{8,12},{9,13},{10,... | collective-permute-start | bytes 1572872 | tf_op jit(solution)/shard_map/ppermute | solution.py:135
  292.7 11.0 %collective-permute-start.59 = (f32[8,1024]{1,0:T(8,128)S(1)}, f32[8,1024]{1,0:T(8,128)S(1)}, u32[]{:S(2)}, u32[]{:S(2)}) collective-permute-start(f32[8,1024]{1,0:T(8,128)S(1)} %add.86), channel_id=1, source_target_pairs={{0,2},{1,3},{2,0},{3,1},{4,6},{5,7},{6,4},{7,5},{8,10},{9,11},{10,... | collective-permute-start | bytes 98312 | tf_op jit(solution)/shard_map/ppermute | solution.py:135
  293.1 10.9 %collective-permute-start.60 = (bf16[128,1024]{1,0:T(8,128)(2,1)}, bf16[128,1024]{1,0:T(8,128)(2,1)S(1)}, u32[]{:S(2)}, u32[]{:S(2)}) collective-permute-start(bf16[128,1024]{1,0:T(8,128)(2,1)} %copy-done.84), channel_id=1, source_target_pairs={{0,16},{1,17},{2,18},{3,19},{4,20},{5,21},{6,22},{7,23},{8,24},{9,... | collective-permute-start | bytes 786440 | tf_op jit(solution)/shard_map/ppermute | solution.py:135
  309.1 29.3 %collective-permute-start.65 = (bf16[3,128,1024]{2,1,0:T(8,128)(2,1)S(1)}, bf16[3,128,1024]{2,1,0:T(8,128)(2,1)S(1)}, u32[]{:S(2)}, u32[]{:S(2)}) collective-permute-start(bf16[3,128,1024]{2,1,0:T(8,128)(2,1)S(1)} %get-tuple-element.470.own_ref), channel_id=1, source_target_pairs={{0,1},{1,0},{2,3},{3,2},{4,5},{5,4},{6,7},{7,6},{8,9},{9,8},{10,11... | collective-permute-start | bytes 2359304 | tf_op jit(solution)/shard_map/ppermute | solution.py:135
  309.2 29.2 %collective-permute-start.64 = (bf16[3,128,1024]{2,1,0:T(8,128)(2,1)S(1)}, bf16[3,128,1024]{2,1,0:T(8,128)(2,1)S(1)}, u32[]{:S(2)}, u32[]{:S(2)}) collective-permute-start(bf16[3,128,1024]{2,1,0:T(8,128)(2,1)S(1)} %get-tuple-element.470.own_ref), channel_id=1, source_target_pairs={{0,2},{1,3},{2,0},{3,1},{4,6},{5,7},{6,4},{7,5},{8,10},{9,11},{10,... | collective-permute-start | bytes 2359304 | tf_op jit(solution)/shard_map/ppermute | solution.py:135
  310.5 13.6 %collective-permute-start.61 = (bf16[32,4224]{1,0:T(8,128)(2,1)S(1)}, bf16[32,4224]{1,0:T(8,128)(2,1)S(1)}, u32[]{:S(2)}, u32[]{:S(2)}) collective-permute-start(bf16[32,4224]{1,0:T(8,128)(2,1)S(1)} %get-tuple-element.459), channel_id=1, source_target_pairs={{0,8},{1,9},{2,10},{3,11},{4,12},{5,13},{6,14},{7,15},{8,0},{9,1},... | collective-permute-start | bytes 811016 | tf_op jit(solution)/shard_map/ppermute | solution.py:135
  312.9 19.0 %collective-permute-start.62 = (bf16[32,4224]{1,0:T(8,128)(2,1)S(1)}, bf16[32,4224]{1,0:T(8,128)(2,1)S(1)}, u32[]{:S(2)}, u32[]{:S(2)}) collective-permute-start(bf16[32,4224]{1,0:T(8,128)(2,1)S(1)} %get-tuple-element.460), channel_id=1, source_target_pairs={{0,16},{1,17},{2,18},{3,19},{4,20},{5,21},{6,22},{7,23},{8,24},{9,... | collective-permute-start | bytes 811016 | tf_op jit(solution)/shard_map/ppermute | solution.py:135
  313.4 24.9 %collective-permute-start.63 = (bf16[32,4224]{1,0:T(8,128)(2,1)S(1)}, bf16[32,4224]{1,0:T(8,128)(2,1)S(1)}, u32[]{:S(2)}, u32[]{:S(2)}) collective-permute-start(bf16[32,4224]{1,0:T(8,128)(2,1)S(1)} %get-tuple-element.461), channel_id=1, source_target_pairs={{0,24},{1,25},{2,26},{3,27},{4,28},{5,29},{6,30},{7,31},{8,16},{9,... | collective-permute-start | bytes 811016 | tf_op jit(solution)/shard_map/ppermute | solution.py:135
  (111 other events, 1455.0 us)
